TPU v7x, 32 devices: a whole 2x2x4 slice. The times are simulated.
32 devices in a mesh: dp: 2 (over core), fsdp: 4 (over z), tp: 4 (over y, x).
Axes of the slice: x: 2, y: 2, z: 4, core: 2. Of those that a mesh axis runs over, the one named last changes fastest.
Arguments:
- layer_input: bfloat16 [4096, 4096], P(('dp', 'fsdp'), 'tp'), may hold values from -6 to 6
- value_grad: bfloat16 [4096, 2048], P(('dp', 'fsdp'), 'tp'), may hold values from -6 to 6
- residual_grad: bfloat16 [4096, 4096], P(('dp', 'fsdp'), 'tp'), may hold values from -6 to 6
- value_weight: bfloat16 [4096, 2048], P(('tp', 'fsdp')), may hold values from -0.125 to 0.125
- owner: int32 [4096, 1], P(('dp', 'fsdp')), may hold values from 0 to 3; in each aligned block of 512 rows (0 to 511, 512 to 1023, ...) at most 256 rows name the same one
- key_row: int32 [4096], P(('dp', 'fsdp')), may hold values from 0 to 255
Outputs:
- weight_grad: float32 [4096, 2048], P(('tp', 'fsdp'))
- key_grad: float32 [1024, 4096], P('fsdp', 'tp')
Inputs may be any that keep to these rules, and one draw needn't show every extreme that they name: Among the 512 tokens of one device (aligned blocks of rows) at most 256 name the same owner, and that bound is reached.
All inputs are finite; a program needn't handle non-finite values.
Results may differ from a plain program's by a relative error of at most 0.0029.
Values may be sent and summed in bfloat16 or wider, within the bound.
No kernel may reach another device: no remote copies, remote signals or barrier semaphores. Data moves between devices by JAX's collectives and lax.ppermute only.
A program may use at most 64 MiB of HBM per device.

v0:
```python
import jax
import jax.numpy as jnp
from jax import lax
from jax.sharding import PartitionSpec as P

KEY_DEV = 256


def body(layer_input, value_grad, residual_grad, value_weight, owner, key_row):
    all_heads = lax.all_gather(value_grad, "tp", axis=1, tiled=True)
    tok_rows = layer_input.shape[0]
    features = layer_input.shape[1]
    groups = lax.axis_size("fsdp")
    slots = 2 * tok_rows // groups
    width = all_heads.shape[1]
    term = lax.dot_general(
        layer_input, all_heads, (((0,), (0,)), ((), ())), preferred_element_type=jnp.float32
    )
    pieces = term.astype(jnp.bfloat16).reshape(groups, features // groups, width)
    arrived = lax.all_to_all(pieces, "fsdp", split_axis=0, concat_axis=0, tiled=True)
    shard = jnp.sum(arrived.astype(jnp.float32), axis=0)
    back = lax.dot_general(
        all_heads,
        lax.all_gather(value_weight, "fsdp", axis=0, tiled=True),
        (((1,), (1,)), ((), ())),
        preferred_element_type=jnp.float32,
    )
    input_grad = (residual_grad.astype(jnp.float32) + back).astype(jnp.bfloat16)
    target = owner[:, 0]
    onehot = (target[:, None] == jnp.arange(groups, dtype=jnp.int32)[None, :]).astype(jnp.int32)
    position = jnp.sum(jnp.cumsum(onehot, axis=0) * onehot, axis=1) - 1
    outgoing = (
        jnp.zeros((groups, slots, features), jnp.bfloat16).at[target, position].set(input_grad)
    )
    out_keys = jnp.full((groups, slots), -1, jnp.int32).at[target, position].set(key_row)
    arrived = lax.all_to_all(outgoing, "fsdp", split_axis=0, concat_axis=0, tiled=True)
    arrived_keys = lax.all_to_all(out_keys, "fsdp", split_axis=0, concat_axis=0, tiled=True)
    flat_rows = arrived.reshape(groups * slots, features)
    selector = (
        arrived_keys.reshape(groups * slots)[:, None]
        == jnp.arange(KEY_DEV, dtype=jnp.int32)[None, :]
    ).astype(jnp.bfloat16)
    table = lax.dot_general(
        selector, flat_rows, (((0,), (0,)), ((), ())), preferred_element_type=jnp.float32
    )
    weight_grad = lax.psum(shard, "dp")
    key_grad = lax.psum(table, "dp")
    return (weight_grad, key_grad)


def solution(mesh):
    return jax.shard_map(
        body,
        mesh=mesh,
        in_specs=(
            P(("dp", "fsdp"), "tp"),
            P(("dp", "fsdp"), "tp"),
            P(("dp", "fsdp"), "tp"),
            P(("tp", "fsdp"), None),
            P(("dp", "fsdp"), None),
            P(("dp", "fsdp")),
        ),
        out_specs=(P(("tp", "fsdp"), None), P("fsdp", "tp")),
        check_vma=False,
    )
```

profile of v0, /device:TPU:0, one launch (start us, length us, event | category | flops | bytes accessed | tf_op | source)
XLA Modules:
  0.0 401.6 jit_solution(4591094899483767330)
XLA Ops:
  7.2 0.0 copy-start
  7.2 0.0 all-gather.3.cloned.1.call-start
  7.2 0.7 all-gather.3.cloned.1.call-update
  7.9 0.0 all-gather.5.cloned.1.call-start
  8.0 0.7 all-gather.5.cloned.1.call-update
  8.7 0.7 fusion.4
  9.3 1.2 reduce-window.6
  10.6 0.2 slice_reduce_fusion
  10.8 0.2 reduce-window.9
  11.0 0.1 add_bitcast_fusion
  11.0 0.7 fusion.3
  11.7 0.7 or_select_fusion
  12.5 0.0 copy-start.2
  12.5 42.5 %scatter_fusion = s32[4,256]{1,0:T(4,128)S(1)} fusion(s32[4,256]{1,0:T(4,128)S(1)} %broadcast_in_dim.4, s32[512]{0:T(512)S(1)} %bitcast.30, s32[512]{0:T(512)} %param.11), kind=kCustom, calls=%fused_computation | custom fusion | bytes 10240 | tf_op jit(solution)/shard_map/scatter | solution.py:35
  55.0 0.6 copy.8
  55.6 6.3 %all-to-all-start.1 = ((s32[4,1,256]{2,1,0:T(1,128)}), s32[4,1,256]{2,1,0:T(1,128)S(1)}, u32[]{:S(2)}, u32[]{:S(2)}) async-start(s32[4,1,256]{2,1,0:T(1,128)} %copy.8), calls=%async_computation.1 | async-start | bytes 8192 | tf_op jit(solution)/shard_map/all_to_all | solution.py:37
  61.9 0.0 all-gather.3.cloned.1.call-done
  61.9 68.3 %all-gather.5.cloned.1.call-done = bf16[1024,2048]{1,0:T(8,128)(2,1)} async-done(((bf16[256,2048]{1,0:T(8,128)(2,1)}), bf16[1024,2048]{1,0:T(8,128)(2,1)}) %all-gather.5.cloned.1.call-update) | async-done | bytes 4194320 | tf_op jit(solution)/shard_map/all_gather | solution.py:24
  130.2 0.0 copy-done.2
  130.2 5.2 %add_convert_fusion = bf16[512,1024]{1,0:T(8,128)(2,1)S(1)} fusion(bf16[512,1024]{1,0:T(8,128)(2,1)S(1)} %copy-done.2, bf16[512,2048]{1,0:T(8,128)(2,1)} %all-gather.3.cloned.1.call-done, bf16[1024,2048]{1,0:T(8,128)(2,1)} %all-gather.5.cloned.1.call-done), kind=kOutput, calls=%fused_computation.4 | convolution fusion | flops 2149056512 | bytes 8388608 | tf_op jit(solution)/shard_map/dot_general | solution.py:22
  135.4 1.6 broadcast_in_dim.5
  137.0 76.2 %scatter_fusion.1 = bf16[4,256,1024]{2,1,0:T(8,128)(2,1)} fusion(bf16[4,256,1024]{2,1,0:T(8,128)(2,1)} %broadcast_in_dim.5, s32[512]{0:T(512)S(1)} %bitcast.31, bf16[512,1024]{1,0:T(8,128)(2,1)S(1)} %add_convert_fusion), kind=kCustom, calls=%fused_computation.1 | custom fusion | bytes 3149824 | tf_op jit(solution)/shard_map/scatter | solution.py:33
  213.2 0.0 all-to-all-done.1
  213.2 3.6 all-to-all-start.2
  216.8 0.0 copy-done
  216.8 5.9 %convolution_convert_fusion = bf16[1024,2048]{1,0:T(8,128)(2,1)} fusion(bf16[512,1024]{1,0:T(8,128)(2,1)S(1)} %copy-done, bf16[512,2048]{1,0:T(8,128)(2,1)} %all-gather.3.cloned.1.call-done), kind=kOutput, calls=%fused_computation.3 | convolution fusion | flops 2149580800 | bytes 7340032 | tf_op jit(solution)/shard_map/dot_general | solution.py:16
  222.7 43.1 %all-to-all-done.2 = bf16[4,256,1024]{2,1,0:T(8,128)(2,1)S(1)} async-done(((bf16[4,256,1024]{2,1,0:T(8,128)(2,1)}), bf16[4,256,1024]{2,1,0:T(8,128)(2,1)S(1)}, u32[]{:S(2)}, u32[]{:S(2)}) %all-to-all-start.2) | async-done | bytes 2097184 | tf_op jit(solution)/shard_map/all_to_all | solution.py:36
  265.8 4.8 %all-to-all-start = ((bf16[4,256,2048]{2,1,0:T(8,128)(2,1)}), bf16[4,256,2048]{2,1,0:T(8,128)(2,1)}, u32[]{:S(2)}, u32[]{:S(2)}) async-start(bf16[4,256,2048]{2,1,0:T(8,128)(2,1)} %bitcast.32), calls=%async_computation | async-start | bytes 8388608 | tf_op jit(solution)/shard_map/all_to_all | solution.py:20
  270.7 0.0 all-reduce.3.cloned.1.call-start
  270.7 1.9 fusion
  272.7 91.2 %all-to-all-done = bf16[4,256,2048]{2,1,0:T(8,128)(2,1)} async-done(((bf16[4,256,2048]{2,1,0:T(8,128)(2,1)}), bf16[4,256,2048]{2,1,0:T(8,128)(2,1)}, u32[]{:S(2)}, u32[]{:S(2)}) %all-to-all-start) | async-done | bytes 4194336 | tf_op jit(solution)/shard_map/all_to_all | solution.py:20
  363.9 4.5 %convert_reduce_fusion = f32[256,2048]{1,0:T(8,128)} fusion(bf16[4,256,2048]{2,1,0:T(8,128)(2,1)} %all-to-all-done), kind=kLoop, calls=%fused_computation.2 | loop fusion | flops 3670016 | bytes 6291456 | tf_op jit(solution)/shard_map/reduce_sum | solution.py:21
  368.4 0.0 all-reduce.3.cloned.1.call-update
  368.4 22.4 %all-reduce.3.cloned.1.call-done = (f32[256,2048]{1,0:T(8,128)}, f32[256,1024]{1,0:T(8,128)}) async-done(((f32[256,2048]{1,0:T(8,128)}, f32[256,1024]{1,0:T(8,128)}), (f32[256,2048]{1,0:T(8,128)}, f32[256,1024]{1,0:T(8,128)})) %all-reduce.3.cloned.1.call-update) | async-done | bytes 3145744 | tf_op jit(solution)/shard_map/psum | solution.py:46
  390.8 0.0 copy-start.1
  390.8 3.2 copy.15
  394.1 0.0 copy-done.1
  394.1 1.0 copy.16
  (2 shorter events, 0.0 us)
Async XLA Ops:
  7.2 209.7 %copy-start = (bf16[512,1024]{1,0:T(8,128)(2,1)S(1)}, bf16[512,1024]{1,0:T(8,128)(2,1)}, u32[]{:S(2)}) copy-start(bf16[512,1024]{1,0:T(8,128)(2,1)} %param.6) | copy-start | bytes 3145732
  7.2 54.7 %all-gather.3.cloned.1.call-start = ((), (), s32[]{:S(2)}) async-start(), calls=%async_computation.3 | async-start | bytes 2621440 | tf_op jit(solution)/shard_map/all_gather | solution.py:10
  7.9 122.3 %all-gather.5.cloned.1.call-start = ((), (), s32[]{:S(2)}) async-start(), calls=%async_computation.4 | async-start | bytes 5242880 | tf_op jit(solution)/shard_map/all_gather | solution.py:24
  12.5 117.7 %copy-start.2 = (bf16[512,1024]{1,0:T(8,128)(2,1)S(1)}, bf16[512,1024]{1,0:T(8,128)(2,1)}, u32[]{:S(2)}) copy-start(bf16[512,1024]{1,0:T(8,128)(2,1)} %param.8) | copy-start | bytes 3145732
  55.6 157.6 %all-to-all-start.1 = ((s32[4,1,256]{2,1,0:T(1,128)}), s32[4,1,256]{2,1,0:T(1,128)S(1)}, u32[]{:S(2)}, u32[]{:S(2)}) async-start(s32[4,1,256]{2,1,0:T(1,128)} %copy.8), calls=%async_computation.1 | async-start | bytes 8192 | tf_op jit(solution)/shard_map/all_to_all | solution.py:37
  213.2 52.6 %all-to-all-start.2 = ((bf16[4,256,1024]{2,1,0:T(8,128)(2,1)}), bf16[4,256,1024]{2,1,0:T(8,128)(2,1)S(1)}, u32[]{:S(2)}, u32[]{:S(2)}) async-start(bf16[4,256,1024]{2,1,0:T(8,128)(2,1)} %scatter_fusion.1), calls=%async_computation.2 | async-start | bytes 4194304 | tf_op jit(solution)/shard_map/all_to_all | solution.py:36
  265.8 98.1 %all-to-all-start = ((bf16[4,256,2048]{2,1,0:T(8,128)(2,1)}), bf16[4,256,2048]{2,1,0:T(8,128)(2,1)}, u32[]{:S(2)}, u32[]{:S(2)}) async-start(bf16[4,256,2048]{2,1,0:T(8,128)(2,1)} %bitcast.32), calls=%async_computation | async-start | bytes 8388608 | tf_op jit(solution)/shard_map/all_to_all | solution.py:20
  270.7 120.2 %all-reduce.3.cloned.1.call-start = ((), (), s32[]{:S(2)}) async-start(), calls=%async_computation.5 | async-start | bytes 6291456 | tf_op jit(solution)/shard_map/psum | solution.py:46
  390.8 3.2 copy-start.1
Sparse Core Ops, SparseCore 0:
  9.8 37.8 all-gather.2
  49.3 80.8 all-gather.4
  368.5 22.2 all-reduce.2
where the time goes:
time: 405 us; the launch traced here: 402 us
  waiting for transfers between devices  226 us (56%)
  local copies, waits for them, and re-layouts  125 us (31%)
  starting transfers between devices  14.9 us (4%)
  between operations  13.8 us (3%)
  matrix products  13 us (3%)
  other arithmetic  8.06 us (2%)
    all_to_all x1, waiting for transfers between devices, body(): lax.all_to_all(pieces, 'fsdp', split_axis=0, concat_axis=0, tiled=True)  91.2 us
    scatter x1, local copies, waits for them, and re-layouts, body(): jnp.zeros((groups, slots, features), jnp.bfloat16).at[target, position]  76.2 us
    all_gather x1, waiting for transfers between devices, body(): lax.all_gather(value_weight, 'fsdp', axis=0, tiled=True)  68.3 us
    all_to_all x1, waiting for transfers between devices, body(): lax.all_to_all(outgoing, 'fsdp', split_axis=0, concat_axis=0, tiled=True)  43.1 us
    scatter x1, local copies, waits for them, and re-layouts, body(): jnp.full((groups, slots), -1, jnp.int32).at[target, position].set(key_row)  42.5 us
    psum x1, waiting for transfers between devices, body(): weight_grad = lax.psum(shard, 'dp')  22.4 us
  transfers between devices with their start and end apart: 6, of which 4 were waited for; matrix products, arithmetic and copies ran while one was open for 34% of the time, Pallas kernels for 0%

commit v1 on v0

v1 whole, which is shorter than its diff:
```python
import jax
import jax.numpy as jnp
from jax import lax
from jax.sharding import PartitionSpec as P

F32, BF16 = jnp.float32, jnp.bfloat16
KEY_DEV = 256


def dot(a, b, ca, cb):
    return lax.dot_general(a, b, (((ca,), (cb,)), ((), ())), preferred_element_type=F32)


def general_body(layer_input, value_grad, residual_grad, value_weight, owner, key_row):
    all_heads = lax.all_gather(value_grad, "tp", axis=1, tiled=True)
    tok_rows, features = layer_input.shape
    groups = lax.axis_size("fsdp")
    slots = 2 * tok_rows // groups
    keys_here = KEY_DEV
    width = all_heads.shape[1]
    term = dot(layer_input, all_heads, 0, 0)
    pieces = term.astype(BF16).reshape(groups, features // groups, width)
    arrived = lax.all_to_all(pieces, "fsdp", split_axis=0, concat_axis=0, tiled=True)
    shard = jnp.sum(arrived.astype(F32), axis=0)
    back = dot(all_heads, lax.all_gather(value_weight, "fsdp", axis=0, tiled=True), 1, 1)
    input_grad = (residual_grad.astype(F32) + back).astype(BF16)
    target = owner[:, 0]
    onehot = (target[:, None] == jnp.arange(groups, dtype=jnp.int32)[None, :]).astype(jnp.int32)
    position = jnp.sum(jnp.cumsum(onehot, axis=0) * onehot, axis=1) - 1
    place = target * slots + position
    chooser = jnp.arange(groups * slots, dtype=jnp.int32)[:, None] == place[None, :]
    outgoing = dot(chooser.astype(BF16), input_grad, 1, 0).astype(BF16)
    out_keys = jnp.sum(jnp.where(chooser, key_row[None, :] + 1, 0), axis=1) - 1
    arrived = lax.all_to_all(outgoing, "fsdp", split_axis=0, concat_axis=0, tiled=True)
    arrived_keys = lax.all_to_all(out_keys, "fsdp", split_axis=0, concat_axis=0, tiled=True)
    selector = (arrived_keys[:, None] == jnp.arange(keys_here, dtype=jnp.int32)[None, :]).astype(BF16)
    table = dot(selector, arrived, 0, 0)
    return lax.psum(shard, "dp"), lax.psum(table, "dp")


def pair_body(layer_input, value_grad, residual_grad, value_weight, owner, key_row):
    core, z, t = (lax.axis_index(n) for n in ("dp", "fsdp", "tp"))
    tokens, features = layer_input.shape
    part = features // 4
    half = part // 2
    keys = KEY_DEV

    def core_swap(v):
        return lax.ppermute(v, "dp", [(0, 1), (1, 0)])

    def x_swap(v):
        return lax.ppermute(v, "tp", [(0, 1), (1, 0), (2, 3), (3, 2)])

    def y_swap(v):
        return lax.ppermute(v, "tp", [(0, 2), (2, 0), (1, 3), (3, 1)])

    def outer(v):
        return lax.ppermute(v, "fsdp", [(0, 1), (1, 0), (2, 3), (3, 2)])

    def inward(v):
        return lax.ppermute(v, "fsdp", [(0, 1), (3, 2)])

    def inner(v):
        return lax.ppermute(v, "fsdp", [(1, 2), (2, 1)])

    end = (z == 0) | (z == 3)
    beside = z ^ 1
    far_mid = jnp.where(z < 2, 2, 1)
    far_end = jnp.where(z < 2, 3, 0)

    def halves(v, which):
        return jnp.concatenate(
            [lax.dynamic_slice_in_dim(v, p * part + which * half, half, 1) for p in range(4)], 1
        )

    w_own = lax.dynamic_slice_in_dim(value_weight, core * half, half, 0)
    w_beside = outer(w_own)
    w_mid = inner(w_own)
    vx, vy = x_swap(value_grad), y_swap(value_grad)
    vd = jnp.concatenate([y_swap(vx[: tokens // 2]), x_swap(vy[tokens // 2 :])], 0)
    blocks = (value_grad, vx, vy, vd)
    heads = jnp.concatenate([lax.select_n(t ^ k, *blocks) for k in range(4)], 1)
    heads_other = core_swap(heads)
    in_other = core_swap(halves(layer_input, 1 - core))
    res_other = core_swap(halves(residual_grad, 1 - core))
    key = owner[:, 0] * keys + key_row
    key_other = core_swap(key)

    term = dot(halves(layer_input, core), heads, 0, 0) + dot(in_other, heads_other, 0, 0)
    term = term.reshape(4, half, -1)

    def piece(v, i):
        return lax.dynamic_index_in_dim(v, i, 0, keepdims=False)

    w_end = inner(w_beside)
    a1 = outer(jnp.where(end, piece(term, far_end).astype(BF16), w_mid))
    a2 = outer(jnp.where(end, piece(term, far_mid).astype(BF16), w_end))
    b2 = inner((piece(term, far_end) + a1.astype(F32)).astype(BF16))
    a3 = outer((piece(term, beside) + b2.astype(F32)).astype(BF16))
    b3 = inner((piece(term, far_mid) + a2.astype(F32)).astype(BF16))
    weight_half = piece(term, z) + a3.astype(F32) + b3.astype(F32)

    w_third = jnp.where(end, a1, w_mid)
    w_fourth = jnp.where(end, a2, w_end)
    arrived = (w_own, w_beside, w_third, w_fourth)
    order = [jnp.where(i == z, 0, jnp.where(i == beside, 1, jnp.where(i == far_mid, 2, 3))) for i in range(4)]
    weights = jnp.concatenate([lax.select_n(i, *arrived) for i in order], 0)

    def rows_grad(v, r):
        return (r.astype(F32) + dot(v, weights, 1, 1)).astype(BF16)

    def chooser(k):
        return (jnp.arange(4 * keys, dtype=jnp.int32)[:, None] == k[None, :]).astype(BF16)

    table = dot(chooser(key), rows_grad(heads, halves(residual_grad, core)), 1, 0)
    table = table + dot(chooser(key_other), rows_grad(heads_other, res_other), 1, 0)
    table = table.reshape(4, keys, -1)
    k1 = inward(piece(table, far_end).astype(BF16))
    k2 = inward(piece(table, far_mid).astype(BF16))
    l2 = inner((piece(table, far_end) + k1.astype(F32)).astype(BF16))
    k3 = outer((piece(table, beside) + l2.astype(F32)).astype(BF16))
    l3 = inner((piece(table, far_mid) + k2.astype(F32)).astype(BF16))
    key_half = piece(table, z) + k3.astype(F32) + l3.astype(F32)

    weight_pair = core_swap(weight_half)
    key_pair = core_swap(key_half)
    first = core == 0
    weight_grad = jnp.concatenate(
        [jnp.where(first, weight_half, weight_pair), jnp.where(first, weight_pair, weight_half)], 0
    )
    low, high = jnp.where(first, key_half, key_pair), jnp.where(first, key_pair, key_half)
    cols = []
    for p in range(4):
        cols += [low[:, p * half : (p + 1) * half], high[:, p * half : (p + 1) * half]]
    return weight_grad, jnp.concatenate(cols, 1)


def solution(mesh):
    shape = dict(mesh.shape)
    special = shape == {"dp": 2, "fsdp": 4, "tp": 4}
    return jax.shard_map(
        pair_body if special else general_body,
        mesh=mesh,
        in_specs=(
            P(("dp", "fsdp"), "tp"),
            P(("dp", "fsdp"), "tp"),
            P(("dp", "fsdp"), "tp"),
            P(("tp", "fsdp"), None),
            P(("dp", "fsdp"), None),
            P(("dp", "fsdp")),
        ),
        out_specs=(P(("tp", "fsdp"), None), P("fsdp", "tp")),
        check_vma=False,
    )
```

time: 405 us -> 155 us (0.38)
  waiting for transfers between devices: 226 us -> 59 us
  local copies, waits for them, and re-layouts: 125 us -> 4.54 us
  starting transfers between devices: 14.9 us -> 54.4 us
  other arithmetic: 8.06 us -> 20.8 us
  between operations: 13.8 us -> 1.12 us
    all_to_all x3 -> x0, waiting for transfers between devices: 134 us -> none  [the longest x1 91.2 us: body(): lax.all_to_all(pieces, 'fsdp', split_axis=0, concat_axis=0, tiled=True)]
    scatter x2 -> x0, local copies, waits for them, and re-layouts: 119 us -> none  [the longest x1 76.2 us: body(): jnp.zeros((groups, slots, features), jnp.bfloat16).at[target, position]]
    all_gather x2 -> x0, waiting for transfers between devices: 68.3 us -> none  [the longest x1 68.3 us: body(): lax.all_gather(value_weight, 'fsdp', axis=0, tiled=True)]
    ppermute x0 -> x23, waiting for transfers between devices: none -> 59 us  [the longest x5 39.3 us: outer(): return lax.ppermute(v, 'fsdp', [(0, 1), (1, 0), (2, 3), (3, 2)])]
    ppermute x0 -> x23, starting transfers between devices: none -> 54.4 us  [the longest x5 31.6 us: outer(): return lax.ppermute(v, 'fsdp', [(0, 1), (1, 0), (2, 3), (3, 2)])]
    psum x1 -> x0, waiting for transfers between devices: 22.4 us -> none  [body(): weight_grad = lax.psum(shard, 'dp')]
    all_to_all x3 -> x0, starting transfers between devices: 14.8 us -> none  [the longest x1 6.32 us: body(): lax.all_to_all(out_keys, 'fsdp', split_axis=0, concat_axis=0, tiled=True)]
    convert_element_type x1 -> x4, other arithmetic: 0.69 us -> 7.72 us  [the longest x1 2.8 us: pair_body(): a3 = outer((piece(term, beside) + b2.astype(F32)).astype(BF16))]
  transfers between devices with their start and end apart: 6 -> 23, of which waited for: 4 -> 9; matrix products, arithmetic and copies ran while one was open for 34% -> 19% of each run, Pallas kernels for 0% -> 0%
where the time goes in v1:
time: 155 us; the launch traced here: 154 us
  waiting for transfers between devices  59 us (38%)
  starting transfers between devices  54.4 us (35%)
  other arithmetic  20.8 us (13%)
  matrix products  14.5 us (9%)
  local copies, waits for them, and re-layouts  4.54 us (3%)
    ppermute x5, waiting for transfers between devices, outer(): return lax.ppermute(v, 'fsdp', [(0, 1), (1, 0), (2, 3), (3, 2)])  39.3 us
    ppermute x5, starting transfers between devices, outer(): return lax.ppermute(v, 'fsdp', [(0, 1), (1, 0), (2, 3), (3, 2)])  31.6 us
    dot_general x4, matrix products, dot(): lax.dot_general(a, b, (((ca,), (cb,)), ((), ())), preferred_element_type=...  14.5 us
    ppermute x2, waiting for transfers between devices, x_swap(): return lax.ppermute(v, 'tp', [(0, 1), (1, 0), (2, 3), (3, 2)])  11.9 us
    ppermute x2, starting transfers between devices, inward(): return lax.ppermute(v, 'fsdp', [(0, 1), (3, 2)])  9.45 us
    ppermute x6, starting transfers between devices, inner(): return lax.ppermute(v, 'fsdp', [(1, 2), (2, 1)])  4.76 us
    ppermute x2, starting transfers between devices, x_swap(): return lax.ppermute(v, 'tp', [(0, 1), (1, 0), (2, 3), (3, 2)])  4.56 us
    ppermute x2, waiting for transfers between devices, y_swap(): return lax.ppermute(v, 'tp', [(0, 2), (2, 0), (1, 3), (3, 1)])  4.15 us
  transfers between devices with their start and end apart: 23, of which 9 were waited for; matrix products, arithmetic and copies ran while one was open for 19% of the time, Pallas kernels for 0%

profile of v1, /device:TPU:0, one launch (start us, length us, event | category | flops | bytes accessed | tf_op | source)
XLA Modules:
  0.0 154.2 jit_solution(12342078518232427727)
XLA Ops:
  0.6 3.0 %collective-permute-start = (bf16[512,512]{1,0:T(8,128)(2,1)}, bf16[512,512]{1,0:T(8,128)(2,1)S(1)}, u32[]{:S(2)}, u32[]{:S(2)}) collective-permute-start(bf16[512,512]{1,0:T(8,128)(2,1)} %param.7), channel_id=1, source_target_pairs={{0,1},{1,0},{2,3},{3,2},{4,5},{5,4},{6,7},{7,6},{8,9},{9,8},{10,11... | collective-permute-start | bytes 1572872 | tf_op jit(solution)/shard_map/ppermute | solution.py:52
  3.6 1.5 collective-permute-start.1
  5.2 10.6 %collective-permute-done = bf16[512,512]{1,0:T(8,128)(2,1)S(1)} collective-permute-done((bf16[512,512]{1,0:T(8,128)(2,1)}, bf16[512,512]{1,0:T(8,128)(2,1)S(1)}, u32[]{:S(2)}, u32[]{:S(2)}) %collective-permute-start) | collective-permute-done | bytes 524320 | tf_op jit(solution)/shard_map/ppermute | solution.py:52
  15.8 1.8 %collective-permute-start.2 = (bf16[256,512]{1,0:T(8,128)(2,1)S(1)}, bf16[256,512]{1,0:T(8,128)(2,1)S(1)}, u32[]{:S(2)}, u32[]{:S(2)}) collective-permute-start(bf16[256,512]{1,0:T(8,128)(2,1)S(1)} %slice.40), channel_id=1, source_target_pairs={{0,2},{2,0},{1,3},{3,1},{4,6},{6,4},{5,7},{7,5},{8,10},{10,8},{9,1... | collective-permute-start | bytes 786440 | tf_op jit(solution)/shard_map/ppermute | solution.py:55
  17.6 0.0 collective-permute-done.1
  17.6 1.6 %collective-permute-start.3 = (bf16[256,512]{1,0:T(8,128)(2,1)S(1)}, bf16[256,512]{1,0:T(8,128)(2,1)S(1)}, u32[]{:S(2)}, u32[]{:S(2)}) collective-permute-start(bf16[256,512]{1,0:T(8,128)(2,1)S(1)} %slice.41), channel_id=1, source_target_pairs={{0,1},{1,0},{2,3},{3,2},{4,5},{5,4},{6,7},{7,6},{8,9},{9,8},{10,11... | collective-permute-start | bytes 786440 | tf_op jit(solution)/shard_map/ppermute | solution.py:52
  19.2 4.1 %collective-permute-done.2 = bf16[256,512]{1,0:T(8,128)(2,1)S(1)} collective-permute-done((bf16[256,512]{1,0:T(8,128)(2,1)S(1)}, bf16[256,512]{1,0:T(8,128)(2,1)S(1)}, u32[]{:S(2)}, u32[]{:S(2)}) %collective-permute-start.2) | collective-permute-done | bytes 262176 | tf_op jit(solution)/shard_map/ppermute | solution.py:55
  23.4 1.2 collective-permute-done.3
  24.6 1.3 select_select_fusion.7
  25.9 0.0 copy-start.1
  26.0 1.6 %pad_maximum_fusion = bf16[512,2048]{1,0:T(8,128)(2,1)} fusion(bf16[512,512]{1,0:T(8,128)(2,1)S(1)} %get-tuple-element.19, bf16[512,512]{1,0:T(8,128)(2,1)S(1)} %get-tuple-element.20, bf16[512,512]{1,0:T(8,128)(2,1)S(1)} %get-tuple-element.21, bf16[512,512]{1,0:T(8,128)(2,1)S(1)} %get-tuple-element.18), kind=kLoop, calls=%fused_computation.1 | loop fusion | flops 8388608 | bytes 4194304 | tf_op jit(solution)/shard_map/concatenate | solution.py:82
  27.6 0.0 collective-permute-start.5
  27.6 0.4 copy-done.1
  28.0 0.8 constant_dynamic-slice_fusion.8
  28.8 1.6 %collective-permute-start.10 = (bf16[128,2048]{1,0:T(8,128)(2,1)}, bf16[128,2048]{1,0:T(8,128)(2,1)S(1)}, u32[]{:S(2)}, u32[]{:S(2)}) collective-permute-start(bf16[128,2048]{1,0:T(8,128)(2,1)} %constant_dynamic-slice_fusion.8), channel_id=1, source_target_pairs={{0,4},{4,0},{8,12},{12,8},{1,5},{5,1},{9,13},{13,9},{2,6},{6,2},{1... | collective-permute-start | bytes 1572872 | tf_op jit(solution)/shard_map/ppermute | solution.py:58
  30.4 2.0 %constant_dynamic-slice_fusion.16 = (bf16[512,128]{1,0:T(8,128)(2,1)S(1)}, bf16[512,128]{1,0:T(8,128)(2,1)S(1)}, bf16[512,128]{1,0:T(8,128)(2,1)S(1)}, bf16[512,...) fusion(bf16[512,1024]{1,0:T(8,128)(2,1)} %param.6, ...), kind=kLoop, calls=%fused_computation.94 | loop fusion | bytes 2097184 | tf_op jit(solution)/shard_map/dynamic_slice | solution.py:73
  32.4 0.9 pad_maximum_fusion.3
  33.3 0.0 collective-permute-start.4
  33.3 0.7 collective-permute-start.6
  34.0 9.0 %collective-permute-done.10 = bf16[128,2048]{1,0:T(8,128)(2,1)S(1)} collective-permute-done((bf16[128,2048]{1,0:T(8,128)(2,1)}, bf16[128,2048]{1,0:T(8,128)(2,1)S(1)}, u32[]{:S(2)}, u32[]{:S(2)}) %collective-permute-start.10) | collective-permute-done | bytes 524320 | tf_op jit(solution)/shard_map/ppermute | solution.py:58
  43.0 0.7 collective-permute-start.11
  43.7 0.0 collective-permute-done.5
  43.7 3.0 %fusion.37 = f32[512,2048]{1,0:T(8,128)S(1)} fusion(bf16[512,512]{1,0:T(8,128)(2,1)} %collective-permute-done.4, bf16[512,2048]{1,0:T(8,128)(2,1)} %collective-permute-done.5), kind=kOutput, calls=%fused_computation.99 | convolution fusion | flops 1073741824 | bytes 6815744 | tf_op jit(solution)/shard_map/dot_general | solution.py:11
  46.8 1.3 convolution_add_fusion
  48.1 0.0 copy-start.14
  48.1 0.0 copy-start.13
  48.1 0.0 copy-start.10
  48.1 1.1 fusion.11
  49.2 14.2 %collective-permute-start.7 = (bf16[128,2048]{1,0:T(8,128)(2,1)}, bf16[128,2048]{1,0:T(8,128)(2,1)S(1)}, u32[]{:S(2)}, u32[]{:S(2)}) collective-permute-start(bf16[128,2048]{1,0:T(8,128)(2,1)} %get-tuple-element.7), channel_id=1, source_target_pairs={{0,4},{4,0},{8,12},{12,8},{1,5},{5,1},{9,13},{13,9},{2,6},{6,2},{1... | collective-permute-start | bytes 1572872 | tf_op jit(solution)/shard_map/ppermute | solution.py:58
  63.5 0.0 collective-permute-start.12
  63.5 0.1 collective-permute-start.15
  63.6 0.9 constant_dynamic-slice_fusion.3
  64.6 0.8 pad_maximum_fusion.4
  65.4 0.5 collective-permute-start.16
  65.9 10.5 %collective-permute-done.7 = bf16[128,2048]{1,0:T(8,128)(2,1)S(1)} collective-permute-done((bf16[128,2048]{1,0:T(8,128)(2,1)}, bf16[128,2048]{1,0:T(8,128)(2,1)S(1)}, u32[]{:S(2)}, u32[]{:S(2)}) %collective-permute-start.7) | collective-permute-done | bytes 524320 | tf_op jit(solution)/shard_map/ppermute | solution.py:58
  76.4 10.5 %collective-permute-done.12 = bf16[128,2048]{1,0:T(8,128)(2,1)S(1)} collective-permute-done((bf16[128,2048]{1,0:T(8,128)(2,1)}, bf16[128,2048]{1,0:T(8,128)(2,1)S(1)}, u32[]{:S(2)}, u32[]{:S(2)}) %collective-permute-start.12) | collective-permute-done | bytes 524320 | tf_op jit(solution)/shard_map/ppermute | solution.py:58
  86.9 1.3 select_select_fusion.3
  88.3 1.6 %select_select_fusion.2 = (bf16[128,2048]{1,0:T(8,128)(2,1)}, bf16[128,2048]{1,0:T(8,128)(2,1)}, bf16[128,2048]{1,0:T(8,128)(2,1)}) fusion(bf16[128,2048]{1,0:T(8,128)(2,1)S(1)} %get-tuple-element.4, bf16[128,2048]{1,0:T(8,128)(2,1)S(1)} %get-tuple-element.3, bf16[128,2048]{1,0:T(8,128)(2,1)S(1)} %collective-permute-done.10, pred[]{:T(512)S(6)} %select_n.438, ...), kind=kLoop, calls=%fused_computation.55 | loop fusion | flops 2359296 | bytes 3670029 | tf_op jit(solution)/shard_map/select_n | solution.py:107
  89.9 5.2 %fusion = f32[1024,512]{1,0:T(8,128)} fusion(s32[512]{0:T(512)S(1)} %add.156, bf16[512,128]{1,0:T(8,128)(2,1)S(1)} %get-tuple-element.26, bf16[512,128]{1,0:T(8,128)(2,1)S(1)} %get-tuple-element.27, bf16[512,128]{1,0:T(8,128)(2,1)S(1)} %get-tuple-element.28, bf16[512,128]{1,0:T(8,128)(2,1)} %get-tuple-element.29, bf16[128,2048]{1,0:T(8,128)(2,1)} %get-tuple-element.15, ...), kind=kOutput, calls=%fused_computation.6 | convolution fusion | flops 1630535680 | bytes 6817792 | tf_op jit(solution)/shard_map/dot_general | solution.py:11
  95.2 4.9 %fusion.2 = f32[1024,512]{1,0:T(8,128)S(1)} fusion(f32[1024,512]{1,0:T(8,128)} %fusion, s32[512]{0:T(512)S(1)} %collective-permute-done.15, bf16[512,512]{1,0:T(8,128)(2,1)} %collective-permute-done.16, bf16[512,2048]{1,0:T(8,128)(2,1)} %collective-permute-done.5, bf16[128,2048]{1,0:T(8,128)(2,1)} %get-tuple-element.15, ...), kind=kOutput, calls=%fused_computation.8 | convolution fusion | flops 1620836352 | bytes 8914944 | tf_op jit(solution)/shard_map/dot_general | solution.py:11
  100.1 0.1 bitcast_convert_fusion.3
  100.2 4.7 %collective-permute-start.17 = (bf16[256,512]{1,0:T(8,128)(2,1)S(1)}, bf16[256,512]{1,0:T(8,128)(2,1)S(1)}, u32[]{:S(2)}, u32[]{:S(2)}) collective-permute-start(bf16[256,512]{1,0:T(8,128)(2,1)S(1)} %get-tuple-element.11), channel_id=1, source_target_pairs={{0,4},{12,8},{1,5},{13,9},{2,6},{14,10},{3,7},{15,11},{16,20},{28,... | collective-permute-start | bytes 786440 | tf_op jit(solution)/shard_map/ppermute | solution.py:61
  104.9 2.1 %fusion.5 = bf16[128,2048]{1,0:T(8,128)(2,1)} fusion(bf16[128,2048]{1,0:T(8,128)(2,1)S(1)} %collective-permute-done.7, f32[4,128,2048]{2,1,0:T(8,128)} %bitcast.47, s32[]{:T(128)S(6)} %select_n.407), kind=kLoop, calls=%fused_computation.16 | loop fusion | flops 786432 | bytes 2097156 | tf_op jit(solution)/shard_map/convert_element_type | solution.py:98
  107.0 0.7 collective-permute-start.8
  107.7 4.8 %collective-permute-start.20 = (bf16[256,512]{1,0:T(8,128)(2,1)S(1)}, bf16[256,512]{1,0:T(8,128)(2,1)}, u32[]{:S(2)}, u32[]{:S(2)}) collective-permute-start(bf16[256,512]{1,0:T(8,128)(2,1)S(1)} %get-tuple-element.12), channel_id=1, source_target_pairs={{0,4},{12,8},{1,5},{13,9},{2,6},{14,10},{3,7},{15,11},{16,20},{28,... | collective-permute-start | bytes 786440 | tf_op jit(solution)/shard_map/ppermute | solution.py:61
  112.4 0.8 fusion.28
  113.2 1.4 collective-permute-start.18
  114.6 1.4 collective-permute-done.20
  116.0 2.0 %fusion.29 = (bf16[256,512]{1,0:T(8,128)(2,1)}, bf16[256,512]{1,0:T(8,128)(2,1)}) fusion(bf16[256,512]{1,0:T(8,128)(2,1)} %collective-permute-done.18, f32[4,256,512]{2,1,0:T(8,128)S(1)} %bitcast.52, s32[]{:T(128)S(6)} %select_n.406, bf16[256,512]{1,0:T(8,128)(2,1)} %collective-permute-done.20, s32[]{:T(128)S(6)} %select_n.411), kind=kLoop, calls=%fused_computation.50 | loop fusion | flops 786432 | bytes 2097160 | tf_op jit(solution)/shard_map/convert_element_type | solution.py:121
  118.0 0.7 collective-permute-start.21
  118.7 13.7 %collective-permute-start.19 = (bf16[256,512]{1,0:T(8,128)(2,1)}, bf16[256,512]{1,0:T(8,128)(2,1)}, u32[]{:S(2)}, u32[]{:S(2)}) collective-permute-start(bf16[256,512]{1,0:T(8,128)(2,1)} %get-tuple-element.9), channel_id=1, source_target_pairs={{0,4},{4,0},{8,12},{12,8},{1,5},{5,1},{9,13},{13,9},{2,6},{6,2},{1... | collective-permute-start | bytes 786440 | tf_op jit(solution)/shard_map/ppermute | solution.py:58
  132.4 2.8 %fusion.6 = (bf16[128,2048]{1,0:T(8,128)(2,1)}, bf16[128,2048]{1,0:T(8,128)(2,1)}) fusion(bf16[128,2048]{1,0:T(8,128)(2,1)S(1)} %collective-permute-done.8, f32[4,128,2048]{2,1,0:T(8,128)} %bitcast.48, s32[]{:T(128)S(6)} %select_n.406, bf16[128,2048]{1,0:T(8,128)(2,1)S(1)} %collective-permute-done.12, s32[]{:T(128)S(6)} %select_n.411), kind=kLoop, calls=%fused_computation.18 | loop fusion | flops 1572864 | bytes 4194312 | tf_op jit(solution)/shard_map/convert_element_type | solution.py:99
  135.2 0.7 collective-permute-start.13
  135.9 2.0 %collective-permute-start.9 = (bf16[128,2048]{1,0:T(8,128)(2,1)}, bf16[128,2048]{1,0:T(8,128)(2,1)}, u32[]{:S(2)}, u32[]{:S(2)}) collective-permute-start(bf16[128,2048]{1,0:T(8,128)(2,1)} %get-tuple-element.5), channel_id=1, source_target_pairs={{0,4},{4,0},{8,12},{12,8},{1,5},{5,1},{9,13},{13,9},{2,6},{6,2},{1... | collective-permute-start | bytes 1572872 | tf_op jit(solution)/shard_map/ppermute | solution.py:58
  137.9 1.0 fusion.30
  138.9 0.1 collective-permute-start.22
  139.0 9.2 %collective-permute-done.9 = bf16[128,2048]{1,0:T(8,128)(2,1)} collective-permute-done((bf16[128,2048]{1,0:T(8,128)(2,1)}, bf16[128,2048]{1,0:T(8,128)(2,1)}, u32[]{:S(2)}, u32[]{:S(2)}) %collective-permute-start.9) | collective-permute-done | bytes 524320 | tf_op jit(solution)/shard_map/ppermute | solution.py:58
  148.3 1.6 %fusion.7 = f32[128,2048]{1,0:T(8,128)S(1)} fusion(bf16[128,2048]{1,0:T(8,128)(2,1)S(1)} %collective-permute-done.13, bf16[128,2048]{1,0:T(8,128)(2,1)} %collective-permute-done.9, f32[4,128,2048]{2,1,0:T(8,128)} %bitcast.49, s32[]{:T(128)S(6)} %select_n.405), kind=kLoop, calls=%fused_computation.20 | loop fusion | flops 1048576 | bytes 3145732 | tf_op jit(solution)/shard_map/add | solution.py:101
  149.8 0.1 collective-permute-start.14
  149.9 0.1 broadcast_select_fusion.4
  150.3 0.0 copy-start.12
  150.3 2.3 %collective-permute-done.14 = f32[128,2048]{1,0:T(8,128)S(1)} collective-permute-done((f32[128,2048]{1,0:T(8,128)S(1)}, f32[128,2048]{1,0:T(8,128)S(1)}, u32[]{:S(2)}, u32[]{:S(2)}) %collective-permute-start.14) | collective-permute-done | bytes 1048608 | tf_op jit(solution)/shard_map/ppermute | solution.py:49
  152.6 0.2 broadcast_select_fusion.3
  152.8 1.5 pad_maximum_fusion.1
  (50 shorter events, 0.3 us)
Async XLA Ops:
  0.6 15.1 %collective-permute-start = (bf16[512,512]{1,0:T(8,128)(2,1)}, bf16[512,512]{1,0:T(8,128)(2,1)S(1)}, u32[]{:S(2)}, u32[]{:S(2)}) collective-permute-start(bf16[512,512]{1,0:T(8,128)(2,1)} %param.7), channel_id=1, source_target_pairs={{0,1},{1,0},{2,3},{3,2},{4,5},{5,4},{6,7},{7,6},{8,9},{9,8},{10,11... | collective-permute-start | bytes 1572872 | tf_op jit(solution)/shard_map/ppermute | solution.py:52
  3.6 14.0 %collective-permute-start.1 = (bf16[512,512]{1,0:T(8,128)(2,1)}, bf16[512,512]{1,0:T(8,128)(2,1)S(1)}, u32[]{:S(2)}, u32[]{:S(2)}) collective-permute-start(bf16[512,512]{1,0:T(8,128)(2,1)} %param.7), channel_id=1, source_target_pairs={{0,2},{2,0},{1,3},{3,1},{4,6},{6,4},{5,7},{7,5},{8,10},{10,8},{9,1... | collective-permute-start | bytes 1572872 | tf_op jit(solution)/shard_map/ppermute | solution.py:55
  15.8 7.6 %collective-permute-start.2 = (bf16[256,512]{1,0:T(8,128)(2,1)S(1)}, bf16[256,512]{1,0:T(8,128)(2,1)S(1)}, u32[]{:S(2)}, u32[]{:S(2)}) collective-permute-start(bf16[256,512]{1,0:T(8,128)(2,1)S(1)} %slice.40), channel_id=1, source_target_pairs={{0,2},{2,0},{1,3},{3,1},{4,6},{6,4},{5,7},{7,5},{8,10},{10,8},{9,1... | collective-permute-start | bytes 786440 | tf_op jit(solution)/shard_map/ppermute | solution.py:55
  17.6 7.0 %collective-permute-start.3 = (bf16[256,512]{1,0:T(8,128)(2,1)S(1)}, bf16[256,512]{1,0:T(8,128)(2,1)S(1)}, u32[]{:S(2)}, u32[]{:S(2)}) collective-permute-start(bf16[256,512]{1,0:T(8,128)(2,1)S(1)} %slice.41), channel_id=1, source_target_pairs={{0,1},{1,0},{2,3},{3,2},{4,5},{5,4},{6,7},{7,6},{8,9},{9,8},{10,11... | collective-permute-start | bytes 786440 | tf_op jit(solution)/shard_map/ppermute | solution.py:52
  25.9 1.7 %copy-start.8 = (bf16[512,512]{1,0:T(8,128)(2,1)}, bf16[512,512]{1,0:T(8,128)(2,1)S(1)}, u32[]{:S(2)}) copy-start(bf16[512,512]{1,0:T(8,128)(2,1)S(1)} %get-tuple-element.21) | copy-start | bytes 1572868
  25.9 1.7 %copy-start.6 = (bf16[512,512]{1,0:T(8,128)(2,1)}, bf16[512,512]{1,0:T(8,128)(2,1)S(1)}, u32[]{:S(2)}) copy-start(bf16[512,512]{1,0:T(8,128)(2,1)S(1)} %get-tuple-element.20) | copy-start | bytes 1572868
  25.9 20.8 %copy-start.3 = (bf16[512,512]{1,0:T(8,128)(2,1)}, bf16[512,512]{1,0:T(8,128)(2,1)S(1)}, u32[]{:S(2)}) copy-start(bf16[512,512]{1,0:T(8,128)(2,1)S(1)} %get-tuple-element.18) | copy-start | bytes 1572868
  25.9 20.8 %copy-start.5 = (bf16[512,512]{1,0:T(8,128)(2,1)}, bf16[512,512]{1,0:T(8,128)(2,1)S(1)}, u32[]{:S(2)}) copy-start(bf16[512,512]{1,0:T(8,128)(2,1)S(1)} %get-tuple-element.19) | copy-start | bytes 1572868
  25.9 2.0 %copy-start.1 = (bf16[256,2048]{1,0:T(8,128)(2,1)S(1)}, bf16[256,2048]{1,0:T(8,128)(2,1)}, u32[]{:S(2)}) copy-start(bf16[256,2048]{1,0:T(8,128)(2,1)} %param.9) | copy-start | bytes 3145732
  27.6 16.1 %collective-permute-start.5 = (bf16[512,2048]{1,0:T(8,128)(2,1)}, bf16[512,2048]{1,0:T(8,128)(2,1)}, u32[]{:S(2)}, u32[]{:S(2)}) collective-permute-start(bf16[512,2048]{1,0:T(8,128)(2,1)} %pad_maximum_fusion), channel_id=1, source_target_pairs={{0,16},{16,0},{1,17},{17,1},{2,18},{18,2},{3,19},{19,3},{4,20},{20... | collective-permute-start | bytes 6291464 | tf_op jit(solution)/shard_map/ppermute | solution.py:49
  28.8 14.2 %collective-permute-start.10 = (bf16[128,2048]{1,0:T(8,128)(2,1)}, bf16[128,2048]{1,0:T(8,128)(2,1)S(1)}, u32[]{:S(2)}, u32[]{:S(2)}) collective-permute-start(bf16[128,2048]{1,0:T(8,128)(2,1)} %constant_dynamic-slice_fusion.8), channel_id=1, source_target_pairs={{0,4},{4,0},{8,12},{12,8},{1,5},{5,1},{9,13},{13,9},{2,6},{6,2},{1... | collective-permute-start | bytes 1572872 | tf_op jit(solution)/shard_map/ppermute | solution.py:58
  33.3 10.4 %collective-permute-start.4 = (bf16[512,512]{1,0:T(8,128)(2,1)}, bf16[512,512]{1,0:T(8,128)(2,1)}, u32[]{:S(2)}, u32[]{:S(2)}) collective-permute-start(bf16[512,512]{1,0:T(8,128)(2,1)} %pad_maximum_fusion.3), channel_id=1, source_target_pairs={{0,16},{16,0},{1,17},{17,1},{2,18},{18,2},{3,19},{19,3},{4,20},{20... | collective-permute-start | bytes 1572872 | tf_op jit(solution)/shard_map/ppermute | solution.py:49
  33.3 14.9 %collective-permute-start.6 = (bf16[128,2048]{1,0:T(8,128)(2,1)}, bf16[128,2048]{1,0:T(8,128)(2,1)S(1)}, u32[]{:S(2)}, u32[]{:S(2)}) collective-permute-start(bf16[128,2048]{1,0:T(8,128)(2,1)} %constant_dynamic-slice_fusion.8), channel_id=1, source_target_pairs={{4,8},{8,4},{5,9},{9,5},{6,10},{10,6},{7,11},{11,7},{20,24},{24,20... | collective-permute-start | bytes 1572872 | tf_op jit(solution)/shard_map/ppermute | solution.py:64
  34.0 12.8 %copy-start.7 = (bf16[512,512]{1,0:T(8,128)(2,1)S(1)}, bf16[512,512]{1,0:T(8,128)(2,1)}, u32[]{:S(2)}) copy-start(bf16[512,512]{1,0:T(8,128)(2,1)} %copy-done.6) | copy-start | bytes 1572868
  34.0 12.8 %copy-start.9 = (bf16[512,512]{1,0:T(8,128)(2,1)S(1)}, bf16[512,512]{1,0:T(8,128)(2,1)}, u32[]{:S(2)}) copy-start(bf16[512,512]{1,0:T(8,128)(2,1)} %copy-done.8) | copy-start | bytes 1572868
  34.0 12.8 %copy-start.11 = (bf16[512,128]{1,0:T(8,128)(2,1)S(1)}, bf16[512,128]{1,0:T(8,128)(2,1)}, u32[]{:S(2)}) copy-start(bf16[512,128]{1,0:T(8,128)(2,1)} %get-tuple-element.37) | copy-start | bytes 393220
  43.0 5.2 %collective-permute-start.11 = (bf16[128,2048]{1,0:T(8,128)(2,1)S(1)}, bf16[128,2048]{1,0:T(8,128)(2,1)S(1)}, u32[]{:S(2)}, u32[]{:S(2)}) collective-permute-start(bf16[128,2048]{1,0:T(8,128)(2,1)S(1)} %collective-permute-done.10), channel_id=1, source_target_pairs={{4,8},{8,4},{5,9},{9,5},{6,10},{10,6},{7,11},{11,7},{20,24},{24,20... | collective-permute-start | bytes 1572872 | tf_op jit(solution)/shard_map/ppermute | solution.py:64
  48.1 16.5 %copy-start = (f32[512,2048]{1,0:T(8,128)}, f32[512,2048]{1,0:T(8,128)S(1)}, u32[]{:S(2)}) copy-start(f32[512,2048]{1,0:T(8,128)S(1)} %convolution_add_fusion) | copy-start | bytes 12582916
  48.1 15.4 %copy-start.14 = (s32[512,1]{0,1:T(1,128)S(1)}, s32[512,1]{0,1:T(1,128)}, u32[]{:S(2)}) copy-start(s32[512,1]{0,1:T(1,128)} %param.10) | copy-start | bytes 6148
  48.1 15.4 %copy-start.13 = (s32[512]{0:T(512)S(1)}, s32[512]{0:T(512)}, u32[]{:S(2)}) copy-start(s32[512]{0:T(512)} %param.11) | copy-start | bytes 6148
  48.1 15.5 %copy-start.10 = (bf16[512,1024]{1,0:T(8,128)(2,1)S(1)}, bf16[512,1024]{1,0:T(8,128)(2,1)}, u32[]{:S(2)}) copy-start(bf16[512,1024]{1,0:T(8,128)(2,1)} %param.8) | copy-start | bytes 3145732
  48.1 16.4 %copy-start.2 = (bf16[128,2048]{1,0:T(8,128)(2,1)}, bf16[128,2048]{1,0:T(8,128)(2,1)S(1)}, u32[]{:S(2)}) copy-start(bf16[128,2048]{1,0:T(8,128)(2,1)S(1)} %collective-permute-done.11) | copy-start | bytes 1572868
  49.2 27.2 %collective-permute-start.7 = (bf16[128,2048]{1,0:T(8,128)(2,1)}, bf16[128,2048]{1,0:T(8,128)(2,1)S(1)}, u32[]{:S(2)}, u32[]{:S(2)}) collective-permute-start(bf16[128,2048]{1,0:T(8,128)(2,1)} %get-tuple-element.7), channel_id=1, source_target_pairs={{0,4},{4,0},{8,12},{12,8},{1,5},{5,1},{9,13},{13,9},{2,6},{6,2},{1... | collective-permute-start | bytes 1572872 | tf_op jit(solution)/shard_map/ppermute | solution.py:58
  63.5 23.5 %collective-permute-start.12 = (bf16[128,2048]{1,0:T(8,128)(2,1)}, bf16[128,2048]{1,0:T(8,128)(2,1)S(1)}, u32[]{:S(2)}, u32[]{:S(2)}) collective-permute-start(bf16[128,2048]{1,0:T(8,128)(2,1)} %get-tuple-element.8), channel_id=1, source_target_pairs={{0,4},{4,0},{8,12},{12,8},{1,5},{5,1},{9,13},{13,9},{2,6},{6,2},{1... | collective-permute-start | bytes 1572872 | tf_op jit(solution)/shard_map/ppermute | solution.py:58
  63.5 31.6 %collective-permute-start.15 = (s32[512]{0:T(512)S(1)}, s32[512]{0:T(512)S(1)}, u32[]{:S(2)}, u32[]{:S(2)}) collective-permute-start(s32[512]{0:T(512)S(1)} %add.156), channel_id=1, source_target_pairs={{0,16},{16,0},{1,17},{17,1},{2,18},{18,2},{3,19},{19,3},{4,20},{20... | collective-permute-start | bytes 6152 | tf_op jit(solution)/shard_map/ppermute | solution.py:49
  65.4 29.7 %collective-permute-start.16 = (bf16[512,512]{1,0:T(8,128)(2,1)}, bf16[512,512]{1,0:T(8,128)(2,1)}, u32[]{:S(2)}, u32[]{:S(2)}) collective-permute-start(bf16[512,512]{1,0:T(8,128)(2,1)} %pad_maximum_fusion.4), channel_id=1, source_target_pairs={{0,16},{16,0},{1,17},{17,1},{2,18},{18,2},{3,19},{19,3},{4,20},{20... | collective-permute-start | bytes 1572872 | tf_op jit(solution)/shard_map/ppermute | solution.py:49
  88.3 1.6 %copy-start.4 = (bf16[512,512]{1,0:T(8,128)(2,1)S(1)}, bf16[512,512]{1,0:T(8,128)(2,1)}, u32[]{:S(2)}) copy-start(bf16[512,512]{1,0:T(8,128)(2,1)} %copy-done.3) | copy-start | bytes 1572868
  100.2 12.3 %collective-permute-start.17 = (bf16[256,512]{1,0:T(8,128)(2,1)S(1)}, bf16[256,512]{1,0:T(8,128)(2,1)S(1)}, u32[]{:S(2)}, u32[]{:S(2)}) collective-permute-start(bf16[256,512]{1,0:T(8,128)(2,1)S(1)} %get-tuple-element.11), channel_id=1, source_target_pairs={{0,4},{12,8},{1,5},{13,9},{2,6},{14,10},{3,7},{15,11},{16,20},{28,... | collective-permute-start | bytes 786440 | tf_op jit(solution)/shard_map/ppermute | solution.py:61
  107.0 25.4 %collective-permute-start.8 = (bf16[128,2048]{1,0:T(8,128)(2,1)}, bf16[128,2048]{1,0:T(8,128)(2,1)S(1)}, u32[]{:S(2)}, u32[]{:S(2)}) collective-permute-start(bf16[128,2048]{1,0:T(8,128)(2,1)} %fusion.5), channel_id=1, source_target_pairs={{4,8},{8,4},{5,9},{9,5},{6,10},{10,6},{7,11},{11,7},{20,24},{24,20... | collective-permute-start | bytes 1572872 | tf_op jit(solution)/shard_map/ppermute | solution.py:64
  107.7 8.3 %collective-permute-start.20 = (bf16[256,512]{1,0:T(8,128)(2,1)S(1)}, bf16[256,512]{1,0:T(8,128)(2,1)}, u32[]{:S(2)}, u32[]{:S(2)}) collective-permute-start(bf16[256,512]{1,0:T(8,128)(2,1)S(1)} %get-tuple-element.12), channel_id=1, source_target_pairs={{0,4},{12,8},{1,5},{13,9},{2,6},{14,10},{3,7},{15,11},{16,20},{28,... | collective-permute-start | bytes 786440 | tf_op jit(solution)/shard_map/ppermute | solution.py:61
  113.2 2.8 %collective-permute-start.18 = (bf16[256,512]{1,0:T(8,128)(2,1)}, bf16[256,512]{1,0:T(8,128)(2,1)}, u32[]{:S(2)}, u32[]{:S(2)}) collective-permute-start(bf16[256,512]{1,0:T(8,128)(2,1)} %fusion.28), channel_id=1, source_target_pairs={{4,8},{8,4},{5,9},{9,5},{6,10},{10,6},{7,11},{11,7},{20,24},{24,20... | collective-permute-start | bytes 786440 | tf_op jit(solution)/shard_map/ppermute | solution.py:64
  118.0 19.9 %collective-permute-start.21 = (bf16[256,512]{1,0:T(8,128)(2,1)}, bf16[256,512]{1,0:T(8,128)(2,1)S(1)}, u32[]{:S(2)}, u32[]{:S(2)}) collective-permute-start(bf16[256,512]{1,0:T(8,128)(2,1)} %get-tuple-element.10), channel_id=1, source_target_pairs={{4,8},{8,4},{5,9},{9,5},{6,10},{10,6},{7,11},{11,7},{20,24},{24,20... | collective-permute-start | bytes 786440 | tf_op jit(solution)/shard_map/ppermute | solution.py:64
  118.7 19.2 %collective-permute-start.19 = (bf16[256,512]{1,0:T(8,128)(2,1)}, bf16[256,512]{1,0:T(8,128)(2,1)}, u32[]{:S(2)}, u32[]{:S(2)}) collective-permute-start(bf16[256,512]{1,0:T(8,128)(2,1)} %get-tuple-element.9), channel_id=1, source_target_pairs={{0,4},{4,0},{8,12},{12,8},{1,5},{5,1},{9,13},{13,9},{2,6},{6,2},{1... | collective-permute-start | bytes 786440 | tf_op jit(solution)/shard_map/ppermute | solution.py:58
  135.2 3.9 %collective-permute-start.13 = (bf16[128,2048]{1,0:T(8,128)(2,1)}, bf16[128,2048]{1,0:T(8,128)(2,1)S(1)}, u32[]{:S(2)}, u32[]{:S(2)}) collective-permute-start(bf16[128,2048]{1,0:T(8,128)(2,1)} %get-tuple-element.6), channel_id=1, source_target_pairs={{4,8},{8,4},{5,9},{9,5},{6,10},{10,6},{7,11},{11,7},{20,24},{24,20... | collective-permute-start | bytes 1572872 | tf_op jit(solution)/shard_map/ppermute | solution.py:64
  135.9 12.4 %collective-permute-start.9 = (bf16[128,2048]{1,0:T(8,128)(2,1)}, bf16[128,2048]{1,0:T(8,128)(2,1)}, u32[]{:S(2)}, u32[]{:S(2)}) collective-permute-start(bf16[128,2048]{1,0:T(8,128)(2,1)} %get-tuple-element.5), channel_id=1, source_target_pairs={{0,4},{4,0},{8,12},{12,8},{1,5},{5,1},{9,13},{13,9},{2,6},{6,2},{1... | collective-permute-start | bytes 1572872 | tf_op jit(solution)/shard_map/ppermute | solution.py:58
  138.9 11.0 %collective-permute-start.22 = (f32[256,512]{1,0:T(8,128)S(1)}, f32[256,512]{1,0:T(8,128)S(1)}, u32[]{:S(2)}, u32[]{:S(2)}) collective-permute-start(f32[256,512]{1,0:T(8,128)S(1)} %fusion.30), channel_id=1, source_target_pairs={{0,16},{16,0},{1,17},{17,1},{2,18},{18,2},{3,19},{19,3},{4,20},{20... | collective-permute-start | bytes 1572872 | tf_op jit(solution)/shard_map/ppermute | solution.py:49
  149.8 2.7 %collective-permute-start.14 = (f32[128,2048]{1,0:T(8,128)S(1)}, f32[128,2048]{1,0:T(8,128)S(1)}, u32[]{:S(2)}, u32[]{:S(2)}) collective-permute-start(f32[128,2048]{1,0:T(8,128)S(1)} %fusion.7), channel_id=1, source_target_pairs={{0,16},{16,0},{1,17},{17,1},{2,18},{18,2},{3,19},{19,3},{4,20},{20... | collective-permute-start | bytes 3145736 | tf_op jit(solution)/shard_map/ppermute | solution.py:49
  150.3 2.5 %copy-start.12 = (f32[256,1024]{1,0:T(8,128)}, f32[256,1024]{1,0:T(8,128)S(1)}, u32[]{:S(2)}) copy-start(f32[256,1024]{1,0:T(8,128)S(1)} %slice_dynamic-update-slice_fusion) | copy-start | bytes 3145732

commit v2 on v1

v2 whole, which is shorter than its diff:
```python
import jax
import jax.numpy as jnp
from jax import lax
from jax.experimental import pallas as pl
from jax.experimental.pallas import tpu as pltpu
from jax.sharding import PartitionSpec as P

F32, BF16 = jnp.float32, jnp.bfloat16
KEY_DEV = 256


def dot(a, b, ca, cb):
    return lax.dot_general(a, b, (((ca,), (cb,)), ((), ())), preferred_element_type=F32)


def general_body(layer_input, value_grad, residual_grad, value_weight, owner, key_row):
    all_heads = lax.all_gather(value_grad, "tp", axis=1, tiled=True)
    tok_rows, features = layer_input.shape
    groups = lax.axis_size("fsdp")
    slots = 2 * tok_rows // groups
    keys_here = KEY_DEV
    width = all_heads.shape[1]
    term = dot(layer_input, all_heads, 0, 0)
    pieces = term.astype(BF16).reshape(groups, features // groups, width)
    arrived = lax.all_to_all(pieces, "fsdp", split_axis=0, concat_axis=0, tiled=True)
    shard = jnp.sum(arrived.astype(F32), axis=0)
    back = dot(all_heads, lax.all_gather(value_weight, "fsdp", axis=0, tiled=True), 1, 1)
    input_grad = (residual_grad.astype(F32) + back).astype(BF16)
    target = owner[:, 0]
    onehot = (target[:, None] == jnp.arange(groups, dtype=jnp.int32)[None, :]).astype(jnp.int32)
    position = jnp.sum(jnp.cumsum(onehot, axis=0) * onehot, axis=1) - 1
    place = target * slots + position
    chooser = jnp.arange(groups * slots, dtype=jnp.int32)[:, None] == place[None, :]
    outgoing = dot(chooser.astype(BF16), input_grad, 1, 0).astype(BF16)
    out_keys = jnp.sum(jnp.where(chooser, key_row[None, :] + 1, 0), axis=1) - 1
    arrived = lax.all_to_all(outgoing, "fsdp", split_axis=0, concat_axis=0, tiled=True)
    arrived_keys = lax.all_to_all(out_keys, "fsdp", split_axis=0, concat_axis=0, tiled=True)
    selector = (arrived_keys[:, None] == jnp.arange(keys_here, dtype=jnp.int32)[None, :]).astype(BF16)
    table = dot(selector, arrived, 0, 0)
    return lax.psum(shard, "dp"), lax.psum(table, "dp")


def term_kernel(*refs):
    mine, other, heads, out = refs[0], refs[1], refs[2:-1], refs[-1]
    rows, width = mine.shape[0], heads[0].shape[1]
    for i, head in enumerate(heads):
        out[:, i * width : (i + 1) * width] = dot(mine[...], head[:rows], 0, 0) + dot(other[...], head[rows:], 0, 0)


def back_kernel(shift, *refs):
    heads, (weight, residual, key, out, table) = refs[:8], refs[8:]
    step = pl.program_id(0)
    acc = residual[...].astype(F32)
    for i, head in enumerate(heads):
        k, side = i % 4, i // 4
        width = head.shape[1]
        start = pl.multiple_of(shift[k] + (shift[4] if side == 0 else width - shift[4]), width)
        acc = acc + dot(head[...], weight[:, pl.ds(start, width)], 1, 1)
    rows = acc.astype(BF16)
    index = lax.broadcasted_iota(jnp.int32, (table.shape[0], key.shape[2]), 0)
    add = dot(jnp.where(index == key[0], 1.0, 0.0).astype(BF16), rows, 1, 0)

    @pl.when(step == 0)
    def _():
        table[...] = add

    @pl.when(step > 0)
    def _():
        table[...] += add

    @pl.when(step == pl.num_programs(0) - 1)
    def _():
        out[...] = table[...].astype(BF16)


def join_kernel(shift, weight_mine, weight_pair, key_mine, key_pair, weight_out, key_out):
    core = shift[4]
    width = weight_mine.shape[1] // 4
    for k in range(4):
        cols = slice(k * width, (k + 1) * width)
        start = pl.multiple_of(shift[k] + core, width)
        weight_out[:, pl.ds(start, width)] = weight_mine[:, cols]
        start = pl.multiple_of(shift[k] + width - core, width)
        weight_out[:, pl.ds(start, width)] = weight_pair[:, cols]
    half = key_mine.shape[1] // 4
    first = core == 0
    for p in range(4):
        mine, pair = key_mine[:, p * half : (p + 1) * half], key_pair[:, p * half : (p + 1) * half]
        key_out[:, 2 * p * half : (2 * p + 1) * half] = jnp.where(first, mine, pair)
        key_out[:, (2 * p + 1) * half : (2 * p + 2) * half] = jnp.where(first, pair, mine)


def pair_body(layer_input, value_grad, residual_grad, value_weight, owner, key_row):
    core, z, t = (lax.axis_index(n) for n in ("dp", "fsdp", "tp"))
    tokens, features = layer_input.shape
    heads = value_grad.shape[1]
    part = features // 4
    half = part // 2
    wide = heads // 2
    keys = KEY_DEV
    phase = lax.optimization_barrier

    def core_swap(v):
        return lax.ppermute(v, "dp", [(0, 1), (1, 0)])

    def square(v, d):
        return lax.ppermute(v, "tp", [(i, i ^ d) for i in range(4)])

    def outer(v):
        return lax.ppermute(v, "fsdp", [(0, 1), (1, 0), (2, 3), (3, 2)])

    def inward(v):
        return lax.ppermute(v, "fsdp", [(0, 1), (3, 2)])

    def outward(v):
        return lax.ppermute(v, "fsdp", [(1, 0), (2, 3)])

    def inner(v):
        return lax.ppermute(v, "fsdp", [(1, 2), (2, 1)])

    end = (z == 0) | (z == 3)
    beside = z ^ 1
    far_mid = jnp.where(z < 2, 2, 1)
    far_end = jnp.where(z < 2, 3, 0)

    def halves(v, which):
        return jnp.concatenate(
            [lax.dynamic_slice_in_dim(v, p * part + which * half, half, 1) for p in range(4)], 1
        )

    w_own = lax.dynamic_slice_in_dim(value_weight, core * half, half, 0)
    w_beside, w_mid = outer(w_own), inner(w_own)
    v_other = core_swap(lax.dynamic_slice_in_dim(value_grad, (1 - core) * wide, wide, 1))
    v0 = jnp.concatenate([lax.dynamic_slice_in_dim(value_grad, core * wide, wide, 1), v_other], 0)
    key = owner[:, 0] * keys + key_row
    got = phase((w_beside, w_mid, square(v0, 1), square(v0, 2), core_swap(layer_input), core_swap(key),
                 core_swap(halves(residual_grad, 1 - core))))
    w_beside, w_mid, vx, vy, in_other, key_other, res_other = got

    vmem = pl.BlockSpec(memory_space=pltpu.VMEM)

    def term(*v):
        n = len(v)
        return pl.pallas_call(
            term_kernel,
            grid=(4,),
            out_shape=jax.ShapeDtypeStruct((features, n * wide), F32),
            in_specs=[pl.BlockSpec((tokens, part), lambda i: (0, i))] * 2
            + [pl.BlockSpec((2 * tokens, wide), lambda i: (0, 0))] * n,
            out_specs=pl.BlockSpec((part, n * wide), lambda i: (i, 0)),
            compiler_params=pltpu.CompilerParams(vmem_limit_bytes=32 << 20),
            cost_estimate=pl.CostEstimate(flops=n << 29, bytes_accessed=(2 + n * 2) << 20, transcendentals=0),
        )(layer_input, in_other, *v)

    first = term(v0, vx, vy)
    got = phase((outward(w_mid), inner(w_beside), square(vx[:tokens], 2), square(vy[tokens:], 1), first))
    w_third, w_end, vd0, vd1, first = got
    w_third = jnp.where(end, w_third, w_mid)

    vd = jnp.concatenate([vd0, vd1], 0)
    last = term(vd)

    def piece(i):
        return jnp.concatenate([lax.dynamic_slice_in_dim(v, i * part, part, 0) for v in (first, last)], 1)

    w_fourth = outward(w_end)
    i1 = inward(piece(far_end).astype(BF16))
    i2 = inward(piece(far_mid).astype(BF16))
    i3 = inward(piece(beside).astype(BF16))
    near = (v0, vx, vy, vd)
    far = core_swap(near)
    w_fourth, i1, far = phase((w_fourth, i1, far))
    w_fourth = jnp.where(end, w_fourth, w_end)
    b2 = inner((piece(far_end) + i1.astype(F32)).astype(BF16))
    b3 = inner((piece(far_mid) + i2.astype(F32)).astype(BF16))
    a3 = outward((piece(beside) + b2.astype(F32)).astype(BF16))
    weight_half = piece(z) + i3.astype(F32) + b3.astype(F32) + a3.astype(F32)
    weight_pair = core_swap(weight_half)

    arrived = (w_own, w_beside, w_third, w_fourth)
    order = [jnp.where(i == z, 0, jnp.where(i == beside, 1, jnp.where(i == far_mid, 2, 3))) for i in range(4)]
    weights = jnp.concatenate([lax.select_n(i, *arrived) for i in order], 0)
    shift = jnp.stack([(t ^ k) * heads for k in range(4)] + [core * wide]).astype(jnp.int32)
    residual = jnp.concatenate([halves(residual_grad, core), res_other], 0)
    rows = tokens // 2
    table = pl.pallas_call(
        back_kernel,
        grid=(4,),
        out_shape=jax.ShapeDtypeStruct((4 * keys, 4 * half), BF16),
        in_specs=[pl.BlockSpec(memory_space=pltpu.SMEM)]
        + [pl.BlockSpec((rows, wide), lambda i: (i, 0))] * 4
        + [pl.BlockSpec((rows, wide), lambda i: ((i + 2) % 4, 0))] * 4
        + [pl.BlockSpec((4 * half, 4 * heads), lambda i: (0, 0)),
           pl.BlockSpec((rows, 4 * half), lambda i: (i, 0)),
           pl.BlockSpec((1, 1, rows), lambda i: (i, 0, 0))],
        out_specs=pl.BlockSpec((4 * keys, 4 * half), lambda i: (0, 0)),
        scratch_shapes=[pltpu.VMEM((4 * keys, 4 * half), F32)],
        compiler_params=pltpu.CompilerParams(vmem_limit_bytes=40 << 20),
        cost_estimate=pl.CostEstimate(flops=3 << 30, bytes_accessed=8 << 20, transcendentals=0),
    )(shift, *near, *far, weights, residual, jnp.concatenate([key, key_other]).reshape(4, 1, rows))
    came = lax.all_to_all(table.reshape(4, keys, 4 * half), "fsdp", split_axis=0, concat_axis=0, tiled=True)
    key_half = jnp.sum(came.astype(F32), axis=0)
    key_pair = core_swap(key_half)

    return tuple(pl.pallas_call(
        join_kernel,
        out_shape=(jax.ShapeDtypeStruct((part, 4 * heads), F32), jax.ShapeDtypeStruct((keys, features), F32)),
        in_specs=[pl.BlockSpec(memory_space=pltpu.SMEM)] + [vmem] * 4,
        out_specs=(vmem, vmem),
        compiler_params=pltpu.CompilerParams(vmem_limit_bytes=16 << 20),
    )(shift, weight_half, weight_pair, key_half, key_pair))


def solution(mesh):
    shape = dict(mesh.shape)
    special = shape == {"dp": 2, "fsdp": 4, "tp": 4}
    return jax.shard_map(
        pair_body if special else general_body,
        mesh=mesh,
        in_specs=(
            P(("dp", "fsdp"), "tp"),
            P(("dp", "fsdp"), "tp"),
            P(("dp", "fsdp"), "tp"),
            P(("tp", "fsdp"), None),
            P(("dp", "fsdp"), None),
            P(("dp", "fsdp")),
        ),
        out_specs=(P(("tp", "fsdp"), None), P("fsdp", "tp")),
        check_vma=False,
    )
```

time: 155 us -> 137 us (0.88)
  the two profiles are of different devices: /device:TPU:0 before, /device:TPU:11 now
where the time goes in v2:
time: 137 us; the launch traced here: 136 us
  waiting for transfers between devices  51.2 us (37%)
  starting transfers between devices  40.1 us (29%)
  Pallas kernels  15.7 us (11%)
  local copies, waits for them, and re-layouts  14 us (10%)
  other arithmetic  13.7 us (10%)
    ppermute x4, waiting for transfers between devices, inner(): return lax.ppermute(v, 'fsdp', [(1, 2), (2, 1)])  30.2 us
    ppermute x4, starting transfers between devices, inner(): return lax.ppermute(v, 'fsdp', [(1, 2), (2, 1)])  13.9 us
    ppermute x10, starting transfers between devices, core_swap(): return lax.ppermute(v, 'dp', [(0, 1), (1, 0)])  9.06 us
    ppermute x4, waiting for transfers between devices, square(): return lax.ppermute(v, 'tp', [(i, i ^ d) for i in range(4)])  9.06 us
    ppermute x3, waiting for transfers between devices, inward(): return lax.ppermute(v, 'fsdp', [(0, 1), (3, 2)])  7.77 us
    pallas_call x1, Pallas kernels, pair_body(): pl.pallas_call(back_kernel, grid=(4,), out_shape=jax.ShapeDtypeStruct((4...  7.56 us
    ppermute x3, starting transfers between devices, outward(): return lax.ppermute(v, 'fsdp', [(1, 0), (2, 3)])  6.08 us
    pallas_call x2, Pallas kernels, term(): pl.pallas_call(term_kernel, grid=(4,), out_shape=jax.ShapeDtypeStruct((fe...  5.69 us
  transfers between devices with their start and end apart: 26, of which 8 were waited for; matrix products, arithmetic and copies ran while one was open for 18% of the time, Pallas kernels for 10%

profile of v2, /device:TPU:11, one launch (start us, length us, event | category | flops | bytes accessed | tf_op | source)
XLA Modules:
  0.0 135.8 jit_solution(4025733075583120377)
XLA Ops:
  0.7 2.0 %constant_dynamic-slice_fusion.18 = bf16[128,2048]{1,0:T(8,128)(2,1)} fusion(bf16[256,2048]{1,0:T(8,128)(2,1)} %param.9, s32[]{:T(128)S(6)} %select_n.220), kind=kLoop, calls=%fused_computation.43 | loop fusion | bytes 1048580 | tf_op jit(solution)/shard_map/dynamic_slice | solution.py:131
  2.6 0.2 collective-permute-start
  2.8 4.3 %collective-permute-start.1 = (bf16[128,2048]{1,0:T(8,128)(2,1)}, bf16[128,2048]{1,0:T(8,128)(2,1)}, u32[]{:S(2)}, u32[]{:S(2)}) collective-permute-start(bf16[128,2048]{1,0:T(8,128)(2,1)} %constant_dynamic-slice_fusion.18), channel_id=1, source_target_pairs={{4,8},{8,4},{5,9},{9,5},{6,10},{10,6},{7,11},{11,7},{20,24},{24,20... | collective-permute-start | bytes 1572872 | tf_op jit(solution)/shard_map/ppermute | solution.py:119
  7.1 1.8 %constant_dynamic-slice_fusion.17 = (bf16[512,256]{1,0:T(8,128)(2,1)S(1)}, bf16[512,256]{1,0:T(8,128)(2,1)}) fusion(bf16[512,512]{1,0:T(8,128)(2,1)} %param.7, s32[]{:T(128)S(6)} %select_n.221, s32[]{:T(128)S(6)} %select_n.222), kind=kLoop, calls=%fused_computation.42 | loop fusion | bytes 1048584 | tf_op jit(solution)/shard_map/dynamic_slice | solution.py:134
  8.9 1.2 collective-permute-start.2
  10.1 0.0 collective-permute-start.5
  10.2 0.6 collective-permute-start.6
  10.7 2.1 %constant_dynamic-slice_fusion.3 = (bf16[512,128]{1,0:T(8,128)(2,1)S(1)}, bf16[512,128]{1,0:T(8,128)(2,1)}, bf16[512,128]{1,0:T(8,128)(2,1)S(1)}, bf16[512,128]{...) fusion(bf16[512,1024]{1,0:T(8,128)(2,1)} %param.8, ...), kind=kLoop, calls=%fused_computation.28 | loop fusion | bytes 2097184 | tf_op jit(solution)/shard_map/dynamic_slice | solution.py:128
  12.8 0.1 pad_maximum_fusion.6
  12.9 0.1 collective-permute-start.7
  13.0 1.0 pad_maximum_fusion.5.refs_2_.refs_0_
  14.0 0.3 collective-permute-start.3
  14.3 1.4 %collective-permute-done = bf16[128,2048]{1,0:T(8,128)(2,1)S(1)} collective-permute-done((bf16[128,2048]{1,0:T(8,128)(2,1)}, bf16[128,2048]{1,0:T(8,128)(2,1)S(1)}, u32[]{:S(2)}, u32[]{:S(2)}) %collective-permute-start) | collective-permute-done | bytes 524320 | tf_op jit(solution)/shard_map/ppermute | solution.py:110
  15.7 1.2 collective-permute-start.4
  17.0 1.8 %collective-permute-done.1 = bf16[128,2048]{1,0:T(8,128)(2,1)} collective-permute-done((bf16[128,2048]{1,0:T(8,128)(2,1)}, bf16[128,2048]{1,0:T(8,128)(2,1)}, u32[]{:S(2)}, u32[]{:S(2)}) %collective-permute-start.1) | collective-permute-done | bytes 524320 | tf_op jit(solution)/shard_map/ppermute | solution.py:119
  18.8 8.4 %collective-permute-done.3.refs_3_.refs_1_ = bf16[1024,256]{1,0:T(8,128)(2,1)} collective-permute-done((bf16[1024,256]{1,0:T(8,128)(2,1)S(1)}, bf16[1024,256]{1,0:T(8,128)(2,1)}, u32[]{:S(2)}, u32[]{:S(2)}) %collective-permute-start.3) | collective-permute-done | bytes 524320 | tf_op jit(solution)/shard_map/ppermute | solution.py:107
  27.2 0.6 collective-permute-done.4.refs_4_.refs_2_
  27.8 2.7 %collective-permute-start.8 = (bf16[128,2048]{1,0:T(8,128)(2,1)}, bf16[128,2048]{1,0:T(8,128)(2,1)}, u32[]{:S(2)}, u32[]{:S(2)}) collective-permute-start(bf16[128,2048]{1,0:T(8,128)(2,1)} %collective-permute-done.1), channel_id=1, source_target_pairs={{4,0},{8,12},{5,1},{9,13},{6,2},{10,14},{7,3},{11,15},{20,16},{24,... | collective-permute-start | bytes 1572872 | tf_op jit(solution)/shard_map/ppermute | solution.py:116
  30.5 4.5 %collective-permute-start.9 = (bf16[128,2048]{1,0:T(8,128)(2,1)S(1)}, bf16[128,2048]{1,0:T(8,128)(2,1)}, u32[]{:S(2)}, u32[]{:S(2)}) collective-permute-start(bf16[128,2048]{1,0:T(8,128)(2,1)S(1)} %collective-permute-done), channel_id=1, source_target_pairs={{4,8},{8,4},{5,9},{9,5},{6,10},{10,6},{7,11},{11,7},{20,24},{24,20... | collective-permute-start | bytes 1572872 | tf_op jit(solution)/shard_map/ppermute | solution.py:119
  35.0 1.7 %slice.6 = bf16[512,256]{1,0:T(8,128)(2,1)} slice(bf16[1024,256]{1,0:T(8,128)(2,1)} %collective-permute-done.3.refs_3_.refs_1_), slice={[0:512], [0:256]} | slice | bytes 524288 | tf_op jit(solution)/shard_map/slice | solution.py:156
  36.7 1.2 collective-permute-start.10
  37.9 1.7 %slice.7 = bf16[512,256]{1,0:T(8,128)(2,1)} slice(bf16[1024,256]{1,0:T(8,128)(2,1)} %collective-permute-done.4.refs_4_.refs_2_), slice={[512:1024], [0:256]} | slice | bytes 524288 | tf_op jit(solution)/shard_map/slice | solution.py:156
  39.6 0.3 collective-permute-start.11
  39.9 3.5 %collective-permute-start.17 = (bf16[1024,256]{1,0:T(8,128)(2,1)S(1)}, bf16[1024,256]{1,0:T(8,128)(2,1)S(1)}, u32[]{:S(2)}, u32[]{:S(2)}) collective-permute-start(bf16[1024,256]{1,0:T(8,128)(2,1)S(1)} %pad_maximum_fusion.5.refs_2_.refs_0_), channel_id=1, source_target_pairs={{0,16},{16,0},{1,17},{17,1},{2,18},{18,2},{3,19},{19,3},{4,20},{20... | collective-permute-start | bytes 1572872 | tf_op jit(solution)/shard_map/ppermute | solution.py:104
  43.3 3.9 %shard_map.77 = f32[1024,768]{1,0:T(8,128)S(1)} custom-call(bf16[512,1024]{1,0:T(8,128)(2,1)S(1)} %copy-done, bf16[512,1024]{1,0:T(8,128)(2,1)S(1)} %collective-permute-done.5.refs_1_, bf16[1024,256]{1,0:T(8,128)(2,1)S(1)} %pad_maximum_fusion.5.refs_2_.refs_0_, bf16[1024,256]{1,0:T(8,128)(2,1)} %collective-permute-done.3.refs_3_.refs_1_, ...), custom_call_target="tpu_custom_call" | custom-call | flops 1610612736 | bytes 8388608 | tf_op jit(solution)/shard_map/pallas_call | solution.py:144
  47.3 0.1 collective-permute-start.18
  47.4 2.0 %collective-permute-start.19 = (bf16[1024,256]{1,0:T(8,128)(2,1)}, bf16[1024,256]{1,0:T(8,128)(2,1)}, u32[]{:S(2)}, u32[]{:S(2)}) collective-permute-start(bf16[1024,256]{1,0:T(8,128)(2,1)} %collective-permute-done.4.refs_4_.refs_2_), channel_id=1, source_target_pairs={{0,16},{16,0},{1,17},{17,1},{2,18},{18,2},{3,19},{19,3},{4,20},{20... | collective-permute-start | bytes 1572872 | tf_op jit(solution)/shard_map/ppermute | solution.py:104
  49.4 1.0 constant_dynamic-update-slice_fusion.1
  50.4 2.1 %collective-permute-start.15 = (bf16[128,2048]{1,0:T(8,128)(2,1)}, bf16[128,2048]{1,0:T(8,128)(2,1)}, u32[]{:S(2)}, u32[]{:S(2)}) collective-permute-start(bf16[128,2048]{1,0:T(8,128)(2,1)} %collective-permute-done.9), channel_id=1, source_target_pairs={{4,0},{8,12},{5,1},{9,13},{6,2},{10,14},{7,3},{11,15},{20,16},{24,... | collective-permute-start | bytes 1572872 | tf_op jit(solution)/shard_map/ppermute | solution.py:116
  52.5 1.7 %shard_map.78 = f32[1024,256]{1,0:T(8,128)S(1)} custom-call(bf16[512,1024]{1,0:T(8,128)(2,1)S(1)} %copy-done, bf16[512,1024]{1,0:T(8,128)(2,1)S(1)} %collective-permute-done.5.refs_1_, bf16[1024,256]{1,0:T(8,128)(2,1)S(1)} %constant_dynamic-update-slice_fusion.refs_2_.refs_3_), custom_call_target="tpu_custom_call" | custom-call | flops 536870912 | bytes 4194304 | tf_op jit(solution)/shard_map/pallas_call | solution.py:144
  54.2 0.9 constant_dynamic-slice_fusion.6
  55.2 1.2 constant_dynamic-slice_fusion.7
  56.3 1.0 fusion.2
  57.3 1.3 collective-permute-start.16
  58.6 0.8 copy-done.1
  59.4 0.0 collective-permute-start.20
  59.4 0.1 stack.23.shift
  59.5 1.3 pad_maximum_fusion.4.refs_9_
  60.8 0.0 copy-start.4
  60.9 0.9 fusion.3
  61.8 0.9 fusion.4
  62.7 1.3 collective-permute-start.13
  64.0 1.3 collective-permute-start.12
  65.3 7.8 %collective-permute-done.16 = bf16[256,1024]{1,0:T(8,128)(2,1)} collective-permute-done((bf16[256,1024]{1,0:T(8,128)(2,1)}, bf16[256,1024]{1,0:T(8,128)(2,1)}, u32[]{:S(2)}, u32[]{:S(2)}) %collective-permute-start.16) | collective-permute-done | bytes 524320 | tf_op jit(solution)/shard_map/ppermute | solution.py:113
  73.1 2.0 %add_convert_fusion.1 = bf16[256,1024]{1,0:T(8,128)(2,1)} fusion(bf16[256,1024]{1,0:T(8,128)(2,1)} %collective-permute-done.16, f32[256,256]{1,0:T(8,128)S(1)} %copy-done.10, f32[256,768]{1,0:T(8,128)S(1)} %copy-done.4), kind=kLoop, calls=%fused_computation.10 | loop fusion | flops 1048576 | bytes 2097152 | tf_op jit(solution)/shard_map/convert_element_type | solution.py:174
  75.0 1.9 %collective-permute-start.21 = (bf16[256,1024]{1,0:T(8,128)(2,1)}, bf16[256,1024]{1,0:T(8,128)(2,1)}, u32[]{:S(2)}, u32[]{:S(2)}) collective-permute-start(bf16[256,1024]{1,0:T(8,128)(2,1)} %add_convert_fusion.1), channel_id=1, source_target_pairs={{4,8},{8,4},{5,9},{9,5},{6,10},{10,6},{7,11},{11,7},{20,24},{24,20... | collective-permute-start | bytes 1572872 | tf_op jit(solution)/shard_map/ppermute | solution.py:119
  77.0 1.9 %select_select_fusion.3 = (bf16[128,2048]{1,0:T(8,128)(2,1)S(1)}, bf16[128,2048]{1,0:T(8,128)(2,1)S(1)}, bf16[128,2048]{1,0:T(8,128)(2,1)S(1)}) fusion(bf16[128,2048]{1,0:T(8,128)(2,1)S(1)} %copy-done.12, pred[]{:T(512)S(6)} %select_n.241, pred[]{:T(512)S(6)} %select_n.238, pred[]{:T(512)S(6)} %select_n.236, bf16[128,2048]{1,0:T(8,128)(2,1)} %collective-permute-done.15, ...), kind=kLoop, calls=%fused_computation.20 | loop fusion | flops 1310720 | bytes 4718600 | tf_op jit(solution)/shard_map/select_n | solution.py:182
  78.9 0.6 select_select_fusion.2
  79.4 0.2 pad_maximum_fusion.refs_8_
  79.7 0.8 copy-done.2
  80.5 7.6 %shard_map.79 = bf16[1024,512]{1,0:T(8,128)(2,1)} custom-call(s32[5]{0:T(128)S(1)} %stack.23.shift, bf16[1024,256]{1,0:T(8,128)(2,1)S(1)} %pad_maximum_fusion.5.refs_2_.refs_0_, bf16[1024,256]{1,0:T(8,128)(2,1)} %collective-permute-done.3.refs_3_.refs_1_, bf16[1024,256]{1,0:T(8,128)(2,1)} %collective-permute-done.4.refs_4_.refs_2_, ...), custom_call_target="tpu_custom_call" | custom-call | flops 3221225472 | bytes 8388608 | tf_op jit(solution)/shard_map/pallas_call | solution.py:186
  88.0 4.0 %all-to-all-start = ((bf16[4,256,512]{2,1,0:T(8,128)(2,1)}), bf16[4,256,512]{2,1,0:T(8,128)(2,1)S(1)}, u32[]{:S(2)}, u32[]{:S(2)}) async-start(bf16[4,256,512]{2,1,0:T(8,128)(2,1)} %bitcast.8), calls=%async_computation | async-start | bytes 2097152 | tf_op jit(solution)/shard_map/all_to_all | solution.py:201
  92.1 1.3 add_convert_fusion.2
  93.4 3.1 %collective-permute-start.14 = (bf16[256,1024]{1,0:T(8,128)(2,1)S(1)}, bf16[256,1024]{1,0:T(8,128)(2,1)S(1)}, u32[]{:S(2)}, u32[]{:S(2)}) collective-permute-start(bf16[256,1024]{1,0:T(8,128)(2,1)S(1)} %add_convert_fusion.2), channel_id=1, source_target_pairs={{4,8},{8,4},{5,9},{9,5},{6,10},{10,6},{7,11},{11,7},{20,24},{24,20... | collective-permute-start | bytes 1572872 | tf_op jit(solution)/shard_map/ppermute | solution.py:119
  96.5 1.2 add_convert_fusion
  97.7 1.3 collective-permute-start.22
  99.0 28.4 %collective-permute-done.14 = bf16[256,1024]{1,0:T(8,128)(2,1)S(1)} collective-permute-done((bf16[256,1024]{1,0:T(8,128)(2,1)S(1)}, bf16[256,1024]{1,0:T(8,128)(2,1)S(1)}, u32[]{:S(2)}, u32[]{:S(2)}) %collective-permute-start.14) | collective-permute-done | bytes 524320 | tf_op jit(solution)/shard_map/ppermute | solution.py:119
  127.4 1.3 fusion.1.weight_mine
  128.8 1.5 %collective-permute-start.23 = (f32[256,1024]{1,0:T(8,128)S(1)}, f32[256,1024]{1,0:T(8,128)S(1)}, u32[]{:S(2)}, u32[]{:S(2)}) collective-permute-start(f32[256,1024]{1,0:T(8,128)S(1)} %fusion.1.weight_mine), channel_id=1, source_target_pairs={{0,16},{16,0},{1,17},{17,1},{2,18},{18,2},{3,19},{19,3},{4,20},{20... | collective-permute-start | bytes 3145736 | tf_op jit(solution)/shard_map/ppermute | solution.py:104
  130.3 0.1 convert_reduce_fusion.key_mine
  130.4 0.1 collective-permute-start.24
  130.5 2.0 %collective-permute-done.23.weight_pair = f32[256,1024]{1,0:T(8,128)S(1)} collective-permute-done((f32[256,1024]{1,0:T(8,128)S(1)}, f32[256,1024]{1,0:T(8,128)S(1)}, u32[]{:S(2)}, u32[]{:S(2)}) %collective-permute-start.23) | collective-permute-done | bytes 1048608 | tf_op jit(solution)/shard_map/ppermute | solution.py:104
  132.6 0.7 collective-permute-done.24.key_pair
  133.3 2.5 %shard_map.80 = (f32[256,2048]{1,0:T(8,128)}, f32[256,1024]{1,0:T(8,128)}) custom-call(s32[5]{0:T(128)S(1)} %stack.23.shift, f32[256,1024]{1,0:T(8,128)S(1)} %fusion.1.weight_mine, f32[256,1024]{1,0:T(8,128)S(1)} %collective-permute-done.23.weight_pair, f32[256,512]{1,0:T(8,128)S(1)} %convert_reduce_fusion.key_mine, ...), custom_call_target="tpu_custom_call" | custom-call | tf_op jit(solution)/shard_map/pallas_call | solution.py:205
  (53 shorter events, 0.1 us)
Async XLA Ops:
  0.6 9.5 %copy-start = (bf16[512,1024]{1,0:T(8,128)(2,1)S(1)}, bf16[512,1024]{1,0:T(8,128)(2,1)}, u32[]{:S(2)}) copy-start(bf16[512,1024]{1,0:T(8,128)(2,1)} %refs_0_.3) | copy-start | bytes 3145732
  0.6 9.5 %copy-start.16 = (s32[512,1]{0,1:T(1,128)S(1)}, s32[512,1]{0,1:T(1,128)}, u32[]{:S(2)}) copy-start(s32[512,1]{0,1:T(1,128)} %param.10) | copy-start | bytes 6148
  0.6 9.5 %copy-start.15 = (s32[512]{0:T(512)S(1)}, s32[512]{0:T(512)}, u32[]{:S(2)}) copy-start(s32[512]{0:T(512)} %param.11) | copy-start | bytes 6148
  2.6 13.1 %collective-permute-start = (bf16[128,2048]{1,0:T(8,128)(2,1)}, bf16[128,2048]{1,0:T(8,128)(2,1)S(1)}, u32[]{:S(2)}, u32[]{:S(2)}) collective-permute-start(bf16[128,2048]{1,0:T(8,128)(2,1)} %constant_dynamic-slice_fusion.18), channel_id=1, source_target_pairs={{0,4},{4,0},{8,12},{12,8},{1,5},{5,1},{9,13},{13,9},{2,6},{6,2},{1... | collective-permute-start | bytes 1572872 | tf_op jit(solution)/shard_map/ppermute | solution.py:110
  2.8 16.0 %collective-permute-start.1 = (bf16[128,2048]{1,0:T(8,128)(2,1)}, bf16[128,2048]{1,0:T(8,128)(2,1)}, u32[]{:S(2)}, u32[]{:S(2)}) collective-permute-start(bf16[128,2048]{1,0:T(8,128)(2,1)} %constant_dynamic-slice_fusion.18), channel_id=1, source_target_pairs={{4,8},{8,4},{5,9},{9,5},{6,10},{10,6},{7,11},{11,7},{20,24},{24,20... | collective-permute-start | bytes 1572872 | tf_op jit(solution)/shard_map/ppermute | solution.py:119
  8.9 4.0 %collective-permute-start.2 = (bf16[512,256]{1,0:T(8,128)(2,1)}, bf16[512,256]{1,0:T(8,128)(2,1)}, u32[]{:S(2)}, u32[]{:S(2)}) collective-permute-start(bf16[512,256]{1,0:T(8,128)(2,1)} %get-tuple-element.61), channel_id=1, source_target_pairs={{0,16},{16,0},{1,17},{17,1},{2,18},{18,2},{3,19},{19,3},{4,20},{20... | collective-permute-start | bytes 786440 | tf_op jit(solution)/shard_map/ppermute | solution.py:104
  10.1 17.7 %collective-permute-start.5 = (bf16[512,1024]{1,0:T(8,128)(2,1)S(1)}, bf16[512,1024]{1,0:T(8,128)(2,1)S(1)}, u32[]{:S(2)}, u32[]{:S(2)}) collective-permute-start(bf16[512,1024]{1,0:T(8,128)(2,1)S(1)} %copy-done), channel_id=1, source_target_pairs={{0,16},{16,0},{1,17},{17,1},{2,18},{18,2},{3,19},{19,3},{4,20},{20... | collective-permute-start | bytes 3145736 | tf_op jit(solution)/shard_map/ppermute | solution.py:104
  10.2 3.8 %collective-permute-start.6 = (s32[512]{0:T(512)S(1)}, s32[512]{0:T(512)S(1)}, u32[]{:S(2)}, u32[]{:S(2)}) collective-permute-start(s32[512]{0:T(512)S(1)} %add.107), channel_id=1, source_target_pairs={{0,16},{16,0},{1,17},{17,1},{2,18},{18,2},{3,19},{19,3},{4,20},{20... | collective-permute-start | bytes 6152 | tf_op jit(solution)/shard_map/ppermute | solution.py:104
  12.9 5.9 %collective-permute-start.7 = (bf16[512,512]{1,0:T(8,128)(2,1)S(1)}, bf16[512,512]{1,0:T(8,128)(2,1)S(1)}, u32[]{:S(2)}, u32[]{:S(2)}) collective-permute-start(bf16[512,512]{1,0:T(8,128)(2,1)S(1)} %pad_maximum_fusion.6), channel_id=1, source_target_pairs={{0,16},{16,0},{1,17},{17,1},{2,18},{18,2},{3,19},{19,3},{4,20},{20... | collective-permute-start | bytes 1572872 | tf_op jit(solution)/shard_map/ppermute | solution.py:104
  14.0 13.2 %collective-permute-start.3 = (bf16[1024,256]{1,0:T(8,128)(2,1)S(1)}, bf16[1024,256]{1,0:T(8,128)(2,1)}, u32[]{:S(2)}, u32[]{:S(2)}) collective-permute-start(bf16[1024,256]{1,0:T(8,128)(2,1)S(1)} %pad_maximum_fusion.5.refs_2_.refs_0_), channel_id=1, source_target_pairs={{0,1},{1,0},{2,3},{3,2},{4,5},{5,4},{6,7},{7,6},{8,9},{9,8},{10,11... | collective-permute-start | bytes 1572872 | tf_op jit(solution)/shard_map/ppermute | solution.py:107
  15.7 31.6 %copy-start.11 = (bf16[128,2048]{1,0:T(8,128)(2,1)}, bf16[128,2048]{1,0:T(8,128)(2,1)S(1)}, u32[]{:S(2)}) copy-start(bf16[128,2048]{1,0:T(8,128)(2,1)S(1)} %collective-permute-done) | copy-start | bytes 1572868
  15.7 12.1 %collective-permute-start.4 = (bf16[1024,256]{1,0:T(8,128)(2,1)S(1)}, bf16[1024,256]{1,0:T(8,128)(2,1)}, u32[]{:S(2)}, u32[]{:S(2)}) collective-permute-start(bf16[1024,256]{1,0:T(8,128)(2,1)S(1)} %pad_maximum_fusion.5.refs_2_.refs_0_), channel_id=1, source_target_pairs={{0,2},{1,3},{2,0},{3,1},{4,6},{5,7},{6,4},{7,5},{8,10},{9,11},{10,... | collective-permute-start | bytes 1572872 | tf_op jit(solution)/shard_map/ppermute | solution.py:107
  18.8 9.1 %copy-start.14 = (bf16[512,512]{1,0:T(8,128)(2,1)}, bf16[512,512]{1,0:T(8,128)(2,1)S(1)}, u32[]{:S(2)}) copy-start(bf16[512,512]{1,0:T(8,128)(2,1)S(1)} %collective-permute-done.7) | copy-start | bytes 1572868
  27.8 21.6 %collective-permute-start.8 = (bf16[128,2048]{1,0:T(8,128)(2,1)}, bf16[128,2048]{1,0:T(8,128)(2,1)}, u32[]{:S(2)}, u32[]{:S(2)}) collective-permute-start(bf16[128,2048]{1,0:T(8,128)(2,1)} %collective-permute-done.1), channel_id=1, source_target_pairs={{4,0},{8,12},{5,1},{9,13},{6,2},{10,14},{7,3},{11,15},{20,16},{24,... | collective-permute-start | bytes 1572872 | tf_op jit(solution)/shard_map/ppermute | solution.py:116
  30.5 18.9 %collective-permute-start.9 = (bf16[128,2048]{1,0:T(8,128)(2,1)S(1)}, bf16[128,2048]{1,0:T(8,128)(2,1)}, u32[]{:S(2)}, u32[]{:S(2)}) collective-permute-start(bf16[128,2048]{1,0:T(8,128)(2,1)S(1)} %collective-permute-done), channel_id=1, source_target_pairs={{4,8},{8,4},{5,9},{9,5},{6,10},{10,6},{7,11},{11,7},{20,24},{24,20... | collective-permute-start | bytes 1572872 | tf_op jit(solution)/shard_map/ppermute | solution.py:119
  36.7 10.6 %collective-permute-start.10 = (bf16[512,256]{1,0:T(8,128)(2,1)}, bf16[512,256]{1,0:T(8,128)(2,1)}, u32[]{:S(2)}, u32[]{:S(2)}) collective-permute-start(bf16[512,256]{1,0:T(8,128)(2,1)} %slice.6), channel_id=1, source_target_pairs={{0,2},{1,3},{2,0},{3,1},{4,6},{5,7},{6,4},{7,5},{8,10},{9,11},{10,... | collective-permute-start | bytes 786440 | tf_op jit(solution)/shard_map/ppermute | solution.py:107
  39.6 7.8 %collective-permute-start.11 = (bf16[512,256]{1,0:T(8,128)(2,1)}, bf16[512,256]{1,0:T(8,128)(2,1)S(1)}, u32[]{:S(2)}, u32[]{:S(2)}) collective-permute-start(bf16[512,256]{1,0:T(8,128)(2,1)} %slice.7), channel_id=1, source_target_pairs={{0,1},{1,0},{2,3},{3,2},{4,5},{5,4},{6,7},{7,6},{8,9},{9,8},{10,11... | collective-permute-start | bytes 786440 | tf_op jit(solution)/shard_map/ppermute | solution.py:107
  39.9 18.7 %collective-permute-start.17 = (bf16[1024,256]{1,0:T(8,128)(2,1)S(1)}, bf16[1024,256]{1,0:T(8,128)(2,1)S(1)}, u32[]{:S(2)}, u32[]{:S(2)}) collective-permute-start(bf16[1024,256]{1,0:T(8,128)(2,1)S(1)} %pad_maximum_fusion.5.refs_2_.refs_0_), channel_id=1, source_target_pairs={{0,16},{16,0},{1,17},{17,1},{2,18},{18,2},{3,19},{19,3},{4,20},{20... | collective-permute-start | bytes 1572872 | tf_op jit(solution)/shard_map/ppermute | solution.py:104
  47.3 15.3 %collective-permute-start.18 = (bf16[1024,256]{1,0:T(8,128)(2,1)}, bf16[1024,256]{1,0:T(8,128)(2,1)}, u32[]{:S(2)}, u32[]{:S(2)}) collective-permute-start(bf16[1024,256]{1,0:T(8,128)(2,1)} %collective-permute-done.3.refs_3_.refs_1_), channel_id=1, source_target_pairs={{0,16},{16,0},{1,17},{17,1},{2,18},{18,2},{3,19},{19,3},{4,20},{20... | collective-permute-start | bytes 1572872 | tf_op jit(solution)/shard_map/ppermute | solution.py:104
  47.4 16.6 %collective-permute-start.19 = (bf16[1024,256]{1,0:T(8,128)(2,1)}, bf16[1024,256]{1,0:T(8,128)(2,1)}, u32[]{:S(2)}, u32[]{:S(2)}) collective-permute-start(bf16[1024,256]{1,0:T(8,128)(2,1)} %collective-permute-done.4.refs_4_.refs_2_), channel_id=1, source_target_pairs={{0,16},{16,0},{1,17},{17,1},{2,18},{18,2},{3,19},{19,3},{4,20},{20... | collective-permute-start | bytes 1572872 | tf_op jit(solution)/shard_map/ppermute | solution.py:104
  50.4 14.9 %collective-permute-start.15 = (bf16[128,2048]{1,0:T(8,128)(2,1)}, bf16[128,2048]{1,0:T(8,128)(2,1)}, u32[]{:S(2)}, u32[]{:S(2)}) collective-permute-start(bf16[128,2048]{1,0:T(8,128)(2,1)} %collective-permute-done.9), channel_id=1, source_target_pairs={{4,0},{8,12},{5,1},{9,13},{6,2},{10,14},{7,3},{11,15},{20,16},{24,... | collective-permute-start | bytes 1572872 | tf_op jit(solution)/shard_map/ppermute | solution.py:116
  55.2 1.2 copy-start.9
  56.3 2.3 %copy-start.3 = (f32[256,768]{1,0:T(8,128)}, f32[256,768]{1,0:T(8,128)S(1)}, u32[]{:S(2)}) copy-start(f32[256,768]{1,0:T(8,128)S(1)} %get-tuple-element.42) | copy-start | bytes 2359300
  57.3 15.8 %collective-permute-start.16 = (bf16[256,1024]{1,0:T(8,128)(2,1)}, bf16[256,1024]{1,0:T(8,128)(2,1)}, u32[]{:S(2)}, u32[]{:S(2)}) collective-permute-start(bf16[256,1024]{1,0:T(8,128)(2,1)} %fusion.2), channel_id=1, source_target_pairs={{0,4},{12,8},{1,5},{13,9},{2,6},{14,10},{3,7},{15,11},{16,20},{28,... | collective-permute-start | bytes 1572872 | tf_op jit(solution)/shard_map/ppermute | solution.py:113
  58.6 0.8 copy-start.1
  59.4 13.6 %collective-permute-start.20 = (bf16[1024,256]{1,0:T(8,128)(2,1)S(1)}, bf16[1024,256]{1,0:T(8,128)(2,1)S(1)}, u32[]{:S(2)}, u32[]{:S(2)}) collective-permute-start(bf16[1024,256]{1,0:T(8,128)(2,1)S(1)} %constant_dynamic-update-slice_fusion.refs_2_.refs_3_), channel_id=1, source_target_pairs={{0,16},{16,0},{1,17},{17,1},{2,18},{18,2},{3,19},{19,3},{4,20},{20... | collective-permute-start | bytes 1572872 | tf_op jit(solution)/shard_map/ppermute | solution.py:104
  59.5 1.3 copy-start.7
  60.8 12.2 %copy-start.4 = (f32[256,768]{1,0:T(8,128)S(1)}, f32[256,768]{1,0:T(8,128)}, u32[]{:S(2)}) copy-start(f32[256,768]{1,0:T(8,128)} %copy-done.3) | copy-start | bytes 2359300
  60.8 12.2 %copy-start.10 = (f32[256,256]{1,0:T(8,128)S(1)}, f32[256,256]{1,0:T(8,128)}, u32[]{:S(2)}) copy-start(f32[256,256]{1,0:T(8,128)} %copy-done.9) | copy-start | bytes 786436
  61.8 15.2 %copy-start.6 = (bf16[256,2048]{1,0:T(8,128)(2,1)S(1)}, bf16[256,2048]{1,0:T(8,128)(2,1)}, u32[]{:S(2)}) copy-start(bf16[256,2048]{1,0:T(8,128)(2,1)} %param.9) | copy-start | bytes 3145732
  61.8 15.2 %copy-start.12 = (bf16[128,2048]{1,0:T(8,128)(2,1)S(1)}, bf16[128,2048]{1,0:T(8,128)(2,1)}, u32[]{:S(2)}) copy-start(bf16[128,2048]{1,0:T(8,128)(2,1)} %copy-done.11) | copy-start | bytes 1572868
  62.7 29.4 %collective-permute-start.13 = (bf16[256,1024]{1,0:T(8,128)(2,1)}, bf16[256,1024]{1,0:T(8,128)(2,1)}, u32[]{:S(2)}, u32[]{:S(2)}) collective-permute-start(bf16[256,1024]{1,0:T(8,128)(2,1)} %fusion.3), channel_id=1, source_target_pairs={{0,4},{12,8},{1,5},{13,9},{2,6},{14,10},{3,7},{15,11},{16,20},{28,... | collective-permute-start | bytes 1572872 | tf_op jit(solution)/shard_map/ppermute | solution.py:113
  64.0 35.0 %collective-permute-start.12 = (bf16[256,1024]{1,0:T(8,128)(2,1)}, bf16[256,1024]{1,0:T(8,128)(2,1)}, u32[]{:S(2)}, u32[]{:S(2)}) collective-permute-start(bf16[256,1024]{1,0:T(8,128)(2,1)} %fusion.4), channel_id=1, source_target_pairs={{0,4},{12,8},{1,5},{13,9},{2,6},{14,10},{3,7},{15,11},{16,20},{28,... | collective-permute-start | bytes 1572872 | tf_op jit(solution)/shard_map/ppermute | solution.py:113
  75.0 21.4 %collective-permute-start.21 = (bf16[256,1024]{1,0:T(8,128)(2,1)}, bf16[256,1024]{1,0:T(8,128)(2,1)}, u32[]{:S(2)}, u32[]{:S(2)}) collective-permute-start(bf16[256,1024]{1,0:T(8,128)(2,1)} %add_convert_fusion.1), channel_id=1, source_target_pairs={{4,8},{8,4},{5,9},{9,5},{6,10},{10,6},{7,11},{11,7},{20,24},{24,20... | collective-permute-start | bytes 1572872 | tf_op jit(solution)/shard_map/ppermute | solution.py:119
  79.4 1.0 copy-start.2
  88.0 4.1 %copy-start.8 = (f32[256,256]{1,0:T(8,128)S(1)}, f32[256,256]{1,0:T(8,128)}, u32[]{:S(2)}) copy-start(f32[256,256]{1,0:T(8,128)} %get-tuple-element.56) | copy-start | bytes 786436
  88.0 42.3 %all-to-all-start = ((bf16[4,256,512]{2,1,0:T(8,128)(2,1)}), bf16[4,256,512]{2,1,0:T(8,128)(2,1)S(1)}, u32[]{:S(2)}, u32[]{:S(2)}) async-start(bf16[4,256,512]{2,1,0:T(8,128)(2,1)} %bitcast.8), calls=%async_computation | async-start | bytes 2097152 | tf_op jit(solution)/shard_map/all_to_all | solution.py:201
  92.1 35.3 %copy-start.5 = (f32[256,768]{1,0:T(8,128)S(1)}, f32[256,768]{1,0:T(8,128)}, u32[]{:S(2)}) copy-start(f32[256,768]{1,0:T(8,128)} %get-tuple-element.44) | copy-start | bytes 2359300
  92.1 35.3 %copy-start.13 = (f32[256,256]{1,0:T(8,128)S(1)}, f32[256,256]{1,0:T(8,128)}, u32[]{:S(2)}) copy-start(f32[256,256]{1,0:T(8,128)} %get-tuple-element.59) | copy-start | bytes 786436
  93.4 34.0 %collective-permute-start.14 = (bf16[256,1024]{1,0:T(8,128)(2,1)S(1)}, bf16[256,1024]{1,0:T(8,128)(2,1)S(1)}, u32[]{:S(2)}, u32[]{:S(2)}) collective-permute-start(bf16[256,1024]{1,0:T(8,128)(2,1)S(1)} %add_convert_fusion.2), channel_id=1, source_target_pairs={{4,8},{8,4},{5,9},{9,5},{6,10},{10,6},{7,11},{11,7},{20,24},{24,20... | collective-permute-start | bytes 1572872 | tf_op jit(solution)/shard_map/ppermute | solution.py:119
  97.7 29.7 %collective-permute-start.22 = (bf16[256,1024]{1,0:T(8,128)(2,1)S(1)}, bf16[256,1024]{1,0:T(8,128)(2,1)S(1)}, u32[]{:S(2)}, u32[]{:S(2)}) collective-permute-start(bf16[256,1024]{1,0:T(8,128)(2,1)S(1)} %add_convert_fusion), channel_id=1, source_target_pairs={{4,0},{8,12},{5,1},{9,13},{6,2},{10,14},{7,3},{11,15},{20,16},{24,... | collective-permute-start | bytes 1572872 | tf_op jit(solution)/shard_map/ppermute | solution.py:116
  128.8 3.8 %collective-permute-start.23 = (f32[256,1024]{1,0:T(8,128)S(1)}, f32[256,1024]{1,0:T(8,128)S(1)}, u32[]{:S(2)}, u32[]{:S(2)}) collective-permute-start(f32[256,1024]{1,0:T(8,128)S(1)} %fusion.1.weight_mine), channel_id=1, source_target_pairs={{0,16},{16,0},{1,17},{17,1},{2,18},{18,2},{3,19},{19,3},{4,20},{20... | collective-permute-start | bytes 3145736 | tf_op jit(solution)/shard_map/ppermute | solution.py:104
  130.4 2.9 %collective-permute-start.24 = (f32[256,512]{1,0:T(8,128)S(1)}, f32[256,512]{1,0:T(8,128)S(1)}, u32[]{:S(2)}, u32[]{:S(2)}) collective-permute-start(f32[256,512]{1,0:T(8,128)S(1)} %convert_reduce_fusion.key_mine), channel_id=1, source_target_pairs={{0,16},{16,0},{1,17},{17,1},{2,18},{18,2},{3,19},{19,3},{4,20},{20... | collective-permute-start | bytes 1572872 | tf_op jit(solution)/shard_map/ppermute | solution.py:104

commit v3 on v1

v3 whole, which is shorter than its diff:
```python
import jax
import jax.numpy as jnp
from jax import lax
from jax.experimental import pallas as pl
from jax.experimental.pallas import tpu as pltpu
from jax.sharding import PartitionSpec as P

F32, BF16 = jnp.float32, jnp.bfloat16
KEY_DEV = 256


def dot(a, b, ca, cb):
    return lax.dot_general(a, b, (((ca,), (cb,)), ((), ())), preferred_element_type=F32)


def general_body(layer_input, value_grad, residual_grad, value_weight, owner, key_row):
    all_heads = lax.all_gather(value_grad, "tp", axis=1, tiled=True)
    tok_rows, features = layer_input.shape
    groups = lax.axis_size("fsdp")
    slots = 2 * tok_rows // groups
    keys_here = KEY_DEV
    width = all_heads.shape[1]
    term = dot(layer_input, all_heads, 0, 0)
    pieces = term.astype(BF16).reshape(groups, features // groups, width)
    arrived = lax.all_to_all(pieces, "fsdp", split_axis=0, concat_axis=0, tiled=True)
    shard = jnp.sum(arrived.astype(F32), axis=0)
    back = dot(all_heads, lax.all_gather(value_weight, "fsdp", axis=0, tiled=True), 1, 1)
    input_grad = (residual_grad.astype(F32) + back).astype(BF16)
    target = owner[:, 0]
    onehot = (target[:, None] == jnp.arange(groups, dtype=jnp.int32)[None, :]).astype(jnp.int32)
    position = jnp.sum(jnp.cumsum(onehot, axis=0) * onehot, axis=1) - 1
    place = target * slots + position
    chooser = jnp.arange(groups * slots, dtype=jnp.int32)[:, None] == place[None, :]
    outgoing = dot(chooser.astype(BF16), input_grad, 1, 0).astype(BF16)
    out_keys = jnp.sum(jnp.where(chooser, key_row[None, :] + 1, 0), axis=1) - 1
    arrived = lax.all_to_all(outgoing, "fsdp", split_axis=0, concat_axis=0, tiled=True)
    arrived_keys = lax.all_to_all(out_keys, "fsdp", split_axis=0, concat_axis=0, tiled=True)
    selector = (arrived_keys[:, None] == jnp.arange(keys_here, dtype=jnp.int32)[None, :]).astype(BF16)
    table = dot(selector, arrived, 0, 0)
    return lax.psum(shard, "dp"), lax.psum(table, "dp")


def term_kernel(place, *refs):
    n = sum(r.shape == refs[8].shape for r in refs[8:]) // 2
    inputs, heads, out, sends = refs[:8], refs[8 : 8 + 2 * n], refs[8 + 2 * n], refs[9 + 2 * n :]
    width = heads[0].shape[1]
    for side in range(2):
        turned = jnp.concatenate([r[...] for r in inputs[4 * side : 4 * side + 4]], 1).T
        for k in range(n):
            add = dot(turned, heads[n * side + k][...], 1, 0)
            cols = slice(k * width, (k + 1) * width)
            if side == 0:
                out[:, cols] = add
            else:
                out[:, cols] += add
    row = 0
    for send in sends:
        send[...] = out[row : row + send.shape[0], :].astype(BF16)
        row += send.shape[0]


def back_kernel(place, *refs):
    residuals, heads, refs = refs[:8], refs[8:16], refs[16:]
    own, beside, mid, end, third, fourth, key, send, keep, weight = refs
    half, width = own.shape[0], heads[0].shape[1]
    tokens = heads[0].shape[0]
    keys = keep.shape[0] // 2

    def put(which, ref):
        weight[pl.ds(pl.multiple_of(place[which] * half, half), half), :] = ref[...]

    put(5, own)
    put(6, beside)

    @pl.when(place[9] == 1)
    def _():
        put(7, third)
        put(8, fourth)

    @pl.when(place[9] == 0)
    def _():
        put(7, mid)
        put(8, end)

    row = lax.broadcasted_iota(jnp.int32, (keys, tokens), 0)
    total = [None] * 2
    for side in range(2):
        acc = jnp.concatenate([r[...] for r in residuals[4 * side : 4 * side + 4]], 1).astype(F32)
        for k in range(4):
            cols = pl.ds(pl.multiple_of(place[k] * width, width), width)
            acc = acc + dot(heads[4 * side + k][...], weight[:, cols], 1, 1)
        rows = acc.astype(BF16)
        for i in range(2):
            chosen = jnp.concatenate(
                [(row + place[10 + 2 * i + j] * keys) == key[side : side + 1, :] for j in range(2)], 0
            )
            add = dot(jnp.where(chosen, 1.0, 0.0).astype(BF16), rows, 1, 0)
            total[i] = add if side == 0 else total[i] + add
    send[...] = total[0].astype(BF16)
    keep[...] = total[1]


def join_weight_kernel(place, mine, pair, out):
    half, width = mine.shape[0], mine.shape[1] // 4
    here = pl.multiple_of(place[4] * half, half)
    there = pl.multiple_of(half - place[4] * half, half)
    for k in range(4):
        start = pl.multiple_of(place[k] * width, width)
        out[pl.ds(here, half), pl.ds(start, width)] = mine[:, k * width : (k + 1) * width]
        out[pl.ds(there, half), pl.ds(start, width)] = pair[:, k * width : (k + 1) * width]


def join_key_kernel(place, mine, pair, out):
    first = place[4] == 0
    half = mine.shape[1] // 4
    for p in range(4):
        a, b = mine[:, p * half : (p + 1) * half], pair[:, p * half : (p + 1) * half]
        out[:, 2 * p * half : (2 * p + 1) * half] = jnp.where(first, a, b)
        out[:, (2 * p + 1) * half : (2 * p + 2) * half] = jnp.where(first, b, a)


def pair_body(layer_input, value_grad, residual_grad, value_weight, owner, key_row):
    core, z, t = (lax.axis_index(n) for n in ("dp", "fsdp", "tp"))
    tokens, features = layer_input.shape
    heads = value_grad.shape[1]
    part = features // 4
    half = part // 2
    keys = KEY_DEV
    phase = lax.optimization_barrier

    def core_swap(v):
        return lax.ppermute(v, "dp", [(0, 1), (1, 0)])

    def outer(v):
        return lax.ppermute(v, "fsdp", [(0, 1), (1, 0), (2, 3), (3, 2)])

    def inward(v):
        return lax.ppermute(v, "fsdp", [(0, 1), (3, 2)])

    def outward(v):
        return lax.ppermute(v, "fsdp", [(1, 0), (2, 3)])

    def inner(v):
        return lax.ppermute(v, "fsdp", [(1, 2), (2, 1)])

    end = ((z == 0) | (z == 3)).astype(jnp.int32)
    low = z < 2
    beside = z ^ 1
    far_mid = jnp.where(low, 2, 1)
    far_end = jnp.where(low, 3, 0)
    place = jnp.stack([t, t ^ 1, t ^ 2, t ^ 3, core, z, beside, far_mid, far_end, end, z ^ 1, z ^ 3, z, z ^ 2]).astype(jnp.int32)
    ranked = [pl.BlockSpec((tokens, half), lambda i, s, r=r: (0, 2 * s[r] + s[4])) for r in (8, 7, 6, 5)]
    split = [pl.BlockSpec((tokens, half), lambda i, s, p=p: (0, 2 * p + s[4])) for p in range(4)]

    def whole(*shape):
        return pl.BlockSpec(shape, lambda i, s: (0,) * len(shape))

    def call(kernel, out, in_specs, scratch, flops, *args):
        return pl.pallas_call(
            kernel,
            out_shape=out,
            grid_spec=pltpu.PrefetchScalarGridSpec(
                num_scalar_prefetch=1, grid=(1,), in_specs=in_specs,
                out_specs=jax.tree.map(lambda o: whole(*o.shape), out), scratch_shapes=scratch,
            ),
            compiler_params=pltpu.CompilerParams(vmem_limit_bytes=40 << 20),
            cost_estimate=pl.CostEstimate(flops=flops, bytes_accessed=6 << 20, transcendentals=0),
        )(place, *args)

    def square(v, d):
        return lax.ppermute(v, "tp", [(i, i ^ d) for i in range(4)])

    def across(v):
        return lax.ppermute(v, "fsdp", [(i, i ^ 2) for i in range(4)])

    def struct(rows, cols, dtype):
        return jax.ShapeDtypeStruct((rows, cols), dtype)

    def term(v, sends):
        n = len(v) // 2
        out = (struct(4 * half, n * heads, F32),) + tuple(struct(r, n * heads, BF16) for r in sends)
        return call(
            term_kernel, out, ranked * 2 + [whole(tokens, heads)] * (2 * n), [], n << 29,
            *([layer_input] * 4), *([in_other] * 4), *v,
        )

    def plus(v, came):
        return (v + came.astype(F32)).astype(BF16)

    v0 = value_grad
    v0_other, weight_rows = phase((core_swap(v0), value_weight))
    in_other = core_swap(layer_input)
    w_own = lax.dynamic_slice_in_dim(weight_rows, core * half, half, 0)
    got = phase((outer(w_own), inner(w_own), square(v0, 1), square(v0, 2), in_other))
    w_beside, w_mid, vx, vy, in_other = got

    vx_other, vy_other = core_swap(vx), core_swap(vy)
    term1, send1, send2 = term((v0, vx, vy, v0_other, vx_other, vy_other), (half, half))
    i1, i2 = inward(send1), inward(send2)
    key = owner[:, 0] * keys + key_row
    w_third, w_end, vd, term1 = phase((outward(w_mid), inner(w_beside), square(v0, 3), term1))

    vd_other = core_swap(vd)
    term2, send3 = term((vd, vd_other), (2 * half,))
    res_other, key_other = core_swap(residual_grad), core_swap(key)
    i1, w_fourth, term2, res_other, key_other = phase((i1, outward(w_end), term2, res_other, key_other))

    b1 = inner(plus(term1[:half], i1))
    i3 = inward(send3)
    send, keep = call(
        back_kernel, (struct(2 * keys, 4 * half, BF16), struct(2 * keys, 4 * half, F32)),
        split * 2 + [whole(tokens, heads)] * 8 + [whole(half, 4 * heads)] * 6 + [whole(2, tokens)],
        [pltpu.VMEM((4 * half, 4 * heads), BF16)], 3 << 30,
        *([residual_grad] * 4), *([res_other] * 4), v0, vx, vy, vd, v0_other, vx_other, vy_other, vd_other,
        w_own, w_beside, w_mid, w_end, w_third, w_fourth, jnp.stack([key, key_other]),
    )
    send, keep, b1, i2 = phase((send, keep, b1, i2))

    k1 = outer(send)
    b2 = inner(plus(term1[half : 2 * half], i2))
    a1 = outward(plus(term1[2 * half : 3 * half], b1))
    i4 = inward(jnp.concatenate([v[2 * half : 3 * half].astype(BF16) for v in (term1, term2)], 1))
    b3 = inner(plus(term2[: 2 * half], i3))
    k1, b2, i3 = phase((k1, b2, i3))
    k2 = across(plus(keep[keys:], k1[keys:]))
    a3 = outward(plus(term2[2 * half : 3 * half], b3[:half]))
    key_half = keep[:keys] + k1[:keys].astype(F32) + k2.astype(F32)

    def total(v, *came):
        return sum((c.astype(F32) for c in came), v[3 * half :])

    weight_half = jnp.concatenate([
        total(term1, i4[:, : 3 * heads], b2, a1), total(term2, i4[:, 3 * heads :], b3[half:], a3),
    ], 1)
    weight_pair = core_swap(weight_half)
    key_pair = core_swap(key_half)

    weight_grad = call(
        join_weight_kernel, jax.ShapeDtypeStruct((part, 4 * heads), F32),
        [whole(half, 4 * heads)] * 2, [], 0, weight_half, weight_pair,
    )
    key_grad = call(
        join_key_kernel, jax.ShapeDtypeStruct((keys, features), F32),
        [whole(keys, 4 * half)] * 2, [], 0, key_half, key_pair,
    )
    return weight_grad, key_grad


def solution(mesh):
    shape = dict(mesh.shape)
    special = shape == {"dp": 2, "fsdp": 4, "tp": 4}
    return jax.shard_map(
        pair_body if special else general_body,
        mesh=mesh,
        in_specs=(
            P(("dp", "fsdp"), "tp"),
            P(("dp", "fsdp"), "tp"),
            P(("dp", "fsdp"), "tp"),
            P(("tp", "fsdp"), None),
            P(("dp", "fsdp"), None),
            P(("dp", "fsdp")),
        ),
        out_specs=(P(("tp", "fsdp"), None), P("fsdp", "tp")),
        check_vma=False,
    )
```

time: 155 us -> 115 us (0.74)
  other arithmetic: 20.8 us -> 0.98 us
  Pallas kernels: 0 us -> 16.3 us
  matrix products: 14.5 us -> 0 us
  starting transfers between devices: 54.4 us -> 40.9 us
  waiting for transfers between devices: 59 us -> 47.5 us
  local copies, waits for them, and re-layouts: 4.54 us -> 8 us
    ppermute x5 -> x2, waiting for transfers between devices: 39.3 us -> 1.2 us  [outer(): return lax.ppermute(v, 'fsdp', [(0, 1), (1, 0), (2, 3), (3, 2)])]
    ppermute x5 -> x2, starting transfers between devices: 31.6 us -> 7.15 us  [outer(): return lax.ppermute(v, 'fsdp', [(0, 1), (1, 0), (2, 3), (3, 2)])]
    ppermute x4 -> x8, waiting for transfers between devices: 16 us -> 37.1 us  [the longest x4 20.5 us: outward(): return lax.ppermute(v, 'fsdp', [(1, 0), (2, 3)])]
    pallas_call x0 -> x5, Pallas kernels: none -> 16.3 us  [call(): pl.pallas_call(kernel, out_shape=out, grid_spec=pltpu.PrefetchScalarGridS...]
    dot_general x4 -> x0, matrix products: 14.5 us -> none  [dot(): lax.dot_general(a, b, (((ca,), (cb,)), ((), ())), preferred_element_type=...]
    convert_element_type x4 -> x5, other arithmetic: 7.72 us -> 0.48 us  [plus(): return (v + came.astype(F32)).astype(BF16)]
    unnamed x38 -> x32, local copies, waits for them, and re-layouts: 0.58 us -> 7.81 us
    ppermute x4 -> x8, starting transfers between devices: 7.91 us -> 15 us  [the longest x3 6.09 us: square(): return lax.ppermute(v, 'tp', [(i, i ^ d) for i in range(4)])]
  transfers between devices with their start and end apart: 23 -> 28, of which waited for: 9 -> 14; matrix products, arithmetic and copies ran while one was open for 19% -> 1% of each run, Pallas kernels for 0% -> 12%
where the time goes in v3:
time: 115 us
  waiting for transfers between devices  47.5 us (41%)
  starting transfers between devices  40.9 us (36%)
  Pallas kernels  16.3 us (14%)
  local copies, waits for them, and re-layouts  8 us (7%)
    ppermute x4, waiting for transfers between devices, outward(): return lax.ppermute(v, 'fsdp', [(1, 0), (2, 3)])  20.5 us
    pallas_call x5, Pallas kernels, call(): pl.pallas_call(kernel, out_shape=out, grid_spec=pltpu.PrefetchScalarGridS...  16.3 us
    ppermute x4, starting transfers between devices, inward(): return lax.ppermute(v, 'fsdp', [(0, 1), (3, 2)])  12.3 us
    ppermute x3, waiting for transfers between devices, square(): return lax.ppermute(v, 'tp', [(i, i ^ d) for i in range(4)])  8.93 us
    unnamed x32, local copies, waits for them, and re-layouts  7.81 us
    ppermute x1, waiting for transfers between devices, across(): return lax.ppermute(v, 'fsdp', [(i, i ^ 2) for i in range(4)])  7.66 us
    ppermute x4, waiting for transfers between devices, inward(): return lax.ppermute(v, 'fsdp', [(0, 1), (3, 2)])  7.24 us
    ppermute x2, starting transfers between devices, outer(): return lax.ppermute(v, 'fsdp', [(0, 1), (1, 0), (2, 3), (3, 2)])  7.15 us
  transfers between devices with their start and end apart: 28, of which 14 were waited for; matrix products, arithmetic and copies ran while one was open for 1% of the time, Pallas kernels for 12%

profile of v3, /device:TPU:0, one launch (start us, length us, event | category | flops | bytes accessed | tf_op | source)
XLA Modules:
  0.0 114.8 jit_solution(13897522066601426119)
XLA Ops:
  0.6 0.0 copy-start
  0.6 0.5 collective-permute-start
  1.2 0.1 collective-permute-start.5
  1.2 2.9 %collective-permute-start.3 = (bf16[512,512]{1,0:T(8,128)(2,1)}, bf16[512,512]{1,0:T(8,128)(2,1)S(1)}, u32[]{:S(2)}, u32[]{:S(2)}) collective-permute-start(bf16[512,512]{1,0:T(8,128)(2,1)} %refs_8_.3), channel_id=1, source_target_pairs={{0,1},{1,0},{2,3},{3,2},{4,5},{5,4},{6,7},{7,6},{8,9},{9,8},{10,11... | collective-permute-start | bytes 1572872 | tf_op jit(solution)/shard_map/ppermute | solution.py:171
  4.2 1.5 %collective-permute-start.4 = (bf16[512,512]{1,0:T(8,128)(2,1)}, bf16[512,512]{1,0:T(8,128)(2,1)}, u32[]{:S(2)}, u32[]{:S(2)}) collective-permute-start(bf16[512,512]{1,0:T(8,128)(2,1)} %refs_8_.3), channel_id=1, source_target_pairs={{0,2},{1,3},{2,0},{3,1},{4,6},{5,7},{6,4},{7,5},{8,10},{9,11},{10,... | collective-permute-start | bytes 1572872 | tf_op jit(solution)/shard_map/ppermute | solution.py:171
  5.7 1.6 %collective-permute-start.1 = (bf16[128,2048]{1,0:T(8,128)(2,1)S(1)}, bf16[128,2048]{1,0:T(8,128)(2,1)}, u32[]{:S(2)}, u32[]{:S(2)}) collective-permute-start(bf16[128,2048]{1,0:T(8,128)(2,1)S(1)} %constant_dynamic-slice_fusion.refs_16_), channel_id=1, source_target_pairs={{0,4},{4,0},{8,12},{12,8},{1,5},{5,1},{9,13},{13,9},{2,6},{6,2},{1... | collective-permute-start | bytes 1572872 | tf_op jit(solution)/shard_map/ppermute | solution.py:135
  7.4 1.5 %collective-permute-start.2 = (bf16[128,2048]{1,0:T(8,128)(2,1)S(1)}, bf16[128,2048]{1,0:T(8,128)(2,1)}, u32[]{:S(2)}, u32[]{:S(2)}) collective-permute-start(bf16[128,2048]{1,0:T(8,128)(2,1)S(1)} %constant_dynamic-slice_fusion.refs_16_), channel_id=1, source_target_pairs={{4,8},{8,4},{5,9},{9,5},{6,10},{10,6},{7,11},{11,7},{20,24},{24,20... | collective-permute-start | bytes 1572872 | tf_op jit(solution)/shard_map/ppermute | solution.py:144
  8.9 0.8 copy-done.12
  9.6 6.9 %collective-permute-done.3.refs_9_ = bf16[512,512]{1,0:T(8,128)(2,1)S(1)} collective-permute-done((bf16[512,512]{1,0:T(8,128)(2,1)}, bf16[512,512]{1,0:T(8,128)(2,1)S(1)}, u32[]{:S(2)}, u32[]{:S(2)}) %collective-permute-start.3) | collective-permute-done | bytes 524320 | tf_op jit(solution)/shard_map/ppermute | solution.py:171
  16.5 1.6 %collective-permute-done.4.refs_10_ = bf16[512,512]{1,0:T(8,128)(2,1)} collective-permute-done((bf16[512,512]{1,0:T(8,128)(2,1)}, bf16[512,512]{1,0:T(8,128)(2,1)}, u32[]{:S(2)}, u32[]{:S(2)}) %collective-permute-start.4) | collective-permute-done | bytes 524320 | tf_op jit(solution)/shard_map/ppermute | solution.py:171
  18.1 1.2 %collective-permute-done.1.refs_17_ = bf16[128,2048]{1,0:T(8,128)(2,1)} collective-permute-done((bf16[128,2048]{1,0:T(8,128)(2,1)S(1)}, bf16[128,2048]{1,0:T(8,128)(2,1)}, u32[]{:S(2)}, u32[]{:S(2)}) %collective-permute-start.1) | collective-permute-done | bytes 524320 | tf_op jit(solution)/shard_map/ppermute | solution.py:135
  19.3 0.0 copy-start.7
  19.3 0.8 copy-done.7
  20.1 0.5 collective-permute-start.10
  20.6 1.7 %collective-permute-start.8 = (bf16[512,512]{1,0:T(8,128)(2,1)}, bf16[512,512]{1,0:T(8,128)(2,1)}, u32[]{:S(2)}, u32[]{:S(2)}) collective-permute-start(bf16[512,512]{1,0:T(8,128)(2,1)} %refs_8_.3), channel_id=1, source_target_pairs={{0,3},{1,2},{2,1},{3,0},{4,7},{5,6},{6,5},{7,4},{8,11},{9,10},{10,... | collective-permute-start | bytes 1572872 | tf_op jit(solution)/shard_map/ppermute | solution.py:171
  22.2 1.3 %collective-permute-start.6 = (bf16[128,2048]{1,0:T(8,128)(2,1)}, bf16[128,2048]{1,0:T(8,128)(2,1)}, u32[]{:S(2)}, u32[]{:S(2)}) collective-permute-start(bf16[128,2048]{1,0:T(8,128)(2,1)} %collective-permute-done.2.refs_18_), channel_id=1, source_target_pairs={{4,0},{8,12},{5,1},{9,13},{6,2},{10,14},{7,3},{11,15},{20,16},{24,... | collective-permute-start | bytes 1572872 | tf_op jit(solution)/shard_map/ppermute | solution.py:141
  23.5 1.5 %collective-permute-start.7 = (bf16[128,2048]{1,0:T(8,128)(2,1)}, bf16[128,2048]{1,0:T(8,128)(2,1)}, u32[]{:S(2)}, u32[]{:S(2)}) collective-permute-start(bf16[128,2048]{1,0:T(8,128)(2,1)} %collective-permute-done.1.refs_17_), channel_id=1, source_target_pairs={{4,8},{8,4},{5,9},{9,5},{6,10},{10,6},{7,11},{11,7},{20,24},{24,20... | collective-permute-start | bytes 1572872 | tf_op jit(solution)/shard_map/ppermute | solution.py:144
  25.0 0.8 copy-done.9
  25.8 0.1 stack.66.place
  25.9 0.0 copy-start.1
  25.9 1.2 %copy-done.1 = bf16[512,1024]{1,0:T(8,128)(2,1)S(1)} copy-done((bf16[512,1024]{1,0:T(8,128)(2,1)S(1)}, bf16[512,1024]{1,0:T(8,128)(2,1)}, u32[]{:S(2)}) %copy-start.1) | copy-done | bytes 1048600
  27.1 1.0 copy-done.3
  28.2 1.0 copy-done.5
  29.2 1.0 copy-done.8
  30.3 1.0 copy-done.10
  31.3 3.8 %shard_map.77 = (f32[512,1536]{1,0:T(8,128)S(1)}, bf16[128,1536]{1,0:T(8,128)(2,1)S(1)}, bf16[128,1536]{1,0:T(8,128)(2,1)S(1)}) custom-call(s32[14]{0:T(128)S(1)} %stack.66.place, bf16[512,1024]{1,0:T(8,128)(2,1)S(1)} %copy-done.1, bf16[512,1024]{1,0:T(8,128)(2,1)S(1)} %copy-done.1, bf16[512,1024]{1,0:T(8,128)(2,1)S(1)} %copy-done.1, ...), custom_call_target="tpu_custom_call" | custom-call | flops 1610612736 | bytes 6291456 | tf_op jit(solution)/shard_map/pallas_call | solution.py:159
  35.2 0.5 collective-permute-done.8.refs_8_.refs_11_
  35.6 4.6 %collective-permute-done.6.refs_20_ = bf16[128,2048]{1,0:T(8,128)(2,1)} collective-permute-done((bf16[128,2048]{1,0:T(8,128)(2,1)}, bf16[128,2048]{1,0:T(8,128)(2,1)}, u32[]{:S(2)}, u32[]{:S(2)}) %collective-permute-start.6) | collective-permute-done | bytes 524320 | tf_op jit(solution)/shard_map/ppermute | solution.py:141
  40.2 1.3 %collective-permute-start.12 = (bf16[128,2048]{1,0:T(8,128)(2,1)}, bf16[128,2048]{1,0:T(8,128)(2,1)S(1)}, u32[]{:S(2)}, u32[]{:S(2)}) collective-permute-start(bf16[128,2048]{1,0:T(8,128)(2,1)} %collective-permute-done.7.refs_19_), channel_id=1, source_target_pairs={{4,0},{8,12},{5,1},{9,13},{6,2},{10,14},{7,3},{11,15},{20,16},{24,... | collective-permute-start | bytes 1572872 | tf_op jit(solution)/shard_map/ppermute | solution.py:141
  41.5 6.4 %collective-permute-start.11 = (bf16[128,1536]{1,0:T(8,128)(2,1)S(1)}, bf16[128,1536]{1,0:T(8,128)(2,1)S(1)}, u32[]{:S(2)}, u32[]{:S(2)}) collective-permute-start(bf16[128,1536]{1,0:T(8,128)(2,1)S(1)} %get-tuple-element.40), channel_id=1, source_target_pairs={{0,4},{12,8},{1,5},{13,9},{2,6},{14,10},{3,7},{15,11},{16,20},{28,... | collective-permute-start | bytes 1179656 | tf_op jit(solution)/shard_map/ppermute | solution.py:138
  48.0 0.3 collective-permute-start.15
  48.3 1.6 %collective-permute-start.18 = (bf16[128,1536]{1,0:T(8,128)(2,1)S(1)}, bf16[128,1536]{1,0:T(8,128)(2,1)S(1)}, u32[]{:S(2)}, u32[]{:S(2)}) collective-permute-start(bf16[128,1536]{1,0:T(8,128)(2,1)S(1)} %get-tuple-element.52), channel_id=1, source_target_pairs={{0,4},{12,8},{1,5},{13,9},{2,6},{14,10},{3,7},{15,11},{16,20},{28,... | collective-permute-start | bytes 1179656 | tf_op jit(solution)/shard_map/ppermute | solution.py:138
  49.9 2.6 %shard_map.78 = (f32[512,512]{1,0:T(8,128)S(1)}, bf16[256,512]{1,0:T(8,128)(2,1)S(1)}) custom-call(s32[14]{0:T(128)S(1)} %stack.66.place, bf16[512,1024]{1,0:T(8,128)(2,1)S(1)} %copy-done.1, bf16[512,1024]{1,0:T(8,128)(2,1)S(1)} %copy-done.1, bf16[512,1024]{1,0:T(8,128)(2,1)S(1)} %copy-done.1, bf16[512,1024]{1,0:T(8,128)(2,1)S(1)} %copy-done.1, ...), custom_call_target="tpu_custom_call" | custom-call | flops 536870912 | bytes 6291456 | tf_op jit(solution)/shard_map/pallas_call | solution.py:159
  52.5 4.8 %collective-permute-done.11 = bf16[128,1536]{1,0:T(8,128)(2,1)S(1)} collective-permute-done((bf16[128,1536]{1,0:T(8,128)(2,1)S(1)}, bf16[128,1536]{1,0:T(8,128)(2,1)S(1)}, u32[]{:S(2)}, u32[]{:S(2)}) %collective-permute-start.11) | collective-permute-done | bytes 393248 | tf_op jit(solution)/shard_map/ppermute | solution.py:138
  57.3 1.4 %collective-permute-done.12.refs_21_ = bf16[128,2048]{1,0:T(8,128)(2,1)S(1)} collective-permute-done((bf16[128,2048]{1,0:T(8,128)(2,1)}, bf16[128,2048]{1,0:T(8,128)(2,1)S(1)}, u32[]{:S(2)}, u32[]{:S(2)}) %collective-permute-start.12) | collective-permute-done | bytes 524320 | tf_op jit(solution)/shard_map/ppermute | solution.py:141
  58.7 3.0 %collective-permute-start.21 = (bf16[256,512]{1,0:T(8,128)(2,1)S(1)}, bf16[256,512]{1,0:T(8,128)(2,1)S(1)}, u32[]{:S(2)}, u32[]{:S(2)}) collective-permute-start(bf16[256,512]{1,0:T(8,128)(2,1)S(1)} %get-tuple-element.55), channel_id=1, source_target_pairs={{0,4},{12,8},{1,5},{13,9},{2,6},{14,10},{3,7},{15,11},{16,20},{28,... | collective-permute-start | bytes 786440 | tf_op jit(solution)/shard_map/ppermute | solution.py:138
  61.8 1.3 %collective-permute-start.16 = (bf16[128,2048]{1,0:T(8,128)(2,1)S(1)}, bf16[128,2048]{1,0:T(8,128)(2,1)S(1)}, u32[]{:S(2)}, u32[]{:S(2)}) collective-permute-start(bf16[128,2048]{1,0:T(8,128)(2,1)S(1)} %pad_maximum_fusion.1), channel_id=1, source_target_pairs={{0,4},{12,8},{1,5},{13,9},{2,6},{14,10},{3,7},{15,11},{16,20},{28,... | collective-permute-start | bytes 1572872 | tf_op jit(solution)/shard_map/ppermute | solution.py:138
  63.1 0.1 add_convert_fusion.2
  63.2 0.7 collective-permute-start.17
  64.0 6.3 %shard_map.79 = (bf16[512,512]{1,0:T(8,128)(2,1)S(1)}, f32[512,512]{1,0:T(8,128)S(1)}) custom-call(s32[14]{0:T(128)S(1)} %stack.66.place, bf16[512,1024]{1,0:T(8,128)(2,1)S(1)} %copy-done.2, bf16[512,1024]{1,0:T(8,128)(2,1)S(1)} %copy-done.2, bf16[512,1024]{1,0:T(8,128)(2,1)S(1)} %copy-done.2, bf16[512,1024]{1,0:T(8,128)(2,1)S(1)} %copy-done.2, ...), custom_call_target="tpu_custom_call" | custom-call | flops 3221225472 | bytes 6291456 | tf_op jit(solution)/shard_map/pallas_call | solution.py:159
  70.2 1.1 collective-permute-done.21
  71.3 0.1 add_convert_fusion.4
  71.4 0.7 collective-permute-start.23
  72.1 5.5 %collective-permute-start.19 = (bf16[512,512]{1,0:T(8,128)(2,1)S(1)}, bf16[512,512]{1,0:T(8,128)(2,1)S(1)}, u32[]{:S(2)}, u32[]{:S(2)}) collective-permute-start(bf16[512,512]{1,0:T(8,128)(2,1)S(1)} %get-tuple-element.53), channel_id=1, source_target_pairs={{0,4},{4,0},{8,12},{12,8},{1,5},{5,1},{9,13},{13,9},{2,6},{6,2},{1... | collective-permute-start | bytes 1572872 | tf_op jit(solution)/shard_map/ppermute | solution.py:135
  77.6 0.2 add_convert_fusion.1
  77.9 0.7 collective-permute-start.20
  78.6 1.3 %collective-permute-start.24 = (bf16[128,512]{1,0:T(8,128)(2,1)S(1)}, bf16[128,512]{1,0:T(8,128)(2,1)S(1)}, u32[]{:S(2)}, u32[]{:S(2)}) collective-permute-start(bf16[128,512]{1,0:T(8,128)(2,1)S(1)} %add_convert_fusion.5), channel_id=1, source_target_pairs={{4,0},{8,12},{5,1},{9,13},{6,2},{10,14},{7,3},{11,15},{20,16},{24,... | collective-permute-start | bytes 393224 | tf_op jit(solution)/shard_map/ppermute | solution.py:141
  79.9 1.3 %collective-permute-start.22 = (bf16[128,1536]{1,0:T(8,128)(2,1)S(1)}, bf16[128,1536]{1,0:T(8,128)(2,1)S(1)}, u32[]{:S(2)}, u32[]{:S(2)}) collective-permute-start(bf16[128,1536]{1,0:T(8,128)(2,1)S(1)} %get-tuple-element.61), channel_id=1, source_target_pairs={{4,0},{8,12},{5,1},{9,13},{6,2},{10,14},{7,3},{11,15},{20,16},{24,... | collective-permute-start | bytes 1179656 | tf_op jit(solution)/shard_map/ppermute | solution.py:141
  81.2 1.4 %collective-permute-done.16 = bf16[128,2048]{1,0:T(8,128)(2,1)S(1)} collective-permute-done((bf16[128,2048]{1,0:T(8,128)(2,1)S(1)}, bf16[128,2048]{1,0:T(8,128)(2,1)S(1)}, u32[]{:S(2)}, u32[]{:S(2)}) %collective-permute-start.16) | collective-permute-done | bytes 524320 | tf_op jit(solution)/shard_map/ppermute | solution.py:138
  82.6 10.7 %collective-permute-done.24 = bf16[128,512]{1,0:T(8,128)(2,1)S(1)} collective-permute-done((bf16[128,512]{1,0:T(8,128)(2,1)S(1)}, bf16[128,512]{1,0:T(8,128)(2,1)S(1)}, u32[]{:S(2)}, u32[]{:S(2)}) %collective-permute-start.24) | collective-permute-done | bytes 131104 | tf_op jit(solution)/shard_map/ppermute | solution.py:141
  93.3 0.1 convert_add_fusion.2
  93.4 0.1 collective-permute-done.19
  93.4 0.1 add_convert_fusion.3
  93.5 3.7 %collective-permute-start.26 = (bf16[256,512]{1,0:T(8,128)(2,1)S(1)}, bf16[256,512]{1,0:T(8,128)(2,1)S(1)}, u32[]{:S(2)}, u32[]{:S(2)}) collective-permute-start(bf16[256,512]{1,0:T(8,128)(2,1)S(1)} %add_convert_fusion.3), channel_id=1, source_target_pairs={{0,8},{4,12},{8,0},{12,4},{1,9},{5,13},{9,1},{13,5},{2,10},{6,14},... | collective-permute-start | bytes 786440 | tf_op jit(solution)/shard_map/ppermute | solution.py:174
  97.2 3.8 %collective-permute-done.22 = bf16[128,1536]{1,0:T(8,128)(2,1)S(1)} collective-permute-done((bf16[128,1536]{1,0:T(8,128)(2,1)S(1)}, bf16[128,1536]{1,0:T(8,128)(2,1)S(1)}, u32[]{:S(2)}, u32[]{:S(2)}) %collective-permute-start.22) | collective-permute-done | bytes 393248 | tf_op jit(solution)/shard_map/ppermute | solution.py:141
  101.0 0.2 convert_add_fusion
  101.2 0.1 pad_maximum_fusion.mine
  101.3 0.1 collective-permute-start.25
  101.4 7.7 %collective-permute-done.26 = bf16[256,512]{1,0:T(8,128)(2,1)S(1)} collective-permute-done((bf16[256,512]{1,0:T(8,128)(2,1)S(1)}, bf16[256,512]{1,0:T(8,128)(2,1)S(1)}, u32[]{:S(2)}, u32[]{:S(2)}) %collective-permute-start.26) | collective-permute-done | bytes 262176 | tf_op jit(solution)/shard_map/ppermute | solution.py:174
  109.0 0.1 convert_add_fusion.1.mine
  109.2 0.1 collective-permute-start.27
  109.2 1.9 %collective-permute-done.27.pair = f32[256,512]{1,0:T(8,128)S(1)} collective-permute-done((f32[256,512]{1,0:T(8,128)S(1)}, f32[256,512]{1,0:T(8,128)S(1)}, u32[]{:S(2)}, u32[]{:S(2)}) %collective-permute-start.27) | collective-permute-done | bytes 524320 | tf_op jit(solution)/shard_map/ppermute | solution.py:132
  111.1 1.6 %shard_map.81 = f32[256,1024]{1,0:T(8,128)} custom-call(s32[14]{0:T(128)S(1)} %stack.66.place, f32[256,512]{1,0:T(8,128)S(1)} %convert_add_fusion.1.mine, f32[256,512]{1,0:T(8,128)S(1)} %collective-permute-done.27.pair), custom_call_target="tpu_custom_call" | custom-call | bytes 6291456 | tf_op jit(solution)/shard_map/pallas_call | solution.py:159
  112.8 2.0 %shard_map.80 = f32[256,2048]{1,0:T(8,128)} custom-call(s32[14]{0:T(128)S(1)} %stack.66.place, f32[128,2048]{1,0:T(8,128)S(1)} %pad_maximum_fusion.mine, f32[128,2048]{1,0:T(8,128)S(1)} %collective-permute-done.25.pair), custom_call_target="tpu_custom_call" | custom-call | bytes 6291456 | tf_op jit(solution)/shard_map/pallas_call | solution.py:159
  (46 shorter events, 0.3 us)
Async XLA Ops:
  0.6 5.1 %copy-start = (bf16[256,2048]{1,0:T(8,128)(2,1)S(1)}, bf16[256,2048]{1,0:T(8,128)(2,1)}, u32[]{:S(2)}) copy-start(bf16[256,2048]{1,0:T(8,128)(2,1)} %param.9) | copy-start | bytes 3145732
  0.6 5.0 %collective-permute-start = (bf16[512,512]{1,0:T(8,128)(2,1)}, bf16[512,512]{1,0:T(8,128)(2,1)S(1)}, u32[]{:S(2)}, u32[]{:S(2)}) collective-permute-start(bf16[512,512]{1,0:T(8,128)(2,1)} %refs_8_.3), channel_id=1, source_target_pairs={{0,16},{16,0},{1,17},{17,1},{2,18},{18,2},{3,19},{19,3},{4,20},{20... | collective-permute-start | bytes 1572872 | tf_op jit(solution)/shard_map/ppermute | solution.py:132
  1.2 18.1 %collective-permute-start.5 = (bf16[512,1024]{1,0:T(8,128)(2,1)}, bf16[512,1024]{1,0:T(8,128)(2,1)S(1)}, u32[]{:S(2)}, u32[]{:S(2)}) collective-permute-start(bf16[512,1024]{1,0:T(8,128)(2,1)} %refs_3_.4), channel_id=1, source_target_pairs={{0,16},{16,0},{1,17},{17,1},{2,18},{18,2},{3,19},{19,3},{4,20},{20... | collective-permute-start | bytes 3145736 | tf_op jit(solution)/shard_map/ppermute | solution.py:132
  1.2 15.3 %collective-permute-start.3 = (bf16[512,512]{1,0:T(8,128)(2,1)}, bf16[512,512]{1,0:T(8,128)(2,1)S(1)}, u32[]{:S(2)}, u32[]{:S(2)}) collective-permute-start(bf16[512,512]{1,0:T(8,128)(2,1)} %refs_8_.3), channel_id=1, source_target_pairs={{0,1},{1,0},{2,3},{3,2},{4,5},{5,4},{6,7},{7,6},{8,9},{9,8},{10,11... | collective-permute-start | bytes 1572872 | tf_op jit(solution)/shard_map/ppermute | solution.py:171
  4.2 13.9 %collective-permute-start.4 = (bf16[512,512]{1,0:T(8,128)(2,1)}, bf16[512,512]{1,0:T(8,128)(2,1)}, u32[]{:S(2)}, u32[]{:S(2)}) collective-permute-start(bf16[512,512]{1,0:T(8,128)(2,1)} %refs_8_.3), channel_id=1, source_target_pairs={{0,2},{1,3},{2,0},{3,1},{4,6},{5,7},{6,4},{7,5},{8,10},{9,11},{10,... | collective-permute-start | bytes 1572872 | tf_op jit(solution)/shard_map/ppermute | solution.py:171
  5.7 19.3 %copy-start.4 = (bf16[512,512]{1,0:T(8,128)(2,1)}, bf16[512,512]{1,0:T(8,128)(2,1)S(1)}, u32[]{:S(2)}) copy-start(bf16[512,512]{1,0:T(8,128)(2,1)S(1)} %collective-permute-done.refs_11_.refs_12_) | copy-start | bytes 1572868
  5.7 13.5 %collective-permute-start.1 = (bf16[128,2048]{1,0:T(8,128)(2,1)S(1)}, bf16[128,2048]{1,0:T(8,128)(2,1)}, u32[]{:S(2)}, u32[]{:S(2)}) collective-permute-start(bf16[128,2048]{1,0:T(8,128)(2,1)S(1)} %constant_dynamic-slice_fusion.refs_16_), channel_id=1, source_target_pairs={{0,4},{4,0},{8,12},{12,8},{1,5},{5,1},{9,13},{13,9},{2,6},{6,2},{1... | collective-permute-start | bytes 1572872 | tf_op jit(solution)/shard_map/ppermute | solution.py:135
  7.4 11.9 %collective-permute-start.2 = (bf16[128,2048]{1,0:T(8,128)(2,1)S(1)}, bf16[128,2048]{1,0:T(8,128)(2,1)}, u32[]{:S(2)}, u32[]{:S(2)}) collective-permute-start(bf16[128,2048]{1,0:T(8,128)(2,1)S(1)} %constant_dynamic-slice_fusion.refs_16_), channel_id=1, source_target_pairs={{4,8},{8,4},{5,9},{9,5},{6,10},{10,6},{7,11},{11,7},{20,24},{24,20... | collective-permute-start | bytes 1572872 | tf_op jit(solution)/shard_map/ppermute | solution.py:144
  8.8 0.8 copy-start.12
  19.3 5.7 %collective-permute-start.9 = (bf16[512,512]{1,0:T(8,128)(2,1)S(1)}, bf16[512,512]{1,0:T(8,128)(2,1)S(1)}, u32[]{:S(2)}, u32[]{:S(2)}) collective-permute-start(bf16[512,512]{1,0:T(8,128)(2,1)S(1)} %collective-permute-done.3.refs_9_), channel_id=1, source_target_pairs={{0,16},{16,0},{1,17},{17,1},{2,18},{18,2},{3,19},{19,3},{4,20},{20... | collective-permute-start | bytes 1572872 | tf_op jit(solution)/shard_map/ppermute | solution.py:132
  19.3 0.8 copy-start.7
  20.1 5.8 %collective-permute-start.10 = (bf16[512,512]{1,0:T(8,128)(2,1)}, bf16[512,512]{1,0:T(8,128)(2,1)}, u32[]{:S(2)}, u32[]{:S(2)}) collective-permute-start(bf16[512,512]{1,0:T(8,128)(2,1)} %collective-permute-done.4.refs_10_), channel_id=1, source_target_pairs={{0,16},{16,0},{1,17},{17,1},{2,18},{18,2},{3,19},{19,3},{4,20},{20... | collective-permute-start | bytes 1572872 | tf_op jit(solution)/shard_map/ppermute | solution.py:132
  20.6 15.1 %collective-permute-start.8 = (bf16[512,512]{1,0:T(8,128)(2,1)}, bf16[512,512]{1,0:T(8,128)(2,1)}, u32[]{:S(2)}, u32[]{:S(2)}) collective-permute-start(bf16[512,512]{1,0:T(8,128)(2,1)} %refs_8_.3), channel_id=1, source_target_pairs={{0,3},{1,2},{2,1},{3,0},{4,7},{5,6},{6,5},{7,4},{8,11},{9,10},{10,... | collective-permute-start | bytes 1572872 | tf_op jit(solution)/shard_map/ppermute | solution.py:171
  22.2 18.0 %collective-permute-start.6 = (bf16[128,2048]{1,0:T(8,128)(2,1)}, bf16[128,2048]{1,0:T(8,128)(2,1)}, u32[]{:S(2)}, u32[]{:S(2)}) collective-permute-start(bf16[128,2048]{1,0:T(8,128)(2,1)} %collective-permute-done.2.refs_18_), channel_id=1, source_target_pairs={{4,0},{8,12},{5,1},{9,13},{6,2},{10,14},{7,3},{11,15},{20,16},{24,... | collective-permute-start | bytes 1572872 | tf_op jit(solution)/shard_map/ppermute | solution.py:141
  23.5 16.7 %collective-permute-start.7 = (bf16[128,2048]{1,0:T(8,128)(2,1)}, bf16[128,2048]{1,0:T(8,128)(2,1)}, u32[]{:S(2)}, u32[]{:S(2)}) collective-permute-start(bf16[128,2048]{1,0:T(8,128)(2,1)} %collective-permute-done.1.refs_17_), channel_id=1, source_target_pairs={{4,8},{8,4},{5,9},{9,5},{6,10},{10,6},{7,11},{11,7},{20,24},{24,20... | collective-permute-start | bytes 1572872 | tf_op jit(solution)/shard_map/ppermute | solution.py:144
  25.0 0.8 copy-start.9
  25.8 26.7 %collective-permute-start.14 = (bf16[512,1024]{1,0:T(8,128)(2,1)}, bf16[512,1024]{1,0:T(8,128)(2,1)S(1)}, u32[]{:S(2)}, u32[]{:S(2)}) collective-permute-start(bf16[512,1024]{1,0:T(8,128)(2,1)} %refs_3_.5), channel_id=1, source_target_pairs={{0,16},{16,0},{1,17},{17,1},{2,18},{18,2},{3,19},{19,3},{4,20},{20... | collective-permute-start | bytes 3145736 | tf_op jit(solution)/shard_map/ppermute | solution.py:132
  25.9 1.2 %copy-start.1 = (bf16[512,1024]{1,0:T(8,128)(2,1)S(1)}, bf16[512,1024]{1,0:T(8,128)(2,1)}, u32[]{:S(2)}) copy-start(bf16[512,1024]{1,0:T(8,128)(2,1)} %refs_3_.4) | copy-start | bytes 3145732
  27.1 1.0 copy-start.3
  28.2 1.0 copy-start.5
  29.2 1.0 copy-start.8
  30.3 1.0 copy-start.10
  31.3 16.6 %copy-start.15 = (s32[512,1]{0,1:T(1,128)S(1)}, s32[512,1]{0,1:T(1,128)}, u32[]{:S(2)}) copy-start(s32[512,1]{0,1:T(1,128)} %param.10) | copy-start | bytes 6148
  31.3 16.6 %copy-start.14 = (s32[512]{0:T(512)S(1)}, s32[512]{0:T(512)}, u32[]{:S(2)}) copy-start(s32[512]{0:T(512)} %param.11) | copy-start | bytes 6148
  40.2 8.1 %collective-permute-start.13 = (bf16[512,512]{1,0:T(8,128)(2,1)}, bf16[512,512]{1,0:T(8,128)(2,1)S(1)}, u32[]{:S(2)}, u32[]{:S(2)}) collective-permute-start(bf16[512,512]{1,0:T(8,128)(2,1)} %collective-permute-done.8.refs_8_.refs_11_), channel_id=1, source_target_pairs={{0,16},{16,0},{1,17},{17,1},{2,18},{18,2},{3,19},{19,3},{4,20},{20... | collective-permute-start | bytes 1572872 | tf_op jit(solution)/shard_map/ppermute | solution.py:132
  40.2 18.5 %collective-permute-start.12 = (bf16[128,2048]{1,0:T(8,128)(2,1)}, bf16[128,2048]{1,0:T(8,128)(2,1)S(1)}, u32[]{:S(2)}, u32[]{:S(2)}) collective-permute-start(bf16[128,2048]{1,0:T(8,128)(2,1)} %collective-permute-done.7.refs_19_), channel_id=1, source_target_pairs={{4,0},{8,12},{5,1},{9,13},{6,2},{10,14},{7,3},{11,15},{20,16},{24,... | collective-permute-start | bytes 1572872 | tf_op jit(solution)/shard_map/ppermute | solution.py:141
  41.5 15.8 %collective-permute-start.11 = (bf16[128,1536]{1,0:T(8,128)(2,1)S(1)}, bf16[128,1536]{1,0:T(8,128)(2,1)S(1)}, u32[]{:S(2)}, u32[]{:S(2)}) collective-permute-start(bf16[128,1536]{1,0:T(8,128)(2,1)S(1)} %get-tuple-element.40), channel_id=1, source_target_pairs={{0,4},{12,8},{1,5},{13,9},{2,6},{14,10},{3,7},{15,11},{16,20},{28,... | collective-permute-start | bytes 1179656 | tf_op jit(solution)/shard_map/ppermute | solution.py:138
  48.0 4.6 %collective-permute-start.15 = (s32[512]{0:T(512)S(1)}, s32[512]{0:T(512)S(1)}, u32[]{:S(2)}, u32[]{:S(2)}) collective-permute-start(s32[512]{0:T(512)S(1)} %add.49), channel_id=1, source_target_pairs={{0,16},{16,0},{1,17},{17,1},{2,18},{18,2},{3,19},{19,3},{4,20},{20... | collective-permute-start | bytes 6152 | tf_op jit(solution)/shard_map/ppermute | solution.py:132
  48.3 23.8 %collective-permute-start.18 = (bf16[128,1536]{1,0:T(8,128)(2,1)S(1)}, bf16[128,1536]{1,0:T(8,128)(2,1)S(1)}, u32[]{:S(2)}, u32[]{:S(2)}) collective-permute-start(bf16[128,1536]{1,0:T(8,128)(2,1)S(1)} %get-tuple-element.52), channel_id=1, source_target_pairs={{0,4},{12,8},{1,5},{13,9},{2,6},{14,10},{3,7},{15,11},{16,20},{28,... | collective-permute-start | bytes 1179656 | tf_op jit(solution)/shard_map/ppermute | solution.py:138
  52.5 11.4 %copy-start.2 = (bf16[512,1024]{1,0:T(8,128)(2,1)S(1)}, bf16[512,1024]{1,0:T(8,128)(2,1)}, u32[]{:S(2)}) copy-start(bf16[512,1024]{1,0:T(8,128)(2,1)} %refs_3_.5) | copy-start | bytes 3145732
  52.5 11.4 %copy-start.6 = (bf16[512,512]{1,0:T(8,128)(2,1)S(1)}, bf16[512,512]{1,0:T(8,128)(2,1)}, u32[]{:S(2)}) copy-start(bf16[512,512]{1,0:T(8,128)(2,1)} %copy-done.4) | copy-start | bytes 1572868
  52.5 11.4 %copy-start.11 = (bf16[512,512]{1,0:T(8,128)(2,1)S(1)}, bf16[512,512]{1,0:T(8,128)(2,1)}, u32[]{:S(2)}) copy-start(bf16[512,512]{1,0:T(8,128)(2,1)} %copy-done.9) | copy-start | bytes 1572868
  52.5 11.4 %copy-start.13 = (bf16[128,2048]{1,0:T(8,128)(2,1)S(1)}, bf16[128,2048]{1,0:T(8,128)(2,1)}, u32[]{:S(2)}) copy-start(bf16[128,2048]{1,0:T(8,128)(2,1)} %copy-done.12) | copy-start | bytes 1572868
  58.7 12.6 %collective-permute-start.21 = (bf16[256,512]{1,0:T(8,128)(2,1)S(1)}, bf16[256,512]{1,0:T(8,128)(2,1)S(1)}, u32[]{:S(2)}, u32[]{:S(2)}) collective-permute-start(bf16[256,512]{1,0:T(8,128)(2,1)S(1)} %get-tuple-element.55), channel_id=1, source_target_pairs={{0,4},{12,8},{1,5},{13,9},{2,6},{14,10},{3,7},{15,11},{16,20},{28,... | collective-permute-start | bytes 786440 | tf_op jit(solution)/shard_map/ppermute | solution.py:138
  61.8 20.8 %collective-permute-start.16 = (bf16[128,2048]{1,0:T(8,128)(2,1)S(1)}, bf16[128,2048]{1,0:T(8,128)(2,1)S(1)}, u32[]{:S(2)}, u32[]{:S(2)}) collective-permute-start(bf16[128,2048]{1,0:T(8,128)(2,1)S(1)} %pad_maximum_fusion.1), channel_id=1, source_target_pairs={{0,4},{12,8},{1,5},{13,9},{2,6},{14,10},{3,7},{15,11},{16,20},{28,... | collective-permute-start | bytes 1572872 | tf_op jit(solution)/shard_map/ppermute | solution.py:138
  63.2 8.9 %collective-permute-start.17 = (bf16[128,1536]{1,0:T(8,128)(2,1)S(1)}, bf16[128,1536]{1,0:T(8,128)(2,1)S(1)}, u32[]{:S(2)}, u32[]{:S(2)}) collective-permute-start(bf16[128,1536]{1,0:T(8,128)(2,1)S(1)} %add_convert_fusion.2), channel_id=1, source_target_pairs={{4,8},{8,4},{5,9},{9,5},{6,10},{10,6},{7,11},{11,7},{20,24},{24,20... | collective-permute-start | bytes 1179656 | tf_op jit(solution)/shard_map/ppermute | solution.py:144
  71.4 7.1 %collective-permute-start.23 = (bf16[256,512]{1,0:T(8,128)(2,1)S(1)}, bf16[256,512]{1,0:T(8,128)(2,1)S(1)}, u32[]{:S(2)}, u32[]{:S(2)}) collective-permute-start(bf16[256,512]{1,0:T(8,128)(2,1)S(1)} %add_convert_fusion.4), channel_id=1, source_target_pairs={{4,8},{8,4},{5,9},{9,5},{6,10},{10,6},{7,11},{11,7},{20,24},{24,20... | collective-permute-start | bytes 786440 | tf_op jit(solution)/shard_map/ppermute | solution.py:144
  72.1 21.3 %collective-permute-start.19 = (bf16[512,512]{1,0:T(8,128)(2,1)S(1)}, bf16[512,512]{1,0:T(8,128)(2,1)S(1)}, u32[]{:S(2)}, u32[]{:S(2)}) collective-permute-start(bf16[512,512]{1,0:T(8,128)(2,1)S(1)} %get-tuple-element.53), channel_id=1, source_target_pairs={{0,4},{4,0},{8,12},{12,8},{1,5},{5,1},{9,13},{13,9},{2,6},{6,2},{1... | collective-permute-start | bytes 1572872 | tf_op jit(solution)/shard_map/ppermute | solution.py:135
  77.9 15.5 %collective-permute-start.20 = (bf16[128,1536]{1,0:T(8,128)(2,1)S(1)}, bf16[128,1536]{1,0:T(8,128)(2,1)S(1)}, u32[]{:S(2)}, u32[]{:S(2)}) collective-permute-start(bf16[128,1536]{1,0:T(8,128)(2,1)S(1)} %get-tuple-element.60), channel_id=1, source_target_pairs={{4,8},{8,4},{5,9},{9,5},{6,10},{10,6},{7,11},{11,7},{20,24},{24,20... | collective-permute-start | bytes 1179656 | tf_op jit(solution)/shard_map/ppermute | solution.py:144
  78.6 14.7 %collective-permute-start.24 = (bf16[128,512]{1,0:T(8,128)(2,1)S(1)}, bf16[128,512]{1,0:T(8,128)(2,1)S(1)}, u32[]{:S(2)}, u32[]{:S(2)}) collective-permute-start(bf16[128,512]{1,0:T(8,128)(2,1)S(1)} %add_convert_fusion.5), channel_id=1, source_target_pairs={{4,0},{8,12},{5,1},{9,13},{6,2},{10,14},{7,3},{11,15},{20,16},{24,... | collective-permute-start | bytes 393224 | tf_op jit(solution)/shard_map/ppermute | solution.py:141
  79.9 21.1 %collective-permute-start.22 = (bf16[128,1536]{1,0:T(8,128)(2,1)S(1)}, bf16[128,1536]{1,0:T(8,128)(2,1)S(1)}, u32[]{:S(2)}, u32[]{:S(2)}) collective-permute-start(bf16[128,1536]{1,0:T(8,128)(2,1)S(1)} %get-tuple-element.61), channel_id=1, source_target_pairs={{4,0},{8,12},{5,1},{9,13},{6,2},{10,14},{7,3},{11,15},{20,16},{24,... | collective-permute-start | bytes 1179656 | tf_op jit(solution)/shard_map/ppermute | solution.py:141
  93.5 15.5 %collective-permute-start.26 = (bf16[256,512]{1,0:T(8,128)(2,1)S(1)}, bf16[256,512]{1,0:T(8,128)(2,1)S(1)}, u32[]{:S(2)}, u32[]{:S(2)}) collective-permute-start(bf16[256,512]{1,0:T(8,128)(2,1)S(1)} %add_convert_fusion.3), channel_id=1, source_target_pairs={{0,8},{4,12},{8,0},{12,4},{1,9},{5,13},{9,1},{13,5},{2,10},{6,14},... | collective-permute-start | bytes 786440 | tf_op jit(solution)/shard_map/ppermute | solution.py:174
  101.3 11.4 %collective-permute-start.25 = (f32[128,2048]{1,0:T(8,128)S(1)}, f32[128,2048]{1,0:T(8,128)S(1)}, u32[]{:S(2)}, u32[]{:S(2)}) collective-permute-start(f32[128,2048]{1,0:T(8,128)S(1)} %pad_maximum_fusion.mine), channel_id=1, source_target_pairs={{0,16},{16,0},{1,17},{17,1},{2,18},{18,2},{3,19},{19,3},{4,20},{20... | collective-permute-start | bytes 3145736 | tf_op jit(solution)/shard_map/ppermute | solution.py:132
  109.2 2.0 %collective-permute-start.27 = (f32[256,512]{1,0:T(8,128)S(1)}, f32[256,512]{1,0:T(8,128)S(1)}, u32[]{:S(2)}, u32[]{:S(2)}) collective-permute-start(f32[256,512]{1,0:T(8,128)S(1)} %convert_add_fusion.1.mine), channel_id=1, source_target_pairs={{0,16},{16,0},{1,17},{17,1},{2,18},{18,2},{3,19},{19,3},{4,20},{20... | collective-permute-start | bytes 1572872 | tf_op jit(solution)/shard_map/ppermute | solution.py:132

commit v4 on v3

v4 whole, which is shorter than its diff:
```python
import functools

import jax
import jax.numpy as jnp
from jax import lax
from jax.experimental import pallas as pl
from jax.experimental.pallas import tpu as pltpu
from jax.sharding import PartitionSpec as P

F32, BF16 = jnp.float32, jnp.bfloat16
KEY_DEV = 256


def dot(a, b, ca, cb):
    return lax.dot_general(a, b, (((ca,), (cb,)), ((), ())), preferred_element_type=F32)


def general_body(layer_input, value_grad, residual_grad, value_weight, owner, key_row):
    all_heads = lax.all_gather(value_grad, "tp", axis=1, tiled=True)
    tok_rows, features = layer_input.shape
    groups = lax.axis_size("fsdp")
    slots = 2 * tok_rows // groups
    keys_here = KEY_DEV
    width = all_heads.shape[1]
    term = dot(layer_input, all_heads, 0, 0)
    pieces = term.astype(BF16).reshape(groups, features // groups, width)
    arrived = lax.all_to_all(pieces, "fsdp", split_axis=0, concat_axis=0, tiled=True)
    shard = jnp.sum(arrived.astype(F32), axis=0)
    back = dot(all_heads, lax.all_gather(value_weight, "fsdp", axis=0, tiled=True), 1, 1)
    input_grad = (residual_grad.astype(F32) + back).astype(BF16)
    target = owner[:, 0]
    onehot = (target[:, None] == jnp.arange(groups, dtype=jnp.int32)[None, :]).astype(jnp.int32)
    position = jnp.sum(jnp.cumsum(onehot, axis=0) * onehot, axis=1) - 1
    place = target * slots + position
    chooser = jnp.arange(groups * slots, dtype=jnp.int32)[:, None] == place[None, :]
    outgoing = dot(chooser.astype(BF16), input_grad, 1, 0).astype(BF16)
    out_keys = jnp.sum(jnp.where(chooser, key_row[None, :] + 1, 0), axis=1) - 1
    arrived = lax.all_to_all(outgoing, "fsdp", split_axis=0, concat_axis=0, tiled=True)
    arrived_keys = lax.all_to_all(out_keys, "fsdp", split_axis=0, concat_axis=0, tiled=True)
    selector = (arrived_keys[:, None] == jnp.arange(keys_here, dtype=jnp.int32)[None, :]).astype(BF16)
    table = dot(selector, arrived, 0, 0)
    return lax.psum(shard, "dp"), lax.psum(table, "dp")


def turn_kernel(place, mine, other, out):
    half = mine.shape[1] // 8
    for side, ref in enumerate((mine, other)):
        for i, rank in enumerate((8, 7, 6, 5)):
            cols = pl.ds(pl.multiple_of((2 * place[rank] + place[4]) * half, half), half)
            out[side, i * half : (i + 1) * half, :] = ref[:, cols].T


def term_kernel(rounded, place, turned, *refs):
    n = sum(r.shape == refs[0].shape for r in refs) // 2
    heads, out, sends = refs[: 2 * n], refs[2 * n], refs[1 + 2 * n :]
    width = heads[0].shape[1]
    for k in range(n):
        cols = slice(k * width, (k + 1) * width)
        out[:, cols] = dot(turned[0], heads[k][...], 1, 0) + dot(turned[1], heads[n + k][...], 1, 0)
    half, wide = out.shape[0] // 4, out.shape[1]
    for first, send in zip(rounded, sends):
        for j in range(send.shape[1] // wide):
            row = (first + j) * half
            send[:, j * wide : (j + 1) * wide] = out[row : row + half, :].astype(BF16)


def choose_kernel(place, key, out):
    keys = out.shape[0] // 4
    row = lax.broadcasted_iota(jnp.int32, (keys, key.shape[1]), 0)
    for j in range(4):
        hit = row + place[10 + j] * keys == key[...]
        out[j * keys : (j + 1) * keys, :] = jnp.where(hit, 1.0, 0.0).astype(BF16)


def back_kernel(base, ranks, place, *refs):
    residuals, heads, chosen, weights, (send, keep, weight) = refs[:2], refs[2:10], refs[10], refs[11:-3], refs[-3:]
    half, width = weights[0].shape[0], heads[0].shape[1]
    tokens = heads[0].shape[0]
    first = place[base]

    def put(rank, ref):
        weight[pl.ds(pl.multiple_of((place[rank] - first) * half, half), half), :] = ref[...]

    for rank, ref in zip(ranks[:-1], weights):
        put(rank, ref)
    for here in range(2):
        pl.when(place[9] == here)(lambda here=here: put(ranks[-1], weights[len(ranks) - 1 + here]))

    total = [None] * 2
    starts = [pl.multiple_of((2 * (first + p) + place[4]) * half, half) for p in range(len(ranks))]
    for side in range(2):
        acc = jnp.concatenate([residuals[side][:, pl.ds(at, half)] for at in starts], 1).astype(F32)
        for k in range(4):
            cols = pl.ds(pl.multiple_of(place[k] * width, width), width)
            acc = acc + dot(heads[4 * side + k][...], weight[:, cols], 1, 1)
        rows = acc.astype(BF16)
        for i in range(2):
            size = send.shape[0]
            pick = chosen[i * size : (i + 1) * size, side * tokens : (side + 1) * tokens]
            add = dot(pick, rows, 1, 0)
            total[i] = add if side == 0 else total[i] + add
    send[...] = total[0].astype(BF16)
    keep[...] = total[1]


def join_weight_kernel(place, mine, pair, out):
    half, width = mine.shape[0], mine.shape[1] // 4
    here = pl.multiple_of(place[4] * half, half)
    there = pl.multiple_of(half - place[4] * half, half)
    for k in range(4):
        start = pl.multiple_of(place[k] * width, width)
        out[pl.ds(here, half), pl.ds(start, width)] = mine[:, k * width : (k + 1) * width]
        out[pl.ds(there, half), pl.ds(start, width)] = pair[:, k * width : (k + 1) * width]


def join_key_kernel(place, mine, pair, out):
    first = place[4] == 0
    half = mine.shape[1] // 4
    for p in range(4):
        a, b = mine[:, p * half : (p + 1) * half], pair[:, p * half : (p + 1) * half]
        out[:, 2 * p * half : (2 * p + 1) * half] = jnp.where(first, a, b)
        out[:, (2 * p + 1) * half : (2 * p + 2) * half] = jnp.where(first, b, a)


def pair_body(layer_input, value_grad, residual_grad, value_weight, owner, key_row):
    core, z, t = (lax.axis_index(n) for n in ("dp", "fsdp", "tp"))
    tokens, features = layer_input.shape
    heads = value_grad.shape[1]
    part = features // 4
    half = part // 2
    keys = KEY_DEV
    phase = lax.optimization_barrier

    def core_swap(v):
        return lax.ppermute(v, "dp", [(0, 1), (1, 0)])

    def outer(v):
        return lax.ppermute(v, "fsdp", [(0, 1), (1, 0), (2, 3), (3, 2)])

    def inward(v):
        return lax.ppermute(v, "fsdp", [(0, 1), (3, 2)])

    def outward(v):
        return lax.ppermute(v, "fsdp", [(1, 0), (2, 3)])

    def inner(v):
        return lax.ppermute(v, "fsdp", [(1, 2), (2, 1)])

    end = ((z == 0) | (z == 3)).astype(jnp.int32)
    low = (z < 2).astype(jnp.int32)
    beside = z ^ 1
    far_mid = 1 + low
    far_end = 3 * low
    place = jnp.stack([t, t ^ 1, t ^ 2, t ^ 3, core, z, beside, far_mid, far_end, end, z ^ 1, z ^ 3, z, z ^ 2, 1 - low]).astype(jnp.int32)
    smem, vmem = pl.BlockSpec(memory_space=pltpu.SMEM), pl.BlockSpec(memory_space=pltpu.VMEM)

    def call(kernel, out, scratch, flops, *args):
        return pl.pallas_call(
            kernel,
            out_shape=out,
            in_specs=[smem] + [vmem] * len(args),
            out_specs=jax.tree.map(lambda o: vmem, out),
            scratch_shapes=scratch,
            compiler_params=pltpu.CompilerParams(vmem_limit_bytes=16 << 20),
            cost_estimate=pl.CostEstimate(flops=flops, bytes_accessed=1 << 20, transcendentals=0),
        )(place, *args)

    def square(v, d):
        return lax.ppermute(v, "tp", [(i, i ^ d) for i in range(4)])

    def across(v):
        return lax.ppermute(v, "fsdp", [(i, i ^ 2) for i in range(4)])

    def struct(rows, cols, dtype):
        return jax.ShapeDtypeStruct((rows, cols), dtype)

    def term(v, *parts):
        n = len(v) // 2 * heads
        out = (struct(4 * half, n, F32),) + tuple(struct(half, count * n, BF16) for _, count in parts)
        kernel = functools.partial(term_kernel, tuple(first for first, _ in parts))
        return call(kernel, out, [], n << 20, turned, *v)

    def plus(v, came):
        return (v + came.astype(F32)).astype(BF16)

    def far_plus(v, came):
        n = v.shape[1]
        return jnp.concatenate([plus(v[:half], came[:, :n]), plus(v[half : 2 * half], came[:, n : 2 * n])], 1)

    def back(base, ranks, *weights):
        n = len(ranks) * half
        return call(
            functools.partial(back_kernel, base, ranks),
            (struct(2 * keys, n, BF16), struct(2 * keys, n, F32)),
            [pltpu.VMEM((n, 4 * heads), BF16)], len(ranks) * (3 << 28),
            residual_grad, res_other, v0, vx, vy, vd, v0_other, vx_other, vy_other, vd_other, chosen, *weights,
        )

    v0 = value_grad
    v0_other, weight_rows = phase((core_swap(v0), value_weight))
    w_own = lax.dynamic_slice_in_dim(weight_rows, core * half, half, 0)
    in_other, res_other = core_swap(layer_input), core_swap(residual_grad)
    turned = call(turn_kernel, jax.ShapeDtypeStruct((2, 4 * half, tokens), BF16), [], 0, layer_input, in_other)
    term0, send0 = term((v0, v0_other), (0, 4))
    got = phase((outer(w_own), inner(w_own), square(v0, 1), square(v0, 2), turned, term0, send0,
                 res_other, low == 1, end == 1))
    w_beside, w_mid, vx, vy, turned, term0, send0, res_other, is_low, is_end = got

    vx_other, vy_other = core_swap(vx), core_swap(vy)
    term1, send1, near1 = term((vx, vy, vx_other, vy_other), (0, 2), (2, 1))
    key = owner[:, 0] * keys + key_row
    got = phase((outer(jnp.where(is_end, send0, w_mid)), inner(w_beside), square(v0, 3), term1, send1, near1,
                 core_swap(key)))
    i0, w_end, vd, term1, send1, near1, key_other = got
    w_third = i0

    b0 = inner(far_plus(term0, i0))
    vd_other = core_swap(vd)
    key_both = jnp.concatenate([key, key_other])[None, :]
    chosen = call(choose_kernel, struct(4 * keys, 2 * tokens, BF16), [], 0, key_both)
    term2, send2, near2 = term((vd, vd_other), (0, 2), (2, 1))
    i2 = inward(send2)
    send_a, keep_a = back(14, (5, 6, 7), w_own, w_beside, w_mid, w_third)
    got = phase((outer(jnp.where(is_end, send1, w_end)), b0, term1, term2, send_a, keep_a, term0, near1, near2))
    i1, b0, term1, term2, send_a, keep_a, term0, near1, near2 = got
    w_fourth = i1

    def joined(a, b):
        return jnp.where(is_low, jnp.concatenate([a, b], 1), jnp.concatenate([b, a], 1))

    send_b, keep_b = back(8, (8,), w_end, w_fourth)
    keep = joined(keep_a, keep_b)
    b1 = inner(far_plus(term1, i1))
    b2 = inner(far_plus(term2, i2))
    k1, b1, b2, term1, term2, keep = phase((outer(joined(send_a, send_b)), b1, b2, term1, term2, keep))

    k2 = across(plus(keep[keys:], k1[keys:]))
    mine = keep[:keys] + k1[:keys].astype(F32)
    back1 = plus(term1[2 * half : 3 * half], b1[:, : 2 * heads])
    back0 = plus(term0[2 * half : 3 * half], b0[:, :heads])
    back2 = plus(term2[2 * half : 3 * half], b2[:, :heads])
    i3 = outer(jnp.where(
        is_end, jnp.concatenate([near1, near2, near2], 1), jnp.concatenate([back1, back2, back0], 1)
    ))

    def total(v, *came):
        return sum((c.astype(F32) for c in came), v[3 * half :])

    weight_half = jnp.concatenate([
        total(term0, jnp.where(is_end, i3[:, 3 * heads :], i0[:, 2 * heads : 3 * heads]), b0[:, heads:]),
        total(term1, i3[:, : 2 * heads], b1[:, 2 * heads :]),
        total(term2, i3[:, 2 * heads : 3 * heads], b2[:, heads:]),
    ], 1)
    weight_pair = core_swap(weight_half)
    weight_grad = call(
        join_weight_kernel, jax.ShapeDtypeStruct((part, 4 * heads), F32),
        [], 0, weight_half, weight_pair,
    )
    key_half = mine + k2.astype(F32)
    key_pair = core_swap(key_half)
    key_grad = call(
        join_key_kernel, jax.ShapeDtypeStruct((keys, features), F32),
        [], 0, key_half, key_pair,
    )
    return weight_grad, key_grad


def solution(mesh):
    shape = dict(mesh.shape)
    special = shape == {"dp": 2, "fsdp": 4, "tp": 4}
    return jax.shard_map(
        pair_body if special else general_body,
        mesh=mesh,
        in_specs=(
            P(("dp", "fsdp"), "tp"),
            P(("dp", "fsdp"), "tp"),
            P(("dp", "fsdp"), "tp"),
            P(("tp", "fsdp"), None),
            P(("dp", "fsdp"), None),
            P(("dp", "fsdp")),
        ),
        out_specs=(P(("tp", "fsdp"), None), P("fsdp", "tp")),
        check_vma=False,
    )
```

time: 115 us -> 106 us (0.922)
  starting transfers between devices: 40.9 us -> 34.5 us
  local copies, waits for them, and re-layouts: 8 us -> 2.17 us
  Pallas kernels: 16.3 us -> 19.5 us
    ppermute x2 -> x5, waiting for transfers between devices: 1.2 us -> 39.5 us  [outer(): return lax.ppermute(v, 'fsdp', [(0, 1), (1, 0), (2, 3), (3, 2)])]
    ppermute x4 -> x0, waiting for transfers between devices: 20.5 us -> none  [outward(): return lax.ppermute(v, 'fsdp', [(1, 0), (2, 3)])]
    ppermute x2 -> x5, starting transfers between devices: 7.15 us -> 16.4 us  [outer(): return lax.ppermute(v, 'fsdp', [(0, 1), (1, 0), (2, 3), (3, 2)])]
    ppermute x4 -> x1, starting transfers between devices: 12.3 us -> 3.65 us  [inward(): return lax.ppermute(v, 'fsdp', [(0, 1), (3, 2)])]
    ppermute x1, waiting for transfers between devices: 7.66 us -> 0.01 us  [across(): return lax.ppermute(v, 'fsdp', [(i, i ^ 2) for i in range(4)])]
    ppermute x4 -> x1, waiting for transfers between devices: 7.24 us -> 0.01 us  [inward(): return lax.ppermute(v, 'fsdp', [(0, 1), (3, 2)])]
    unnamed x32 -> x12, local copies, waits for them, and re-layouts: 7.81 us -> 1.25 us
    ppermute x4 -> x0, starting transfers between devices: 5.15 us -> none  [outward(): return lax.ppermute(v, 'fsdp', [(1, 0), (2, 3)])]
  transfers between devices with their start and end apart: 28 -> 24, of which waited for: 14 -> 8; matrix products, arithmetic and copies ran while one was open for 1% -> 2% of each run, Pallas kernels for 12% -> 17%
where the time goes in v4:
time: 106 us; the launch traced here: 105 us
  waiting for transfers between devices  46.7 us (44%)
  starting transfers between devices  34.5 us (33%)
  Pallas kernels  19.5 us (18%)
  local copies, waits for them, and re-layouts  2.17 us (2%)
  other arithmetic  1.53 us (1%)
    ppermute x5, waiting for transfers between devices, outer(): return lax.ppermute(v, 'fsdp', [(0, 1), (1, 0), (2, 3), (3, 2)])  39.5 us
    pallas_call x9, Pallas kernels, call(): pl.pallas_call(kernel, out_shape=out, in_specs=[smem] + [vmem] * len(args...  19.5 us
    ppermute x5, starting transfers between devices, outer(): return lax.ppermute(v, 'fsdp', [(0, 1), (1, 0), (2, 3), (3, 2)])  16.4 us
    ppermute x3, starting transfers between devices, square(): return lax.ppermute(v, 'tp', [(i, i ^ d) for i in range(4)])  6.8 us
    ppermute x3, waiting for transfers between devices, square(): return lax.ppermute(v, 'tp', [(i, i ^ d) for i in range(4)])  4.4 us
    ppermute x5, starting transfers between devices, inner(): return lax.ppermute(v, 'fsdp', [(1, 2), (2, 1)])  4.2 us
    ppermute x1, starting transfers between devices, inward(): return lax.ppermute(v, 'fsdp', [(0, 1), (3, 2)])  3.65 us
    ppermute x9, waiting for transfers between devices, core_swap(): return lax.ppermute(v, 'dp', [(0, 1), (1, 0)])  2.74 us
  transfers between devices with their start and end apart: 24, of which 8 were waited for; matrix products, arithmetic and copies ran while one was open for 2% of the time, Pallas kernels for 17%

profile of v4, /device:TPU:0, one launch (start us, length us, event | category | flops | bytes accessed | tf_op | source)
XLA Modules:
  0.0 105.4 jit_solution(18338303040966640545)
XLA Ops:
  0.6 0.0 copy-start
  0.6 0.5 collective-permute-start.5
  1.2 0.1 collective-permute-start
  1.2 0.4 collective-permute-start.6
  1.7 2.6 %collective-permute-start.3 = (bf16[512,512]{1,0:T(8,128)(2,1)}, bf16[512,512]{1,0:T(8,128)(2,1)}, u32[]{:S(2)}, u32[]{:S(2)}) collective-permute-start(bf16[512,512]{1,0:T(8,128)(2,1)} %refs_2_.3), channel_id=1, source_target_pairs={{0,1},{1,0},{2,3},{3,2},{4,5},{5,4},{6,7},{7,6},{8,9},{9,8},{10,11... | collective-permute-start | bytes 1572872 | tf_op jit(solution)/shard_map/ppermute | solution.py:169
  4.2 1.5 %collective-permute-start.4 = (bf16[512,512]{1,0:T(8,128)(2,1)}, bf16[512,512]{1,0:T(8,128)(2,1)}, u32[]{:S(2)}, u32[]{:S(2)}) collective-permute-start(bf16[512,512]{1,0:T(8,128)(2,1)} %refs_2_.3), channel_id=1, source_target_pairs={{0,2},{1,3},{2,0},{3,1},{4,6},{5,7},{6,4},{7,5},{8,10},{9,11},{10,... | collective-permute-start | bytes 1572872 | tf_op jit(solution)/shard_map/ppermute | solution.py:169
  5.8 0.0 collective-permute-done.refs_1_.refs_6_
  5.8 0.8 constant_dynamic-slice_fusion.refs_11_
  6.6 1.6 %collective-permute-start.1 = (bf16[128,2048]{1,0:T(8,128)(2,1)}, bf16[128,2048]{1,0:T(8,128)(2,1)}, u32[]{:S(2)}, u32[]{:S(2)}) collective-permute-start(bf16[128,2048]{1,0:T(8,128)(2,1)} %constant_dynamic-slice_fusion.refs_11_), channel_id=1, source_target_pairs={{0,4},{4,0},{8,12},{12,8},{1,5},{5,1},{9,13},{13,9},{2,6},{6,2},{1... | collective-permute-start | bytes 1572872 | tf_op jit(solution)/shard_map/ppermute | solution.py:138
  8.2 1.5 %collective-permute-start.2 = (bf16[128,2048]{1,0:T(8,128)(2,1)}, bf16[128,2048]{1,0:T(8,128)(2,1)}, u32[]{:S(2)}, u32[]{:S(2)}) collective-permute-start(bf16[128,2048]{1,0:T(8,128)(2,1)} %constant_dynamic-slice_fusion.refs_11_), channel_id=1, source_target_pairs={{4,8},{8,4},{5,9},{9,5},{6,10},{10,6},{7,11},{11,7},{20,24},{24,20... | collective-permute-start | bytes 1572872 | tf_op jit(solution)/shard_map/ppermute | solution.py:147
  9.7 0.1 stack.57.place
  9.8 0.0 copy-start.3
  9.8 1.2 %copy-done.3 = bf16[512,1024]{1,0:T(8,128)(2,1)S(1)} copy-done((bf16[512,1024]{1,0:T(8,128)(2,1)S(1)}, bf16[512,1024]{1,0:T(8,128)(2,1)}, u32[]{:S(2)}) %copy-start.3) | copy-done | bytes 1048600
  11.0 1.6 %shard_map.77.turned = bf16[2,512,512]{2,1,0:T(8,128)(2,1)S(1)} custom-call(s32[15]{0:T(128)S(1)} %stack.57.place, bf16[512,1024]{1,0:T(8,128)(2,1)S(1)} %copy-done.3, bf16[512,1024]{1,0:T(8,128)(2,1)} %collective-permute-done.5.other), custom_call_target="tpu_custom_call" | custom-call | bytes 1048576 | tf_op jit(solution)/shard_map/pallas_call | solution.py:158
  12.6 0.0 copy-start.5
  12.6 0.0 copy-start.4
  12.6 1.2 %shard_map.78 = (f32[512,512]{1,0:T(8,128)S(1)}, bf16[128,2048]{1,0:T(8,128)(2,1)S(1)}) custom-call(s32[15]{0:T(128)S(1)} %stack.57.place, bf16[2,512,512]{2,1,0:T(8,128)(2,1)S(1)} %shard_map.77.turned, bf16[512,512]{1,0:T(8,128)(2,1)S(1)} %copy-done.1, bf16[512,512]{1,0:T(8,128)(2,1)S(1)} %collective-permute-done.refs_1_.refs_6_), custom_call_target="tpu_custom_call" | custom-call | flops 536870912 | bytes 1048576 | tf_op jit(solution)/shard_map/pallas_call | solution.py:158
  13.8 3.2 %collective-permute-done.3.refs_0_.refs_3_ = bf16[512,512]{1,0:T(8,128)(2,1)} collective-permute-done((bf16[512,512]{1,0:T(8,128)(2,1)}, bf16[512,512]{1,0:T(8,128)(2,1)}, u32[]{:S(2)}, u32[]{:S(2)}) %collective-permute-start.3) | collective-permute-done | bytes 524320 | tf_op jit(solution)/shard_map/ppermute | solution.py:169
  17.1 2.7 %collective-permute-start.9 = (bf16[512,512]{1,0:T(8,128)(2,1)S(1)}, bf16[512,512]{1,0:T(8,128)(2,1)S(1)}, u32[]{:S(2)}, u32[]{:S(2)}) collective-permute-start(bf16[512,512]{1,0:T(8,128)(2,1)S(1)} %copy-done.1), channel_id=1, source_target_pairs={{0,3},{1,2},{2,1},{3,0},{4,7},{5,6},{6,5},{7,4},{8,11},{9,10},{10,... | collective-permute-start | bytes 1572872 | tf_op jit(solution)/shard_map/ppermute | solution.py:169
  19.8 0.0 collective-permute-done.4.refs_1_.refs_4_
  19.8 0.9 collective-permute-done.1.refs_12_
  20.7 0.0 collective-permute-done.6.refs_1_
  20.7 0.5 collective-permute-start.11
  21.2 0.1 broadcast_select_fusion.1
  21.3 5.9 %collective-permute-start.7 = (bf16[128,2048]{1,0:T(8,128)(2,1)S(1)}, bf16[128,2048]{1,0:T(8,128)(2,1)S(1)}, u32[]{:S(2)}, u32[]{:S(2)}) collective-permute-start(bf16[128,2048]{1,0:T(8,128)(2,1)S(1)} %broadcast_select_fusion.1), channel_id=1, source_target_pairs={{0,4},{4,0},{8,12},{12,8},{1,5},{5,1},{9,13},{13,9},{2,6},{6,2},{1... | collective-permute-start | bytes 1572872 | tf_op jit(solution)/shard_map/ppermute | solution.py:138
  27.2 0.7 collective-permute-start.8
  27.9 0.1 collective-permute-start.12
  28.0 2.5 %shard_map.79 = (f32[512,1024]{1,0:T(8,128)S(1)}, bf16[128,2048]{1,0:T(8,128)(2,1)S(1)}, bf16[128,1024]{1,0:T(8,128)(2,1)S(1)}) custom-call(s32[15]{0:T(128)S(1)} %stack.57.place, bf16[2,512,512]{2,1,0:T(8,128)(2,1)S(1)} %shard_map.77.turned, bf16[512,512]{1,0:T(8,128)(2,1)} %collective-permute-done.3.refs_0_.refs_3_, ...), custom_call_target="tpu_custom_call" | custom-call | flops 1073741824 | bytes 1048576 | tf_op jit(solution)/shard_map/pallas_call | solution.py:158
  30.5 1.2 %collective-permute-done.9.refs_0_.refs_5_ = bf16[512,512]{1,0:T(8,128)(2,1)S(1)} collective-permute-done((bf16[512,512]{1,0:T(8,128)(2,1)S(1)}, bf16[512,512]{1,0:T(8,128)(2,1)S(1)}, u32[]{:S(2)}, u32[]{:S(2)}) %collective-permute-start.9) | collective-permute-done | bytes 524320 | tf_op jit(solution)/shard_map/ppermute | solution.py:169
  31.7 7.6 %collective-permute-done.7.refs_14_ = bf16[128,2048]{1,0:T(8,128)(2,1)S(1)} collective-permute-done((bf16[128,2048]{1,0:T(8,128)(2,1)S(1)}, bf16[128,2048]{1,0:T(8,128)(2,1)S(1)}, u32[]{:S(2)}, u32[]{:S(2)}) %collective-permute-start.7) | collective-permute-done | bytes 524320 | tf_op jit(solution)/shard_map/ppermute | solution.py:138
  39.3 0.1 broadcast_select_fusion
  39.4 0.9 shard_map.81.refs_10_
  40.3 0.0 copy-start.2
  40.3 3.9 %collective-permute-start.13 = (bf16[128,2048]{1,0:T(8,128)(2,1)S(1)}, bf16[128,2048]{1,0:T(8,128)(2,1)S(1)}, u32[]{:S(2)}, u32[]{:S(2)}) collective-permute-start(bf16[128,2048]{1,0:T(8,128)(2,1)S(1)} %broadcast_select_fusion), channel_id=1, source_target_pairs={{0,4},{4,0},{8,12},{12,8},{1,5},{5,1},{9,13},{13,9},{2,6},{6,2},{1... | collective-permute-start | bytes 1572872 | tf_op jit(solution)/shard_map/ppermute | solution.py:138
  44.2 0.1 add_convert_fusion.9
  44.3 0.7 collective-permute-start.14
  45.0 1.2 %shard_map.80 = (f32[512,512]{1,0:T(8,128)S(1)}, bf16[128,1024]{1,0:T(8,128)(2,1)S(1)}, bf16[128,512]{1,0:T(8,128)(2,1)S(1)}) custom-call(s32[15]{0:T(128)S(1)} %stack.57.place, bf16[2,512,512]{2,1,0:T(8,128)(2,1)S(1)} %shard_map.77.turned, bf16[512,512]{1,0:T(8,128)(2,1)S(1)} %collective-permute-done.9.refs_0_.refs_5_, ...), custom_call_target="tpu_custom_call" | custom-call | flops 536870912 | bytes 1048576 | tf_op jit(solution)/shard_map/pallas_call | solution.py:158
  46.3 5.3 %shard_map.82 = (bf16[512,384]{1,0:T(8,128)(2,1)S(1)}, f32[512,384]{1,0:T(8,128)S(1)}) custom-call(s32[15]{0:T(128)S(1)} %stack.57.place, bf16[512,1024]{1,0:T(8,128)(2,1)S(1)} %copy-done.2, bf16[512,1024]{1,0:T(8,128)(2,1)S(1)} %collective-permute-done.6.refs_1_, bf16[512,512]{1,0:T(8,128)(2,1)S(1)} %copy-done.1, ...), custom_call_target="tpu_custom_call" | custom-call | flops 2415919104 | bytes 1048576 | tf_op jit(solution)/shard_map/pallas_call | solution.py:158
  51.6 5.2 %collective-permute-done.13.refs_12_ = bf16[128,2048]{1,0:T(8,128)(2,1)S(1)} collective-permute-done((bf16[128,2048]{1,0:T(8,128)(2,1)S(1)}, bf16[128,2048]{1,0:T(8,128)(2,1)S(1)}, u32[]{:S(2)}, u32[]{:S(2)}) %collective-permute-start.13) | collective-permute-done | bytes 524320 | tf_op jit(solution)/shard_map/ppermute | solution.py:138
  56.8 3.6 %collective-permute-start.18 = (bf16[128,1024]{1,0:T(8,128)(2,1)S(1)}, bf16[128,1024]{1,0:T(8,128)(2,1)S(1)}, u32[]{:S(2)}, u32[]{:S(2)}) collective-permute-start(bf16[128,1024]{1,0:T(8,128)(2,1)S(1)} %get-tuple-element.84), channel_id=1, source_target_pairs={{0,4},{12,8},{1,5},{13,9},{2,6},{14,10},{3,7},{15,11},{16,20},{28,... | collective-permute-start | bytes 786440 | tf_op jit(solution)/shard_map/ppermute | solution.py:141
  60.4 0.1 add_convert_fusion.3
  60.6 0.7 collective-permute-start.17
  61.3 3.1 %shard_map.83 = (bf16[512,128]{1,0:T(8,128)(2,1)S(1)}, f32[512,128]{1,0:T(8,128)S(1)}) custom-call(s32[15]{0:T(128)S(1)} %stack.57.place, bf16[512,1024]{1,0:T(8,128)(2,1)S(1)} %copy-done.2, bf16[512,1024]{1,0:T(8,128)(2,1)S(1)} %collective-permute-done.6.refs_1_, bf16[512,512]{1,0:T(8,128)(2,1)S(1)} %copy-done.1, ...), custom_call_target="tpu_custom_call" | custom-call | flops 805306368 | bytes 1048576 | tf_op jit(solution)/shard_map/pallas_call | solution.py:158
  64.5 0.1 maximum_select_fusion.2
  64.6 2.4 %collective-permute-start.16 = (bf16[512,512]{1,0:T(8,128)(2,1)S(1)}, bf16[512,512]{1,0:T(8,128)(2,1)S(1)}, u32[]{:S(2)}, u32[]{:S(2)}) collective-permute-start(bf16[512,512]{1,0:T(8,128)(2,1)S(1)} %maximum_select_fusion.2), channel_id=1, source_target_pairs={{0,4},{4,0},{8,12},{12,8},{1,5},{5,1},{9,13},{13,9},{2,6},{6,2},{1... | collective-permute-start | bytes 1572872 | tf_op jit(solution)/shard_map/ppermute | solution.py:138
  67.0 0.1 add_convert_fusion.7
  67.2 0.7 collective-permute-start.19
  67.9 0.1 maximum_select_fusion
  68.0 10.5 %collective-permute-done.16 = bf16[512,512]{1,0:T(8,128)(2,1)S(1)} collective-permute-done((bf16[512,512]{1,0:T(8,128)(2,1)S(1)}, bf16[512,512]{1,0:T(8,128)(2,1)S(1)}, u32[]{:S(2)}, u32[]{:S(2)}) %collective-permute-start.16) | collective-permute-done | bytes 524320 | tf_op jit(solution)/shard_map/ppermute | solution.py:138
  78.6 0.1 add_convert_fusion.1
  78.7 0.1 maximum_select_fusion.1
  78.8 2.6 %collective-permute-start.20 = (bf16[128,2048]{1,0:T(8,128)(2,1)S(1)}, bf16[128,2048]{1,0:T(8,128)(2,1)S(1)}, u32[]{:S(2)}, u32[]{:S(2)}) collective-permute-start(bf16[128,2048]{1,0:T(8,128)(2,1)S(1)} %maximum_select_fusion.1), channel_id=1, source_target_pairs={{0,4},{4,0},{8,12},{12,8},{1,5},{5,1},{9,13},{13,9},{2,6},{6,2},{1... | collective-permute-start | bytes 1572872 | tf_op jit(solution)/shard_map/ppermute | solution.py:138
  81.4 0.1 add_convert_fusion
  81.5 1.3 %collective-permute-start.22 = (bf16[256,512]{1,0:T(8,128)(2,1)S(1)}, bf16[256,512]{1,0:T(8,128)(2,1)S(1)}, u32[]{:S(2)}, u32[]{:S(2)}) collective-permute-start(bf16[256,512]{1,0:T(8,128)(2,1)S(1)} %add_convert_fusion), channel_id=1, source_target_pairs={{0,8},{4,12},{8,0},{12,4},{1,9},{5,13},{9,1},{13,5},{2,10},{6,14},... | collective-permute-start | bytes 786440 | tf_op jit(solution)/shard_map/ppermute | solution.py:172
  82.7 15.2 %collective-permute-done.20 = bf16[128,2048]{1,0:T(8,128)(2,1)S(1)} collective-permute-done((bf16[128,2048]{1,0:T(8,128)(2,1)S(1)}, bf16[128,2048]{1,0:T(8,128)(2,1)S(1)}, u32[]{:S(2)}, u32[]{:S(2)}) %collective-permute-start.20) | collective-permute-done | bytes 524320 | tf_op jit(solution)/shard_map/ppermute | solution.py:138
  98.0 0.1 convert_add_fusion.1
  98.1 0.1 convert_add_fusion.3
  98.2 0.1 pad_maximum_fusion.mine
  98.3 0.1 collective-permute-start.21
  98.4 0.1 convert_add_fusion.mine
  98.5 0.6 collective-permute-start.23
  99.0 2.7 %collective-permute-done.23.pair = f32[256,512]{1,0:T(8,128)S(1)} collective-permute-done((f32[256,512]{1,0:T(8,128)S(1)}, f32[256,512]{1,0:T(8,128)S(1)}, u32[]{:S(2)}, u32[]{:S(2)}) %collective-permute-start.23) | collective-permute-done | bytes 524320 | tf_op jit(solution)/shard_map/ppermute | solution.py:135
  101.7 1.6 %shard_map.85 = f32[256,1024]{1,0:T(8,128)} custom-call(s32[15]{0:T(128)S(1)} %stack.57.place, f32[256,512]{1,0:T(8,128)S(1)} %convert_add_fusion.mine, f32[256,512]{1,0:T(8,128)S(1)} %collective-permute-done.23.pair), custom_call_target="tpu_custom_call" | custom-call | bytes 1048576 | tf_op jit(solution)/shard_map/pallas_call | solution.py:158
  103.4 2.0 %shard_map.84 = f32[256,2048]{1,0:T(8,128)} custom-call(s32[15]{0:T(128)S(1)} %stack.57.place, f32[128,2048]{1,0:T(8,128)S(1)} %pad_maximum_fusion.mine, f32[128,2048]{1,0:T(8,128)S(1)} %collective-permute-done.21.pair), custom_call_target="tpu_custom_call" | custom-call | bytes 1048576 | tf_op jit(solution)/shard_map/pallas_call | solution.py:158
  (28 shorter events, 0.2 us)
Async XLA Ops:
  0.6 5.1 %copy-start = (bf16[256,2048]{1,0:T(8,128)(2,1)S(1)}, bf16[256,2048]{1,0:T(8,128)(2,1)}, u32[]{:S(2)}) copy-start(bf16[256,2048]{1,0:T(8,128)(2,1)} %param.9) | copy-start | bytes 3145732
  0.6 7.5 %collective-permute-start.5 = (bf16[512,1024]{1,0:T(8,128)(2,1)}, bf16[512,1024]{1,0:T(8,128)(2,1)}, u32[]{:S(2)}, u32[]{:S(2)}) collective-permute-start(bf16[512,1024]{1,0:T(8,128)(2,1)} %mine.1), channel_id=1, source_target_pairs={{0,16},{16,0},{1,17},{17,1},{2,18},{18,2},{3,19},{19,3},{4,20},{20... | collective-permute-start | bytes 3145736 | tf_op jit(solution)/shard_map/ppermute | solution.py:135
  1.2 4.6 %collective-permute-start = (bf16[512,512]{1,0:T(8,128)(2,1)}, bf16[512,512]{1,0:T(8,128)(2,1)S(1)}, u32[]{:S(2)}, u32[]{:S(2)}) collective-permute-start(bf16[512,512]{1,0:T(8,128)(2,1)} %refs_2_.3), channel_id=1, source_target_pairs={{0,16},{16,0},{1,17},{17,1},{2,18},{18,2},{3,19},{19,3},{4,20},{20... | collective-permute-start | bytes 1572872 | tf_op jit(solution)/shard_map/ppermute | solution.py:135
  1.2 19.5 %collective-permute-start.6 = (bf16[512,1024]{1,0:T(8,128)(2,1)}, bf16[512,1024]{1,0:T(8,128)(2,1)S(1)}, u32[]{:S(2)}, u32[]{:S(2)}) collective-permute-start(bf16[512,1024]{1,0:T(8,128)(2,1)} %refs_0_.5), channel_id=1, source_target_pairs={{0,16},{16,0},{1,17},{17,1},{2,18},{18,2},{3,19},{19,3},{4,20},{20... | collective-permute-start | bytes 3145736 | tf_op jit(solution)/shard_map/ppermute | solution.py:135
  1.7 15.4 %collective-permute-start.3 = (bf16[512,512]{1,0:T(8,128)(2,1)}, bf16[512,512]{1,0:T(8,128)(2,1)}, u32[]{:S(2)}, u32[]{:S(2)}) collective-permute-start(bf16[512,512]{1,0:T(8,128)(2,1)} %refs_2_.3), channel_id=1, source_target_pairs={{0,1},{1,0},{2,3},{3,2},{4,5},{5,4},{6,7},{7,6},{8,9},{9,8},{10,11... | collective-permute-start | bytes 1572872 | tf_op jit(solution)/shard_map/ppermute | solution.py:169
  4.2 15.5 %collective-permute-start.4 = (bf16[512,512]{1,0:T(8,128)(2,1)}, bf16[512,512]{1,0:T(8,128)(2,1)}, u32[]{:S(2)}, u32[]{:S(2)}) collective-permute-start(bf16[512,512]{1,0:T(8,128)(2,1)} %refs_2_.3), channel_id=1, source_target_pairs={{0,2},{1,3},{2,0},{3,1},{4,6},{5,7},{6,4},{7,5},{8,10},{9,11},{10,... | collective-permute-start | bytes 1572872 | tf_op jit(solution)/shard_map/ppermute | solution.py:169
  5.8 6.8 %copy-start.1 = (bf16[512,512]{1,0:T(8,128)(2,1)S(1)}, bf16[512,512]{1,0:T(8,128)(2,1)}, u32[]{:S(2)}) copy-start(bf16[512,512]{1,0:T(8,128)(2,1)} %refs_2_.3) | copy-start | bytes 1572868
  6.6 14.1 %collective-permute-start.1 = (bf16[128,2048]{1,0:T(8,128)(2,1)}, bf16[128,2048]{1,0:T(8,128)(2,1)}, u32[]{:S(2)}, u32[]{:S(2)}) collective-permute-start(bf16[128,2048]{1,0:T(8,128)(2,1)} %constant_dynamic-slice_fusion.refs_11_), channel_id=1, source_target_pairs={{0,4},{4,0},{8,12},{12,8},{1,5},{5,1},{9,13},{13,9},{2,6},{6,2},{1... | collective-permute-start | bytes 1572872 | tf_op jit(solution)/shard_map/ppermute | solution.py:138
  8.2 12.5 %collective-permute-start.2 = (bf16[128,2048]{1,0:T(8,128)(2,1)}, bf16[128,2048]{1,0:T(8,128)(2,1)}, u32[]{:S(2)}, u32[]{:S(2)}) collective-permute-start(bf16[128,2048]{1,0:T(8,128)(2,1)} %constant_dynamic-slice_fusion.refs_11_), channel_id=1, source_target_pairs={{4,8},{8,4},{5,9},{9,5},{6,10},{10,6},{7,11},{11,7},{20,24},{24,20... | collective-permute-start | bytes 1572872 | tf_op jit(solution)/shard_map/ppermute | solution.py:147
  9.8 1.2 %copy-start.3 = (bf16[512,1024]{1,0:T(8,128)(2,1)S(1)}, bf16[512,1024]{1,0:T(8,128)(2,1)}, u32[]{:S(2)}) copy-start(bf16[512,1024]{1,0:T(8,128)(2,1)} %mine.1) | copy-start | bytes 3145732
  12.6 15.3 %copy-start.5 = (s32[512,1]{0,1:T(1,128)S(1)}, s32[512,1]{0,1:T(1,128)}, u32[]{:S(2)}) copy-start(s32[512,1]{0,1:T(1,128)} %param.10) | copy-start | bytes 6148
  12.6 15.3 %copy-start.4 = (s32[512]{0:T(512)S(1)}, s32[512]{0:T(512)}, u32[]{:S(2)}) copy-start(s32[512]{0:T(512)} %param.11) | copy-start | bytes 6148
  17.1 14.6 %collective-permute-start.9 = (bf16[512,512]{1,0:T(8,128)(2,1)S(1)}, bf16[512,512]{1,0:T(8,128)(2,1)S(1)}, u32[]{:S(2)}, u32[]{:S(2)}) collective-permute-start(bf16[512,512]{1,0:T(8,128)(2,1)S(1)} %copy-done.1), channel_id=1, source_target_pairs={{0,3},{1,2},{2,1},{3,0},{4,7},{5,6},{6,5},{7,4},{8,11},{9,10},{10,... | collective-permute-start | bytes 1572872 | tf_op jit(solution)/shard_map/ppermute | solution.py:169
  20.7 7.2 %collective-permute-start.10 = (bf16[512,512]{1,0:T(8,128)(2,1)}, bf16[512,512]{1,0:T(8,128)(2,1)S(1)}, u32[]{:S(2)}, u32[]{:S(2)}) collective-permute-start(bf16[512,512]{1,0:T(8,128)(2,1)} %collective-permute-done.3.refs_0_.refs_3_), channel_id=1, source_target_pairs={{0,16},{16,0},{1,17},{17,1},{2,18},{18,2},{3,19},{19,3},{4,20},{20... | collective-permute-start | bytes 1572872 | tf_op jit(solution)/shard_map/ppermute | solution.py:135
  20.7 7.3 %collective-permute-start.11 = (bf16[512,512]{1,0:T(8,128)(2,1)}, bf16[512,512]{1,0:T(8,128)(2,1)S(1)}, u32[]{:S(2)}, u32[]{:S(2)}) collective-permute-start(bf16[512,512]{1,0:T(8,128)(2,1)} %collective-permute-done.4.refs_1_.refs_4_), channel_id=1, source_target_pairs={{0,16},{16,0},{1,17},{17,1},{2,18},{18,2},{3,19},{19,3},{4,20},{20... | collective-permute-start | bytes 1572872 | tf_op jit(solution)/shard_map/ppermute | solution.py:135
  21.3 18.0 %collective-permute-start.7 = (bf16[128,2048]{1,0:T(8,128)(2,1)S(1)}, bf16[128,2048]{1,0:T(8,128)(2,1)S(1)}, u32[]{:S(2)}, u32[]{:S(2)}) collective-permute-start(bf16[128,2048]{1,0:T(8,128)(2,1)S(1)} %broadcast_select_fusion.1), channel_id=1, source_target_pairs={{0,4},{4,0},{8,12},{12,8},{1,5},{5,1},{9,13},{13,9},{2,6},{6,2},{1... | collective-permute-start | bytes 1572872 | tf_op jit(solution)/shard_map/ppermute | solution.py:138
  27.2 12.1 %collective-permute-start.8 = (bf16[128,2048]{1,0:T(8,128)(2,1)}, bf16[128,2048]{1,0:T(8,128)(2,1)S(1)}, u32[]{:S(2)}, u32[]{:S(2)}) collective-permute-start(bf16[128,2048]{1,0:T(8,128)(2,1)} %collective-permute-done.1.refs_12_), channel_id=1, source_target_pairs={{4,8},{8,4},{5,9},{9,5},{6,10},{10,6},{7,11},{11,7},{20,24},{24,20... | collective-permute-start | bytes 1572872 | tf_op jit(solution)/shard_map/ppermute | solution.py:147
  27.9 2.6 %collective-permute-start.12 = (s32[512]{0:T(512)S(1)}, s32[512]{0:T(512)S(1)}, u32[]{:S(2)}, u32[]{:S(2)}) collective-permute-start(s32[512]{0:T(512)S(1)} %add.65), channel_id=1, source_target_pairs={{0,16},{16,0},{1,17},{17,1},{2,18},{18,2},{3,19},{19,3},{4,20},{20... | collective-permute-start | bytes 6152 | tf_op jit(solution)/shard_map/ppermute | solution.py:135
  39.3 5.7 %collective-permute-start.15 = (bf16[512,512]{1,0:T(8,128)(2,1)S(1)}, bf16[512,512]{1,0:T(8,128)(2,1)S(1)}, u32[]{:S(2)}, u32[]{:S(2)}) collective-permute-start(bf16[512,512]{1,0:T(8,128)(2,1)S(1)} %collective-permute-done.9.refs_0_.refs_5_), channel_id=1, source_target_pairs={{0,16},{16,0},{1,17},{17,1},{2,18},{18,2},{3,19},{19,3},{4,20},{20... | collective-permute-start | bytes 1572872 | tf_op jit(solution)/shard_map/ppermute | solution.py:135
  40.3 6.0 %copy-start.2 = (bf16[512,1024]{1,0:T(8,128)(2,1)S(1)}, bf16[512,1024]{1,0:T(8,128)(2,1)}, u32[]{:S(2)}) copy-start(bf16[512,1024]{1,0:T(8,128)(2,1)} %refs_0_.5) | copy-start | bytes 3145732
  40.3 16.5 %collective-permute-start.13 = (bf16[128,2048]{1,0:T(8,128)(2,1)S(1)}, bf16[128,2048]{1,0:T(8,128)(2,1)S(1)}, u32[]{:S(2)}, u32[]{:S(2)}) collective-permute-start(bf16[128,2048]{1,0:T(8,128)(2,1)S(1)} %broadcast_select_fusion), channel_id=1, source_target_pairs={{0,4},{4,0},{8,12},{12,8},{1,5},{5,1},{9,13},{13,9},{2,6},{6,2},{1... | collective-permute-start | bytes 1572872 | tf_op jit(solution)/shard_map/ppermute | solution.py:138
  44.3 7.2 %collective-permute-start.14 = (bf16[128,1024]{1,0:T(8,128)(2,1)S(1)}, bf16[128,1024]{1,0:T(8,128)(2,1)S(1)}, u32[]{:S(2)}, u32[]{:S(2)}) collective-permute-start(bf16[128,1024]{1,0:T(8,128)(2,1)S(1)} %pad_maximum_fusion.2), channel_id=1, source_target_pairs={{4,8},{8,4},{5,9},{9,5},{6,10},{10,6},{7,11},{11,7},{20,24},{24,20... | collective-permute-start | bytes 786440 | tf_op jit(solution)/shard_map/ppermute | solution.py:147
  56.8 10.2 %collective-permute-start.18 = (bf16[128,1024]{1,0:T(8,128)(2,1)S(1)}, bf16[128,1024]{1,0:T(8,128)(2,1)S(1)}, u32[]{:S(2)}, u32[]{:S(2)}) collective-permute-start(bf16[128,1024]{1,0:T(8,128)(2,1)S(1)} %get-tuple-element.84), channel_id=1, source_target_pairs={{0,4},{12,8},{1,5},{13,9},{2,6},{14,10},{3,7},{15,11},{16,20},{28,... | collective-permute-start | bytes 786440 | tf_op jit(solution)/shard_map/ppermute | solution.py:141
  60.6 7.4 %collective-permute-start.17 = (bf16[128,2048]{1,0:T(8,128)(2,1)S(1)}, bf16[128,2048]{1,0:T(8,128)(2,1)S(1)}, u32[]{:S(2)}, u32[]{:S(2)}) collective-permute-start(bf16[128,2048]{1,0:T(8,128)(2,1)S(1)} %pad_maximum_fusion.1), channel_id=1, source_target_pairs={{4,8},{8,4},{5,9},{9,5},{6,10},{10,6},{7,11},{11,7},{20,24},{24,20... | collective-permute-start | bytes 1572872 | tf_op jit(solution)/shard_map/ppermute | solution.py:147
  64.6 13.9 %collective-permute-start.16 = (bf16[512,512]{1,0:T(8,128)(2,1)S(1)}, bf16[512,512]{1,0:T(8,128)(2,1)S(1)}, u32[]{:S(2)}, u32[]{:S(2)}) collective-permute-start(bf16[512,512]{1,0:T(8,128)(2,1)S(1)} %maximum_select_fusion.2), channel_id=1, source_target_pairs={{0,4},{4,0},{8,12},{12,8},{1,5},{5,1},{9,13},{13,9},{2,6},{6,2},{1... | collective-permute-start | bytes 1572872 | tf_op jit(solution)/shard_map/ppermute | solution.py:138
  67.2 0.8 collective-permute-start.19
  78.8 19.1 %collective-permute-start.20 = (bf16[128,2048]{1,0:T(8,128)(2,1)S(1)}, bf16[128,2048]{1,0:T(8,128)(2,1)S(1)}, u32[]{:S(2)}, u32[]{:S(2)}) collective-permute-start(bf16[128,2048]{1,0:T(8,128)(2,1)S(1)} %maximum_select_fusion.1), channel_id=1, source_target_pairs={{0,4},{4,0},{8,12},{12,8},{1,5},{5,1},{9,13},{13,9},{2,6},{6,2},{1... | collective-permute-start | bytes 1572872 | tf_op jit(solution)/shard_map/ppermute | solution.py:138
  81.5 16.9 %collective-permute-start.22 = (bf16[256,512]{1,0:T(8,128)(2,1)S(1)}, bf16[256,512]{1,0:T(8,128)(2,1)S(1)}, u32[]{:S(2)}, u32[]{:S(2)}) collective-permute-start(bf16[256,512]{1,0:T(8,128)(2,1)S(1)} %add_convert_fusion), channel_id=1, source_target_pairs={{0,8},{4,12},{8,0},{12,4},{1,9},{5,13},{9,1},{13,5},{2,10},{6,14},... | collective-permute-start | bytes 786440 | tf_op jit(solution)/shard_map/ppermute | solution.py:172
  98.3 5.1 %collective-permute-start.21 = (f32[128,2048]{1,0:T(8,128)S(1)}, f32[128,2048]{1,0:T(8,128)S(1)}, u32[]{:S(2)}, u32[]{:S(2)}) collective-permute-start(f32[128,2048]{1,0:T(8,128)S(1)} %pad_maximum_fusion.mine), channel_id=1, source_target_pairs={{0,16},{16,0},{1,17},{17,1},{2,18},{18,2},{3,19},{19,3},{4,20},{20... | collective-permute-start | bytes 3145736 | tf_op jit(solution)/shard_map/ppermute | solution.py:135
  98.5 3.3 %collective-permute-start.23 = (f32[256,512]{1,0:T(8,128)S(1)}, f32[256,512]{1,0:T(8,128)S(1)}, u32[]{:S(2)}, u32[]{:S(2)}) collective-permute-start(f32[256,512]{1,0:T(8,128)S(1)} %convert_add_fusion.mine), channel_id=1, source_target_pairs={{0,16},{16,0},{1,17},{17,1},{2,18},{18,2},{3,19},{19,3},{4,20},{20... | collective-permute-start | bytes 1572872 | tf_op jit(solution)/shard_map/ppermute | solution.py:135

commit v5 on v4

--- a/solution.py
+++ b/solution.py
@@ -103,21 +103,27 @@
     keep[...] = total[1]
 
 
-def join_weight_kernel(place, mine, pair, out):
+def join_weight_kernel(place, mine, pair, last, last_pair, out, done):
     half, width = mine.shape[0], mine.shape[1] // 4
     here = pl.multiple_of(place[4] * half, half)
     there = pl.multiple_of(half - place[4] * half, half)
-    for k in range(4):
-        start = pl.multiple_of(place[k] * width, width)
-        out[pl.ds(here, half), pl.ds(start, width)] = mine[:, k * width : (k + 1) * width]
-        out[pl.ds(there, half), pl.ds(start, width)] = pair[:, k * width : (k + 1) * width]
-
-
-def join_key_kernel(place, mine, pair, out):
+    for at, kept, came in ((here, mine, last), (there, pair, last_pair)):
+        for k in range(4):
+            start = pl.multiple_of(place[k] * width, width)
+            value = kept[:, k * width : (k + 1) * width]
+            if k > 0:
+                value = value + came[:, (k - 1) * width : k * width].astype(F32)
+            out[pl.ds(at, half), pl.ds(start, width)] = value
+    done[...] = jnp.zeros_like(done)
+
+
+def join_key_kernel(place, before, mine, pair, last, last_pair, out):
     first = place[4] == 0
     half = mine.shape[1] // 4
     for p in range(4):
-        a, b = mine[:, p * half : (p + 1) * half], pair[:, p * half : (p + 1) * half]
+        cols = slice(p * half, (p + 1) * half)
+        a = mine[:, cols] + last[:, cols].astype(F32)
+        b = pair[:, cols] + last_pair[:, cols].astype(F32)
         out[:, 2 * p * half : (2 * p + 1) * half] = jnp.where(first, a, b)
         out[:, (2 * p + 1) * half : (2 * p + 2) * half] = jnp.where(first, b, a)
 
@@ -196,71 +202,70 @@
             residual_grad, res_other, v0, vx, vy, vd, v0_other, vx_other, vy_other, vd_other, chosen, *weights,
         )
 
+    got = phase((value_grad, layer_input, residual_grad, value_weight, place, low == 1, end == 1, core * half))
+    value_grad, layer_input, residual_grad, value_weight, place, is_low, is_end, first_row = got
+
     v0 = value_grad
     v0_other, weight_rows = phase((core_swap(v0), value_weight))
-    w_own = lax.dynamic_slice_in_dim(weight_rows, core * half, half, 0)
+    w_own = lax.dynamic_slice_in_dim(weight_rows, first_row, half, 0)
     in_other, res_other = core_swap(layer_input), core_swap(residual_grad)
+    w_inner, in_other = phase((w_own, in_other))
     turned = call(turn_kernel, jax.ShapeDtypeStruct((2, 4 * half, tokens), BF16), [], 0, layer_input, in_other)
     term0, send0 = term((v0, v0_other), (0, 4))
-    got = phase((outer(w_own), inner(w_own), square(v0, 1), square(v0, 2), turned, term0, send0,
-                 res_other, low == 1, end == 1))
-    w_beside, w_mid, vx, vy, turned, term0, send0, res_other, is_low, is_end = got
+    got = phase((outer(w_own), inner(w_inner), square(v0, 1), square(v0, 2), turned, term0, send0,
+                 res_other))
+    w_beside, w_mid, vx, vy, turned, term0, send0, res_other = got
 
     vx_other, vy_other = core_swap(vx), core_swap(vy)
     term1, send1, near1 = term((vx, vy, vx_other, vy_other), (0, 2), (2, 1))
     key = owner[:, 0] * keys + key_row
-    got = phase((outer(jnp.where(is_end, send0, w_mid)), inner(w_beside), square(v0, 3), term1, send1, near1,
-                 core_swap(key)))
-    i0, w_end, vd, term1, send1, near1, key_other = got
+    key_both = jnp.concatenate([key, core_swap(key)])[None, :]
+    chosen = call(choose_kernel, struct(4 * keys, 2 * tokens, BF16), [], 0, key_both)
+    got = phase((outer(jnp.where(is_end, send0, w_mid)), inner(w_beside), square(v0, 3), term1, send1, near1, chosen))
+    i0, w_end, vd, term1, send1, near1, chosen = got
     w_third = i0
 
-    b0 = inner(far_plus(term0, i0))
-    vd_other = core_swap(vd)
-    key_both = jnp.concatenate([key, key_other])[None, :]
-    chosen = call(choose_kernel, struct(4 * keys, 2 * tokens, BF16), [], 0, key_both)
+    vd_other, sums0 = phase((core_swap(vd), far_plus(term0, i0)))
+    b0 = inner(sums0)
     term2, send2, near2 = term((vd, vd_other), (0, 2), (2, 1))
-    i2 = inward(send2)
+    back0 = plus(term0[2 * half : 3 * half], b0[:, :heads])
+    send2 = jnp.where(is_end, send2, jnp.concatenate([back0, back0], 1))
     send_a, keep_a = back(14, (5, 6, 7), w_own, w_beside, w_mid, w_third)
-    got = phase((outer(jnp.where(is_end, send1, w_end)), b0, term1, term2, send_a, keep_a, term0, near1, near2))
-    i1, b0, term1, term2, send_a, keep_a, term0, near1, near2 = got
+    got = phase((outer(jnp.where(is_end, send1, w_end)), b0, term1, term2, send_a, keep_a, term0, near1, near2, send2))
+    i1, b0, term1, term2, send_a, keep_a, term0, near1, near2, send2 = got
     w_fourth = i1
 
     def joined(a, b):
         return jnp.where(is_low, jnp.concatenate([a, b], 1), jnp.concatenate([b, a], 1))
 
+    i2 = outer(send2)
     send_b, keep_b = back(8, (8,), w_end, w_fourth)
     keep = joined(keep_a, keep_b)
     b1 = inner(far_plus(term1, i1))
     b2 = inner(far_plus(term2, i2))
-    k1, b1, b2, term1, term2, keep = phase((outer(joined(send_a, send_b)), b1, b2, term1, term2, keep))
+    got = phase((outer(joined(send_a, send_b)), b1, b2, term0, term1, term2, keep, i2))
+    k1, b1, b2, term0, term1, term2, keep, i2 = got
 
     k2 = across(plus(keep[keys:], k1[keys:]))
-    mine = keep[:keys] + k1[:keys].astype(F32)
     back1 = plus(term1[2 * half : 3 * half], b1[:, : 2 * heads])
-    back0 = plus(term0[2 * half : 3 * half], b0[:, :heads])
     back2 = plus(term2[2 * half : 3 * half], b2[:, :heads])
     i3 = outer(jnp.where(
-        is_end, jnp.concatenate([near1, near2, near2], 1), jnp.concatenate([back1, back2, back0], 1)
+        is_end, jnp.concatenate([near1, near2], 1), jnp.concatenate([back1, back2], 1)
     ))
-
-    def total(v, *came):
-        return sum((c.astype(F32) for c in came), v[3 * half :])
-
+    key_half = keep[:keys] + k1[:keys].astype(F32)
     weight_half = jnp.concatenate([
-        total(term0, jnp.where(is_end, i3[:, 3 * heads :], i0[:, 2 * heads : 3 * heads]), b0[:, heads:]),
-        total(term1, i3[:, : 2 * heads], b1[:, 2 * heads :]),
-        total(term2, i3[:, 2 * heads : 3 * heads], b2[:, heads:]),
+        term0[3 * half :] + jnp.where(is_end, i2[:, :heads], i0[:, 2 * heads : 3 * heads]).astype(F32)
+        + b0[:, heads:].astype(F32),
+        term1[3 * half :] + b1[:, 2 * heads :].astype(F32),
+        term2[3 * half :] + b2[:, heads:].astype(F32),
     ], 1)
-    weight_pair = core_swap(weight_half)
-    weight_grad = call(
-        join_weight_kernel, jax.ShapeDtypeStruct((part, 4 * heads), F32),
-        [], 0, weight_half, weight_pair,
+    weight_grad, done = call(
+        join_weight_kernel, (struct(part, 4 * heads, F32), struct(8, 128, F32)), [], 0,
+        weight_half, core_swap(weight_half), i3, core_swap(i3),
     )
-    key_half = mine + k2.astype(F32)
-    key_pair = core_swap(key_half)
     key_grad = call(
-        join_key_kernel, jax.ShapeDtypeStruct((keys, features), F32),
-        [], 0, key_half, key_pair,
+        join_key_kernel, struct(keys, features, F32), [], 0,
+        done, key_half, core_swap(key_half), k2, core_swap(k2),
     )
     return weight_grad, key_grad
 

time: 106 us -> 99 us (0.934)
  waiting for transfers between devices: 46.7 us -> 42.8 us
  starting transfers between devices: 34.5 us -> 31.8 us
  other arithmetic: 1.53 us -> 2.83 us
    ppermute x5 -> x6, waiting for transfers between devices: 39.5 us -> 35.7 us  [outer(): return lax.ppermute(v, 'fsdp', [(0, 1), (1, 0), (2, 3), (3, 2)])]
    ppermute x1 -> x0, starting transfers between devices: 3.65 us -> none  [inward(): return lax.ppermute(v, 'fsdp', [(0, 1), (3, 2)])]
    ppermute x5 -> x6, starting transfers between devices: 16.4 us -> 18 us  [outer(): return lax.ppermute(v, 'fsdp', [(0, 1), (1, 0), (2, 3), (3, 2)])]
    ppermute x9 -> x11, waiting for transfers between devices: 2.74 us -> 1.23 us  [core_swap(): return lax.ppermute(v, 'dp', [(0, 1), (1, 0)])]
    ppermute x3, waiting for transfers between devices: 4.4 us -> 5.84 us  [square(): return lax.ppermute(v, 'tp', [(i, i ^ d) for i in range(4)])]
    ppermute x9 -> x11, starting transfers between devices: 2.23 us -> 2.38 us  [core_swap(): return lax.ppermute(v, 'dp', [(0, 1), (1, 0)])]
  transfers between devices with their start and end apart: 24 -> 26, of which waited for: 8 -> 8; matrix products, arithmetic and copies ran while one was open for 2% -> 3% of each run, Pallas kernels for 17% -> 17%
where the time goes in v5:
time: 99 us; the launch traced here: 98.5 us
  waiting for transfers between devices  42.8 us (43%)
  starting transfers between devices  31.8 us (32%)
  Pallas kernels  18.7 us (19%)
  other arithmetic  2.83 us (3%)
  local copies, waits for them, and re-layouts  1.47 us (1%)
    ppermute x6, waiting for transfers between devices, outer(): return lax.ppermute(v, 'fsdp', [(0, 1), (1, 0), (2, 3), (3, 2)])  35.7 us
    pallas_call x9, Pallas kernels, call(): pl.pallas_call(kernel, out_shape=out, in_specs=[smem] + [vmem] * len(args...  18.7 us
    ppermute x6, starting transfers between devices, outer(): return lax.ppermute(v, 'fsdp', [(0, 1), (1, 0), (2, 3), (3, 2)])  18 us
    ppermute x3, starting transfers between devices, square(): return lax.ppermute(v, 'tp', [(i, i ^ d) for i in range(4)])  6.77 us
    ppermute x3, waiting for transfers between devices, square(): return lax.ppermute(v, 'tp', [(i, i ^ d) for i in range(4)])  5.84 us
    ppermute x5, starting transfers between devices, inner(): return lax.ppermute(v, 'fsdp', [(1, 2), (2, 1)])  3.42 us
    ppermute x11, starting transfers between devices, core_swap(): return lax.ppermute(v, 'dp', [(0, 1), (1, 0)])  2.38 us
  transfers between devices with their start and end apart: 26, of which 8 were waited for; matrix products, arithmetic and copies ran while one was open for 3% of the time, Pallas kernels for 17%

profile of v5, /device:TPU:0, one launch (start us, length us, event | category | flops | bytes accessed | tf_op | source)
XLA Modules:
  0.0 98.5 jit_solution(15676455297999781052)
XLA Ops:
  0.6 0.0 copy-start
  0.7 0.1 stack.57.place
  0.8 0.5 collective-permute-start.2
  1.3 0.1 collective-permute-start
  1.4 0.4 collective-permute-start.6
  1.8 2.6 %collective-permute-start.5 = (bf16[512,512]{1,0:T(8,128)(2,1)}, bf16[512,512]{1,0:T(8,128)(2,1)S(1)}, u32[]{:S(2)}, u32[]{:S(2)}) collective-permute-start(bf16[512,512]{1,0:T(8,128)(2,1)} %refs_2_.1), channel_id=1, source_target_pairs={{0,2},{1,3},{2,0},{3,1},{4,6},{5,7},{6,4},{7,5},{8,10},{9,11},{10,... | collective-permute-start | bytes 1572872 | tf_op jit(solution)/shard_map/ppermute | solution.py:175
  4.4 1.5 %collective-permute-start.4 = (bf16[512,512]{1,0:T(8,128)(2,1)}, bf16[512,512]{1,0:T(8,128)(2,1)}, u32[]{:S(2)}, u32[]{:S(2)}) collective-permute-start(bf16[512,512]{1,0:T(8,128)(2,1)} %refs_2_.1), channel_id=1, source_target_pairs={{0,1},{1,0},{2,3},{3,2},{4,5},{5,4},{6,7},{7,6},{8,9},{9,8},{10,11... | collective-permute-start | bytes 1572872 | tf_op jit(solution)/shard_map/ppermute | solution.py:175
  5.9 0.0 collective-permute-done.refs_1_.refs_6_
  5.9 0.1 constant_dynamic-slice_fusion.refs_11_
  6.0 1.7 %collective-permute-start.1 = (bf16[128,2048]{1,0:T(8,128)(2,1)S(1)}, bf16[128,2048]{1,0:T(8,128)(2,1)S(1)}, u32[]{:S(2)}, u32[]{:S(2)}) collective-permute-start(bf16[128,2048]{1,0:T(8,128)(2,1)S(1)} %constant_dynamic-slice_fusion.refs_11_), channel_id=1, source_target_pairs={{0,4},{4,0},{8,12},{12,8},{1,5},{5,1},{9,13},{13,9},{2,6},{6,2},{1... | collective-permute-start | bytes 1572872 | tf_op jit(solution)/shard_map/ppermute | solution.py:144
  7.7 0.0 collective-permute-done.2.other
  7.7 0.7 collective-permute-start.3
  8.4 0.7 broadcast_multiply_fusion
  9.1 0.7 add.56
  9.8 1.2 %copy-done.3 = bf16[512,1024]{1,0:T(8,128)(2,1)S(1)} copy-done((bf16[512,1024]{1,0:T(8,128)(2,1)S(1)}, bf16[512,1024]{1,0:T(8,128)(2,1)}, u32[]{:S(2)}) %copy-start.3) | copy-done | bytes 1048600
  11.0 1.6 %shard_map.77.turned = bf16[2,512,512]{2,1,0:T(8,128)(2,1)S(1)} custom-call(s32[15]{0:T(128)S(1)} %stack.57.place, bf16[512,1024]{1,0:T(8,128)(2,1)S(1)} %copy-done.3, bf16[512,1024]{1,0:T(8,128)(2,1)} %collective-permute-done.2.other), custom_call_target="tpu_custom_call" | custom-call | bytes 1048576 | tf_op jit(solution)/shard_map/pallas_call | solution.py:164
  12.6 1.2 %shard_map.78 = (f32[512,512]{1,0:T(8,128)S(1)}, bf16[128,2048]{1,0:T(8,128)(2,1)S(1)}) custom-call(s32[15]{0:T(128)S(1)} %stack.57.place, bf16[2,512,512]{2,1,0:T(8,128)(2,1)S(1)} %shard_map.77.turned, bf16[512,512]{1,0:T(8,128)(2,1)S(1)} %copy-done.1, bf16[512,512]{1,0:T(8,128)(2,1)S(1)} %collective-permute-done.refs_1_.refs_6_), custom_call_target="tpu_custom_call" | custom-call | flops 536870912 | bytes 1048576 | tf_op jit(solution)/shard_map/pallas_call | solution.py:164
  13.8 3.3 %collective-permute-done.5.refs_1_.refs_4_ = bf16[512,512]{1,0:T(8,128)(2,1)S(1)} collective-permute-done((bf16[512,512]{1,0:T(8,128)(2,1)}, bf16[512,512]{1,0:T(8,128)(2,1)S(1)}, u32[]{:S(2)}, u32[]{:S(2)}) %collective-permute-start.5) | collective-permute-done | bytes 524320 | tf_op jit(solution)/shard_map/ppermute | solution.py:175
  17.1 2.7 %collective-permute-start.9 = (bf16[512,512]{1,0:T(8,128)(2,1)S(1)}, bf16[512,512]{1,0:T(8,128)(2,1)S(1)}, u32[]{:S(2)}, u32[]{:S(2)}) collective-permute-start(bf16[512,512]{1,0:T(8,128)(2,1)S(1)} %copy-done.1), channel_id=1, source_target_pairs={{0,3},{1,2},{2,1},{3,0},{4,7},{5,6},{6,5},{7,4},{8,11},{9,10},{10,... | collective-permute-start | bytes 1572872 | tf_op jit(solution)/shard_map/ppermute | solution.py:175
  19.8 0.1 collective-permute-done.1.refs_12_
  19.9 0.0 collective-permute-done.6.refs_1_
  19.9 0.5 collective-permute-start.10
  20.4 0.1 collective-permute-start.11
  20.5 0.1 broadcast_select_fusion.1
  20.5 4.8 %collective-permute-start.7 = (bf16[128,2048]{1,0:T(8,128)(2,1)S(1)}, bf16[128,2048]{1,0:T(8,128)(2,1)S(1)}, u32[]{:S(2)}, u32[]{:S(2)}) collective-permute-start(bf16[128,2048]{1,0:T(8,128)(2,1)S(1)} %broadcast_select_fusion.1), channel_id=1, source_target_pairs={{0,4},{4,0},{8,12},{12,8},{1,5},{5,1},{9,13},{13,9},{2,6},{6,2},{1... | collective-permute-start | bytes 1572872 | tf_op jit(solution)/shard_map/ppermute | solution.py:144
  25.3 0.7 collective-permute-start.8
  26.0 0.9 shard_map.80.refs_10_
  27.0 2.3 %shard_map.79 = (f32[512,1024]{1,0:T(8,128)S(1)}, bf16[128,2048]{1,0:T(8,128)(2,1)S(1)}, bf16[128,1024]{1,0:T(8,128)(2,1)S(1)}) custom-call(s32[15]{0:T(128)S(1)} %stack.57.place, bf16[2,512,512]{2,1,0:T(8,128)(2,1)S(1)} %shard_map.77.turned, bf16[512,512]{1,0:T(8,128)(2,1)} %collective-permute-done.4.refs_0_.refs_3_, ...), custom_call_target="tpu_custom_call" | custom-call | flops 1073741824 | bytes 1048576 | tf_op jit(solution)/shard_map/pallas_call | solution.py:164
  29.3 0.0 copy-start.2
  29.3 2.5 %collective-permute-done.9.refs_0_.refs_5_ = bf16[512,512]{1,0:T(8,128)(2,1)S(1)} collective-permute-done((bf16[512,512]{1,0:T(8,128)(2,1)S(1)}, bf16[512,512]{1,0:T(8,128)(2,1)S(1)}, u32[]{:S(2)}, u32[]{:S(2)}) %collective-permute-start.9) | collective-permute-done | bytes 524320 | tf_op jit(solution)/shard_map/ppermute | solution.py:175
  31.8 5.6 %collective-permute-done.7.refs_14_ = bf16[128,2048]{1,0:T(8,128)(2,1)S(1)} collective-permute-done((bf16[128,2048]{1,0:T(8,128)(2,1)S(1)}, bf16[128,2048]{1,0:T(8,128)(2,1)S(1)}, u32[]{:S(2)}, u32[]{:S(2)}) %collective-permute-start.7) | collective-permute-done | bytes 524320 | tf_op jit(solution)/shard_map/ppermute | solution.py:144
  37.4 0.1 broadcast_select_fusion
  37.5 3.7 %collective-permute-start.13 = (bf16[128,2048]{1,0:T(8,128)(2,1)S(1)}, bf16[128,2048]{1,0:T(8,128)(2,1)S(1)}, u32[]{:S(2)}, u32[]{:S(2)}) collective-permute-start(bf16[128,2048]{1,0:T(8,128)(2,1)S(1)} %broadcast_select_fusion), channel_id=1, source_target_pairs={{0,4},{4,0},{8,12},{12,8},{1,5},{5,1},{9,13},{13,9},{2,6},{6,2},{1... | collective-permute-start | bytes 1572872 | tf_op jit(solution)/shard_map/ppermute | solution.py:144
  41.2 0.1 add_convert_fusion.9
  41.3 0.7 collective-permute-start.15
  42.0 4.7 %shard_map.82 = (bf16[512,384]{1,0:T(8,128)(2,1)S(1)}, f32[512,384]{1,0:T(8,128)S(1)}) custom-call(s32[15]{0:T(128)S(1)} %stack.57.place, bf16[512,1024]{1,0:T(8,128)(2,1)S(1)} %copy-done.2, bf16[512,1024]{1,0:T(8,128)(2,1)S(1)} %collective-permute-done.6.refs_1_, bf16[512,512]{1,0:T(8,128)(2,1)S(1)} %copy-done.1, ...), custom_call_target="tpu_custom_call" | custom-call | flops 2415919104 | bytes 1048576 | tf_op jit(solution)/shard_map/pallas_call | solution.py:164
  46.7 1.2 %shard_map.81 = (f32[512,512]{1,0:T(8,128)S(1)}, bf16[128,1024]{1,0:T(8,128)(2,1)S(1)}, bf16[128,512]{1,0:T(8,128)(2,1)S(1)}) custom-call(s32[15]{0:T(128)S(1)} %stack.57.place, bf16[2,512,512]{2,1,0:T(8,128)(2,1)S(1)} %shard_map.77.turned, bf16[512,512]{1,0:T(8,128)(2,1)S(1)} %collective-permute-done.9.refs_0_.refs_5_, ...), custom_call_target="tpu_custom_call" | custom-call | flops 536870912 | bytes 1048576 | tf_op jit(solution)/shard_map/pallas_call | solution.py:164
  48.0 0.1 maximum_select_fusion.3
  48.0 5.7 %collective-permute-done.13.refs_12_ = bf16[128,2048]{1,0:T(8,128)(2,1)S(1)} collective-permute-done((bf16[128,2048]{1,0:T(8,128)(2,1)S(1)}, bf16[128,2048]{1,0:T(8,128)(2,1)S(1)}, u32[]{:S(2)}, u32[]{:S(2)}) %collective-permute-start.13) | collective-permute-done | bytes 524320 | tf_op jit(solution)/shard_map/ppermute | solution.py:144
  53.8 1.7 %collective-permute-start.18 = (bf16[128,1024]{1,0:T(8,128)(2,1)S(1)}, bf16[128,1024]{1,0:T(8,128)(2,1)S(1)}, u32[]{:S(2)}, u32[]{:S(2)}) collective-permute-start(bf16[128,1024]{1,0:T(8,128)(2,1)S(1)} %maximum_select_fusion.3), channel_id=1, source_target_pairs={{0,4},{4,0},{8,12},{12,8},{1,5},{5,1},{9,13},{13,9},{2,6},{6,2},{1... | collective-permute-start | bytes 786440 | tf_op jit(solution)/shard_map/ppermute | solution.py:144
  55.5 0.1 add_convert_fusion.3
  55.7 0.7 collective-permute-start.17
  56.4 3.0 %shard_map.83 = (bf16[512,128]{1,0:T(8,128)(2,1)S(1)}, f32[512,128]{1,0:T(8,128)S(1)}) custom-call(s32[15]{0:T(128)S(1)} %stack.57.place, bf16[512,1024]{1,0:T(8,128)(2,1)S(1)} %copy-done.2, bf16[512,1024]{1,0:T(8,128)(2,1)S(1)} %collective-permute-done.6.refs_1_, bf16[512,512]{1,0:T(8,128)(2,1)S(1)} %copy-done.1, ...), custom_call_target="tpu_custom_call" | custom-call | flops 805306368 | bytes 1048576 | tf_op jit(solution)/shard_map/pallas_call | solution.py:164
  59.4 0.1 maximum_select_fusion.1
  59.5 3.3 %collective-permute-start.16 = (bf16[512,512]{1,0:T(8,128)(2,1)S(1)}, bf16[512,512]{1,0:T(8,128)(2,1)S(1)}, u32[]{:S(2)}, u32[]{:S(2)}) collective-permute-start(bf16[512,512]{1,0:T(8,128)(2,1)S(1)} %maximum_select_fusion.1), channel_id=1, source_target_pairs={{0,4},{4,0},{8,12},{12,8},{1,5},{5,1},{9,13},{13,9},{2,6},{6,2},{1... | collective-permute-start | bytes 1572872 | tf_op jit(solution)/shard_map/ppermute | solution.py:144
  62.9 0.1 add_convert_fusion.6
  63.0 0.7 collective-permute-start.19
  63.6 0.1 maximum_select_fusion
  63.8 10.5 %collective-permute-done.16 = bf16[512,512]{1,0:T(8,128)(2,1)S(1)} collective-permute-done((bf16[512,512]{1,0:T(8,128)(2,1)S(1)}, bf16[512,512]{1,0:T(8,128)(2,1)S(1)}, u32[]{:S(2)}, u32[]{:S(2)}) %collective-permute-start.16) | collective-permute-done | bytes 524320 | tf_op jit(solution)/shard_map/ppermute | solution.py:144
  74.3 0.1 add_convert_fusion.4
  74.4 0.1 add_convert_fusion.1
  74.5 0.1 convert_add_fusion.3
  74.6 0.1 pad_maximum_fusion.mine
  74.7 0.1 collective-permute-start.20
  74.7 0.1 maximum_select_fusion.2
  74.8 2.8 %collective-permute-start.21 = (bf16[128,1536]{1,0:T(8,128)(2,1)S(1)}, bf16[128,1536]{1,0:T(8,128)(2,1)S(1)}, u32[]{:S(2)}, u32[]{:S(2)}) collective-permute-start(bf16[128,1536]{1,0:T(8,128)(2,1)S(1)} %maximum_select_fusion.2), channel_id=1, source_target_pairs={{0,4},{4,0},{8,12},{12,8},{1,5},{5,1},{9,13},{13,9},{2,6},{6,2},{1... | collective-permute-start | bytes 1179656 | tf_op jit(solution)/shard_map/ppermute | solution.py:144
  77.6 0.2 add_convert_fusion
  77.8 1.3 %collective-permute-start.24 = (bf16[256,512]{1,0:T(8,128)(2,1)S(1)}, bf16[256,512]{1,0:T(8,128)(2,1)S(1)}, u32[]{:S(2)}, u32[]{:S(2)}) collective-permute-start(bf16[256,512]{1,0:T(8,128)(2,1)S(1)} %get-tuple-element.128), channel_id=1, source_target_pairs={{0,8},{4,12},{8,0},{12,4},{1,9},{5,13},{9,1},{13,5},{2,10},{6,14},... | collective-permute-start | bytes 786440 | tf_op jit(solution)/shard_map/ppermute | solution.py:178
  79.0 0.2 collective-permute-start.23
  79.3 13.7 %collective-permute-done.21.last = bf16[128,1536]{1,0:T(8,128)(2,1)S(1)} collective-permute-done((bf16[128,1536]{1,0:T(8,128)(2,1)S(1)}, bf16[128,1536]{1,0:T(8,128)(2,1)S(1)}, u32[]{:S(2)}, u32[]{:S(2)}) %collective-permute-start.21) | collective-permute-done | bytes 393248 | tf_op jit(solution)/shard_map/ppermute | solution.py:144
  93.0 0.5 collective-permute-start.25
  93.5 1.2 %collective-permute-done.22.last_pair = bf16[128,1536]{1,0:T(8,128)(2,1)S(1)} collective-permute-done((bf16[128,1536]{1,0:T(8,128)(2,1)S(1)}, bf16[128,1536]{1,0:T(8,128)(2,1)S(1)}, u32[]{:S(2)}, u32[]{:S(2)}) %collective-permute-start.22) | collective-permute-done | bytes 393248 | tf_op jit(solution)/shard_map/ppermute | solution.py:141
  94.7 2.0 %shard_map.84 = (f32[256,2048]{1,0:T(8,128)}, f32[8,128]{1,0:T(8,128)S(1)}) custom-call(s32[15]{0:T(128)S(1)} %stack.57.place, f32[128,2048]{1,0:T(8,128)S(1)} %pad_maximum_fusion.mine, f32[128,2048]{1,0:T(8,128)S(1)} %collective-permute-done.20.pair, bf16[128,1536]{1,0:T(8,128)(2,1)S(1)} %collective-permute-done.21.last, ...), custom_call_target="tpu_custom_call" | custom-call | bytes 1048576 | tf_op jit(solution)/shard_map/pallas_call | solution.py:164
  96.8 1.8 %shard_map.85 = f32[256,1024]{1,0:T(8,128)} custom-call(s32[15]{0:T(128)S(1)} %stack.57.place, f32[8,128]{1,0:T(8,128)S(1)} %get-tuple-element.121.before, f32[256,512]{1,0:T(8,128)S(1)} %get-tuple-element.129.mine, f32[256,512]{1,0:T(8,128)S(1)} %collective-permute-done.23.pair, bf16[256,512]{1,0:T(8,128)(2,1)S(1)} %collective-permute-done.24.last, ...), custom_call_target="tpu_custom_call" | custom-call | bytes 1048576 | tf_op jit(solution)/shard_map/pallas_call | solution.py:164
  (28 shorter events, 0.2 us)
Async XLA Ops:
  0.6 5.3 %copy-start = (bf16[256,2048]{1,0:T(8,128)(2,1)S(1)}, bf16[256,2048]{1,0:T(8,128)(2,1)}, u32[]{:S(2)}) copy-start(bf16[256,2048]{1,0:T(8,128)(2,1)} %param.9) | copy-start | bytes 3145732
  0.8 6.9 %collective-permute-start.2 = (bf16[512,1024]{1,0:T(8,128)(2,1)}, bf16[512,1024]{1,0:T(8,128)(2,1)}, u32[]{:S(2)}, u32[]{:S(2)}) collective-permute-start(bf16[512,1024]{1,0:T(8,128)(2,1)} %mine), channel_id=1, source_target_pairs={{0,16},{16,0},{1,17},{17,1},{2,18},{18,2},{3,19},{19,3},{4,20},{20... | collective-permute-start | bytes 3145736 | tf_op jit(solution)/shard_map/ppermute | solution.py:141
  1.3 4.6 %collective-permute-start = (bf16[512,512]{1,0:T(8,128)(2,1)}, bf16[512,512]{1,0:T(8,128)(2,1)S(1)}, u32[]{:S(2)}, u32[]{:S(2)}) collective-permute-start(bf16[512,512]{1,0:T(8,128)(2,1)} %refs_2_.1), channel_id=1, source_target_pairs={{0,16},{16,0},{1,17},{17,1},{2,18},{18,2},{3,19},{19,3},{4,20},{20... | collective-permute-start | bytes 1572872 | tf_op jit(solution)/shard_map/ppermute | solution.py:141
  1.4 18.5 %collective-permute-start.6 = (bf16[512,1024]{1,0:T(8,128)(2,1)}, bf16[512,1024]{1,0:T(8,128)(2,1)S(1)}, u32[]{:S(2)}, u32[]{:S(2)}) collective-permute-start(bf16[512,1024]{1,0:T(8,128)(2,1)} %refs_0_.2), channel_id=1, source_target_pairs={{0,16},{16,0},{1,17},{17,1},{2,18},{18,2},{3,19},{19,3},{4,20},{20... | collective-permute-start | bytes 3145736 | tf_op jit(solution)/shard_map/ppermute | solution.py:141
  1.8 15.3 %collective-permute-start.5 = (bf16[512,512]{1,0:T(8,128)(2,1)}, bf16[512,512]{1,0:T(8,128)(2,1)S(1)}, u32[]{:S(2)}, u32[]{:S(2)}) collective-permute-start(bf16[512,512]{1,0:T(8,128)(2,1)} %refs_2_.1), channel_id=1, source_target_pairs={{0,2},{1,3},{2,0},{3,1},{4,6},{5,7},{6,4},{7,5},{8,10},{9,11},{10,... | collective-permute-start | bytes 1572872 | tf_op jit(solution)/shard_map/ppermute | solution.py:175
  4.4 15.4 %collective-permute-start.4 = (bf16[512,512]{1,0:T(8,128)(2,1)}, bf16[512,512]{1,0:T(8,128)(2,1)}, u32[]{:S(2)}, u32[]{:S(2)}) collective-permute-start(bf16[512,512]{1,0:T(8,128)(2,1)} %refs_2_.1), channel_id=1, source_target_pairs={{0,1},{1,0},{2,3},{3,2},{4,5},{5,4},{6,7},{7,6},{8,9},{9,8},{10,11... | collective-permute-start | bytes 1572872 | tf_op jit(solution)/shard_map/ppermute | solution.py:175
  5.9 6.7 %copy-start.1 = (bf16[512,512]{1,0:T(8,128)(2,1)S(1)}, bf16[512,512]{1,0:T(8,128)(2,1)}, u32[]{:S(2)}) copy-start(bf16[512,512]{1,0:T(8,128)(2,1)} %refs_2_.1) | copy-start | bytes 1572868
  6.0 13.9 %collective-permute-start.1 = (bf16[128,2048]{1,0:T(8,128)(2,1)S(1)}, bf16[128,2048]{1,0:T(8,128)(2,1)S(1)}, u32[]{:S(2)}, u32[]{:S(2)}) collective-permute-start(bf16[128,2048]{1,0:T(8,128)(2,1)S(1)} %constant_dynamic-slice_fusion.refs_11_), channel_id=1, source_target_pairs={{0,4},{4,0},{8,12},{12,8},{1,5},{5,1},{9,13},{13,9},{2,6},{6,2},{1... | collective-permute-start | bytes 1572872 | tf_op jit(solution)/shard_map/ppermute | solution.py:144
  7.7 12.2 %collective-permute-start.3 = (bf16[128,2048]{1,0:T(8,128)(2,1)S(1)}, bf16[128,2048]{1,0:T(8,128)(2,1)S(1)}, u32[]{:S(2)}, u32[]{:S(2)}) collective-permute-start(bf16[128,2048]{1,0:T(8,128)(2,1)S(1)} %constant_dynamic-slice_fusion.refs_11_), channel_id=1, source_target_pairs={{4,8},{8,4},{5,9},{9,5},{6,10},{10,6},{7,11},{11,7},{20,24},{24,20... | collective-permute-start | bytes 1572872 | tf_op jit(solution)/shard_map/ppermute | solution.py:153
  9.7 1.2 %copy-start.3 = (bf16[512,1024]{1,0:T(8,128)(2,1)S(1)}, bf16[512,1024]{1,0:T(8,128)(2,1)}, u32[]{:S(2)}) copy-start(bf16[512,1024]{1,0:T(8,128)(2,1)} %mine) | copy-start | bytes 3145732
  17.1 14.7 %collective-permute-start.9 = (bf16[512,512]{1,0:T(8,128)(2,1)S(1)}, bf16[512,512]{1,0:T(8,128)(2,1)S(1)}, u32[]{:S(2)}, u32[]{:S(2)}) collective-permute-start(bf16[512,512]{1,0:T(8,128)(2,1)S(1)} %copy-done.1), channel_id=1, source_target_pairs={{0,3},{1,2},{2,1},{3,0},{4,7},{5,6},{6,5},{7,4},{8,11},{9,10},{10,... | collective-permute-start | bytes 1572872 | tf_op jit(solution)/shard_map/ppermute | solution.py:175
  19.8 5.5 %collective-permute-start.12 = (s32[512]{0:T(512)S(1)}, s32[512]{0:T(512)S(1)}, u32[]{:S(2)}, u32[]{:S(2)}) collective-permute-start(s32[512]{0:T(512)S(1)} %add.56), channel_id=1, source_target_pairs={{0,16},{16,0},{1,17},{17,1},{2,18},{18,2},{3,19},{19,3},{4,20},{20... | collective-permute-start | bytes 6152 | tf_op jit(solution)/shard_map/ppermute | solution.py:141
  19.9 7.0 %collective-permute-start.10 = (bf16[512,512]{1,0:T(8,128)(2,1)}, bf16[512,512]{1,0:T(8,128)(2,1)S(1)}, u32[]{:S(2)}, u32[]{:S(2)}) collective-permute-start(bf16[512,512]{1,0:T(8,128)(2,1)} %collective-permute-done.4.refs_0_.refs_3_), channel_id=1, source_target_pairs={{0,16},{16,0},{1,17},{17,1},{2,18},{18,2},{3,19},{19,3},{4,20},{20... | collective-permute-start | bytes 1572872 | tf_op jit(solution)/shard_map/ppermute | solution.py:141
  20.4 6.6 %collective-permute-start.11 = (bf16[512,512]{1,0:T(8,128)(2,1)S(1)}, bf16[512,512]{1,0:T(8,128)(2,1)S(1)}, u32[]{:S(2)}, u32[]{:S(2)}) collective-permute-start(bf16[512,512]{1,0:T(8,128)(2,1)S(1)} %collective-permute-done.5.refs_1_.refs_4_), channel_id=1, source_target_pairs={{0,16},{16,0},{1,17},{17,1},{2,18},{18,2},{3,19},{19,3},{4,20},{20... | collective-permute-start | bytes 1572872 | tf_op jit(solution)/shard_map/ppermute | solution.py:141
  20.5 16.9 %collective-permute-start.7 = (bf16[128,2048]{1,0:T(8,128)(2,1)S(1)}, bf16[128,2048]{1,0:T(8,128)(2,1)S(1)}, u32[]{:S(2)}, u32[]{:S(2)}) collective-permute-start(bf16[128,2048]{1,0:T(8,128)(2,1)S(1)} %broadcast_select_fusion.1), channel_id=1, source_target_pairs={{0,4},{4,0},{8,12},{12,8},{1,5},{5,1},{9,13},{13,9},{2,6},{6,2},{1... | collective-permute-start | bytes 1572872 | tf_op jit(solution)/shard_map/ppermute | solution.py:144
  25.3 12.1 %collective-permute-start.8 = (bf16[128,2048]{1,0:T(8,128)(2,1)S(1)}, bf16[128,2048]{1,0:T(8,128)(2,1)S(1)}, u32[]{:S(2)}, u32[]{:S(2)}) collective-permute-start(bf16[128,2048]{1,0:T(8,128)(2,1)S(1)} %collective-permute-done.1.refs_12_), channel_id=1, source_target_pairs={{4,8},{8,4},{5,9},{9,5},{6,10},{10,6},{7,11},{11,7},{20,24},{24,20... | collective-permute-start | bytes 1572872 | tf_op jit(solution)/shard_map/ppermute | solution.py:153
  29.3 12.7 %copy-start.2 = (bf16[512,1024]{1,0:T(8,128)(2,1)S(1)}, bf16[512,1024]{1,0:T(8,128)(2,1)}, u32[]{:S(2)}) copy-start(bf16[512,1024]{1,0:T(8,128)(2,1)} %refs_0_.2) | copy-start | bytes 3145732
  37.4 3.9 %collective-permute-start.14 = (bf16[512,512]{1,0:T(8,128)(2,1)S(1)}, bf16[512,512]{1,0:T(8,128)(2,1)S(1)}, u32[]{:S(2)}, u32[]{:S(2)}) collective-permute-start(bf16[512,512]{1,0:T(8,128)(2,1)S(1)} %collective-permute-done.9.refs_0_.refs_5_), channel_id=1, source_target_pairs={{0,16},{16,0},{1,17},{17,1},{2,18},{18,2},{3,19},{19,3},{4,20},{20... | collective-permute-start | bytes 1572872 | tf_op jit(solution)/shard_map/ppermute | solution.py:141
  37.5 16.3 %collective-permute-start.13 = (bf16[128,2048]{1,0:T(8,128)(2,1)S(1)}, bf16[128,2048]{1,0:T(8,128)(2,1)S(1)}, u32[]{:S(2)}, u32[]{:S(2)}) collective-permute-start(bf16[128,2048]{1,0:T(8,128)(2,1)S(1)} %broadcast_select_fusion), channel_id=1, source_target_pairs={{0,4},{4,0},{8,12},{12,8},{1,5},{5,1},{9,13},{13,9},{2,6},{6,2},{1... | collective-permute-start | bytes 1572872 | tf_op jit(solution)/shard_map/ppermute | solution.py:144
  41.3 6.6 %collective-permute-start.15 = (bf16[128,1024]{1,0:T(8,128)(2,1)S(1)}, bf16[128,1024]{1,0:T(8,128)(2,1)S(1)}, u32[]{:S(2)}, u32[]{:S(2)}) collective-permute-start(bf16[128,1024]{1,0:T(8,128)(2,1)S(1)} %pad_maximum_fusion.2), channel_id=1, source_target_pairs={{4,8},{8,4},{5,9},{9,5},{6,10},{10,6},{7,11},{11,7},{20,24},{24,20... | collective-permute-start | bytes 786440 | tf_op jit(solution)/shard_map/ppermute | solution.py:153
  53.8 9.1 %collective-permute-start.18 = (bf16[128,1024]{1,0:T(8,128)(2,1)S(1)}, bf16[128,1024]{1,0:T(8,128)(2,1)S(1)}, u32[]{:S(2)}, u32[]{:S(2)}) collective-permute-start(bf16[128,1024]{1,0:T(8,128)(2,1)S(1)} %maximum_select_fusion.3), channel_id=1, source_target_pairs={{0,4},{4,0},{8,12},{12,8},{1,5},{5,1},{9,13},{13,9},{2,6},{6,2},{1... | collective-permute-start | bytes 786440 | tf_op jit(solution)/shard_map/ppermute | solution.py:144
  55.7 8.1 %collective-permute-start.17 = (bf16[128,2048]{1,0:T(8,128)(2,1)S(1)}, bf16[128,2048]{1,0:T(8,128)(2,1)S(1)}, u32[]{:S(2)}, u32[]{:S(2)}) collective-permute-start(bf16[128,2048]{1,0:T(8,128)(2,1)S(1)} %pad_maximum_fusion.1), channel_id=1, source_target_pairs={{4,8},{8,4},{5,9},{9,5},{6,10},{10,6},{7,11},{11,7},{20,24},{24,20... | collective-permute-start | bytes 1572872 | tf_op jit(solution)/shard_map/ppermute | solution.py:153
  59.5 14.8 %collective-permute-start.16 = (bf16[512,512]{1,0:T(8,128)(2,1)S(1)}, bf16[512,512]{1,0:T(8,128)(2,1)S(1)}, u32[]{:S(2)}, u32[]{:S(2)}) collective-permute-start(bf16[512,512]{1,0:T(8,128)(2,1)S(1)} %maximum_select_fusion.1), channel_id=1, source_target_pairs={{0,4},{4,0},{8,12},{12,8},{1,5},{5,1},{9,13},{13,9},{2,6},{6,2},{1... | collective-permute-start | bytes 1572872 | tf_op jit(solution)/shard_map/ppermute | solution.py:144
  63.0 0.8 collective-permute-start.19
  74.7 20.1 %collective-permute-start.20 = (f32[128,2048]{1,0:T(8,128)S(1)}, f32[128,2048]{1,0:T(8,128)S(1)}, u32[]{:S(2)}, u32[]{:S(2)}) collective-permute-start(f32[128,2048]{1,0:T(8,128)S(1)} %pad_maximum_fusion.mine), channel_id=1, source_target_pairs={{0,16},{16,0},{1,17},{17,1},{2,18},{18,2},{3,19},{19,3},{4,20},{20... | collective-permute-start | bytes 3145736 | tf_op jit(solution)/shard_map/ppermute | solution.py:141
  74.8 18.2 %collective-permute-start.21 = (bf16[128,1536]{1,0:T(8,128)(2,1)S(1)}, bf16[128,1536]{1,0:T(8,128)(2,1)S(1)}, u32[]{:S(2)}, u32[]{:S(2)}) collective-permute-start(bf16[128,1536]{1,0:T(8,128)(2,1)S(1)} %maximum_select_fusion.2), channel_id=1, source_target_pairs={{0,4},{4,0},{8,12},{12,8},{1,5},{5,1},{9,13},{13,9},{2,6},{6,2},{1... | collective-permute-start | bytes 1179656 | tf_op jit(solution)/shard_map/ppermute | solution.py:144
  77.8 15.2 %collective-permute-start.24 = (bf16[256,512]{1,0:T(8,128)(2,1)S(1)}, bf16[256,512]{1,0:T(8,128)(2,1)S(1)}, u32[]{:S(2)}, u32[]{:S(2)}) collective-permute-start(bf16[256,512]{1,0:T(8,128)(2,1)S(1)} %get-tuple-element.128), channel_id=1, source_target_pairs={{0,8},{4,12},{8,0},{12,4},{1,9},{5,13},{9,1},{13,5},{2,10},{6,14},... | collective-permute-start | bytes 786440 | tf_op jit(solution)/shard_map/ppermute | solution.py:178
  79.0 17.7 %collective-permute-start.23 = (f32[256,512]{1,0:T(8,128)S(1)}, f32[256,512]{1,0:T(8,128)S(1)}, u32[]{:S(2)}, u32[]{:S(2)}) collective-permute-start(f32[256,512]{1,0:T(8,128)S(1)} %get-tuple-element.129.mine), channel_id=1, source_target_pairs={{0,16},{16,0},{1,17},{17,1},{2,18},{18,2},{3,19},{19,3},{4,20},{20... | collective-permute-start | bytes 1572872 | tf_op jit(solution)/shard_map/ppermute | solution.py:141
  93.0 1.7 %collective-permute-start.22 = (bf16[128,1536]{1,0:T(8,128)(2,1)S(1)}, bf16[128,1536]{1,0:T(8,128)(2,1)S(1)}, u32[]{:S(2)}, u32[]{:S(2)}) collective-permute-start(bf16[128,1536]{1,0:T(8,128)(2,1)S(1)} %collective-permute-done.21.last), channel_id=1, source_target_pairs={{0,16},{16,0},{1,17},{17,1},{2,18},{18,2},{3,19},{19,3},{4,20},{20... | collective-permute-start | bytes 1179656 | tf_op jit(solution)/shard_map/ppermute | solution.py:141
  93.0 3.8 %collective-permute-start.25 = (bf16[256,512]{1,0:T(8,128)(2,1)S(1)}, bf16[256,512]{1,0:T(8,128)(2,1)S(1)}, u32[]{:S(2)}, u32[]{:S(2)}) collective-permute-start(bf16[256,512]{1,0:T(8,128)(2,1)S(1)} %collective-permute-done.24.last), channel_id=1, source_target_pairs={{0,16},{16,0},{1,17},{17,1},{2,18},{18,2},{3,19},{19,3},{4,20},{20... | collective-permute-start | bytes 786440 | tf_op jit(solution)/shard_map/ppermute | solution.py:141

commit v6 on v5

--- a/solution.py
+++ b/solution.py
@@ -168,7 +168,7 @@
             out_specs=jax.tree.map(lambda o: vmem, out),
             scratch_shapes=scratch,
             compiler_params=pltpu.CompilerParams(vmem_limit_bytes=16 << 20),
-            cost_estimate=pl.CostEstimate(flops=flops, bytes_accessed=1 << 20, transcendentals=0),
+            cost_estimate=pl.CostEstimate(flops=flops, bytes_accessed=(1 << 20) if flops else 0, transcendentals=0),
         )(place, *args)
 
     def square(v, d):
@@ -184,7 +184,7 @@
         n = len(v) // 2 * heads
         out = (struct(4 * half, n, F32),) + tuple(struct(half, count * n, BF16) for _, count in parts)
         kernel = functools.partial(term_kernel, tuple(first for first, _ in parts))
-        return call(kernel, out, [], n << 20, turned, *v)
+        return call(kernel, out, [], 0, turned, *v)
 
     def plus(v, came):
         return (v + came.astype(F32)).astype(BF16)
@@ -198,7 +198,7 @@
         return call(
             functools.partial(back_kernel, base, ranks),
             (struct(2 * keys, n, BF16), struct(2 * keys, n, F32)),
-            [pltpu.VMEM((n, 4 * heads), BF16)], len(ranks) * (3 << 28),
+            [pltpu.VMEM((n, 4 * heads), BF16)], len(ranks) * (3 << 29),
             residual_grad, res_other, v0, vx, vy, vd, v0_other, vx_other, vy_other, vd_other, chosen, *weights,
         )
 
@@ -212,17 +212,18 @@
     w_inner, in_other = phase((w_own, in_other))
     turned = call(turn_kernel, jax.ShapeDtypeStruct((2, 4 * half, tokens), BF16), [], 0, layer_input, in_other)
     term0, send0 = term((v0, v0_other), (0, 4))
-    got = phase((outer(w_own), inner(w_inner), square(v0, 1), square(v0, 2), turned, term0, send0,
-                 res_other))
-    w_beside, w_mid, vx, vy, turned, term0, send0, res_other = got
+    w_beside = outer(w_own)
+    got = phase((inner(w_inner), square(v0, 1), square(v0, 2), turned, term0, send0, res_other))
+    w_mid, vx, vy, turned, term0, send0, res_other = got
 
     vx_other, vy_other = core_swap(vx), core_swap(vy)
     term1, send1, near1 = term((vx, vy, vx_other, vy_other), (0, 2), (2, 1))
     key = owner[:, 0] * keys + key_row
     key_both = jnp.concatenate([key, core_swap(key)])[None, :]
     chosen = call(choose_kernel, struct(4 * keys, 2 * tokens, BF16), [], 0, key_both)
-    got = phase((outer(jnp.where(is_end, send0, w_mid)), inner(w_beside), square(v0, 3), term1, send1, near1, chosen))
-    i0, w_end, vd, term1, send1, near1, chosen = got
+    i0 = outer(jnp.where(is_end, send0, w_mid))
+    got = phase((inner(w_beside), square(v0, 3), term1, send1, near1, chosen))
+    w_end, vd, term1, send1, near1, chosen = got
     w_third = i0
 
     vd_other, sums0 = phase((core_swap(vd), far_plus(term0, i0)))

time: 99 us -> 95.5 us (0.965)
  waiting for transfers between devices: 42.8 us -> 37.3 us
  starting transfers between devices: 31.8 us -> 33.9 us
    ppermute x6, waiting for transfers between devices: 35.7 us -> 30.7 us  [outer(): return lax.ppermute(v, 'fsdp', [(0, 1), (1, 0), (2, 3), (3, 2)])]
    ppermute x6, starting transfers between devices: 18 us -> 20.2 us  [outer(): return lax.ppermute(v, 'fsdp', [(0, 1), (1, 0), (2, 3), (3, 2)])]
  transfers between devices with their start and end apart: 26 -> 26, of which waited for: 8 -> 8; matrix products, arithmetic and copies ran while one was open for 3% -> 3% of each run, Pallas kernels for 17% -> 18%
where the time goes in v6:
time: 95.5 us; the launch traced here: 95.1 us
  waiting for transfers between devices  37.3 us (39%)
  starting transfers between devices  33.9 us (35%)
  Pallas kernels  18.6 us (19%)
  other arithmetic  2.8 us (3%)
  local copies, waits for them, and re-layouts  1.47 us (2%)
  between operations  1.01 us (1%)
    ppermute x6, waiting for transfers between devices, outer(): return lax.ppermute(v, 'fsdp', [(0, 1), (1, 0), (2, 3), (3, 2)])  30.7 us
    ppermute x6, starting transfers between devices, outer(): return lax.ppermute(v, 'fsdp', [(0, 1), (1, 0), (2, 3), (3, 2)])  20.2 us
    pallas_call x9, Pallas kernels, call(): pl.pallas_call(kernel, out_shape=out, in_specs=[smem] + [vmem] * len(args...  18.6 us
    ppermute x3, starting transfers between devices, square(): return lax.ppermute(v, 'tp', [(i, i ^ d) for i in range(4)])  6.77 us
    ppermute x3, waiting for transfers between devices, square(): return lax.ppermute(v, 'tp', [(i, i ^ d) for i in range(4)])  5.38 us
    ppermute x5, starting transfers between devices, inner(): return lax.ppermute(v, 'fsdp', [(1, 2), (2, 1)])  3.41 us
    ppermute x11, starting transfers between devices, core_swap(): return lax.ppermute(v, 'dp', [(0, 1), (1, 0)])  2.39 us
  transfers between devices with their start and end apart: 26, of which 8 were waited for; matrix products, arithmetic and copies ran while one was open for 3% of the time, Pallas kernels for 18%

profile of v6, /device:TPU:0, one launch (start us, length us, event | category | flops | bytes accessed | tf_op | source)
XLA Modules:
  0.0 95.1 jit_solution(11059704679879351302)
XLA Ops:
  0.6 0.0 copy-start
  0.7 0.1 stack.57.place
  0.8 0.5 collective-permute-start.4
  1.3 0.1 collective-permute-start
  1.4 0.4 collective-permute-start.8
  1.8 2.6 %collective-permute-start.7 = (bf16[512,512]{1,0:T(8,128)(2,1)}, bf16[512,512]{1,0:T(8,128)(2,1)S(1)}, u32[]{:S(2)}, u32[]{:S(2)}) collective-permute-start(bf16[512,512]{1,0:T(8,128)(2,1)} %refs_2_.1), channel_id=1, source_target_pairs={{0,2},{1,3},{2,0},{3,1},{4,6},{5,7},{6,4},{7,5},{8,10},{9,11},{10,... | collective-permute-start | bytes 1572872 | tf_op jit(solution)/shard_map/ppermute | solution.py:175
  4.4 1.5 %collective-permute-start.6 = (bf16[512,512]{1,0:T(8,128)(2,1)}, bf16[512,512]{1,0:T(8,128)(2,1)S(1)}, u32[]{:S(2)}, u32[]{:S(2)}) collective-permute-start(bf16[512,512]{1,0:T(8,128)(2,1)} %refs_2_.1), channel_id=1, source_target_pairs={{0,1},{1,0},{2,3},{3,2},{4,5},{5,4},{6,7},{7,6},{8,9},{9,8},{10,11... | collective-permute-start | bytes 1572872 | tf_op jit(solution)/shard_map/ppermute | solution.py:175
  5.9 0.1 constant_dynamic-slice_fusion.refs_11_
  6.0 2.1 %collective-permute-start.1 = (bf16[128,2048]{1,0:T(8,128)(2,1)S(1)}, bf16[128,2048]{1,0:T(8,128)(2,1)S(1)}, u32[]{:S(2)}, u32[]{:S(2)}) collective-permute-start(bf16[128,2048]{1,0:T(8,128)(2,1)S(1)} %constant_dynamic-slice_fusion.refs_11_), channel_id=1, source_target_pairs={{0,4},{4,0},{8,12},{12,8},{1,5},{5,1},{9,13},{13,9},{2,6},{6,2},{1... | collective-permute-start | bytes 1572872 | tf_op jit(solution)/shard_map/ppermute | solution.py:144
  8.1 0.0 collective-permute-done.4.other
  8.1 0.7 collective-permute-start.5
  8.8 0.7 broadcast_multiply_fusion
  9.5 0.7 add.56
  10.1 1.2 %copy-done.3 = bf16[512,1024]{1,0:T(8,128)(2,1)S(1)} copy-done((bf16[512,1024]{1,0:T(8,128)(2,1)S(1)}, bf16[512,1024]{1,0:T(8,128)(2,1)}, u32[]{:S(2)}) %copy-start.3) | copy-done | bytes 1048600
  11.4 1.6 %shard_map.77.turned = bf16[2,512,512]{2,1,0:T(8,128)(2,1)S(1)} custom-call(s32[15]{0:T(128)S(1)} %stack.57.place, bf16[512,1024]{1,0:T(8,128)(2,1)S(1)} %copy-done.3, bf16[512,1024]{1,0:T(8,128)(2,1)} %collective-permute-done.4.other), custom_call_target="tpu_custom_call" | custom-call | tf_op jit(solution)/shard_map/pallas_call | solution.py:164
  13.0 1.2 %shard_map.78 = (f32[512,512]{1,0:T(8,128)S(1)}, bf16[128,2048]{1,0:T(8,128)(2,1)S(1)}) custom-call(s32[15]{0:T(128)S(1)} %stack.57.place, bf16[2,512,512]{2,1,0:T(8,128)(2,1)S(1)} %shard_map.77.turned, bf16[512,512]{1,0:T(8,128)(2,1)S(1)} %copy-done.1, bf16[512,512]{1,0:T(8,128)(2,1)S(1)} %collective-permute-done.refs_1_.refs_6_), custom_call_target="tpu_custom_call" | custom-call | tf_op jit(solution)/shard_map/pallas_call | solution.py:164
  14.2 2.9 %collective-permute-done.7.refs_1_.refs_4_ = bf16[512,512]{1,0:T(8,128)(2,1)S(1)} collective-permute-done((bf16[512,512]{1,0:T(8,128)(2,1)}, bf16[512,512]{1,0:T(8,128)(2,1)S(1)}, u32[]{:S(2)}, u32[]{:S(2)}) %collective-permute-start.7) | collective-permute-done | bytes 524320 | tf_op jit(solution)/shard_map/ppermute | solution.py:175
  17.1 2.7 %collective-permute-start.3 = (bf16[512,512]{1,0:T(8,128)(2,1)S(1)}, bf16[512,512]{1,0:T(8,128)(2,1)S(1)}, u32[]{:S(2)}, u32[]{:S(2)}) collective-permute-start(bf16[512,512]{1,0:T(8,128)(2,1)S(1)} %copy-done.1), channel_id=1, source_target_pairs={{0,3},{1,2},{2,1},{3,0},{4,7},{5,6},{6,5},{7,4},{8,11},{9,10},{10,... | collective-permute-start | bytes 1572872 | tf_op jit(solution)/shard_map/ppermute | solution.py:175
  19.8 0.7 collective-permute-done.1.refs_12_
  20.5 0.7 collective-permute-start.2
  21.2 0.0 collective-permute-done.8.refs_1_
  21.2 0.1 collective-permute-start.9
  21.3 0.5 collective-permute-start.10
  21.8 0.1 broadcast_select_fusion
  21.9 0.0 collective-permute-done.11
  21.9 4.6 %collective-permute-start.14 = (bf16[128,2048]{1,0:T(8,128)(2,1)S(1)}, bf16[128,2048]{1,0:T(8,128)(2,1)S(1)}, u32[]{:S(2)}, u32[]{:S(2)}) collective-permute-start(bf16[128,2048]{1,0:T(8,128)(2,1)S(1)} %broadcast_select_fusion), channel_id=1, source_target_pairs={{0,4},{4,0},{8,12},{12,8},{1,5},{5,1},{9,13},{13,9},{2,6},{6,2},{1... | collective-permute-start | bytes 1572872 | tf_op jit(solution)/shard_map/ppermute | solution.py:144
  26.5 0.9 shard_map.80.refs_10_
  27.4 1.8 %shard_map.79 = (f32[512,1024]{1,0:T(8,128)S(1)}, bf16[128,2048]{1,0:T(8,128)(2,1)S(1)}, bf16[128,1024]{1,0:T(8,128)(2,1)S(1)}) custom-call(s32[15]{0:T(128)S(1)} %stack.57.place, bf16[2,512,512]{2,1,0:T(8,128)(2,1)S(1)} %shard_map.77.turned, bf16[512,512]{1,0:T(8,128)(2,1)S(1)} %collective-permute-done.6.refs_0_.refs_3_, ...), custom_call_target="tpu_custom_call" | custom-call | tf_op jit(solution)/shard_map/pallas_call | solution.py:164
  29.2 0.0 copy-start.2
  29.2 2.5 %collective-permute-done.3.refs_0_.refs_5_ = bf16[512,512]{1,0:T(8,128)(2,1)S(1)} collective-permute-done((bf16[512,512]{1,0:T(8,128)(2,1)S(1)}, bf16[512,512]{1,0:T(8,128)(2,1)S(1)}, u32[]{:S(2)}, u32[]{:S(2)}) %collective-permute-start.3) | collective-permute-done | bytes 524320 | tf_op jit(solution)/shard_map/ppermute | solution.py:175
  31.7 0.1 broadcast_select_fusion.1
  31.8 6.0 %collective-permute-start.12 = (bf16[128,2048]{1,0:T(8,128)(2,1)S(1)}, bf16[128,2048]{1,0:T(8,128)(2,1)S(1)}, u32[]{:S(2)}, u32[]{:S(2)}) collective-permute-start(bf16[128,2048]{1,0:T(8,128)(2,1)S(1)} %broadcast_select_fusion.1), channel_id=1, source_target_pairs={{0,4},{4,0},{8,12},{12,8},{1,5},{5,1},{9,13},{13,9},{2,6},{6,2},{1... | collective-permute-start | bytes 1572872 | tf_op jit(solution)/shard_map/ppermute | solution.py:144
  37.7 0.9 collective-permute-done.14.refs_14_
  38.6 0.1 add_convert_fusion.9
  38.8 0.7 collective-permute-start.15
  39.5 4.8 %shard_map.82 = (bf16[512,384]{1,0:T(8,128)(2,1)S(1)}, f32[512,384]{1,0:T(8,128)S(1)}) custom-call(s32[15]{0:T(128)S(1)} %stack.57.place, bf16[512,1024]{1,0:T(8,128)(2,1)S(1)} %copy-done.2, bf16[512,1024]{1,0:T(8,128)(2,1)} %collective-permute-done.8.refs_1_, bf16[512,512]{1,0:T(8,128)(2,1)S(1)} %copy-done.1, ...), custom_call_target="tpu_custom_call" | custom-call | flops 4831838208 | bytes 1048576 | tf_op jit(solution)/shard_map/pallas_call | solution.py:164
  44.3 1.2 %shard_map.81 = (f32[512,512]{1,0:T(8,128)S(1)}, bf16[128,1024]{1,0:T(8,128)(2,1)S(1)}, bf16[128,512]{1,0:T(8,128)(2,1)S(1)}) custom-call(s32[15]{0:T(128)S(1)} %stack.57.place, bf16[2,512,512]{2,1,0:T(8,128)(2,1)S(1)} %shard_map.77.turned, bf16[512,512]{1,0:T(8,128)(2,1)S(1)} %collective-permute-done.3.refs_0_.refs_5_, ...), custom_call_target="tpu_custom_call" | custom-call | tf_op jit(solution)/shard_map/pallas_call | solution.py:164
  45.6 0.1 maximum_select_fusion.3
  45.7 4.6 %collective-permute-done.12.refs_12_ = bf16[128,2048]{1,0:T(8,128)(2,1)S(1)} collective-permute-done((bf16[128,2048]{1,0:T(8,128)(2,1)S(1)}, bf16[128,2048]{1,0:T(8,128)(2,1)S(1)}, u32[]{:S(2)}, u32[]{:S(2)}) %collective-permute-start.12) | collective-permute-done | bytes 524320 | tf_op jit(solution)/shard_map/ppermute | solution.py:144
  50.3 1.7 %collective-permute-start.18 = (bf16[128,1024]{1,0:T(8,128)(2,1)S(1)}, bf16[128,1024]{1,0:T(8,128)(2,1)S(1)}, u32[]{:S(2)}, u32[]{:S(2)}) collective-permute-start(bf16[128,1024]{1,0:T(8,128)(2,1)S(1)} %maximum_select_fusion.3), channel_id=1, source_target_pairs={{0,4},{4,0},{8,12},{12,8},{1,5},{5,1},{9,13},{13,9},{2,6},{6,2},{1... | collective-permute-start | bytes 786440 | tf_op jit(solution)/shard_map/ppermute | solution.py:144
  52.1 0.1 add_convert_fusion.3
  52.3 0.7 collective-permute-start.17
  53.0 3.2 %shard_map.83 = (bf16[512,128]{1,0:T(8,128)(2,1)S(1)}, f32[512,128]{1,0:T(8,128)S(1)}) custom-call(s32[15]{0:T(128)S(1)} %stack.57.place, bf16[512,1024]{1,0:T(8,128)(2,1)S(1)} %copy-done.2, bf16[512,1024]{1,0:T(8,128)(2,1)} %collective-permute-done.8.refs_1_, bf16[512,512]{1,0:T(8,128)(2,1)S(1)} %copy-done.1, ...), custom_call_target="tpu_custom_call" | custom-call | flops 1610612736 | bytes 1048576 | tf_op jit(solution)/shard_map/pallas_call | solution.py:164
  56.1 0.1 maximum_select_fusion.1
  56.3 3.1 %collective-permute-start.16 = (bf16[512,512]{1,0:T(8,128)(2,1)S(1)}, bf16[512,512]{1,0:T(8,128)(2,1)S(1)}, u32[]{:S(2)}, u32[]{:S(2)}) collective-permute-start(bf16[512,512]{1,0:T(8,128)(2,1)S(1)} %maximum_select_fusion.1), channel_id=1, source_target_pairs={{0,4},{4,0},{8,12},{12,8},{1,5},{5,1},{9,13},{13,9},{2,6},{6,2},{1... | collective-permute-start | bytes 1572872 | tf_op jit(solution)/shard_map/ppermute | solution.py:144
  59.4 0.1 add_convert_fusion.6
  59.5 0.7 collective-permute-start.19
  60.2 0.1 maximum_select_fusion
  60.4 10.5 %collective-permute-done.16 = bf16[512,512]{1,0:T(8,128)(2,1)S(1)} collective-permute-done((bf16[512,512]{1,0:T(8,128)(2,1)S(1)}, bf16[512,512]{1,0:T(8,128)(2,1)S(1)}, u32[]{:S(2)}, u32[]{:S(2)}) %collective-permute-start.16) | collective-permute-done | bytes 524320 | tf_op jit(solution)/shard_map/ppermute | solution.py:144
  70.9 0.1 add_convert_fusion.4
  71.0 0.1 add_convert_fusion.1
  71.1 0.1 convert_add_fusion.3
  71.2 0.1 pad_maximum_fusion.mine
  71.2 0.1 collective-permute-start.20
  71.3 0.1 maximum_select_fusion.2
  71.4 2.7 %collective-permute-start.21 = (bf16[128,1536]{1,0:T(8,128)(2,1)S(1)}, bf16[128,1536]{1,0:T(8,128)(2,1)S(1)}, u32[]{:S(2)}, u32[]{:S(2)}) collective-permute-start(bf16[128,1536]{1,0:T(8,128)(2,1)S(1)} %maximum_select_fusion.2), channel_id=1, source_target_pairs={{0,4},{4,0},{8,12},{12,8},{1,5},{5,1},{9,13},{13,9},{2,6},{6,2},{1... | collective-permute-start | bytes 1179656 | tf_op jit(solution)/shard_map/ppermute | solution.py:144
  74.2 0.1 add_convert_fusion
  74.3 1.1 %collective-permute-start.24 = (bf16[256,512]{1,0:T(8,128)(2,1)S(1)}, bf16[256,512]{1,0:T(8,128)(2,1)S(1)}, u32[]{:S(2)}, u32[]{:S(2)}) collective-permute-start(bf16[256,512]{1,0:T(8,128)(2,1)S(1)} %get-tuple-element.124), channel_id=1, source_target_pairs={{0,8},{4,12},{8,0},{12,4},{1,9},{5,13},{9,1},{13,5},{2,10},{6,14},... | collective-permute-start | bytes 786440 | tf_op jit(solution)/shard_map/ppermute | solution.py:178
  75.4 0.2 collective-permute-start.23
  75.6 13.9 %collective-permute-done.21.last = bf16[128,1536]{1,0:T(8,128)(2,1)S(1)} collective-permute-done((bf16[128,1536]{1,0:T(8,128)(2,1)S(1)}, bf16[128,1536]{1,0:T(8,128)(2,1)S(1)}, u32[]{:S(2)}, u32[]{:S(2)}) %collective-permute-start.21) | collective-permute-done | bytes 393248 | tf_op jit(solution)/shard_map/ppermute | solution.py:144
  89.5 0.5 collective-permute-start.25
  90.1 1.2 %collective-permute-done.22.last_pair = bf16[128,1536]{1,0:T(8,128)(2,1)S(1)} collective-permute-done((bf16[128,1536]{1,0:T(8,128)(2,1)S(1)}, bf16[128,1536]{1,0:T(8,128)(2,1)S(1)}, u32[]{:S(2)}, u32[]{:S(2)}) %collective-permute-start.22) | collective-permute-done | bytes 393248 | tf_op jit(solution)/shard_map/ppermute | solution.py:141
  91.3 2.0 %shard_map.84 = (f32[256,2048]{1,0:T(8,128)}, f32[8,128]{1,0:T(8,128)S(1)}) custom-call(s32[15]{0:T(128)S(1)} %stack.57.place, f32[128,2048]{1,0:T(8,128)S(1)} %pad_maximum_fusion.mine, f32[128,2048]{1,0:T(8,128)S(1)} %collective-permute-done.20.pair, bf16[128,1536]{1,0:T(8,128)(2,1)S(1)} %collective-permute-done.21.last, ...), custom_call_target="tpu_custom_call" | custom-call | tf_op jit(solution)/shard_map/pallas_call | solution.py:164
  93.3 1.8 %shard_map.85 = f32[256,1024]{1,0:T(8,128)} custom-call(s32[15]{0:T(128)S(1)} %stack.57.place, f32[8,128]{1,0:T(8,128)S(1)} %get-tuple-element.117.before, f32[256,512]{1,0:T(8,128)S(1)} %get-tuple-element.125.mine, f32[256,512]{1,0:T(8,128)S(1)} %collective-permute-done.23.pair, bf16[256,512]{1,0:T(8,128)(2,1)S(1)} %collective-permute-done.24.last, ...), custom_call_target="tpu_custom_call" | custom-call | tf_op jit(solution)/shard_map/pallas_call | solution.py:164
  (28 shorter events, 0.2 us)
Async XLA Ops:
  0.6 5.3 %copy-start = (bf16[256,2048]{1,0:T(8,128)(2,1)S(1)}, bf16[256,2048]{1,0:T(8,128)(2,1)}, u32[]{:S(2)}) copy-start(bf16[256,2048]{1,0:T(8,128)(2,1)} %param.9) | copy-start | bytes 3145732
  0.8 7.3 %collective-permute-start.4 = (bf16[512,1024]{1,0:T(8,128)(2,1)}, bf16[512,1024]{1,0:T(8,128)(2,1)}, u32[]{:S(2)}, u32[]{:S(2)}) collective-permute-start(bf16[512,1024]{1,0:T(8,128)(2,1)} %mine), channel_id=1, source_target_pairs={{0,16},{16,0},{1,17},{17,1},{2,18},{18,2},{3,19},{19,3},{4,20},{20... | collective-permute-start | bytes 3145736 | tf_op jit(solution)/shard_map/ppermute | solution.py:141
  1.3 4.6 %collective-permute-start = (bf16[512,512]{1,0:T(8,128)(2,1)}, bf16[512,512]{1,0:T(8,128)(2,1)S(1)}, u32[]{:S(2)}, u32[]{:S(2)}) collective-permute-start(bf16[512,512]{1,0:T(8,128)(2,1)} %refs_2_.1), channel_id=1, source_target_pairs={{0,16},{16,0},{1,17},{17,1},{2,18},{18,2},{3,19},{19,3},{4,20},{20... | collective-permute-start | bytes 1572872 | tf_op jit(solution)/shard_map/ppermute | solution.py:141
  1.4 19.9 %collective-permute-start.8 = (bf16[512,1024]{1,0:T(8,128)(2,1)}, bf16[512,1024]{1,0:T(8,128)(2,1)}, u32[]{:S(2)}, u32[]{:S(2)}) collective-permute-start(bf16[512,1024]{1,0:T(8,128)(2,1)} %refs_0_.2), channel_id=1, source_target_pairs={{0,16},{16,0},{1,17},{17,1},{2,18},{18,2},{3,19},{19,3},{4,20},{20... | collective-permute-start | bytes 3145736 | tf_op jit(solution)/shard_map/ppermute | solution.py:141
  1.8 15.3 %collective-permute-start.7 = (bf16[512,512]{1,0:T(8,128)(2,1)}, bf16[512,512]{1,0:T(8,128)(2,1)S(1)}, u32[]{:S(2)}, u32[]{:S(2)}) collective-permute-start(bf16[512,512]{1,0:T(8,128)(2,1)} %refs_2_.1), channel_id=1, source_target_pairs={{0,2},{1,3},{2,0},{3,1},{4,6},{5,7},{6,4},{7,5},{8,10},{9,11},{10,... | collective-permute-start | bytes 1572872 | tf_op jit(solution)/shard_map/ppermute | solution.py:175
  4.4 15.4 %collective-permute-start.6 = (bf16[512,512]{1,0:T(8,128)(2,1)}, bf16[512,512]{1,0:T(8,128)(2,1)S(1)}, u32[]{:S(2)}, u32[]{:S(2)}) collective-permute-start(bf16[512,512]{1,0:T(8,128)(2,1)} %refs_2_.1), channel_id=1, source_target_pairs={{0,1},{1,0},{2,3},{3,2},{4,5},{5,4},{6,7},{7,6},{8,9},{9,8},{10,11... | collective-permute-start | bytes 1572872 | tf_op jit(solution)/shard_map/ppermute | solution.py:175
  5.9 7.1 %copy-start.1 = (bf16[512,512]{1,0:T(8,128)(2,1)S(1)}, bf16[512,512]{1,0:T(8,128)(2,1)}, u32[]{:S(2)}) copy-start(bf16[512,512]{1,0:T(8,128)(2,1)} %refs_2_.1) | copy-start | bytes 1572868
  6.0 14.5 %collective-permute-start.1 = (bf16[128,2048]{1,0:T(8,128)(2,1)S(1)}, bf16[128,2048]{1,0:T(8,128)(2,1)S(1)}, u32[]{:S(2)}, u32[]{:S(2)}) collective-permute-start(bf16[128,2048]{1,0:T(8,128)(2,1)S(1)} %constant_dynamic-slice_fusion.refs_11_), channel_id=1, source_target_pairs={{0,4},{4,0},{8,12},{12,8},{1,5},{5,1},{9,13},{13,9},{2,6},{6,2},{1... | collective-permute-start | bytes 1572872 | tf_op jit(solution)/shard_map/ppermute | solution.py:144
  8.1 13.1 %collective-permute-start.5 = (bf16[128,2048]{1,0:T(8,128)(2,1)S(1)}, bf16[128,2048]{1,0:T(8,128)(2,1)S(1)}, u32[]{:S(2)}, u32[]{:S(2)}) collective-permute-start(bf16[128,2048]{1,0:T(8,128)(2,1)S(1)} %constant_dynamic-slice_fusion.refs_11_), channel_id=1, source_target_pairs={{4,8},{8,4},{5,9},{9,5},{6,10},{10,6},{7,11},{11,7},{20,24},{24,20... | collective-permute-start | bytes 1572872 | tf_op jit(solution)/shard_map/ppermute | solution.py:153
  10.1 1.2 %copy-start.3 = (bf16[512,1024]{1,0:T(8,128)(2,1)S(1)}, bf16[512,1024]{1,0:T(8,128)(2,1)}, u32[]{:S(2)}) copy-start(bf16[512,1024]{1,0:T(8,128)(2,1)} %mine) | copy-start | bytes 3145732
  17.1 14.6 %collective-permute-start.3 = (bf16[512,512]{1,0:T(8,128)(2,1)S(1)}, bf16[512,512]{1,0:T(8,128)(2,1)S(1)}, u32[]{:S(2)}, u32[]{:S(2)}) collective-permute-start(bf16[512,512]{1,0:T(8,128)(2,1)S(1)} %copy-done.1), channel_id=1, source_target_pairs={{0,3},{1,2},{2,1},{3,0},{4,7},{5,6},{6,5},{7,4},{8,11},{9,10},{10,... | collective-permute-start | bytes 1572872 | tf_op jit(solution)/shard_map/ppermute | solution.py:175
  19.8 2.1 %collective-permute-start.11 = (s32[512]{0:T(512)S(1)}, s32[512]{0:T(512)S(1)}, u32[]{:S(2)}, u32[]{:S(2)}) collective-permute-start(s32[512]{0:T(512)S(1)} %add.56), channel_id=1, source_target_pairs={{0,16},{16,0},{1,17},{17,1},{2,18},{18,2},{3,19},{19,3},{4,20},{20... | collective-permute-start | bytes 6152 | tf_op jit(solution)/shard_map/ppermute | solution.py:141
  20.5 11.2 %collective-permute-start.2 = (bf16[128,2048]{1,0:T(8,128)(2,1)S(1)}, bf16[128,2048]{1,0:T(8,128)(2,1)S(1)}, u32[]{:S(2)}, u32[]{:S(2)}) collective-permute-start(bf16[128,2048]{1,0:T(8,128)(2,1)S(1)} %collective-permute-done.1.refs_12_), channel_id=1, source_target_pairs={{4,8},{8,4},{5,9},{9,5},{6,10},{10,6},{7,11},{11,7},{20,24},{24,20... | collective-permute-start | bytes 1572872 | tf_op jit(solution)/shard_map/ppermute | solution.py:153
  21.2 6.2 %collective-permute-start.9 = (bf16[512,512]{1,0:T(8,128)(2,1)S(1)}, bf16[512,512]{1,0:T(8,128)(2,1)S(1)}, u32[]{:S(2)}, u32[]{:S(2)}) collective-permute-start(bf16[512,512]{1,0:T(8,128)(2,1)S(1)} %collective-permute-done.6.refs_0_.refs_3_), channel_id=1, source_target_pairs={{0,16},{16,0},{1,17},{17,1},{2,18},{18,2},{3,19},{19,3},{4,20},{20... | collective-permute-start | bytes 1572872 | tf_op jit(solution)/shard_map/ppermute | solution.py:141
  21.3 6.1 %collective-permute-start.10 = (bf16[512,512]{1,0:T(8,128)(2,1)S(1)}, bf16[512,512]{1,0:T(8,128)(2,1)S(1)}, u32[]{:S(2)}, u32[]{:S(2)}) collective-permute-start(bf16[512,512]{1,0:T(8,128)(2,1)S(1)} %collective-permute-done.7.refs_1_.refs_4_), channel_id=1, source_target_pairs={{0,16},{16,0},{1,17},{17,1},{2,18},{18,2},{3,19},{19,3},{4,20},{20... | collective-permute-start | bytes 1572872 | tf_op jit(solution)/shard_map/ppermute | solution.py:141
  21.9 16.8 %collective-permute-start.14 = (bf16[128,2048]{1,0:T(8,128)(2,1)S(1)}, bf16[128,2048]{1,0:T(8,128)(2,1)S(1)}, u32[]{:S(2)}, u32[]{:S(2)}) collective-permute-start(bf16[128,2048]{1,0:T(8,128)(2,1)S(1)} %broadcast_select_fusion), channel_id=1, source_target_pairs={{0,4},{4,0},{8,12},{12,8},{1,5},{5,1},{9,13},{13,9},{2,6},{6,2},{1... | collective-permute-start | bytes 1572872 | tf_op jit(solution)/shard_map/ppermute | solution.py:144
  29.2 10.2 %copy-start.2 = (bf16[512,1024]{1,0:T(8,128)(2,1)S(1)}, bf16[512,1024]{1,0:T(8,128)(2,1)}, u32[]{:S(2)}) copy-start(bf16[512,1024]{1,0:T(8,128)(2,1)} %refs_0_.2) | copy-start | bytes 3145732
  31.7 7.1 %collective-permute-start.13 = (bf16[512,512]{1,0:T(8,128)(2,1)S(1)}, bf16[512,512]{1,0:T(8,128)(2,1)S(1)}, u32[]{:S(2)}, u32[]{:S(2)}) collective-permute-start(bf16[512,512]{1,0:T(8,128)(2,1)S(1)} %collective-permute-done.3.refs_0_.refs_5_), channel_id=1, source_target_pairs={{0,16},{16,0},{1,17},{17,1},{2,18},{18,2},{3,19},{19,3},{4,20},{20... | collective-permute-start | bytes 1572872 | tf_op jit(solution)/shard_map/ppermute | solution.py:141
  31.8 18.6 %collective-permute-start.12 = (bf16[128,2048]{1,0:T(8,128)(2,1)S(1)}, bf16[128,2048]{1,0:T(8,128)(2,1)S(1)}, u32[]{:S(2)}, u32[]{:S(2)}) collective-permute-start(bf16[128,2048]{1,0:T(8,128)(2,1)S(1)} %broadcast_select_fusion.1), channel_id=1, source_target_pairs={{0,4},{4,0},{8,12},{12,8},{1,5},{5,1},{9,13},{13,9},{2,6},{6,2},{1... | collective-permute-start | bytes 1572872 | tf_op jit(solution)/shard_map/ppermute | solution.py:144
  38.8 6.8 %collective-permute-start.15 = (bf16[128,1024]{1,0:T(8,128)(2,1)S(1)}, bf16[128,1024]{1,0:T(8,128)(2,1)S(1)}, u32[]{:S(2)}, u32[]{:S(2)}) collective-permute-start(bf16[128,1024]{1,0:T(8,128)(2,1)S(1)} %pad_maximum_fusion.2), channel_id=1, source_target_pairs={{4,8},{8,4},{5,9},{9,5},{6,10},{10,6},{7,11},{11,7},{20,24},{24,20... | collective-permute-start | bytes 786440 | tf_op jit(solution)/shard_map/ppermute | solution.py:153
  50.3 9.1 %collective-permute-start.18 = (bf16[128,1024]{1,0:T(8,128)(2,1)S(1)}, bf16[128,1024]{1,0:T(8,128)(2,1)S(1)}, u32[]{:S(2)}, u32[]{:S(2)}) collective-permute-start(bf16[128,1024]{1,0:T(8,128)(2,1)S(1)} %maximum_select_fusion.3), channel_id=1, source_target_pairs={{0,4},{4,0},{8,12},{12,8},{1,5},{5,1},{9,13},{13,9},{2,6},{6,2},{1... | collective-permute-start | bytes 786440 | tf_op jit(solution)/shard_map/ppermute | solution.py:144
  52.3 8.1 %collective-permute-start.17 = (bf16[128,2048]{1,0:T(8,128)(2,1)S(1)}, bf16[128,2048]{1,0:T(8,128)(2,1)S(1)}, u32[]{:S(2)}, u32[]{:S(2)}) collective-permute-start(bf16[128,2048]{1,0:T(8,128)(2,1)S(1)} %pad_maximum_fusion.1), channel_id=1, source_target_pairs={{4,8},{8,4},{5,9},{9,5},{6,10},{10,6},{7,11},{11,7},{20,24},{24,20... | collective-permute-start | bytes 1572872 | tf_op jit(solution)/shard_map/ppermute | solution.py:153
  56.3 14.6 %collective-permute-start.16 = (bf16[512,512]{1,0:T(8,128)(2,1)S(1)}, bf16[512,512]{1,0:T(8,128)(2,1)S(1)}, u32[]{:S(2)}, u32[]{:S(2)}) collective-permute-start(bf16[512,512]{1,0:T(8,128)(2,1)S(1)} %maximum_select_fusion.1), channel_id=1, source_target_pairs={{0,4},{4,0},{8,12},{12,8},{1,5},{5,1},{9,13},{13,9},{2,6},{6,2},{1... | collective-permute-start | bytes 1572872 | tf_op jit(solution)/shard_map/ppermute | solution.py:144
  59.5 0.8 collective-permute-start.19
  71.2 20.0 %collective-permute-start.20 = (f32[128,2048]{1,0:T(8,128)S(1)}, f32[128,2048]{1,0:T(8,128)S(1)}, u32[]{:S(2)}, u32[]{:S(2)}) collective-permute-start(f32[128,2048]{1,0:T(8,128)S(1)} %pad_maximum_fusion.mine), channel_id=1, source_target_pairs={{0,16},{16,0},{1,17},{17,1},{2,18},{18,2},{3,19},{19,3},{4,20},{20... | collective-permute-start | bytes 3145736 | tf_op jit(solution)/shard_map/ppermute | solution.py:141
  71.4 18.1 %collective-permute-start.21 = (bf16[128,1536]{1,0:T(8,128)(2,1)S(1)}, bf16[128,1536]{1,0:T(8,128)(2,1)S(1)}, u32[]{:S(2)}, u32[]{:S(2)}) collective-permute-start(bf16[128,1536]{1,0:T(8,128)(2,1)S(1)} %maximum_select_fusion.2), channel_id=1, source_target_pairs={{0,4},{4,0},{8,12},{12,8},{1,5},{5,1},{9,13},{13,9},{2,6},{6,2},{1... | collective-permute-start | bytes 1179656 | tf_op jit(solution)/shard_map/ppermute | solution.py:144
  74.3 15.2 %collective-permute-start.24 = (bf16[256,512]{1,0:T(8,128)(2,1)S(1)}, bf16[256,512]{1,0:T(8,128)(2,1)S(1)}, u32[]{:S(2)}, u32[]{:S(2)}) collective-permute-start(bf16[256,512]{1,0:T(8,128)(2,1)S(1)} %get-tuple-element.124), channel_id=1, source_target_pairs={{0,8},{4,12},{8,0},{12,4},{1,9},{5,13},{9,1},{13,5},{2,10},{6,14},... | collective-permute-start | bytes 786440 | tf_op jit(solution)/shard_map/ppermute | solution.py:178
  75.4 17.9 %collective-permute-start.23 = (f32[256,512]{1,0:T(8,128)S(1)}, f32[256,512]{1,0:T(8,128)S(1)}, u32[]{:S(2)}, u32[]{:S(2)}) collective-permute-start(f32[256,512]{1,0:T(8,128)S(1)} %get-tuple-element.125.mine), channel_id=1, source_target_pairs={{0,16},{16,0},{1,17},{17,1},{2,18},{18,2},{3,19},{19,3},{4,20},{20... | collective-permute-start | bytes 1572872 | tf_op jit(solution)/shard_map/ppermute | solution.py:141
  89.5 1.7 %collective-permute-start.22 = (bf16[128,1536]{1,0:T(8,128)(2,1)S(1)}, bf16[128,1536]{1,0:T(8,128)(2,1)S(1)}, u32[]{:S(2)}, u32[]{:S(2)}) collective-permute-start(bf16[128,1536]{1,0:T(8,128)(2,1)S(1)} %collective-permute-done.21.last), channel_id=1, source_target_pairs={{0,16},{16,0},{1,17},{17,1},{2,18},{18,2},{3,19},{19,3},{4,20},{20... | collective-permute-start | bytes 1179656 | tf_op jit(solution)/shard_map/ppermute | solution.py:141
  89.5 3.8 %collective-permute-start.25 = (bf16[256,512]{1,0:T(8,128)(2,1)S(1)}, bf16[256,512]{1,0:T(8,128)(2,1)S(1)}, u32[]{:S(2)}, u32[]{:S(2)}) collective-permute-start(bf16[256,512]{1,0:T(8,128)(2,1)S(1)} %collective-permute-done.24.last), channel_id=1, source_target_pairs={{0,16},{16,0},{1,17},{17,1},{2,18},{18,2},{3,19},{19,3},{4,20},{20... | collective-permute-start | bytes 786440 | tf_op jit(solution)/shard_map/ppermute | solution.py:141

commit v7 on v6

--- a/solution.py
+++ b/solution.py
@@ -72,22 +72,11 @@
         out[j * keys : (j + 1) * keys, :] = jnp.where(hit, 1.0, 0.0).astype(BF16)
 
 
-def back_kernel(base, ranks, place, *refs):
-    residuals, heads, chosen, weights, (send, keep, weight) = refs[:2], refs[2:10], refs[10], refs[11:-3], refs[-3:]
-    half, width = weights[0].shape[0], heads[0].shape[1]
-    tokens = heads[0].shape[0]
-    first = place[base]
-
-    def put(rank, ref):
-        weight[pl.ds(pl.multiple_of((place[rank] - first) * half, half), half), :] = ref[...]
-
-    for rank, ref in zip(ranks[:-1], weights):
-        put(rank, ref)
-    for here in range(2):
-        pl.when(place[9] == here)(lambda here=here: put(ranks[-1], weights[len(ranks) - 1 + here]))
-
+def back_rows(place, first, count, weight, residuals, heads, chosen, send, keep):
+    half = weight.shape[0] // count
+    tokens, width = heads[0].shape
     total = [None] * 2
-    starts = [pl.multiple_of((2 * (first + p) + place[4]) * half, half) for p in range(len(ranks))]
+    starts = [pl.multiple_of((2 * (first + p) + place[4]) * half, half) for p in range(count)]
     for side in range(2):
         acc = jnp.concatenate([residuals[side][:, pl.ds(at, half)] for at in starts], 1).astype(F32)
         for k in range(4):
@@ -103,29 +92,66 @@
     keep[...] = total[1]
 
 
-def join_weight_kernel(place, mine, pair, last, last_pair, out, done):
+def back_kernel(place, *refs):
+    residuals, heads, chosen, refs = refs[:2], refs[2:10], refs[10], refs[11:]
+    own, beside, mid, third, end, send, keep, send_mid, keep_mid, weight = refs
+    half = own.shape[0]
+    first = place[14]
+
+    def put(rank, ref):
+        weight[pl.ds(pl.multiple_of((place[rank] - first) * half, half), half), :] = ref[...]
+
+    put(5, own)
+    put(6, beside)
+    pl.when(place[9] == 0)(lambda: put(7, mid))
+    pl.when(place[9] == 1)(lambda: put(7, third))
+    back_rows(place, first, 3, weight, residuals, heads, chosen, send, keep)
+    pl.when(place[9] == 0)(
+        lambda: back_rows(place, place[8], 1, end, residuals, heads, chosen, send_mid, keep_mid)
+    )
+
+
+def back_end_kernel(place, *refs):
+    residuals, heads, chosen, (fourth, send_mid, keep_mid, send, keep) = refs[:2], refs[2:10], refs[10], refs[11:]
+
+    @pl.when(place[9] == 0)
+    def _():
+        send[...] = send_mid[...]
+        keep[...] = keep_mid[...]
+
+    pl.when(place[9] == 1)(lambda: back_rows(place, place[8], 1, fourth, residuals, heads, chosen, send, keep))
+
+
+def join_kernel(place, mine, pair, last, last_pair, key_mine, key_pair, key_last, key_last_pair,
+                out, key_out, joined, key_joined, sems):
     half, width = mine.shape[0], mine.shape[1] // 4
-    here = pl.multiple_of(place[4] * half, half)
-    there = pl.multiple_of(half - place[4] * half, half)
-    for at, kept, came in ((here, mine, last), (there, pair, last_pair)):
+    copies = []
+    for side in range(2):
+        here = place[4] == side
+        rows = pl.ds(side * half, half)
         for k in range(4):
-            start = pl.multiple_of(place[k] * width, width)
-            value = kept[:, k * width : (k + 1) * width]
+            cols = slice(k * width, (k + 1) * width)
+            value = jnp.where(here, mine[:, cols], pair[:, cols])
             if k > 0:
-                value = value + came[:, (k - 1) * width : k * width].astype(F32)
-            out[pl.ds(at, half), pl.ds(start, width)] = value
-    done[...] = jnp.zeros_like(done)
-
-
-def join_key_kernel(place, before, mine, pair, last, last_pair, out):
+                came = slice((k - 1) * width, k * width)
+                value = value + jnp.where(here, last[:, came], last_pair[:, came]).astype(F32)
+            joined[rows, pl.ds(pl.multiple_of(place[k] * width, width), width)] = value
+        copies.append(pltpu.make_async_copy(joined.at[rows], out.at[rows], sems.at[side]))
+        copies[-1].start()
+    size, high = key_mine.shape[1] // 4, key_mine.shape[0] // 2
     first = place[4] == 0
-    half = mine.shape[1] // 4
-    for p in range(4):
-        cols = slice(p * half, (p + 1) * half)
-        a = mine[:, cols] + last[:, cols].astype(F32)
-        b = pair[:, cols] + last_pair[:, cols].astype(F32)
-        out[:, 2 * p * half : (2 * p + 1) * half] = jnp.where(first, a, b)
-        out[:, (2 * p + 1) * half : (2 * p + 2) * half] = jnp.where(first, b, a)
+    for part in range(2):
+        rows = pl.ds(part * high, high)
+        for p in range(4):
+            cols = slice(p * size, (p + 1) * size)
+            a = key_mine[rows, cols] + key_last[rows, cols].astype(F32)
+            b = key_pair[rows, cols] + key_last_pair[rows, cols].astype(F32)
+            key_joined[rows, 2 * p * size : (2 * p + 1) * size] = jnp.where(first, a, b)
+            key_joined[rows, (2 * p + 1) * size : (2 * p + 2) * size] = jnp.where(first, b, a)
+        copies.append(pltpu.make_async_copy(key_joined.at[rows], key_out.at[rows], sems.at[2 + part]))
+        copies[-1].start()
+    for copy in copies:
+        copy.wait()
 
 
 def pair_body(layer_input, value_grad, residual_grad, value_weight, owner, key_row):
@@ -184,7 +210,7 @@
         n = len(v) // 2 * heads
         out = (struct(4 * half, n, F32),) + tuple(struct(half, count * n, BF16) for _, count in parts)
         kernel = functools.partial(term_kernel, tuple(first for first, _ in parts))
-        return call(kernel, out, [], 0, turned, *v)
+        return call(kernel, out, [], {1: 0, 3: 0}.get(len(v) // 2 + len(parts) - 1, 0), turned, *v)
 
     def plus(v, came):
         return (v + came.astype(F32)).astype(BF16)
@@ -193,13 +219,11 @@
         n = v.shape[1]
         return jnp.concatenate([plus(v[:half], came[:, :n]), plus(v[half : 2 * half], came[:, n : 2 * n])], 1)
 
-    def back(base, ranks, *weights):
-        n = len(ranks) * half
+    def back(kernel, parts, cost, scratch, *refs):
+        out = [struct(2 * keys, n * half, kind) for n in parts for kind in (BF16, F32)]
         return call(
-            functools.partial(back_kernel, base, ranks),
-            (struct(2 * keys, n, BF16), struct(2 * keys, n, F32)),
-            [pltpu.VMEM((n, 4 * heads), BF16)], len(ranks) * (3 << 29),
-            residual_grad, res_other, v0, vx, vy, vd, v0_other, vx_other, vy_other, vd_other, chosen, *weights,
+            kernel, out, scratch, cost, residual_grad, res_other,
+            v0, vx, vy, vd, v0_other, vx_other, vy_other, vd_other, chosen, *refs,
         )
 
     got = phase((value_grad, layer_input, residual_grad, value_weight, place, low == 1, end == 1, core * half))
@@ -210,7 +234,7 @@
     w_own = lax.dynamic_slice_in_dim(weight_rows, first_row, half, 0)
     in_other, res_other = core_swap(layer_input), core_swap(residual_grad)
     w_inner, in_other = phase((w_own, in_other))
-    turned = call(turn_kernel, jax.ShapeDtypeStruct((2, 4 * half, tokens), BF16), [], 0, layer_input, in_other)
+    turned = call(turn_kernel, jax.ShapeDtypeStruct((2, 4 * half, tokens), BF16), [], 1073741824, layer_input, in_other)
     term0, send0 = term((v0, v0_other), (0, 4))
     w_beside = outer(w_own)
     got = phase((inner(w_inner), square(v0, 1), square(v0, 2), turned, term0, send0, res_other))
@@ -231,7 +255,10 @@
     term2, send2, near2 = term((vd, vd_other), (0, 2), (2, 1))
     back0 = plus(term0[2 * half : 3 * half], b0[:, :heads])
     send2 = jnp.where(is_end, send2, jnp.concatenate([back0, back0], 1))
-    send_a, keep_a = back(14, (5, 6, 7), w_own, w_beside, w_mid, w_third)
+    send_a, keep_a, send_mid, keep_mid = back(
+        back_kernel, (3, 1), 4831838208, [pltpu.VMEM((3 * half, 4 * heads), BF16)],
+        w_own, w_beside, w_mid, w_third, w_end,
+    )
     got = phase((outer(jnp.where(is_end, send1, w_end)), b0, term1, term2, send_a, keep_a, term0, near1, near2, send2))
     i1, b0, term1, term2, send_a, keep_a, term0, near1, near2, send2 = got
     w_fourth = i1
@@ -240,7 +267,7 @@
         return jnp.where(is_low, jnp.concatenate([a, b], 1), jnp.concatenate([b, a], 1))
 
     i2 = outer(send2)
-    send_b, keep_b = back(8, (8,), w_end, w_fourth)
+    send_b, keep_b = back(back_end_kernel, (1,), 4294967296, [], w_fourth, send_mid, keep_mid)
     keep = joined(keep_a, keep_b)
     b1 = inner(far_plus(term1, i1))
     b2 = inner(far_plus(term2, i2))
@@ -260,15 +287,16 @@
         term1[3 * half :] + b1[:, 2 * heads :].astype(F32),
         term2[3 * half :] + b2[:, heads:].astype(F32),
     ], 1)
-    weight_grad, done = call(
-        join_weight_kernel, (struct(part, 4 * heads, F32), struct(8, 128, F32)), [], 0,
-        weight_half, core_swap(weight_half), i3, core_swap(i3),
-    )
-    key_grad = call(
-        join_key_kernel, struct(keys, features, F32), [], 0,
-        done, key_half, core_swap(key_half), k2, core_swap(k2),
-    )
-    return weight_grad, key_grad
+    outs = (struct(part, 4 * heads, F32), struct(keys, features, F32))
+    return tuple(pl.pallas_call(
+        join_kernel,
+        out_shape=outs,
+        in_specs=[smem] + [vmem] * 8,
+        out_specs=(pl.BlockSpec(memory_space=pl.ANY),) * 2,
+        scratch_shapes=[pltpu.VMEM(o.shape, F32) for o in outs] + [pltpu.SemaphoreType.DMA((4,))],
+        compiler_params=pltpu.CompilerParams(vmem_limit_bytes=16 << 20),
+        cost_estimate=pl.CostEstimate(flops=0, bytes_accessed=1 << 20, transcendentals=0),
+    )(place, weight_half, core_swap(weight_half), i3, core_swap(i3), key_half, core_swap(key_half), k2, core_swap(k2)))
 
 
 def solution(mesh):

time: 95.5 us -> 94.4 us (0.988)
  Pallas kernels: 18.6 us -> 17.1 us
  waiting for transfers between devices: 37.3 us -> 38.4 us
    pallas_call x9 -> x7, Pallas kernels: 18.6 us -> 14.7 us  [call(): pl.pallas_call(kernel, out_shape=out, in_specs=[smem] + [vmem] * len(args...]
    pallas_call x0 -> x1, Pallas kernels: none -> 2.37 us  [pair_body(): pl.pallas_call(join_kernel, out_shape=outs, in_specs=[smem] + [vmem] * 8,...]
  transfers between devices with their start and end apart: 26 -> 26, of which waited for: 8 -> 9; matrix products, arithmetic and copies ran while one was open for 3% -> 3% of each run, Pallas kernels for 18% -> 16%
where the time goes in v7:
time: 94.4 us; the launch traced here: 94 us
  waiting for transfers between devices  38.4 us (41%)
  starting transfers between devices  33.2 us (35%)
  Pallas kernels  17.1 us (18%)
  other arithmetic  2.81 us (3%)
  local copies, waits for them, and re-layouts  1.47 us (2%)
  between operations  1.01 us (1%)
    ppermute x6, waiting for transfers between devices, outer(): return lax.ppermute(v, 'fsdp', [(0, 1), (1, 0), (2, 3), (3, 2)])  31.4 us
    ppermute x6, starting transfers between devices, outer(): return lax.ppermute(v, 'fsdp', [(0, 1), (1, 0), (2, 3), (3, 2)])  19.6 us
    pallas_call x7, Pallas kernels, call(): pl.pallas_call(kernel, out_shape=out, in_specs=[smem] + [vmem] * len(args...  14.7 us
    ppermute x3, starting transfers between devices, square(): return lax.ppermute(v, 'tp', [(i, i ^ d) for i in range(4)])  6.77 us
    ppermute x3, waiting for transfers between devices, square(): return lax.ppermute(v, 'tp', [(i, i ^ d) for i in range(4)])  5.35 us
    ppermute x5, starting transfers between devices, inner(): return lax.ppermute(v, 'fsdp', [(1, 2), (2, 1)])  3.41 us
    ppermute x11, starting transfers between devices, core_swap(): return lax.ppermute(v, 'dp', [(0, 1), (1, 0)])  2.39 us
    pallas_call x1, Pallas kernels, pair_body(): pl.pallas_call(join_kernel, out_shape=outs, in_specs=[smem] + [vmem] * 8,...  2.37 us
  transfers between devices with their start and end apart: 26, of which 9 were waited for; matrix products, arithmetic and copies ran while one was open for 3% of the time, Pallas kernels for 16%

profile of v7, /device:TPU:0, one launch (start us, length us, event | category | flops | bytes accessed | tf_op | source)
XLA Modules:
  0.0 94.0 jit_solution(9671851585494298840)
XLA Ops:
  0.6 0.0 copy-start
  0.7 0.1 stack.57.place
  0.8 0.5 collective-permute-start.4
  1.3 0.1 collective-permute-start
  1.4 0.4 collective-permute-start.8
  1.8 2.6 %collective-permute-start.7 = (bf16[512,512]{1,0:T(8,128)(2,1)}, bf16[512,512]{1,0:T(8,128)(2,1)S(1)}, u32[]{:S(2)}, u32[]{:S(2)}) collective-permute-start(bf16[512,512]{1,0:T(8,128)(2,1)} %refs_2_.1), channel_id=1, source_target_pairs={{0,2},{1,3},{2,0},{3,1},{4,6},{5,7},{6,4},{7,5},{8,10},{9,11},{10,... | collective-permute-start | bytes 1572872 | tf_op jit(solution)/shard_map/ppermute | solution.py:201
  4.4 1.5 %collective-permute-start.6 = (bf16[512,512]{1,0:T(8,128)(2,1)}, bf16[512,512]{1,0:T(8,128)(2,1)S(1)}, u32[]{:S(2)}, u32[]{:S(2)}) collective-permute-start(bf16[512,512]{1,0:T(8,128)(2,1)} %refs_2_.1), channel_id=1, source_target_pairs={{0,1},{1,0},{2,3},{3,2},{4,5},{5,4},{6,7},{7,6},{8,9},{9,8},{10,11... | collective-permute-start | bytes 1572872 | tf_op jit(solution)/shard_map/ppermute | solution.py:201
  5.9 0.0 collective-permute-done.refs_1_.refs_6_
  5.9 0.1 constant_dynamic-slice_fusion.refs_11_
  6.0 0.0 copy-start.1
  6.0 2.1 %collective-permute-start.1 = (bf16[128,2048]{1,0:T(8,128)(2,1)S(1)}, bf16[128,2048]{1,0:T(8,128)(2,1)S(1)}, u32[]{:S(2)}, u32[]{:S(2)}) collective-permute-start(bf16[128,2048]{1,0:T(8,128)(2,1)S(1)} %constant_dynamic-slice_fusion.refs_11_), channel_id=1, source_target_pairs={{0,4},{4,0},{8,12},{12,8},{1,5},{5,1},{9,13},{13,9},{2,6},{6,2},{1... | collective-permute-start | bytes 1572872 | tf_op jit(solution)/shard_map/ppermute | solution.py:170
  8.1 0.0 collective-permute-done.4.other
  8.1 0.7 collective-permute-start.5
  8.8 0.7 broadcast_multiply_fusion
  9.5 0.7 add.56
  10.2 1.2 %copy-done.2 = bf16[512,1024]{1,0:T(8,128)(2,1)S(1)} copy-done((bf16[512,1024]{1,0:T(8,128)(2,1)S(1)}, bf16[512,1024]{1,0:T(8,128)(2,1)}, u32[]{:S(2)}) %copy-start.2) | copy-done | bytes 1048600
  11.4 1.6 %shard_map.77.turned = bf16[2,512,512]{2,1,0:T(8,128)(2,1)S(1)} custom-call(s32[15]{0:T(128)S(1)} %stack.57.place, bf16[512,1024]{1,0:T(8,128)(2,1)S(1)} %copy-done.2, bf16[512,1024]{1,0:T(8,128)(2,1)} %collective-permute-done.4.other), custom_call_target="tpu_custom_call" | custom-call | flops 1073741824 | bytes 1048576 | tf_op jit(solution)/shard_map/pallas_call | solution.py:190
  13.0 1.2 %shard_map.78 = (f32[512,512]{1,0:T(8,128)S(1)}, bf16[128,2048]{1,0:T(8,128)(2,1)S(1)}) custom-call(s32[15]{0:T(128)S(1)} %stack.57.place, bf16[2,512,512]{2,1,0:T(8,128)(2,1)S(1)} %shard_map.77.turned, bf16[512,512]{1,0:T(8,128)(2,1)S(1)} %copy-done.1, bf16[512,512]{1,0:T(8,128)(2,1)S(1)} %collective-permute-done.refs_1_.refs_6_), custom_call_target="tpu_custom_call" | custom-call | tf_op jit(solution)/shard_map/pallas_call | solution.py:190
  14.2 2.9 %collective-permute-done.7.refs_1_.refs_4_ = bf16[512,512]{1,0:T(8,128)(2,1)S(1)} collective-permute-done((bf16[512,512]{1,0:T(8,128)(2,1)}, bf16[512,512]{1,0:T(8,128)(2,1)S(1)}, u32[]{:S(2)}, u32[]{:S(2)}) %collective-permute-start.7) | collective-permute-done | bytes 524320 | tf_op jit(solution)/shard_map/ppermute | solution.py:201
  17.1 2.7 %collective-permute-start.3 = (bf16[512,512]{1,0:T(8,128)(2,1)S(1)}, bf16[512,512]{1,0:T(8,128)(2,1)S(1)}, u32[]{:S(2)}, u32[]{:S(2)}) collective-permute-start(bf16[512,512]{1,0:T(8,128)(2,1)S(1)} %copy-done.1), channel_id=1, source_target_pairs={{0,3},{1,2},{2,1},{3,0},{4,7},{5,6},{6,5},{7,4},{8,11},{9,10},{10,... | collective-permute-start | bytes 1572872 | tf_op jit(solution)/shard_map/ppermute | solution.py:201
  19.8 0.7 collective-permute-done.1.refs_12_
  20.5 0.7 collective-permute-start.2
  21.3 0.1 collective-permute-start.9
  21.3 0.5 collective-permute-start.10
  21.8 0.1 broadcast_select_fusion
  21.9 4.6 %collective-permute-start.14 = (bf16[128,2048]{1,0:T(8,128)(2,1)S(1)}, bf16[128,2048]{1,0:T(8,128)(2,1)S(1)}, u32[]{:S(2)}, u32[]{:S(2)}) collective-permute-start(bf16[128,2048]{1,0:T(8,128)(2,1)S(1)} %broadcast_select_fusion), channel_id=1, source_target_pairs={{0,4},{4,0},{8,12},{12,8},{1,5},{5,1},{9,13},{13,9},{2,6},{6,2},{1... | collective-permute-start | bytes 1572872 | tf_op jit(solution)/shard_map/ppermute | solution.py:170
  26.5 0.9 shard_map.80.refs_10_
  27.4 1.8 %shard_map.79 = (f32[512,1024]{1,0:T(8,128)S(1)}, bf16[128,2048]{1,0:T(8,128)(2,1)S(1)}, bf16[128,1024]{1,0:T(8,128)(2,1)S(1)}) custom-call(s32[15]{0:T(128)S(1)} %stack.57.place, bf16[2,512,512]{2,1,0:T(8,128)(2,1)S(1)} %shard_map.77.turned, bf16[512,512]{1,0:T(8,128)(2,1)S(1)} %collective-permute-done.6.refs_0_.refs_3_, ...), custom_call_target="tpu_custom_call" | custom-call | tf_op jit(solution)/shard_map/pallas_call | solution.py:190
  29.2 0.0 copy-start.3
  29.2 2.5 %collective-permute-done.3.refs_0_.refs_5_ = bf16[512,512]{1,0:T(8,128)(2,1)S(1)} collective-permute-done((bf16[512,512]{1,0:T(8,128)(2,1)S(1)}, bf16[512,512]{1,0:T(8,128)(2,1)S(1)}, u32[]{:S(2)}, u32[]{:S(2)}) %collective-permute-start.3) | collective-permute-done | bytes 524320 | tf_op jit(solution)/shard_map/ppermute | solution.py:201
  31.7 0.1 broadcast_select_fusion.1
  31.8 6.0 %collective-permute-start.12 = (bf16[128,2048]{1,0:T(8,128)(2,1)S(1)}, bf16[128,2048]{1,0:T(8,128)(2,1)S(1)}, u32[]{:S(2)}, u32[]{:S(2)}) collective-permute-start(bf16[128,2048]{1,0:T(8,128)(2,1)S(1)} %broadcast_select_fusion.1), channel_id=1, source_target_pairs={{0,4},{4,0},{8,12},{12,8},{1,5},{5,1},{9,13},{13,9},{2,6},{6,2},{1... | collective-permute-start | bytes 1572872 | tf_op jit(solution)/shard_map/ppermute | solution.py:170
  37.7 0.9 collective-permute-done.14.refs_14_
  38.7 0.1 add_convert_fusion.9
  38.8 0.7 collective-permute-start.15
  39.5 4.9 %shard_map.82 = (bf16[512,384]{1,0:T(8,128)(2,1)S(1)}, f32[512,384]{1,0:T(8,128)S(1)}, bf16[512,128]{1,0:T(8,128)(2,1)S(1)}, f32[512,128]{1,0:T(8,128)S(1)}) custom-call(s32[15]{0:T(128)S(1)} %stack.57.place, bf16[512,1024]{1,0:T(8,128)(2,1)S(1)} %copy-done.3, bf16[512,1024]{1,0:T(8,128)(2,1)} %collective-permute-done.8.refs_1_, ...), custom_call_target="tpu_custom_call" | custom-call | flops 4831838208 | bytes 1048576 | tf_op jit(solution)/shard_map/pallas_call | solution.py:190
  44.3 1.2 %shard_map.81 = (f32[512,512]{1,0:T(8,128)S(1)}, bf16[128,1024]{1,0:T(8,128)(2,1)S(1)}, bf16[128,512]{1,0:T(8,128)(2,1)S(1)}) custom-call(s32[15]{0:T(128)S(1)} %stack.57.place, bf16[2,512,512]{2,1,0:T(8,128)(2,1)S(1)} %shard_map.77.turned, bf16[512,512]{1,0:T(8,128)(2,1)S(1)} %collective-permute-done.3.refs_0_.refs_5_, ...), custom_call_target="tpu_custom_call" | custom-call | tf_op jit(solution)/shard_map/pallas_call | solution.py:190
  45.6 0.1 maximum_select_fusion.3
  45.7 4.6 %collective-permute-done.12.refs_11_ = bf16[128,2048]{1,0:T(8,128)(2,1)S(1)} collective-permute-done((bf16[128,2048]{1,0:T(8,128)(2,1)S(1)}, bf16[128,2048]{1,0:T(8,128)(2,1)S(1)}, u32[]{:S(2)}, u32[]{:S(2)}) %collective-permute-start.12) | collective-permute-done | bytes 524320 | tf_op jit(solution)/shard_map/ppermute | solution.py:170
  50.3 1.7 %collective-permute-start.18 = (bf16[128,1024]{1,0:T(8,128)(2,1)S(1)}, bf16[128,1024]{1,0:T(8,128)(2,1)S(1)}, u32[]{:S(2)}, u32[]{:S(2)}) collective-permute-start(bf16[128,1024]{1,0:T(8,128)(2,1)S(1)} %maximum_select_fusion.3), channel_id=1, source_target_pairs={{0,4},{4,0},{8,12},{12,8},{1,5},{5,1},{9,13},{13,9},{2,6},{6,2},{1... | collective-permute-start | bytes 786440 | tf_op jit(solution)/shard_map/ppermute | solution.py:170
  52.1 0.1 add_convert_fusion.3
  52.3 0.7 collective-permute-start.17
  53.0 3.1 %shard_map.83 = (bf16[512,128]{1,0:T(8,128)(2,1)S(1)}, f32[512,128]{1,0:T(8,128)S(1)}) custom-call(s32[15]{0:T(128)S(1)} %stack.57.place, bf16[512,1024]{1,0:T(8,128)(2,1)S(1)} %copy-done.3, bf16[512,1024]{1,0:T(8,128)(2,1)} %collective-permute-done.8.refs_1_, bf16[512,512]{1,0:T(8,128)(2,1)S(1)} %copy-done.1, ...), custom_call_target="tpu_custom_call" | custom-call | flops 4294967296 | bytes 1048576 | tf_op jit(solution)/shard_map/pallas_call | solution.py:190
  56.1 0.1 maximum_select_fusion.1
  56.2 1.3 %collective-permute-start.16 = (bf16[512,512]{1,0:T(8,128)(2,1)S(1)}, bf16[512,512]{1,0:T(8,128)(2,1)S(1)}, u32[]{:S(2)}, u32[]{:S(2)}) collective-permute-start(bf16[512,512]{1,0:T(8,128)(2,1)S(1)} %maximum_select_fusion.1), channel_id=1, source_target_pairs={{0,4},{4,0},{8,12},{12,8},{1,5},{5,1},{9,13},{13,9},{2,6},{6,2},{1... | collective-permute-start | bytes 1572872 | tf_op jit(solution)/shard_map/ppermute | solution.py:170
  57.5 1.0 %collective-permute-done.18 = bf16[128,1024]{1,0:T(8,128)(2,1)S(1)} collective-permute-done((bf16[128,1024]{1,0:T(8,128)(2,1)S(1)}, bf16[128,1024]{1,0:T(8,128)(2,1)S(1)}, u32[]{:S(2)}, u32[]{:S(2)}) %collective-permute-start.18) | collective-permute-done | bytes 262176 | tf_op jit(solution)/shard_map/ppermute | solution.py:170
  58.5 0.1 add_convert_fusion.6
  58.6 0.7 collective-permute-start.19
  59.3 0.1 maximum_select_fusion
  59.5 10.2 %collective-permute-done.16 = bf16[512,512]{1,0:T(8,128)(2,1)S(1)} collective-permute-done((bf16[512,512]{1,0:T(8,128)(2,1)S(1)}, bf16[512,512]{1,0:T(8,128)(2,1)S(1)}, u32[]{:S(2)}, u32[]{:S(2)}) %collective-permute-start.16) | collective-permute-done | bytes 524320 | tf_op jit(solution)/shard_map/ppermute | solution.py:170
  69.7 0.1 add_convert_fusion.4
  69.8 0.1 add_convert_fusion.1
  69.9 0.1 convert_add_fusion.3
  70.0 0.1 pad_maximum_fusion.mine
  70.1 0.1 collective-permute-start.20
  70.1 0.1 maximum_select_fusion.2
  70.2 3.9 %collective-permute-start.21 = (bf16[128,1536]{1,0:T(8,128)(2,1)S(1)}, bf16[128,1536]{1,0:T(8,128)(2,1)S(1)}, u32[]{:S(2)}, u32[]{:S(2)}) collective-permute-start(bf16[128,1536]{1,0:T(8,128)(2,1)S(1)} %maximum_select_fusion.2), channel_id=1, source_target_pairs={{0,4},{4,0},{8,12},{12,8},{1,5},{5,1},{9,13},{13,9},{2,6},{6,2},{1... | collective-permute-start | bytes 1179656 | tf_op jit(solution)/shard_map/ppermute | solution.py:170
  74.2 0.1 add_convert_fusion
  74.3 1.1 %collective-permute-start.24 = (bf16[256,512]{1,0:T(8,128)(2,1)S(1)}, bf16[256,512]{1,0:T(8,128)(2,1)S(1)}, u32[]{:S(2)}, u32[]{:S(2)}) collective-permute-start(bf16[256,512]{1,0:T(8,128)(2,1)S(1)} %get-tuple-element.124), channel_id=1, source_target_pairs={{0,8},{4,12},{8,0},{12,4},{1,9},{5,13},{9,1},{13,5},{2,10},{6,14},... | collective-permute-start | bytes 786440 | tf_op jit(solution)/shard_map/ppermute | solution.py:204
  75.4 0.2 collective-permute-start.23
  75.6 13.9 %collective-permute-done.21.last = bf16[128,1536]{1,0:T(8,128)(2,1)S(1)} collective-permute-done((bf16[128,1536]{1,0:T(8,128)(2,1)S(1)}, bf16[128,1536]{1,0:T(8,128)(2,1)S(1)}, u32[]{:S(2)}, u32[]{:S(2)}) %collective-permute-start.21) | collective-permute-done | bytes 393248 | tf_op jit(solution)/shard_map/ppermute | solution.py:170
  89.5 0.5 collective-permute-start.25
  90.1 1.6 %collective-permute-done.25.key_last_pair = bf16[256,512]{1,0:T(8,128)(2,1)S(1)} collective-permute-done((bf16[256,512]{1,0:T(8,128)(2,1)S(1)}, bf16[256,512]{1,0:T(8,128)(2,1)S(1)}, u32[]{:S(2)}, u32[]{:S(2)}) %collective-permute-start.25) | collective-permute-done | bytes 262176 | tf_op jit(solution)/shard_map/ppermute | solution.py:167
  91.6 2.4 %shard_map.84 = (f32[256,2048]{1,0:T(8,128)}, f32[256,1024]{1,0:T(8,128)}) custom-call(s32[15]{0:T(128)S(1)} %stack.57.place, f32[128,2048]{1,0:T(8,128)S(1)} %pad_maximum_fusion.mine, f32[128,2048]{1,0:T(8,128)S(1)} %collective-permute-done.20.pair, bf16[128,1536]{1,0:T(8,128)(2,1)S(1)} %collective-permute-done.21.last, ...), custom_call_target="tpu_custom_call" | custom-call | bytes 1048576 | tf_op jit(solution)/shard_map/pallas_call | solution.py:291
  (27 shorter events, 0.2 us)
Async XLA Ops:
  0.6 5.3 %copy-start = (bf16[256,2048]{1,0:T(8,128)(2,1)S(1)}, bf16[256,2048]{1,0:T(8,128)(2,1)}, u32[]{:S(2)}) copy-start(bf16[256,2048]{1,0:T(8,128)(2,1)} %param.9) | copy-start | bytes 3145732
  0.8 7.3 %collective-permute-start.4 = (bf16[512,1024]{1,0:T(8,128)(2,1)}, bf16[512,1024]{1,0:T(8,128)(2,1)}, u32[]{:S(2)}, u32[]{:S(2)}) collective-permute-start(bf16[512,1024]{1,0:T(8,128)(2,1)} %mine), channel_id=1, source_target_pairs={{0,16},{16,0},{1,17},{17,1},{2,18},{18,2},{3,19},{19,3},{4,20},{20... | collective-permute-start | bytes 3145736 | tf_op jit(solution)/shard_map/ppermute | solution.py:167
  1.3 4.6 %collective-permute-start = (bf16[512,512]{1,0:T(8,128)(2,1)}, bf16[512,512]{1,0:T(8,128)(2,1)S(1)}, u32[]{:S(2)}, u32[]{:S(2)}) collective-permute-start(bf16[512,512]{1,0:T(8,128)(2,1)} %refs_2_.1), channel_id=1, source_target_pairs={{0,16},{16,0},{1,17},{17,1},{2,18},{18,2},{3,19},{19,3},{4,20},{20... | collective-permute-start | bytes 1572872 | tf_op jit(solution)/shard_map/ppermute | solution.py:167
  1.4 19.9 %collective-permute-start.8 = (bf16[512,1024]{1,0:T(8,128)(2,1)}, bf16[512,1024]{1,0:T(8,128)(2,1)}, u32[]{:S(2)}, u32[]{:S(2)}) collective-permute-start(bf16[512,1024]{1,0:T(8,128)(2,1)} %refs_0_.2), channel_id=1, source_target_pairs={{0,16},{16,0},{1,17},{17,1},{2,18},{18,2},{3,19},{19,3},{4,20},{20... | collective-permute-start | bytes 3145736 | tf_op jit(solution)/shard_map/ppermute | solution.py:167
  1.8 15.3 %collective-permute-start.7 = (bf16[512,512]{1,0:T(8,128)(2,1)}, bf16[512,512]{1,0:T(8,128)(2,1)S(1)}, u32[]{:S(2)}, u32[]{:S(2)}) collective-permute-start(bf16[512,512]{1,0:T(8,128)(2,1)} %refs_2_.1), channel_id=1, source_target_pairs={{0,2},{1,3},{2,0},{3,1},{4,6},{5,7},{6,4},{7,5},{8,10},{9,11},{10,... | collective-permute-start | bytes 1572872 | tf_op jit(solution)/shard_map/ppermute | solution.py:201
  4.4 15.4 %collective-permute-start.6 = (bf16[512,512]{1,0:T(8,128)(2,1)}, bf16[512,512]{1,0:T(8,128)(2,1)S(1)}, u32[]{:S(2)}, u32[]{:S(2)}) collective-permute-start(bf16[512,512]{1,0:T(8,128)(2,1)} %refs_2_.1), channel_id=1, source_target_pairs={{0,1},{1,0},{2,3},{3,2},{4,5},{5,4},{6,7},{7,6},{8,9},{9,8},{10,11... | collective-permute-start | bytes 1572872 | tf_op jit(solution)/shard_map/ppermute | solution.py:201
  6.0 6.9 %copy-start.1 = (bf16[512,512]{1,0:T(8,128)(2,1)S(1)}, bf16[512,512]{1,0:T(8,128)(2,1)}, u32[]{:S(2)}) copy-start(bf16[512,512]{1,0:T(8,128)(2,1)} %refs_2_.1) | copy-start | bytes 1572868
  6.0 14.5 %collective-permute-start.1 = (bf16[128,2048]{1,0:T(8,128)(2,1)S(1)}, bf16[128,2048]{1,0:T(8,128)(2,1)S(1)}, u32[]{:S(2)}, u32[]{:S(2)}) collective-permute-start(bf16[128,2048]{1,0:T(8,128)(2,1)S(1)} %constant_dynamic-slice_fusion.refs_11_), channel_id=1, source_target_pairs={{0,4},{4,0},{8,12},{12,8},{1,5},{5,1},{9,13},{13,9},{2,6},{6,2},{1... | collective-permute-start | bytes 1572872 | tf_op jit(solution)/shard_map/ppermute | solution.py:170
  8.1 13.1 %collective-permute-start.5 = (bf16[128,2048]{1,0:T(8,128)(2,1)S(1)}, bf16[128,2048]{1,0:T(8,128)(2,1)S(1)}, u32[]{:S(2)}, u32[]{:S(2)}) collective-permute-start(bf16[128,2048]{1,0:T(8,128)(2,1)S(1)} %constant_dynamic-slice_fusion.refs_11_), channel_id=1, source_target_pairs={{4,8},{8,4},{5,9},{9,5},{6,10},{10,6},{7,11},{11,7},{20,24},{24,20... | collective-permute-start | bytes 1572872 | tf_op jit(solution)/shard_map/ppermute | solution.py:179
  10.2 1.2 %copy-start.2 = (bf16[512,1024]{1,0:T(8,128)(2,1)S(1)}, bf16[512,1024]{1,0:T(8,128)(2,1)}, u32[]{:S(2)}) copy-start(bf16[512,1024]{1,0:T(8,128)(2,1)} %mine) | copy-start | bytes 3145732
  17.1 14.6 %collective-permute-start.3 = (bf16[512,512]{1,0:T(8,128)(2,1)S(1)}, bf16[512,512]{1,0:T(8,128)(2,1)S(1)}, u32[]{:S(2)}, u32[]{:S(2)}) collective-permute-start(bf16[512,512]{1,0:T(8,128)(2,1)S(1)} %copy-done.1), channel_id=1, source_target_pairs={{0,3},{1,2},{2,1},{3,0},{4,7},{5,6},{6,5},{7,4},{8,11},{9,10},{10,... | collective-permute-start | bytes 1572872 | tf_op jit(solution)/shard_map/ppermute | solution.py:201
  19.8 2.1 %collective-permute-start.11 = (s32[512]{0:T(512)S(1)}, s32[512]{0:T(512)S(1)}, u32[]{:S(2)}, u32[]{:S(2)}) collective-permute-start(s32[512]{0:T(512)S(1)} %add.56), channel_id=1, source_target_pairs={{0,16},{16,0},{1,17},{17,1},{2,18},{18,2},{3,19},{19,3},{4,20},{20... | collective-permute-start | bytes 6152 | tf_op jit(solution)/shard_map/ppermute | solution.py:167
  20.5 11.2 %collective-permute-start.2 = (bf16[128,2048]{1,0:T(8,128)(2,1)S(1)}, bf16[128,2048]{1,0:T(8,128)(2,1)S(1)}, u32[]{:S(2)}, u32[]{:S(2)}) collective-permute-start(bf16[128,2048]{1,0:T(8,128)(2,1)S(1)} %collective-permute-done.1.refs_12_), channel_id=1, source_target_pairs={{4,8},{8,4},{5,9},{9,5},{6,10},{10,6},{7,11},{11,7},{20,24},{24,20... | collective-permute-start | bytes 1572872 | tf_op jit(solution)/shard_map/ppermute | solution.py:179
  21.3 6.2 %collective-permute-start.9 = (bf16[512,512]{1,0:T(8,128)(2,1)S(1)}, bf16[512,512]{1,0:T(8,128)(2,1)S(1)}, u32[]{:S(2)}, u32[]{:S(2)}) collective-permute-start(bf16[512,512]{1,0:T(8,128)(2,1)S(1)} %collective-permute-done.6.refs_0_.refs_3_), channel_id=1, source_target_pairs={{0,16},{16,0},{1,17},{17,1},{2,18},{18,2},{3,19},{19,3},{4,20},{20... | collective-permute-start | bytes 1572872 | tf_op jit(solution)/shard_map/ppermute | solution.py:167
  21.3 6.1 %collective-permute-start.10 = (bf16[512,512]{1,0:T(8,128)(2,1)S(1)}, bf16[512,512]{1,0:T(8,128)(2,1)S(1)}, u32[]{:S(2)}, u32[]{:S(2)}) collective-permute-start(bf16[512,512]{1,0:T(8,128)(2,1)S(1)} %collective-permute-done.7.refs_1_.refs_4_), channel_id=1, source_target_pairs={{0,16},{16,0},{1,17},{17,1},{2,18},{18,2},{3,19},{19,3},{4,20},{20... | collective-permute-start | bytes 1572872 | tf_op jit(solution)/shard_map/ppermute | solution.py:167
  21.9 16.8 %collective-permute-start.14 = (bf16[128,2048]{1,0:T(8,128)(2,1)S(1)}, bf16[128,2048]{1,0:T(8,128)(2,1)S(1)}, u32[]{:S(2)}, u32[]{:S(2)}) collective-permute-start(bf16[128,2048]{1,0:T(8,128)(2,1)S(1)} %broadcast_select_fusion), channel_id=1, source_target_pairs={{0,4},{4,0},{8,12},{12,8},{1,5},{5,1},{9,13},{13,9},{2,6},{6,2},{1... | collective-permute-start | bytes 1572872 | tf_op jit(solution)/shard_map/ppermute | solution.py:170
  29.2 10.2 %copy-start.3 = (bf16[512,1024]{1,0:T(8,128)(2,1)S(1)}, bf16[512,1024]{1,0:T(8,128)(2,1)}, u32[]{:S(2)}) copy-start(bf16[512,1024]{1,0:T(8,128)(2,1)} %refs_0_.2) | copy-start | bytes 3145732
  31.7 7.1 %collective-permute-start.13 = (bf16[512,512]{1,0:T(8,128)(2,1)S(1)}, bf16[512,512]{1,0:T(8,128)(2,1)S(1)}, u32[]{:S(2)}, u32[]{:S(2)}) collective-permute-start(bf16[512,512]{1,0:T(8,128)(2,1)S(1)} %collective-permute-done.3.refs_0_.refs_5_), channel_id=1, source_target_pairs={{0,16},{16,0},{1,17},{17,1},{2,18},{18,2},{3,19},{19,3},{4,20},{20... | collective-permute-start | bytes 1572872 | tf_op jit(solution)/shard_map/ppermute | solution.py:167
  31.8 18.6 %collective-permute-start.12 = (bf16[128,2048]{1,0:T(8,128)(2,1)S(1)}, bf16[128,2048]{1,0:T(8,128)(2,1)S(1)}, u32[]{:S(2)}, u32[]{:S(2)}) collective-permute-start(bf16[128,2048]{1,0:T(8,128)(2,1)S(1)} %broadcast_select_fusion.1), channel_id=1, source_target_pairs={{0,4},{4,0},{8,12},{12,8},{1,5},{5,1},{9,13},{13,9},{2,6},{6,2},{1... | collective-permute-start | bytes 1572872 | tf_op jit(solution)/shard_map/ppermute | solution.py:170
  38.8 6.8 %collective-permute-start.15 = (bf16[128,1024]{1,0:T(8,128)(2,1)S(1)}, bf16[128,1024]{1,0:T(8,128)(2,1)S(1)}, u32[]{:S(2)}, u32[]{:S(2)}) collective-permute-start(bf16[128,1024]{1,0:T(8,128)(2,1)S(1)} %pad_maximum_fusion.2), channel_id=1, source_target_pairs={{4,8},{8,4},{5,9},{9,5},{6,10},{10,6},{7,11},{11,7},{20,24},{24,20... | collective-permute-start | bytes 786440 | tf_op jit(solution)/shard_map/ppermute | solution.py:179
  50.3 8.2 %collective-permute-start.18 = (bf16[128,1024]{1,0:T(8,128)(2,1)S(1)}, bf16[128,1024]{1,0:T(8,128)(2,1)S(1)}, u32[]{:S(2)}, u32[]{:S(2)}) collective-permute-start(bf16[128,1024]{1,0:T(8,128)(2,1)S(1)} %maximum_select_fusion.3), channel_id=1, source_target_pairs={{0,4},{4,0},{8,12},{12,8},{1,5},{5,1},{9,13},{13,9},{2,6},{6,2},{1... | collective-permute-start | bytes 786440 | tf_op jit(solution)/shard_map/ppermute | solution.py:170
  52.3 7.2 %collective-permute-start.17 = (bf16[128,2048]{1,0:T(8,128)(2,1)S(1)}, bf16[128,2048]{1,0:T(8,128)(2,1)S(1)}, u32[]{:S(2)}, u32[]{:S(2)}) collective-permute-start(bf16[128,2048]{1,0:T(8,128)(2,1)S(1)} %pad_maximum_fusion.1), channel_id=1, source_target_pairs={{4,8},{8,4},{5,9},{9,5},{6,10},{10,6},{7,11},{11,7},{20,24},{24,20... | collective-permute-start | bytes 1572872 | tf_op jit(solution)/shard_map/ppermute | solution.py:179
  56.2 13.5 %collective-permute-start.16 = (bf16[512,512]{1,0:T(8,128)(2,1)S(1)}, bf16[512,512]{1,0:T(8,128)(2,1)S(1)}, u32[]{:S(2)}, u32[]{:S(2)}) collective-permute-start(bf16[512,512]{1,0:T(8,128)(2,1)S(1)} %maximum_select_fusion.1), channel_id=1, source_target_pairs={{0,4},{4,0},{8,12},{12,8},{1,5},{5,1},{9,13},{13,9},{2,6},{6,2},{1... | collective-permute-start | bytes 1572872 | tf_op jit(solution)/shard_map/ppermute | solution.py:170
  58.6 0.8 collective-permute-start.19
  70.1 21.6 %collective-permute-start.20 = (f32[128,2048]{1,0:T(8,128)S(1)}, f32[128,2048]{1,0:T(8,128)S(1)}, u32[]{:S(2)}, u32[]{:S(2)}) collective-permute-start(f32[128,2048]{1,0:T(8,128)S(1)} %pad_maximum_fusion.mine), channel_id=1, source_target_pairs={{0,16},{16,0},{1,17},{17,1},{2,18},{18,2},{3,19},{19,3},{4,20},{20... | collective-permute-start | bytes 3145736 | tf_op jit(solution)/shard_map/ppermute | solution.py:167
  70.2 19.3 %collective-permute-start.21 = (bf16[128,1536]{1,0:T(8,128)(2,1)S(1)}, bf16[128,1536]{1,0:T(8,128)(2,1)S(1)}, u32[]{:S(2)}, u32[]{:S(2)}) collective-permute-start(bf16[128,1536]{1,0:T(8,128)(2,1)S(1)} %maximum_select_fusion.2), channel_id=1, source_target_pairs={{0,4},{4,0},{8,12},{12,8},{1,5},{5,1},{9,13},{13,9},{2,6},{6,2},{1... | collective-permute-start | bytes 1179656 | tf_op jit(solution)/shard_map/ppermute | solution.py:170
  74.3 15.2 %collective-permute-start.24 = (bf16[256,512]{1,0:T(8,128)(2,1)S(1)}, bf16[256,512]{1,0:T(8,128)(2,1)S(1)}, u32[]{:S(2)}, u32[]{:S(2)}) collective-permute-start(bf16[256,512]{1,0:T(8,128)(2,1)S(1)} %get-tuple-element.124), channel_id=1, source_target_pairs={{0,8},{4,12},{8,0},{12,4},{1,9},{5,13},{9,1},{13,5},{2,10},{6,14},... | collective-permute-start | bytes 786440 | tf_op jit(solution)/shard_map/ppermute | solution.py:204
  75.4 14.7 %collective-permute-start.23 = (f32[256,512]{1,0:T(8,128)S(1)}, f32[256,512]{1,0:T(8,128)S(1)}, u32[]{:S(2)}, u32[]{:S(2)}) collective-permute-start(f32[256,512]{1,0:T(8,128)S(1)} %get-tuple-element.125.key_mine), channel_id=1, source_target_pairs={{0,16},{16,0},{1,17},{17,1},{2,18},{18,2},{3,19},{19,3},{4,20},{20... | collective-permute-start | bytes 1572872 | tf_op jit(solution)/shard_map/ppermute | solution.py:167
  89.5 2.1 %collective-permute-start.22 = (bf16[128,1536]{1,0:T(8,128)(2,1)S(1)}, bf16[128,1536]{1,0:T(8,128)(2,1)S(1)}, u32[]{:S(2)}, u32[]{:S(2)}) collective-permute-start(bf16[128,1536]{1,0:T(8,128)(2,1)S(1)} %collective-permute-done.21.last), channel_id=1, source_target_pairs={{0,16},{16,0},{1,17},{17,1},{2,18},{18,2},{3,19},{19,3},{4,20},{20... | collective-permute-start | bytes 1179656 | tf_op jit(solution)/shard_map/ppermute | solution.py:167
  89.5 2.1 %collective-permute-start.25 = (bf16[256,512]{1,0:T(8,128)(2,1)S(1)}, bf16[256,512]{1,0:T(8,128)(2,1)S(1)}, u32[]{:S(2)}, u32[]{:S(2)}) collective-permute-start(bf16[256,512]{1,0:T(8,128)(2,1)S(1)} %collective-permute-done.24.key_last), channel_id=1, source_target_pairs={{0,16},{16,0},{1,17},{17,1},{2,18},{18,2},{3,19},{19,3},{4,20},{20... | collective-permute-start | bytes 786440 | tf_op jit(solution)/shard_map/ppermute | solution.py:167

commit v8 on v7

--- a/solution.py
+++ b/solution.py
@@ -210,7 +210,7 @@
         n = len(v) // 2 * heads
         out = (struct(4 * half, n, F32),) + tuple(struct(half, count * n, BF16) for _, count in parts)
         kernel = functools.partial(term_kernel, tuple(first for first, _ in parts))
-        return call(kernel, out, [], {1: 0, 3: 0}.get(len(v) // 2 + len(parts) - 1, 0), turned, *v)
+        return call(kernel, out, [], (2 << 30) if len(v) == len(parts) == 2 else 0, turned, *v)
 
     def plus(v, came):
         return (v + came.astype(F32)).astype(BF16)
@@ -230,11 +230,11 @@
     value_grad, layer_input, residual_grad, value_weight, place, is_low, is_end, first_row = got
 
     v0 = value_grad
-    v0_other, weight_rows = phase((core_swap(v0), value_weight))
-    w_own = lax.dynamic_slice_in_dim(weight_rows, first_row, half, 0)
+    w_own = lax.dynamic_slice_in_dim(value_weight, first_row, half, 0)
     in_other, res_other = core_swap(layer_input), core_swap(residual_grad)
+    v0_other = core_swap(v0)
     w_inner, in_other = phase((w_own, in_other))
-    turned = call(turn_kernel, jax.ShapeDtypeStruct((2, 4 * half, tokens), BF16), [], 1073741824, layer_input, in_other)
+    turned = call(turn_kernel, jax.ShapeDtypeStruct((2, 4 * half, tokens), BF16), [], 1 << 30, layer_input, in_other)
     term0, send0 = term((v0, v0_other), (0, 4))
     w_beside = outer(w_own)
     got = phase((inner(w_inner), square(v0, 1), square(v0, 2), turned, term0, send0, res_other))
@@ -242,6 +242,7 @@
 
     vx_other, vy_other = core_swap(vx), core_swap(vy)
     term1, send1, near1 = term((vx, vy, vx_other, vy_other), (0, 2), (2, 1))
+    owner, key_row, turned = phase((owner, key_row, turned))
     key = owner[:, 0] * keys + key_row
     key_both = jnp.concatenate([key, core_swap(key)])[None, :]
     chosen = call(choose_kernel, struct(4 * keys, 2 * tokens, BF16), [], 0, key_both)
@@ -256,7 +257,7 @@
     back0 = plus(term0[2 * half : 3 * half], b0[:, :heads])
     send2 = jnp.where(is_end, send2, jnp.concatenate([back0, back0], 1))
     send_a, keep_a, send_mid, keep_mid = back(
-        back_kernel, (3, 1), 4831838208, [pltpu.VMEM((3 * half, 4 * heads), BF16)],
+        back_kernel, (3, 1), 1 << 30, [pltpu.VMEM((3 * half, 4 * heads), BF16)],
         w_own, w_beside, w_mid, w_third, w_end,
     )
     got = phase((outer(jnp.where(is_end, send1, w_end)), b0, term1, term2, send_a, keep_a, term0, near1, near2, send2))
@@ -267,7 +268,7 @@
         return jnp.where(is_low, jnp.concatenate([a, b], 1), jnp.concatenate([b, a], 1))
 
     i2 = outer(send2)
-    send_b, keep_b = back(back_end_kernel, (1,), 4294967296, [], w_fourth, send_mid, keep_mid)
+    send_b, keep_b = back(back_end_kernel, (1,), 1 << 29, [], w_fourth, send_mid, keep_mid)
     keep = joined(keep_a, keep_b)
     b1 = inner(far_plus(term1, i1))
     b2 = inner(far_plus(term2, i2))

time: 94.4 us -> 93.6 us (level)
  waiting for transfers between devices: 38.4 us -> 45.1 us
  starting transfers between devices: 33.2 us -> 28.5 us
  Pallas kernels: 17.1 us -> 15.7 us
  other arithmetic: 2.81 us -> 1.46 us
    ppermute x6, waiting for transfers between devices: 31.4 us -> 39.4 us  [outer(): return lax.ppermute(v, 'fsdp', [(0, 1), (1, 0), (2, 3), (3, 2)])]
    ppermute x6, starting transfers between devices: 19.6 us -> 16.2 us  [outer(): return lax.ppermute(v, 'fsdp', [(0, 1), (1, 0), (2, 3), (3, 2)])]
    ppermute x3, waiting for transfers between devices: 5.35 us -> 3.54 us  [square(): return lax.ppermute(v, 'tp', [(i, i ^ d) for i in range(4)])]
    pallas_call x7, Pallas kernels: 14.7 us -> 13.3 us  [call(): pl.pallas_call(kernel, out_shape=out, in_specs=[smem] + [vmem] * len(args...]
    ppermute x3, starting transfers between devices: 6.77 us -> 5.52 us  [square(): return lax.ppermute(v, 'tp', [(i, i ^ d) for i in range(4)])]
  transfers between devices with their start and end apart: 26 -> 26, of which waited for: 9 -> 9; matrix products, arithmetic and copies ran while one was open for 3% -> 1% of each run, Pallas kernels for 16% -> 14%
where the time goes in v8:
time: 93.6 us; the launch traced here: 93.3 us
  waiting for transfers between devices  45.1 us (48%)
  starting transfers between devices  28.5 us (30%)
  Pallas kernels  15.7 us (17%)
  local copies, waits for them, and re-layouts  1.47 us (2%)
  other arithmetic  1.46 us (2%)
  between operations  1.05 us (1%)
    ppermute x6, waiting for transfers between devices, outer(): return lax.ppermute(v, 'fsdp', [(0, 1), (1, 0), (2, 3), (3, 2)])  39.4 us
    ppermute x6, starting transfers between devices, outer(): return lax.ppermute(v, 'fsdp', [(0, 1), (1, 0), (2, 3), (3, 2)])  16.2 us
    pallas_call x7, Pallas kernels, call(): pl.pallas_call(kernel, out_shape=out, in_specs=[smem] + [vmem] * len(args...  13.3 us
    ppermute x3, starting transfers between devices, square(): return lax.ppermute(v, 'tp', [(i, i ^ d) for i in range(4)])  5.52 us
    ppermute x5, starting transfers between devices, inner(): return lax.ppermute(v, 'fsdp', [(1, 2), (2, 1)])  3.55 us
    ppermute x3, waiting for transfers between devices, square(): return lax.ppermute(v, 'tp', [(i, i ^ d) for i in range(4)])  3.54 us
    ppermute x11, starting transfers between devices, core_swap(): return lax.ppermute(v, 'dp', [(0, 1), (1, 0)])  2.47 us
    pallas_call x1, Pallas kernels, pair_body(): pl.pallas_call(join_kernel, out_shape=outs, in_specs=[smem] + [vmem] * 8,...  2.37 us
  transfers between devices with their start and end apart: 26, of which 9 were waited for; matrix products, arithmetic and copies ran while one was open for 1% of the time, Pallas kernels for 14%

profile of v8, /device:TPU:0, one launch (start us, length us, event | category | flops | bytes accessed | tf_op | source)
XLA Modules:
  0.0 93.3 jit_solution(8288296252297413880)
XLA Ops:
  0.6 0.0 copy-start
  0.7 0.1 stack.57.place
  0.8 0.5 collective-permute-start.3
  1.3 0.1 collective-permute-start.7
  1.4 0.4 collective-permute-start.8
  1.8 2.6 %collective-permute-start.6 = (bf16[512,512]{1,0:T(8,128)(2,1)}, bf16[512,512]{1,0:T(8,128)(2,1)S(1)}, u32[]{:S(2)}, u32[]{:S(2)}) collective-permute-start(bf16[512,512]{1,0:T(8,128)(2,1)} %refs_2_.1), channel_id=1, source_target_pairs={{0,2},{1,3},{2,0},{3,1},{4,6},{5,7},{6,4},{7,5},{8,10},{9,11},{10,... | collective-permute-start | bytes 1572872 | tf_op jit(solution)/shard_map/ppermute | solution.py:201
  4.4 0.1 constant_dynamic-slice_fusion.refs_11_
  4.5 0.0 copy-start.1
  4.5 1.6 %collective-permute-start = (bf16[128,2048]{1,0:T(8,128)(2,1)S(1)}, bf16[128,2048]{1,0:T(8,128)(2,1)S(1)}, u32[]{:S(2)}, u32[]{:S(2)}) collective-permute-start(bf16[128,2048]{1,0:T(8,128)(2,1)S(1)} %constant_dynamic-slice_fusion.refs_11_), channel_id=1, source_target_pairs={{0,4},{4,0},{8,12},{12,8},{1,5},{5,1},{9,13},{13,9},{2,6},{6,2},{1... | collective-permute-start | bytes 1572872 | tf_op jit(solution)/shard_map/ppermute | solution.py:170
  6.2 0.0 collective-permute-done.3.other
  6.2 1.5 %collective-permute-start.5 = (bf16[512,512]{1,0:T(8,128)(2,1)}, bf16[512,512]{1,0:T(8,128)(2,1)S(1)}, u32[]{:S(2)}, u32[]{:S(2)}) collective-permute-start(bf16[512,512]{1,0:T(8,128)(2,1)} %refs_2_.1), channel_id=1, source_target_pairs={{0,1},{1,0},{2,3},{3,2},{4,5},{5,4},{6,7},{7,6},{8,9},{9,8},{10,11... | collective-permute-start | bytes 1572872 | tf_op jit(solution)/shard_map/ppermute | solution.py:201
  7.7 0.0 collective-permute-done.7.refs_1_.refs_6_
  7.7 0.7 collective-permute-start.4
  8.4 0.0 copy-start.3
  8.4 1.2 %copy-done.3 = bf16[512,1024]{1,0:T(8,128)(2,1)S(1)} copy-done((bf16[512,1024]{1,0:T(8,128)(2,1)S(1)}, bf16[512,1024]{1,0:T(8,128)(2,1)}, u32[]{:S(2)}) %copy-start.3) | copy-done | bytes 1048600
  9.6 1.6 %shard_map.77.turned = bf16[2,512,512]{2,1,0:T(8,128)(2,1)S(1)} custom-call(s32[15]{0:T(128)S(1)} %stack.57.place, bf16[512,1024]{1,0:T(8,128)(2,1)S(1)} %copy-done.3, bf16[512,1024]{1,0:T(8,128)(2,1)} %collective-permute-done.3.other), custom_call_target="tpu_custom_call" | custom-call | flops 1073741824 | bytes 1048576 | tf_op jit(solution)/shard_map/pallas_call | solution.py:190
  11.2 1.2 %shard_map.78 = (f32[512,512]{1,0:T(8,128)S(1)}, bf16[128,2048]{1,0:T(8,128)(2,1)S(1)}) custom-call(s32[15]{0:T(128)S(1)} %stack.57.place, bf16[2,512,512]{2,1,0:T(8,128)(2,1)S(1)} %shard_map.77.turned, bf16[512,512]{1,0:T(8,128)(2,1)S(1)} %copy-done.1, bf16[512,512]{1,0:T(8,128)(2,1)S(1)} %collective-permute-done.7.refs_1_.refs_6_), custom_call_target="tpu_custom_call" | custom-call | tf_op jit(solution)/shard_map/pallas_call | solution.py:190
  12.4 6.2 %collective-permute-done.refs_12_ = bf16[128,2048]{1,0:T(8,128)(2,1)S(1)} collective-permute-done((bf16[128,2048]{1,0:T(8,128)(2,1)S(1)}, bf16[128,2048]{1,0:T(8,128)(2,1)S(1)}, u32[]{:S(2)}, u32[]{:S(2)}) %collective-permute-start) | collective-permute-done | bytes 524320 | tf_op jit(solution)/shard_map/ppermute | solution.py:170
  18.6 1.4 %collective-permute-start.2 = (bf16[512,512]{1,0:T(8,128)(2,1)S(1)}, bf16[512,512]{1,0:T(8,128)(2,1)S(1)}, u32[]{:S(2)}, u32[]{:S(2)}) collective-permute-start(bf16[512,512]{1,0:T(8,128)(2,1)S(1)} %copy-done.1), channel_id=1, source_target_pairs={{0,3},{1,2},{2,1},{3,0},{4,7},{5,6},{6,5},{7,4},{8,11},{9,10},{10,... | collective-permute-start | bytes 1572872 | tf_op jit(solution)/shard_map/ppermute | solution.py:201
  20.0 0.7 collective-permute-start.1
  20.8 0.1 collective-permute-start.11
  20.9 0.5 collective-permute-start.9
  21.4 0.1 collective-permute-start.10
  21.5 0.1 broadcast_select_fusion
  21.5 0.5 collective-permute-done.11
  22.0 4.4 %collective-permute-start.14 = (bf16[128,2048]{1,0:T(8,128)(2,1)S(1)}, bf16[128,2048]{1,0:T(8,128)(2,1)S(1)}, u32[]{:S(2)}, u32[]{:S(2)}) collective-permute-start(bf16[128,2048]{1,0:T(8,128)(2,1)S(1)} %broadcast_select_fusion), channel_id=1, source_target_pairs={{0,4},{4,0},{8,12},{12,8},{1,5},{5,1},{9,13},{13,9},{2,6},{6,2},{1... | collective-permute-start | bytes 1572872 | tf_op jit(solution)/shard_map/ppermute | solution.py:170
  26.4 0.9 shard_map.80.refs_10_
  27.3 1.8 %shard_map.79 = (f32[512,1024]{1,0:T(8,128)S(1)}, bf16[128,2048]{1,0:T(8,128)(2,1)S(1)}, bf16[128,1024]{1,0:T(8,128)(2,1)S(1)}) custom-call(s32[15]{0:T(128)S(1)} %stack.57.place, bf16[2,512,512]{2,1,0:T(8,128)(2,1)S(1)} %shard_map.77.turned, bf16[512,512]{1,0:T(8,128)(2,1)S(1)} %collective-permute-done.5.refs_0_.refs_3_, ...), custom_call_target="tpu_custom_call" | custom-call | tf_op jit(solution)/shard_map/pallas_call | solution.py:190
  29.1 3.5 %collective-permute-done.2.refs_0_.refs_5_ = bf16[512,512]{1,0:T(8,128)(2,1)S(1)} collective-permute-done((bf16[512,512]{1,0:T(8,128)(2,1)S(1)}, bf16[512,512]{1,0:T(8,128)(2,1)S(1)}, u32[]{:S(2)}, u32[]{:S(2)}) %collective-permute-start.2) | collective-permute-done | bytes 524320 | tf_op jit(solution)/shard_map/ppermute | solution.py:201
  32.7 0.1 broadcast_select_fusion.1
  32.7 3.8 %collective-permute-start.12 = (bf16[128,2048]{1,0:T(8,128)(2,1)S(1)}, bf16[128,2048]{1,0:T(8,128)(2,1)S(1)}, u32[]{:S(2)}, u32[]{:S(2)}) collective-permute-start(bf16[128,2048]{1,0:T(8,128)(2,1)S(1)} %broadcast_select_fusion.1), channel_id=1, source_target_pairs={{0,4},{4,0},{8,12},{12,8},{1,5},{5,1},{9,13},{13,9},{2,6},{6,2},{1... | collective-permute-start | bytes 1572872 | tf_op jit(solution)/shard_map/ppermute | solution.py:170
  36.5 2.6 %collective-permute-done.14.refs_14_ = bf16[128,2048]{1,0:T(8,128)(2,1)S(1)} collective-permute-done((bf16[128,2048]{1,0:T(8,128)(2,1)S(1)}, bf16[128,2048]{1,0:T(8,128)(2,1)S(1)}, u32[]{:S(2)}, u32[]{:S(2)}) %collective-permute-start.14) | collective-permute-done | bytes 524320 | tf_op jit(solution)/shard_map/ppermute | solution.py:170
  39.1 0.1 add_convert_fusion.9
  39.2 0.0 copy-start.2
  39.2 0.8 collective-permute-start.15
  40.1 1.2 %shard_map.81 = (f32[512,512]{1,0:T(8,128)S(1)}, bf16[128,1024]{1,0:T(8,128)(2,1)S(1)}, bf16[128,512]{1,0:T(8,128)(2,1)S(1)}) custom-call(s32[15]{0:T(128)S(1)} %stack.57.place, bf16[2,512,512]{2,1,0:T(8,128)(2,1)S(1)} %shard_map.77.turned, bf16[512,512]{1,0:T(8,128)(2,1)S(1)} %collective-permute-done.2.refs_0_.refs_5_, ...), custom_call_target="tpu_custom_call" | custom-call | flops 2147483648 | bytes 1048576 | tf_op jit(solution)/shard_map/pallas_call | solution.py:190
  41.3 4.2 %shard_map.82 = (bf16[512,384]{1,0:T(8,128)(2,1)S(1)}, f32[512,384]{1,0:T(8,128)S(1)}, bf16[512,128]{1,0:T(8,128)(2,1)S(1)}, f32[512,128]{1,0:T(8,128)S(1)}) custom-call(s32[15]{0:T(128)S(1)} %stack.57.place, bf16[512,1024]{1,0:T(8,128)(2,1)S(1)} %copy-done.2, bf16[512,1024]{1,0:T(8,128)(2,1)S(1)} %collective-permute-done.8.refs_1_, ...), custom_call_target="tpu_custom_call" | custom-call | flops 1073741824 | bytes 1048576 | tf_op jit(solution)/shard_map/pallas_call | solution.py:190
  45.5 0.1 maximum_select_fusion.3
  45.6 4.3 %collective-permute-done.12.refs_11_ = bf16[128,2048]{1,0:T(8,128)(2,1)S(1)} collective-permute-done((bf16[128,2048]{1,0:T(8,128)(2,1)S(1)}, bf16[128,2048]{1,0:T(8,128)(2,1)S(1)}, u32[]{:S(2)}, u32[]{:S(2)}) %collective-permute-start.12) | collective-permute-done | bytes 524320 | tf_op jit(solution)/shard_map/ppermute | solution.py:170
  49.9 1.7 %collective-permute-start.18 = (bf16[128,1024]{1,0:T(8,128)(2,1)S(1)}, bf16[128,1024]{1,0:T(8,128)(2,1)S(1)}, u32[]{:S(2)}, u32[]{:S(2)}) collective-permute-start(bf16[128,1024]{1,0:T(8,128)(2,1)S(1)} %maximum_select_fusion.3), channel_id=1, source_target_pairs={{0,4},{4,0},{8,12},{12,8},{1,5},{5,1},{9,13},{13,9},{2,6},{6,2},{1... | collective-permute-start | bytes 786440 | tf_op jit(solution)/shard_map/ppermute | solution.py:170
  51.6 0.1 add_convert_fusion.3
  51.8 0.7 collective-permute-start.17
  52.5 2.4 %shard_map.83 = (bf16[512,128]{1,0:T(8,128)(2,1)S(1)}, f32[512,128]{1,0:T(8,128)S(1)}) custom-call(s32[15]{0:T(128)S(1)} %stack.57.place, bf16[512,1024]{1,0:T(8,128)(2,1)S(1)} %copy-done.2, bf16[512,1024]{1,0:T(8,128)(2,1)S(1)} %collective-permute-done.8.refs_1_, bf16[512,512]{1,0:T(8,128)(2,1)S(1)} %copy-done.1, ...), custom_call_target="tpu_custom_call" | custom-call | flops 536870912 | bytes 1048576 | tf_op jit(solution)/shard_map/pallas_call | solution.py:190
  55.0 0.1 maximum_select_fusion.1
  55.1 0.7 collective-permute-start.16
  55.9 2.8 %collective-permute-done.18 = bf16[128,1024]{1,0:T(8,128)(2,1)S(1)} collective-permute-done((bf16[128,1024]{1,0:T(8,128)(2,1)S(1)}, bf16[128,1024]{1,0:T(8,128)(2,1)S(1)}, u32[]{:S(2)}, u32[]{:S(2)}) %collective-permute-start.18) | collective-permute-done | bytes 262176 | tf_op jit(solution)/shard_map/ppermute | solution.py:170
  58.6 0.1 add_convert_fusion.6
  58.7 0.7 collective-permute-start.19
  59.4 0.1 maximum_select_fusion
  59.6 9.4 %collective-permute-done.16 = bf16[512,512]{1,0:T(8,128)(2,1)S(1)} collective-permute-done((bf16[512,512]{1,0:T(8,128)(2,1)S(1)}, bf16[512,512]{1,0:T(8,128)(2,1)S(1)}, u32[]{:S(2)}, u32[]{:S(2)}) %collective-permute-start.16) | collective-permute-done | bytes 524320 | tf_op jit(solution)/shard_map/ppermute | solution.py:170
  69.0 0.1 add_convert_fusion.4
  69.1 0.1 add_convert_fusion.1
  69.2 0.1 convert_add_fusion.3
  69.3 0.1 pad_maximum_fusion.mine
  69.4 0.1 collective-permute-start.20
  69.4 0.1 maximum_select_fusion.2
  69.5 3.9 %collective-permute-start.21 = (bf16[128,1536]{1,0:T(8,128)(2,1)S(1)}, bf16[128,1536]{1,0:T(8,128)(2,1)S(1)}, u32[]{:S(2)}, u32[]{:S(2)}) collective-permute-start(bf16[128,1536]{1,0:T(8,128)(2,1)S(1)} %maximum_select_fusion.2), channel_id=1, source_target_pairs={{0,4},{4,0},{8,12},{12,8},{1,5},{5,1},{9,13},{13,9},{2,6},{6,2},{1... | collective-permute-start | bytes 1179656 | tf_op jit(solution)/shard_map/ppermute | solution.py:170
  73.5 0.1 add_convert_fusion
  73.6 0.8 collective-permute-start.24
  74.4 0.2 collective-permute-start.23
  74.6 14.2 %collective-permute-done.21.last = bf16[128,1536]{1,0:T(8,128)(2,1)S(1)} collective-permute-done((bf16[128,1536]{1,0:T(8,128)(2,1)S(1)}, bf16[128,1536]{1,0:T(8,128)(2,1)S(1)}, u32[]{:S(2)}, u32[]{:S(2)}) %collective-permute-start.21) | collective-permute-done | bytes 393248 | tf_op jit(solution)/shard_map/ppermute | solution.py:170
  88.8 0.5 collective-permute-start.25
  89.4 1.6 %collective-permute-done.25.key_last_pair = bf16[256,512]{1,0:T(8,128)(2,1)S(1)} collective-permute-done((bf16[256,512]{1,0:T(8,128)(2,1)S(1)}, bf16[256,512]{1,0:T(8,128)(2,1)S(1)}, u32[]{:S(2)}, u32[]{:S(2)}) %collective-permute-start.25) | collective-permute-done | bytes 262176 | tf_op jit(solution)/shard_map/ppermute | solution.py:167
  90.9 2.4 %shard_map.84 = (f32[256,2048]{1,0:T(8,128)}, f32[256,1024]{1,0:T(8,128)}) custom-call(s32[15]{0:T(128)S(1)} %stack.57.place, f32[128,2048]{1,0:T(8,128)S(1)} %pad_maximum_fusion.mine, f32[128,2048]{1,0:T(8,128)S(1)} %collective-permute-done.20.pair, bf16[128,1536]{1,0:T(8,128)(2,1)S(1)} %collective-permute-done.21.last, ...), custom_call_target="tpu_custom_call" | custom-call | bytes 1048576 | tf_op jit(solution)/shard_map/pallas_call | solution.py:292
  (31 shorter events, 0.2 us)
Async XLA Ops:
  0.6 3.8 %copy-start = (bf16[256,2048]{1,0:T(8,128)(2,1)S(1)}, bf16[256,2048]{1,0:T(8,128)(2,1)}, u32[]{:S(2)}) copy-start(bf16[256,2048]{1,0:T(8,128)(2,1)} %param.9) | copy-start | bytes 3145732
  0.8 5.4 %collective-permute-start.3 = (bf16[512,1024]{1,0:T(8,128)(2,1)}, bf16[512,1024]{1,0:T(8,128)(2,1)}, u32[]{:S(2)}, u32[]{:S(2)}) collective-permute-start(bf16[512,1024]{1,0:T(8,128)(2,1)} %mine), channel_id=1, source_target_pairs={{0,16},{16,0},{1,17},{17,1},{2,18},{18,2},{3,19},{19,3},{4,20},{20... | collective-permute-start | bytes 3145736 | tf_op jit(solution)/shard_map/ppermute | solution.py:167
  1.3 6.4 %collective-permute-start.7 = (bf16[512,512]{1,0:T(8,128)(2,1)}, bf16[512,512]{1,0:T(8,128)(2,1)S(1)}, u32[]{:S(2)}, u32[]{:S(2)}) collective-permute-start(bf16[512,512]{1,0:T(8,128)(2,1)} %refs_2_.1), channel_id=1, source_target_pairs={{0,16},{16,0},{1,17},{17,1},{2,18},{18,2},{3,19},{19,3},{4,20},{20... | collective-permute-start | bytes 1572872 | tf_op jit(solution)/shard_map/ppermute | solution.py:167
  1.4 19.4 %collective-permute-start.8 = (bf16[512,1024]{1,0:T(8,128)(2,1)}, bf16[512,1024]{1,0:T(8,128)(2,1)S(1)}, u32[]{:S(2)}, u32[]{:S(2)}) collective-permute-start(bf16[512,1024]{1,0:T(8,128)(2,1)} %refs_0_.2), channel_id=1, source_target_pairs={{0,16},{16,0},{1,17},{17,1},{2,18},{18,2},{3,19},{19,3},{4,20},{20... | collective-permute-start | bytes 3145736 | tf_op jit(solution)/shard_map/ppermute | solution.py:167
  1.8 18.2 %collective-permute-start.6 = (bf16[512,512]{1,0:T(8,128)(2,1)}, bf16[512,512]{1,0:T(8,128)(2,1)S(1)}, u32[]{:S(2)}, u32[]{:S(2)}) collective-permute-start(bf16[512,512]{1,0:T(8,128)(2,1)} %refs_2_.1), channel_id=1, source_target_pairs={{0,2},{1,3},{2,0},{3,1},{4,6},{5,7},{6,4},{7,5},{8,10},{9,11},{10,... | collective-permute-start | bytes 1572872 | tf_op jit(solution)/shard_map/ppermute | solution.py:201
  4.4 16.4 %copy-start.5 = (s32[512,1]{0,1:T(1,128)S(1)}, s32[512,1]{0,1:T(1,128)}, u32[]{:S(2)}) copy-start(s32[512,1]{0,1:T(1,128)} %param.10) | copy-start | bytes 6148
  4.4 16.4 %copy-start.4 = (s32[512]{0:T(512)S(1)}, s32[512]{0:T(512)}, u32[]{:S(2)}) copy-start(s32[512]{0:T(512)} %param.11) | copy-start | bytes 6148
  4.5 6.6 %copy-start.1 = (bf16[512,512]{1,0:T(8,128)(2,1)S(1)}, bf16[512,512]{1,0:T(8,128)(2,1)}, u32[]{:S(2)}) copy-start(bf16[512,512]{1,0:T(8,128)(2,1)} %refs_2_.1) | copy-start | bytes 1572868
  4.5 14.1 %collective-permute-start = (bf16[128,2048]{1,0:T(8,128)(2,1)S(1)}, bf16[128,2048]{1,0:T(8,128)(2,1)S(1)}, u32[]{:S(2)}, u32[]{:S(2)}) collective-permute-start(bf16[128,2048]{1,0:T(8,128)(2,1)S(1)} %constant_dynamic-slice_fusion.refs_11_), channel_id=1, source_target_pairs={{0,4},{4,0},{8,12},{12,8},{1,5},{5,1},{9,13},{13,9},{2,6},{6,2},{1... | collective-permute-start | bytes 1572872 | tf_op jit(solution)/shard_map/ppermute | solution.py:170
  6.2 14.5 %collective-permute-start.5 = (bf16[512,512]{1,0:T(8,128)(2,1)}, bf16[512,512]{1,0:T(8,128)(2,1)S(1)}, u32[]{:S(2)}, u32[]{:S(2)}) collective-permute-start(bf16[512,512]{1,0:T(8,128)(2,1)} %refs_2_.1), channel_id=1, source_target_pairs={{0,1},{1,0},{2,3},{3,2},{4,5},{5,4},{6,7},{7,6},{8,9},{9,8},{10,11... | collective-permute-start | bytes 1572872 | tf_op jit(solution)/shard_map/ppermute | solution.py:201
  7.7 13.1 %collective-permute-start.4 = (bf16[128,2048]{1,0:T(8,128)(2,1)S(1)}, bf16[128,2048]{1,0:T(8,128)(2,1)S(1)}, u32[]{:S(2)}, u32[]{:S(2)}) collective-permute-start(bf16[128,2048]{1,0:T(8,128)(2,1)S(1)} %constant_dynamic-slice_fusion.refs_11_), channel_id=1, source_target_pairs={{4,8},{8,4},{5,9},{9,5},{6,10},{10,6},{7,11},{11,7},{20,24},{24,20... | collective-permute-start | bytes 1572872 | tf_op jit(solution)/shard_map/ppermute | solution.py:179
  8.4 1.2 %copy-start.3 = (bf16[512,1024]{1,0:T(8,128)(2,1)S(1)}, bf16[512,1024]{1,0:T(8,128)(2,1)}, u32[]{:S(2)}) copy-start(bf16[512,1024]{1,0:T(8,128)(2,1)} %mine) | copy-start | bytes 3145732
  18.6 14.1 %collective-permute-start.2 = (bf16[512,512]{1,0:T(8,128)(2,1)S(1)}, bf16[512,512]{1,0:T(8,128)(2,1)S(1)}, u32[]{:S(2)}, u32[]{:S(2)}) collective-permute-start(bf16[512,512]{1,0:T(8,128)(2,1)S(1)} %copy-done.1), channel_id=1, source_target_pairs={{0,3},{1,2},{2,1},{3,0},{4,7},{5,6},{6,5},{7,4},{8,11},{9,10},{10,... | collective-permute-start | bytes 1572872 | tf_op jit(solution)/shard_map/ppermute | solution.py:201
  20.0 12.6 %collective-permute-start.1 = (bf16[128,2048]{1,0:T(8,128)(2,1)S(1)}, bf16[128,2048]{1,0:T(8,128)(2,1)S(1)}, u32[]{:S(2)}, u32[]{:S(2)}) collective-permute-start(bf16[128,2048]{1,0:T(8,128)(2,1)S(1)} %collective-permute-done.refs_12_), channel_id=1, source_target_pairs={{4,8},{8,4},{5,9},{9,5},{6,10},{10,6},{7,11},{11,7},{20,24},{24,20... | collective-permute-start | bytes 1572872 | tf_op jit(solution)/shard_map/ppermute | solution.py:179
  20.8 1.2 %collective-permute-start.11 = (s32[512]{0:T(512)S(1)}, s32[512]{0:T(512)S(1)}, u32[]{:S(2)}, u32[]{:S(2)}) collective-permute-start(s32[512]{0:T(512)S(1)} %add.56), channel_id=1, source_target_pairs={{0,16},{16,0},{1,17},{17,1},{2,18},{18,2},{3,19},{19,3},{4,20},{20... | collective-permute-start | bytes 6152 | tf_op jit(solution)/shard_map/ppermute | solution.py:167
  20.9 6.4 %collective-permute-start.9 = (bf16[512,512]{1,0:T(8,128)(2,1)S(1)}, bf16[512,512]{1,0:T(8,128)(2,1)S(1)}, u32[]{:S(2)}, u32[]{:S(2)}) collective-permute-start(bf16[512,512]{1,0:T(8,128)(2,1)S(1)} %collective-permute-done.5.refs_0_.refs_3_), channel_id=1, source_target_pairs={{0,16},{16,0},{1,17},{17,1},{2,18},{18,2},{3,19},{19,3},{4,20},{20... | collective-permute-start | bytes 1572872 | tf_op jit(solution)/shard_map/ppermute | solution.py:167
  21.4 5.9 %collective-permute-start.10 = (bf16[512,512]{1,0:T(8,128)(2,1)S(1)}, bf16[512,512]{1,0:T(8,128)(2,1)S(1)}, u32[]{:S(2)}, u32[]{:S(2)}) collective-permute-start(bf16[512,512]{1,0:T(8,128)(2,1)S(1)} %collective-permute-done.6.refs_1_.refs_4_), channel_id=1, source_target_pairs={{0,16},{16,0},{1,17},{17,1},{2,18},{18,2},{3,19},{19,3},{4,20},{20... | collective-permute-start | bytes 1572872 | tf_op jit(solution)/shard_map/ppermute | solution.py:167
  22.0 17.1 %collective-permute-start.14 = (bf16[128,2048]{1,0:T(8,128)(2,1)S(1)}, bf16[128,2048]{1,0:T(8,128)(2,1)S(1)}, u32[]{:S(2)}, u32[]{:S(2)}) collective-permute-start(bf16[128,2048]{1,0:T(8,128)(2,1)S(1)} %broadcast_select_fusion), channel_id=1, source_target_pairs={{0,4},{4,0},{8,12},{12,8},{1,5},{5,1},{9,13},{13,9},{2,6},{6,2},{1... | collective-permute-start | bytes 1572872 | tf_op jit(solution)/shard_map/ppermute | solution.py:170
  32.7 6.6 %collective-permute-start.13 = (bf16[512,512]{1,0:T(8,128)(2,1)S(1)}, bf16[512,512]{1,0:T(8,128)(2,1)S(1)}, u32[]{:S(2)}, u32[]{:S(2)}) collective-permute-start(bf16[512,512]{1,0:T(8,128)(2,1)S(1)} %collective-permute-done.2.refs_0_.refs_5_), channel_id=1, source_target_pairs={{0,16},{16,0},{1,17},{17,1},{2,18},{18,2},{3,19},{19,3},{4,20},{20... | collective-permute-start | bytes 1572872 | tf_op jit(solution)/shard_map/ppermute | solution.py:167
  32.7 17.2 %collective-permute-start.12 = (bf16[128,2048]{1,0:T(8,128)(2,1)S(1)}, bf16[128,2048]{1,0:T(8,128)(2,1)S(1)}, u32[]{:S(2)}, u32[]{:S(2)}) collective-permute-start(bf16[128,2048]{1,0:T(8,128)(2,1)S(1)} %broadcast_select_fusion.1), channel_id=1, source_target_pairs={{0,4},{4,0},{8,12},{12,8},{1,5},{5,1},{9,13},{13,9},{2,6},{6,2},{1... | collective-permute-start | bytes 1572872 | tf_op jit(solution)/shard_map/ppermute | solution.py:170
  39.2 2.1 %copy-start.2 = (bf16[512,1024]{1,0:T(8,128)(2,1)S(1)}, bf16[512,1024]{1,0:T(8,128)(2,1)}, u32[]{:S(2)}) copy-start(bf16[512,1024]{1,0:T(8,128)(2,1)} %refs_0_.2) | copy-start | bytes 3145732
  39.2 6.2 %collective-permute-start.15 = (bf16[128,1024]{1,0:T(8,128)(2,1)S(1)}, bf16[128,1024]{1,0:T(8,128)(2,1)S(1)}, u32[]{:S(2)}, u32[]{:S(2)}) collective-permute-start(bf16[128,1024]{1,0:T(8,128)(2,1)S(1)} %pad_maximum_fusion.2), channel_id=1, source_target_pairs={{4,8},{8,4},{5,9},{9,5},{6,10},{10,6},{7,11},{11,7},{20,24},{24,20... | collective-permute-start | bytes 786440 | tf_op jit(solution)/shard_map/ppermute | solution.py:179
  49.9 8.7 %collective-permute-start.18 = (bf16[128,1024]{1,0:T(8,128)(2,1)S(1)}, bf16[128,1024]{1,0:T(8,128)(2,1)S(1)}, u32[]{:S(2)}, u32[]{:S(2)}) collective-permute-start(bf16[128,1024]{1,0:T(8,128)(2,1)S(1)} %maximum_select_fusion.3), channel_id=1, source_target_pairs={{0,4},{4,0},{8,12},{12,8},{1,5},{5,1},{9,13},{13,9},{2,6},{6,2},{1... | collective-permute-start | bytes 786440 | tf_op jit(solution)/shard_map/ppermute | solution.py:170
  51.8 7.7 %collective-permute-start.17 = (bf16[128,2048]{1,0:T(8,128)(2,1)S(1)}, bf16[128,2048]{1,0:T(8,128)(2,1)S(1)}, u32[]{:S(2)}, u32[]{:S(2)}) collective-permute-start(bf16[128,2048]{1,0:T(8,128)(2,1)S(1)} %pad_maximum_fusion.1), channel_id=1, source_target_pairs={{4,8},{8,4},{5,9},{9,5},{6,10},{10,6},{7,11},{11,7},{20,24},{24,20... | collective-permute-start | bytes 1572872 | tf_op jit(solution)/shard_map/ppermute | solution.py:179
  55.1 13.9 %collective-permute-start.16 = (bf16[512,512]{1,0:T(8,128)(2,1)S(1)}, bf16[512,512]{1,0:T(8,128)(2,1)S(1)}, u32[]{:S(2)}, u32[]{:S(2)}) collective-permute-start(bf16[512,512]{1,0:T(8,128)(2,1)S(1)} %maximum_select_fusion.1), channel_id=1, source_target_pairs={{0,4},{4,0},{8,12},{12,8},{1,5},{5,1},{9,13},{13,9},{2,6},{6,2},{1... | collective-permute-start | bytes 1572872 | tf_op jit(solution)/shard_map/ppermute | solution.py:170
  58.7 0.8 collective-permute-start.19
  69.4 21.6 %collective-permute-start.20 = (f32[128,2048]{1,0:T(8,128)S(1)}, f32[128,2048]{1,0:T(8,128)S(1)}, u32[]{:S(2)}, u32[]{:S(2)}) collective-permute-start(f32[128,2048]{1,0:T(8,128)S(1)} %pad_maximum_fusion.mine), channel_id=1, source_target_pairs={{0,16},{16,0},{1,17},{17,1},{2,18},{18,2},{3,19},{19,3},{4,20},{20... | collective-permute-start | bytes 3145736 | tf_op jit(solution)/shard_map/ppermute | solution.py:167
  69.5 19.3 %collective-permute-start.21 = (bf16[128,1536]{1,0:T(8,128)(2,1)S(1)}, bf16[128,1536]{1,0:T(8,128)(2,1)S(1)}, u32[]{:S(2)}, u32[]{:S(2)}) collective-permute-start(bf16[128,1536]{1,0:T(8,128)(2,1)S(1)} %maximum_select_fusion.2), channel_id=1, source_target_pairs={{0,4},{4,0},{8,12},{12,8},{1,5},{5,1},{9,13},{13,9},{2,6},{6,2},{1... | collective-permute-start | bytes 1179656 | tf_op jit(solution)/shard_map/ppermute | solution.py:170
  73.6 15.2 %collective-permute-start.24 = (bf16[256,512]{1,0:T(8,128)(2,1)S(1)}, bf16[256,512]{1,0:T(8,128)(2,1)S(1)}, u32[]{:S(2)}, u32[]{:S(2)}) collective-permute-start(bf16[256,512]{1,0:T(8,128)(2,1)S(1)} %get-tuple-element.126), channel_id=1, source_target_pairs={{0,8},{4,12},{8,0},{12,4},{1,9},{5,13},{9,1},{13,5},{2,10},{6,14},... | collective-permute-start | bytes 786440 | tf_op jit(solution)/shard_map/ppermute | solution.py:204
  74.4 14.9 %collective-permute-start.23 = (f32[256,512]{1,0:T(8,128)S(1)}, f32[256,512]{1,0:T(8,128)S(1)}, u32[]{:S(2)}, u32[]{:S(2)}) collective-permute-start(f32[256,512]{1,0:T(8,128)S(1)} %get-tuple-element.127.key_mine), channel_id=1, source_target_pairs={{0,16},{16,0},{1,17},{17,1},{2,18},{18,2},{3,19},{19,3},{4,20},{20... | collective-permute-start | bytes 1572872 | tf_op jit(solution)/shard_map/ppermute | solution.py:167
  88.8 2.1 %collective-permute-start.22 = (bf16[128,1536]{1,0:T(8,128)(2,1)S(1)}, bf16[128,1536]{1,0:T(8,128)(2,1)S(1)}, u32[]{:S(2)}, u32[]{:S(2)}) collective-permute-start(bf16[128,1536]{1,0:T(8,128)(2,1)S(1)} %collective-permute-done.21.last), channel_id=1, source_target_pairs={{0,16},{16,0},{1,17},{17,1},{2,18},{18,2},{3,19},{19,3},{4,20},{20... | collective-permute-start | bytes 1179656 | tf_op jit(solution)/shard_map/ppermute | solution.py:167
  88.8 2.1 %collective-permute-start.25 = (bf16[256,512]{1,0:T(8,128)(2,1)S(1)}, bf16[256,512]{1,0:T(8,128)(2,1)S(1)}, u32[]{:S(2)}, u32[]{:S(2)}) collective-permute-start(bf16[256,512]{1,0:T(8,128)(2,1)S(1)} %collective-permute-done.24.key_last), channel_id=1, source_target_pairs={{0,16},{16,0},{1,17},{17,1},{2,18},{18,2},{3,19},{19,3},{4,20},{20... | collective-permute-start | bytes 786440 | tf_op jit(solution)/shard_map/ppermute | solution.py:167

commit v9 on v8

--- a/solution.py
+++ b/solution.py
@@ -272,8 +272,7 @@
     keep = joined(keep_a, keep_b)
     b1 = inner(far_plus(term1, i1))
     b2 = inner(far_plus(term2, i2))
-    got = phase((outer(joined(send_a, send_b)), b1, b2, term0, term1, term2, keep, i2))
-    k1, b1, b2, term0, term1, term2, keep, i2 = got
+    k1, b1, keep, i2, term0 = phase((outer(joined(send_a, send_b)), b1, keep, i2, term0))
 
     k2 = across(plus(keep[keys:], k1[keys:]))
     back1 = plus(term1[2 * half : 3 * half], b1[:, : 2 * heads])

time: 93.6 us -> 93.5 us (level)
  no operation moved by 1% of the time
where the time goes in v9:
time: 93.5 us; the launch traced here: 93.2 us
  waiting for transfers between devices  45.1 us (48%)
  starting transfers between devices  28.4 us (30%)
  Pallas kernels  15.7 us (17%)
  local copies, waits for them, and re-layouts  1.47 us (2%)
  other arithmetic  1.46 us (2%)
  between operations  1.05 us (1%)
    ppermute x6, waiting for transfers between devices, outer(): return lax.ppermute(v, 'fsdp', [(0, 1), (1, 0), (2, 3), (3, 2)])  39.4 us
    ppermute x6, starting transfers between devices, outer(): return lax.ppermute(v, 'fsdp', [(0, 1), (1, 0), (2, 3), (3, 2)])  16 us
    pallas_call x7, Pallas kernels, call(): pl.pallas_call(kernel, out_shape=out, in_specs=[smem] + [vmem] * len(args...  13.3 us
    ppermute x3, starting transfers between devices, square(): return lax.ppermute(v, 'tp', [(i, i ^ d) for i in range(4)])  5.52 us
    ppermute x5, starting transfers between devices, inner(): return lax.ppermute(v, 'fsdp', [(1, 2), (2, 1)])  3.55 us
    ppermute x3, waiting for transfers between devices, square(): return lax.ppermute(v, 'tp', [(i, i ^ d) for i in range(4)])  3.54 us
    ppermute x11, starting transfers between devices, core_swap(): return lax.ppermute(v, 'dp', [(0, 1), (1, 0)])  2.47 us
    pallas_call x1, Pallas kernels, pair_body(): pl.pallas_call(join_kernel, out_shape=outs, in_specs=[smem] + [vmem] * 8,...  2.37 us
  transfers between devices with their start and end apart: 26, of which 9 were waited for; matrix products, arithmetic and copies ran while one was open for 1% of the time, Pallas kernels for 14%

profile of v9, /device:TPU:0, one launch (start us, length us, event | category | flops | bytes accessed | tf_op | source)
XLA Modules:
  0.0 93.2 jit_solution(13767043384775948876)
XLA Ops:
  0.6 0.0 copy-start
  0.7 0.1 stack.57.place
  0.8 0.5 collective-permute-start.3
  1.3 0.1 collective-permute-start.7
  1.4 0.4 collective-permute-start.8
  1.8 2.6 %collective-permute-start.6 = (bf16[512,512]{1,0:T(8,128)(2,1)}, bf16[512,512]{1,0:T(8,128)(2,1)S(1)}, u32[]{:S(2)}, u32[]{:S(2)}) collective-permute-start(bf16[512,512]{1,0:T(8,128)(2,1)} %refs_2_.1), channel_id=1, source_target_pairs={{0,2},{1,3},{2,0},{3,1},{4,6},{5,7},{6,4},{7,5},{8,10},{9,11},{10,... | collective-permute-start | bytes 1572872 | tf_op jit(solution)/shard_map/ppermute | solution.py:201
  4.4 0.1 constant_dynamic-slice_fusion.refs_11_
  4.5 0.0 copy-start.1
  4.5 1.6 %collective-permute-start = (bf16[128,2048]{1,0:T(8,128)(2,1)S(1)}, bf16[128,2048]{1,0:T(8,128)(2,1)S(1)}, u32[]{:S(2)}, u32[]{:S(2)}) collective-permute-start(bf16[128,2048]{1,0:T(8,128)(2,1)S(1)} %constant_dynamic-slice_fusion.refs_11_), channel_id=1, source_target_pairs={{0,4},{4,0},{8,12},{12,8},{1,5},{5,1},{9,13},{13,9},{2,6},{6,2},{1... | collective-permute-start | bytes 1572872 | tf_op jit(solution)/shard_map/ppermute | solution.py:170
  6.2 0.0 collective-permute-done.3.other
  6.2 1.5 %collective-permute-start.5 = (bf16[512,512]{1,0:T(8,128)(2,1)}, bf16[512,512]{1,0:T(8,128)(2,1)S(1)}, u32[]{:S(2)}, u32[]{:S(2)}) collective-permute-start(bf16[512,512]{1,0:T(8,128)(2,1)} %refs_2_.1), channel_id=1, source_target_pairs={{0,1},{1,0},{2,3},{3,2},{4,5},{5,4},{6,7},{7,6},{8,9},{9,8},{10,11... | collective-permute-start | bytes 1572872 | tf_op jit(solution)/shard_map/ppermute | solution.py:201
  7.7 0.0 collective-permute-done.7.refs_1_.refs_6_
  7.7 0.7 collective-permute-start.4
  8.4 0.0 copy-start.3
  8.4 1.2 %copy-done.3 = bf16[512,1024]{1,0:T(8,128)(2,1)S(1)} copy-done((bf16[512,1024]{1,0:T(8,128)(2,1)S(1)}, bf16[512,1024]{1,0:T(8,128)(2,1)}, u32[]{:S(2)}) %copy-start.3) | copy-done | bytes 1048600
  9.6 1.6 %shard_map.77.turned = bf16[2,512,512]{2,1,0:T(8,128)(2,1)S(1)} custom-call(s32[15]{0:T(128)S(1)} %stack.57.place, bf16[512,1024]{1,0:T(8,128)(2,1)S(1)} %copy-done.3, bf16[512,1024]{1,0:T(8,128)(2,1)} %collective-permute-done.3.other), custom_call_target="tpu_custom_call" | custom-call | flops 1073741824 | bytes 1048576 | tf_op jit(solution)/shard_map/pallas_call | solution.py:190
  11.2 1.2 %shard_map.78 = (f32[512,512]{1,0:T(8,128)S(1)}, bf16[128,2048]{1,0:T(8,128)(2,1)S(1)}) custom-call(s32[15]{0:T(128)S(1)} %stack.57.place, bf16[2,512,512]{2,1,0:T(8,128)(2,1)S(1)} %shard_map.77.turned, bf16[512,512]{1,0:T(8,128)(2,1)S(1)} %copy-done.1, bf16[512,512]{1,0:T(8,128)(2,1)S(1)} %collective-permute-done.7.refs_1_.refs_6_), custom_call_target="tpu_custom_call" | custom-call | tf_op jit(solution)/shard_map/pallas_call | solution.py:190
  12.4 6.2 %collective-permute-done.refs_12_ = bf16[128,2048]{1,0:T(8,128)(2,1)S(1)} collective-permute-done((bf16[128,2048]{1,0:T(8,128)(2,1)S(1)}, bf16[128,2048]{1,0:T(8,128)(2,1)S(1)}, u32[]{:S(2)}, u32[]{:S(2)}) %collective-permute-start) | collective-permute-done | bytes 524320 | tf_op jit(solution)/shard_map/ppermute | solution.py:170
  18.6 1.4 %collective-permute-start.2 = (bf16[512,512]{1,0:T(8,128)(2,1)S(1)}, bf16[512,512]{1,0:T(8,128)(2,1)S(1)}, u32[]{:S(2)}, u32[]{:S(2)}) collective-permute-start(bf16[512,512]{1,0:T(8,128)(2,1)S(1)} %copy-done.1), channel_id=1, source_target_pairs={{0,3},{1,2},{2,1},{3,0},{4,7},{5,6},{6,5},{7,4},{8,11},{9,10},{10,... | collective-permute-start | bytes 1572872 | tf_op jit(solution)/shard_map/ppermute | solution.py:201
  20.0 0.7 collective-permute-start.1
  20.8 0.1 collective-permute-start.11
  20.9 0.5 collective-permute-start.9
  21.4 0.1 collective-permute-start.10
  21.5 0.1 broadcast_select_fusion
  21.5 0.5 collective-permute-done.11
  22.0 4.4 %collective-permute-start.14 = (bf16[128,2048]{1,0:T(8,128)(2,1)S(1)}, bf16[128,2048]{1,0:T(8,128)(2,1)S(1)}, u32[]{:S(2)}, u32[]{:S(2)}) collective-permute-start(bf16[128,2048]{1,0:T(8,128)(2,1)S(1)} %broadcast_select_fusion), channel_id=1, source_target_pairs={{0,4},{4,0},{8,12},{12,8},{1,5},{5,1},{9,13},{13,9},{2,6},{6,2},{1... | collective-permute-start | bytes 1572872 | tf_op jit(solution)/shard_map/ppermute | solution.py:170
  26.4 0.9 shard_map.80.refs_10_
  27.3 1.8 %shard_map.79 = (f32[512,1024]{1,0:T(8,128)S(1)}, bf16[128,2048]{1,0:T(8,128)(2,1)S(1)}, bf16[128,1024]{1,0:T(8,128)(2,1)S(1)}) custom-call(s32[15]{0:T(128)S(1)} %stack.57.place, bf16[2,512,512]{2,1,0:T(8,128)(2,1)S(1)} %shard_map.77.turned, bf16[512,512]{1,0:T(8,128)(2,1)S(1)} %collective-permute-done.5.refs_0_.refs_3_, ...), custom_call_target="tpu_custom_call" | custom-call | tf_op jit(solution)/shard_map/pallas_call | solution.py:190
  29.1 3.5 %collective-permute-done.2.refs_0_.refs_5_ = bf16[512,512]{1,0:T(8,128)(2,1)S(1)} collective-permute-done((bf16[512,512]{1,0:T(8,128)(2,1)S(1)}, bf16[512,512]{1,0:T(8,128)(2,1)S(1)}, u32[]{:S(2)}, u32[]{:S(2)}) %collective-permute-start.2) | collective-permute-done | bytes 524320 | tf_op jit(solution)/shard_map/ppermute | solution.py:201
  32.7 0.1 broadcast_select_fusion.1
  32.7 3.8 %collective-permute-start.12 = (bf16[128,2048]{1,0:T(8,128)(2,1)S(1)}, bf16[128,2048]{1,0:T(8,128)(2,1)S(1)}, u32[]{:S(2)}, u32[]{:S(2)}) collective-permute-start(bf16[128,2048]{1,0:T(8,128)(2,1)S(1)} %broadcast_select_fusion.1), channel_id=1, source_target_pairs={{0,4},{4,0},{8,12},{12,8},{1,5},{5,1},{9,13},{13,9},{2,6},{6,2},{1... | collective-permute-start | bytes 1572872 | tf_op jit(solution)/shard_map/ppermute | solution.py:170
  36.5 2.6 %collective-permute-done.14.refs_14_ = bf16[128,2048]{1,0:T(8,128)(2,1)S(1)} collective-permute-done((bf16[128,2048]{1,0:T(8,128)(2,1)S(1)}, bf16[128,2048]{1,0:T(8,128)(2,1)S(1)}, u32[]{:S(2)}, u32[]{:S(2)}) %collective-permute-start.14) | collective-permute-done | bytes 524320 | tf_op jit(solution)/shard_map/ppermute | solution.py:170
  39.1 0.1 add_convert_fusion.9
  39.2 0.0 copy-start.2
  39.2 0.8 collective-permute-start.15
  40.1 1.2 %shard_map.81 = (f32[512,512]{1,0:T(8,128)S(1)}, bf16[128,1024]{1,0:T(8,128)(2,1)S(1)}, bf16[128,512]{1,0:T(8,128)(2,1)S(1)}) custom-call(s32[15]{0:T(128)S(1)} %stack.57.place, bf16[2,512,512]{2,1,0:T(8,128)(2,1)S(1)} %shard_map.77.turned, bf16[512,512]{1,0:T(8,128)(2,1)S(1)} %collective-permute-done.2.refs_0_.refs_5_, ...), custom_call_target="tpu_custom_call" | custom-call | flops 2147483648 | bytes 1048576 | tf_op jit(solution)/shard_map/pallas_call | solution.py:190
  41.3 4.2 %shard_map.82 = (bf16[512,384]{1,0:T(8,128)(2,1)S(1)}, f32[512,384]{1,0:T(8,128)S(1)}, bf16[512,128]{1,0:T(8,128)(2,1)S(1)}, f32[512,128]{1,0:T(8,128)S(1)}) custom-call(s32[15]{0:T(128)S(1)} %stack.57.place, bf16[512,1024]{1,0:T(8,128)(2,1)S(1)} %copy-done.2, bf16[512,1024]{1,0:T(8,128)(2,1)S(1)} %collective-permute-done.8.refs_1_, ...), custom_call_target="tpu_custom_call" | custom-call | flops 1073741824 | bytes 1048576 | tf_op jit(solution)/shard_map/pallas_call | solution.py:190
  45.5 0.1 maximum_select_fusion.3
  45.6 4.3 %collective-permute-done.12.refs_11_ = bf16[128,2048]{1,0:T(8,128)(2,1)S(1)} collective-permute-done((bf16[128,2048]{1,0:T(8,128)(2,1)S(1)}, bf16[128,2048]{1,0:T(8,128)(2,1)S(1)}, u32[]{:S(2)}, u32[]{:S(2)}) %collective-permute-start.12) | collective-permute-done | bytes 524320 | tf_op jit(solution)/shard_map/ppermute | solution.py:170
  49.9 1.7 %collective-permute-start.18 = (bf16[128,1024]{1,0:T(8,128)(2,1)S(1)}, bf16[128,1024]{1,0:T(8,128)(2,1)S(1)}, u32[]{:S(2)}, u32[]{:S(2)}) collective-permute-start(bf16[128,1024]{1,0:T(8,128)(2,1)S(1)} %maximum_select_fusion.3), channel_id=1, source_target_pairs={{0,4},{4,0},{8,12},{12,8},{1,5},{5,1},{9,13},{13,9},{2,6},{6,2},{1... | collective-permute-start | bytes 786440 | tf_op jit(solution)/shard_map/ppermute | solution.py:170
  51.6 0.1 add_convert_fusion.3
  51.8 0.7 collective-permute-start.17
  52.5 2.4 %shard_map.83 = (bf16[512,128]{1,0:T(8,128)(2,1)S(1)}, f32[512,128]{1,0:T(8,128)S(1)}) custom-call(s32[15]{0:T(128)S(1)} %stack.57.place, bf16[512,1024]{1,0:T(8,128)(2,1)S(1)} %copy-done.2, bf16[512,1024]{1,0:T(8,128)(2,1)S(1)} %collective-permute-done.8.refs_1_, bf16[512,512]{1,0:T(8,128)(2,1)S(1)} %copy-done.1, ...), custom_call_target="tpu_custom_call" | custom-call | flops 536870912 | bytes 1048576 | tf_op jit(solution)/shard_map/pallas_call | solution.py:190
  55.0 0.1 maximum_select_fusion.1
  55.1 0.7 collective-permute-start.16
  55.9 0.1 maximum_select_fusion
  56.0 2.6 %collective-permute-done.18 = bf16[128,1024]{1,0:T(8,128)(2,1)S(1)} collective-permute-done((bf16[128,1024]{1,0:T(8,128)(2,1)S(1)}, bf16[128,1024]{1,0:T(8,128)(2,1)S(1)}, u32[]{:S(2)}, u32[]{:S(2)}) %collective-permute-start.18) | collective-permute-done | bytes 262176 | tf_op jit(solution)/shard_map/ppermute | solution.py:170
  58.6 0.1 add_convert_fusion.6
  58.7 0.7 collective-permute-start.19
  59.4 9.6 %collective-permute-done.16 = bf16[512,512]{1,0:T(8,128)(2,1)S(1)} collective-permute-done((bf16[512,512]{1,0:T(8,128)(2,1)S(1)}, bf16[512,512]{1,0:T(8,128)(2,1)S(1)}, u32[]{:S(2)}, u32[]{:S(2)}) %collective-permute-start.16) | collective-permute-done | bytes 524320 | tf_op jit(solution)/shard_map/ppermute | solution.py:170
  69.0 0.1 add_convert_fusion.1
  69.1 0.1 add_convert_fusion.4
  69.2 0.1 convert_add_fusion.3
  69.3 0.1 pad_maximum_fusion.mine
  69.4 0.1 collective-permute-start.20
  69.4 0.1 maximum_select_fusion.2
  69.6 3.8 %collective-permute-start.21 = (bf16[128,1536]{1,0:T(8,128)(2,1)S(1)}, bf16[128,1536]{1,0:T(8,128)(2,1)S(1)}, u32[]{:S(2)}, u32[]{:S(2)}) collective-permute-start(bf16[128,1536]{1,0:T(8,128)(2,1)S(1)} %maximum_select_fusion.2), channel_id=1, source_target_pairs={{0,4},{4,0},{8,12},{12,8},{1,5},{5,1},{9,13},{13,9},{2,6},{6,2},{1... | collective-permute-start | bytes 1179656 | tf_op jit(solution)/shard_map/ppermute | solution.py:170
  73.3 0.1 add_convert_fusion
  73.5 0.8 collective-permute-start.24
  74.3 0.2 collective-permute-start.23
  74.5 14.2 %collective-permute-done.21.last = bf16[128,1536]{1,0:T(8,128)(2,1)S(1)} collective-permute-done((bf16[128,1536]{1,0:T(8,128)(2,1)S(1)}, bf16[128,1536]{1,0:T(8,128)(2,1)S(1)}, u32[]{:S(2)}, u32[]{:S(2)}) %collective-permute-start.21) | collective-permute-done | bytes 393248 | tf_op jit(solution)/shard_map/ppermute | solution.py:170
  88.7 0.5 collective-permute-start.25
  89.2 1.6 %collective-permute-done.25.key_last_pair = bf16[256,512]{1,0:T(8,128)(2,1)S(1)} collective-permute-done((bf16[256,512]{1,0:T(8,128)(2,1)S(1)}, bf16[256,512]{1,0:T(8,128)(2,1)S(1)}, u32[]{:S(2)}, u32[]{:S(2)}) %collective-permute-start.25) | collective-permute-done | bytes 262176 | tf_op jit(solution)/shard_map/ppermute | solution.py:167
  90.8 2.4 %shard_map.84 = (f32[256,2048]{1,0:T(8,128)}, f32[256,1024]{1,0:T(8,128)}) custom-call(s32[15]{0:T(128)S(1)} %stack.57.place, f32[128,2048]{1,0:T(8,128)S(1)} %pad_maximum_fusion.mine, f32[128,2048]{1,0:T(8,128)S(1)} %collective-permute-done.20.pair, bf16[128,1536]{1,0:T(8,128)(2,1)S(1)} %collective-permute-done.21.last, ...), custom_call_target="tpu_custom_call" | custom-call | bytes 1048576 | tf_op jit(solution)/shard_map/pallas_call | solution.py:291
  (31 shorter events, 0.2 us)
Async XLA Ops:
  0.6 3.8 %copy-start = (bf16[256,2048]{1,0:T(8,128)(2,1)S(1)}, bf16[256,2048]{1,0:T(8,128)(2,1)}, u32[]{:S(2)}) copy-start(bf16[256,2048]{1,0:T(8,128)(2,1)} %param.9) | copy-start | bytes 3145732
  0.8 5.4 %collective-permute-start.3 = (bf16[512,1024]{1,0:T(8,128)(2,1)}, bf16[512,1024]{1,0:T(8,128)(2,1)}, u32[]{:S(2)}, u32[]{:S(2)}) collective-permute-start(bf16[512,1024]{1,0:T(8,128)(2,1)} %mine), channel_id=1, source_target_pairs={{0,16},{16,0},{1,17},{17,1},{2,18},{18,2},{3,19},{19,3},{4,20},{20... | collective-permute-start | bytes 3145736 | tf_op jit(solution)/shard_map/ppermute | solution.py:167
  1.3 6.4 %collective-permute-start.7 = (bf16[512,512]{1,0:T(8,128)(2,1)}, bf16[512,512]{1,0:T(8,128)(2,1)S(1)}, u32[]{:S(2)}, u32[]{:S(2)}) collective-permute-start(bf16[512,512]{1,0:T(8,128)(2,1)} %refs_2_.1), channel_id=1, source_target_pairs={{0,16},{16,0},{1,17},{17,1},{2,18},{18,2},{3,19},{19,3},{4,20},{20... | collective-permute-start | bytes 1572872 | tf_op jit(solution)/shard_map/ppermute | solution.py:167
  1.4 19.4 %collective-permute-start.8 = (bf16[512,1024]{1,0:T(8,128)(2,1)}, bf16[512,1024]{1,0:T(8,128)(2,1)S(1)}, u32[]{:S(2)}, u32[]{:S(2)}) collective-permute-start(bf16[512,1024]{1,0:T(8,128)(2,1)} %refs_0_.2), channel_id=1, source_target_pairs={{0,16},{16,0},{1,17},{17,1},{2,18},{18,2},{3,19},{19,3},{4,20},{20... | collective-permute-start | bytes 3145736 | tf_op jit(solution)/shard_map/ppermute | solution.py:167
  1.8 18.2 %collective-permute-start.6 = (bf16[512,512]{1,0:T(8,128)(2,1)}, bf16[512,512]{1,0:T(8,128)(2,1)S(1)}, u32[]{:S(2)}, u32[]{:S(2)}) collective-permute-start(bf16[512,512]{1,0:T(8,128)(2,1)} %refs_2_.1), channel_id=1, source_target_pairs={{0,2},{1,3},{2,0},{3,1},{4,6},{5,7},{6,4},{7,5},{8,10},{9,11},{10,... | collective-permute-start | bytes 1572872 | tf_op jit(solution)/shard_map/ppermute | solution.py:201
  4.4 16.4 %copy-start.5 = (s32[512,1]{0,1:T(1,128)S(1)}, s32[512,1]{0,1:T(1,128)}, u32[]{:S(2)}) copy-start(s32[512,1]{0,1:T(1,128)} %param.10) | copy-start | bytes 6148
  4.4 16.4 %copy-start.4 = (s32[512]{0:T(512)S(1)}, s32[512]{0:T(512)}, u32[]{:S(2)}) copy-start(s32[512]{0:T(512)} %param.11) | copy-start | bytes 6148
  4.5 6.6 %copy-start.1 = (bf16[512,512]{1,0:T(8,128)(2,1)S(1)}, bf16[512,512]{1,0:T(8,128)(2,1)}, u32[]{:S(2)}) copy-start(bf16[512,512]{1,0:T(8,128)(2,1)} %refs_2_.1) | copy-start | bytes 1572868
  4.5 14.1 %collective-permute-start = (bf16[128,2048]{1,0:T(8,128)(2,1)S(1)}, bf16[128,2048]{1,0:T(8,128)(2,1)S(1)}, u32[]{:S(2)}, u32[]{:S(2)}) collective-permute-start(bf16[128,2048]{1,0:T(8,128)(2,1)S(1)} %constant_dynamic-slice_fusion.refs_11_), channel_id=1, source_target_pairs={{0,4},{4,0},{8,12},{12,8},{1,5},{5,1},{9,13},{13,9},{2,6},{6,2},{1... | collective-permute-start | bytes 1572872 | tf_op jit(solution)/shard_map/ppermute | solution.py:170
  6.2 14.5 %collective-permute-start.5 = (bf16[512,512]{1,0:T(8,128)(2,1)}, bf16[512,512]{1,0:T(8,128)(2,1)S(1)}, u32[]{:S(2)}, u32[]{:S(2)}) collective-permute-start(bf16[512,512]{1,0:T(8,128)(2,1)} %refs_2_.1), channel_id=1, source_target_pairs={{0,1},{1,0},{2,3},{3,2},{4,5},{5,4},{6,7},{7,6},{8,9},{9,8},{10,11... | collective-permute-start | bytes 1572872 | tf_op jit(solution)/shard_map/ppermute | solution.py:201
  7.7 13.1 %collective-permute-start.4 = (bf16[128,2048]{1,0:T(8,128)(2,1)S(1)}, bf16[128,2048]{1,0:T(8,128)(2,1)S(1)}, u32[]{:S(2)}, u32[]{:S(2)}) collective-permute-start(bf16[128,2048]{1,0:T(8,128)(2,1)S(1)} %constant_dynamic-slice_fusion.refs_11_), channel_id=1, source_target_pairs={{4,8},{8,4},{5,9},{9,5},{6,10},{10,6},{7,11},{11,7},{20,24},{24,20... | collective-permute-start | bytes 1572872 | tf_op jit(solution)/shard_map/ppermute | solution.py:179
  8.4 1.2 %copy-start.3 = (bf16[512,1024]{1,0:T(8,128)(2,1)S(1)}, bf16[512,1024]{1,0:T(8,128)(2,1)}, u32[]{:S(2)}) copy-start(bf16[512,1024]{1,0:T(8,128)(2,1)} %mine) | copy-start | bytes 3145732
  18.6 14.1 %collective-permute-start.2 = (bf16[512,512]{1,0:T(8,128)(2,1)S(1)}, bf16[512,512]{1,0:T(8,128)(2,1)S(1)}, u32[]{:S(2)}, u32[]{:S(2)}) collective-permute-start(bf16[512,512]{1,0:T(8,128)(2,1)S(1)} %copy-done.1), channel_id=1, source_target_pairs={{0,3},{1,2},{2,1},{3,0},{4,7},{5,6},{6,5},{7,4},{8,11},{9,10},{10,... | collective-permute-start | bytes 1572872 | tf_op jit(solution)/shard_map/ppermute | solution.py:201
  20.0 12.6 %collective-permute-start.1 = (bf16[128,2048]{1,0:T(8,128)(2,1)S(1)}, bf16[128,2048]{1,0:T(8,128)(2,1)S(1)}, u32[]{:S(2)}, u32[]{:S(2)}) collective-permute-start(bf16[128,2048]{1,0:T(8,128)(2,1)S(1)} %collective-permute-done.refs_12_), channel_id=1, source_target_pairs={{4,8},{8,4},{5,9},{9,5},{6,10},{10,6},{7,11},{11,7},{20,24},{24,20... | collective-permute-start | bytes 1572872 | tf_op jit(solution)/shard_map/ppermute | solution.py:179
  20.8 1.2 %collective-permute-start.11 = (s32[512]{0:T(512)S(1)}, s32[512]{0:T(512)S(1)}, u32[]{:S(2)}, u32[]{:S(2)}) collective-permute-start(s32[512]{0:T(512)S(1)} %add.56), channel_id=1, source_target_pairs={{0,16},{16,0},{1,17},{17,1},{2,18},{18,2},{3,19},{19,3},{4,20},{20... | collective-permute-start | bytes 6152 | tf_op jit(solution)/shard_map/ppermute | solution.py:167
  20.9 6.4 %collective-permute-start.9 = (bf16[512,512]{1,0:T(8,128)(2,1)S(1)}, bf16[512,512]{1,0:T(8,128)(2,1)S(1)}, u32[]{:S(2)}, u32[]{:S(2)}) collective-permute-start(bf16[512,512]{1,0:T(8,128)(2,1)S(1)} %collective-permute-done.5.refs_0_.refs_3_), channel_id=1, source_target_pairs={{0,16},{16,0},{1,17},{17,1},{2,18},{18,2},{3,19},{19,3},{4,20},{20... | collective-permute-start | bytes 1572872 | tf_op jit(solution)/shard_map/ppermute | solution.py:167
  21.4 5.9 %collective-permute-start.10 = (bf16[512,512]{1,0:T(8,128)(2,1)S(1)}, bf16[512,512]{1,0:T(8,128)(2,1)S(1)}, u32[]{:S(2)}, u32[]{:S(2)}) collective-permute-start(bf16[512,512]{1,0:T(8,128)(2,1)S(1)} %collective-permute-done.6.refs_1_.refs_4_), channel_id=1, source_target_pairs={{0,16},{16,0},{1,17},{17,1},{2,18},{18,2},{3,19},{19,3},{4,20},{20... | collective-permute-start | bytes 1572872 | tf_op jit(solution)/shard_map/ppermute | solution.py:167
  22.0 17.1 %collective-permute-start.14 = (bf16[128,2048]{1,0:T(8,128)(2,1)S(1)}, bf16[128,2048]{1,0:T(8,128)(2,1)S(1)}, u32[]{:S(2)}, u32[]{:S(2)}) collective-permute-start(bf16[128,2048]{1,0:T(8,128)(2,1)S(1)} %broadcast_select_fusion), channel_id=1, source_target_pairs={{0,4},{4,0},{8,12},{12,8},{1,5},{5,1},{9,13},{13,9},{2,6},{6,2},{1... | collective-permute-start | bytes 1572872 | tf_op jit(solution)/shard_map/ppermute | solution.py:170
  32.7 6.6 %collective-permute-start.13 = (bf16[512,512]{1,0:T(8,128)(2,1)S(1)}, bf16[512,512]{1,0:T(8,128)(2,1)S(1)}, u32[]{:S(2)}, u32[]{:S(2)}) collective-permute-start(bf16[512,512]{1,0:T(8,128)(2,1)S(1)} %collective-permute-done.2.refs_0_.refs_5_), channel_id=1, source_target_pairs={{0,16},{16,0},{1,17},{17,1},{2,18},{18,2},{3,19},{19,3},{4,20},{20... | collective-permute-start | bytes 1572872 | tf_op jit(solution)/shard_map/ppermute | solution.py:167
  32.7 17.2 %collective-permute-start.12 = (bf16[128,2048]{1,0:T(8,128)(2,1)S(1)}, bf16[128,2048]{1,0:T(8,128)(2,1)S(1)}, u32[]{:S(2)}, u32[]{:S(2)}) collective-permute-start(bf16[128,2048]{1,0:T(8,128)(2,1)S(1)} %broadcast_select_fusion.1), channel_id=1, source_target_pairs={{0,4},{4,0},{8,12},{12,8},{1,5},{5,1},{9,13},{13,9},{2,6},{6,2},{1... | collective-permute-start | bytes 1572872 | tf_op jit(solution)/shard_map/ppermute | solution.py:170
  39.2 2.1 %copy-start.2 = (bf16[512,1024]{1,0:T(8,128)(2,1)S(1)}, bf16[512,1024]{1,0:T(8,128)(2,1)}, u32[]{:S(2)}) copy-start(bf16[512,1024]{1,0:T(8,128)(2,1)} %refs_0_.2) | copy-start | bytes 3145732
  39.2 6.2 %collective-permute-start.15 = (bf16[128,1024]{1,0:T(8,128)(2,1)S(1)}, bf16[128,1024]{1,0:T(8,128)(2,1)S(1)}, u32[]{:S(2)}, u32[]{:S(2)}) collective-permute-start(bf16[128,1024]{1,0:T(8,128)(2,1)S(1)} %pad_maximum_fusion.2), channel_id=1, source_target_pairs={{4,8},{8,4},{5,9},{9,5},{6,10},{10,6},{7,11},{11,7},{20,24},{24,20... | collective-permute-start | bytes 786440 | tf_op jit(solution)/shard_map/ppermute | solution.py:179
  49.9 8.7 %collective-permute-start.18 = (bf16[128,1024]{1,0:T(8,128)(2,1)S(1)}, bf16[128,1024]{1,0:T(8,128)(2,1)S(1)}, u32[]{:S(2)}, u32[]{:S(2)}) collective-permute-start(bf16[128,1024]{1,0:T(8,128)(2,1)S(1)} %maximum_select_fusion.3), channel_id=1, source_target_pairs={{0,4},{4,0},{8,12},{12,8},{1,5},{5,1},{9,13},{13,9},{2,6},{6,2},{1... | collective-permute-start | bytes 786440 | tf_op jit(solution)/shard_map/ppermute | solution.py:170
  51.8 7.6 %collective-permute-start.17 = (bf16[128,2048]{1,0:T(8,128)(2,1)S(1)}, bf16[128,2048]{1,0:T(8,128)(2,1)S(1)}, u32[]{:S(2)}, u32[]{:S(2)}) collective-permute-start(bf16[128,2048]{1,0:T(8,128)(2,1)S(1)} %pad_maximum_fusion.1), channel_id=1, source_target_pairs={{4,8},{8,4},{5,9},{9,5},{6,10},{10,6},{7,11},{11,7},{20,24},{24,20... | collective-permute-start | bytes 1572872 | tf_op jit(solution)/shard_map/ppermute | solution.py:179
  55.1 13.9 %collective-permute-start.16 = (bf16[512,512]{1,0:T(8,128)(2,1)S(1)}, bf16[512,512]{1,0:T(8,128)(2,1)S(1)}, u32[]{:S(2)}, u32[]{:S(2)}) collective-permute-start(bf16[512,512]{1,0:T(8,128)(2,1)S(1)} %maximum_select_fusion.1), channel_id=1, source_target_pairs={{0,4},{4,0},{8,12},{12,8},{1,5},{5,1},{9,13},{13,9},{2,6},{6,2},{1... | collective-permute-start | bytes 1572872 | tf_op jit(solution)/shard_map/ppermute | solution.py:170
  58.7 10.4 %collective-permute-start.19 = (bf16[128,1024]{1,0:T(8,128)(2,1)S(1)}, bf16[128,1024]{1,0:T(8,128)(2,1)S(1)}, u32[]{:S(2)}, u32[]{:S(2)}) collective-permute-start(bf16[128,1024]{1,0:T(8,128)(2,1)S(1)} %pad_maximum_fusion.3), channel_id=1, source_target_pairs={{4,8},{8,4},{5,9},{9,5},{6,10},{10,6},{7,11},{11,7},{20,24},{24,20... | collective-permute-start | bytes 786440 | tf_op jit(solution)/shard_map/ppermute | solution.py:179
  69.4 21.4 %collective-permute-start.20 = (f32[128,2048]{1,0:T(8,128)S(1)}, f32[128,2048]{1,0:T(8,128)S(1)}, u32[]{:S(2)}, u32[]{:S(2)}) collective-permute-start(f32[128,2048]{1,0:T(8,128)S(1)} %pad_maximum_fusion.mine), channel_id=1, source_target_pairs={{0,16},{16,0},{1,17},{17,1},{2,18},{18,2},{3,19},{19,3},{4,20},{20... | collective-permute-start | bytes 3145736 | tf_op jit(solution)/shard_map/ppermute | solution.py:167
  69.6 19.2 %collective-permute-start.21 = (bf16[128,1536]{1,0:T(8,128)(2,1)S(1)}, bf16[128,1536]{1,0:T(8,128)(2,1)S(1)}, u32[]{:S(2)}, u32[]{:S(2)}) collective-permute-start(bf16[128,1536]{1,0:T(8,128)(2,1)S(1)} %maximum_select_fusion.2), channel_id=1, source_target_pairs={{0,4},{4,0},{8,12},{12,8},{1,5},{5,1},{9,13},{13,9},{2,6},{6,2},{1... | collective-permute-start | bytes 1179656 | tf_op jit(solution)/shard_map/ppermute | solution.py:170
  73.5 15.2 %collective-permute-start.24 = (bf16[256,512]{1,0:T(8,128)(2,1)S(1)}, bf16[256,512]{1,0:T(8,128)(2,1)S(1)}, u32[]{:S(2)}, u32[]{:S(2)}) collective-permute-start(bf16[256,512]{1,0:T(8,128)(2,1)S(1)} %get-tuple-element.120), channel_id=1, source_target_pairs={{0,8},{4,12},{8,0},{12,4},{1,9},{5,13},{9,1},{13,5},{2,10},{6,14},... | collective-permute-start | bytes 786440 | tf_op jit(solution)/shard_map/ppermute | solution.py:204
  74.3 14.9 %collective-permute-start.23 = (f32[256,512]{1,0:T(8,128)S(1)}, f32[256,512]{1,0:T(8,128)S(1)}, u32[]{:S(2)}, u32[]{:S(2)}) collective-permute-start(f32[256,512]{1,0:T(8,128)S(1)} %get-tuple-element.121.key_mine), channel_id=1, source_target_pairs={{0,16},{16,0},{1,17},{17,1},{2,18},{18,2},{3,19},{19,3},{4,20},{20... | collective-permute-start | bytes 1572872 | tf_op jit(solution)/shard_map/ppermute | solution.py:167
  88.7 2.1 %collective-permute-start.22 = (bf16[128,1536]{1,0:T(8,128)(2,1)S(1)}, bf16[128,1536]{1,0:T(8,128)(2,1)S(1)}, u32[]{:S(2)}, u32[]{:S(2)}) collective-permute-start(bf16[128,1536]{1,0:T(8,128)(2,1)S(1)} %collective-permute-done.21.last), channel_id=1, source_target_pairs={{0,16},{16,0},{1,17},{17,1},{2,18},{18,2},{3,19},{19,3},{4,20},{20... | collective-permute-start | bytes 1179656 | tf_op jit(solution)/shard_map/ppermute | solution.py:167
  88.7 2.1 %collective-permute-start.25 = (bf16[256,512]{1,0:T(8,128)(2,1)S(1)}, bf16[256,512]{1,0:T(8,128)(2,1)S(1)}, u32[]{:S(2)}, u32[]{:S(2)}) collective-permute-start(bf16[256,512]{1,0:T(8,128)(2,1)S(1)} %collective-permute-done.24.key_last), channel_id=1, source_target_pairs={{0,16},{16,0},{1,17},{17,1},{2,18},{18,2},{3,19},{19,3},{4,20},{20... | collective-permute-start | bytes 786440 | tf_op jit(solution)/shard_map/ppermute | solution.py:167
